TPU v7x, 32 devices: a whole 2x2x4 slice. The times are simulated.
32 devices in a mesh: groups: 2 (over y), gx: 16 (over z, x, core).
Axes of the slice: x: 2, y: 2, z: 4, core: 2. Of those that a mesh axis runs over, the one named last changes fastest.
Arguments:
- x_vec: float32 [1024, 8, 128], P(('groups', 'gx')), parts along dimension 0, may hold values from -6 to 6
- r_vec: float32 [1024, 8, 128], P(('groups', 'gx')), parts along dimension 0, may hold values from -40 to 40
- q_vec: float32 [1024, 8, 128], P(('groups', 'gx')), parts along dimension 0, may hold values from -40 to 40
- d_vec: float32 [1024, 8, 128], P(('groups', 'gx')), parts along dimension 0, may hold values from -6 to 6
- diag_blocks: bfloat16 [1024, 128, 128], P(('groups', 'gx')), parts along dimension 0, may hold values from -4 to 4
- off_blocks: bfloat16 [1024, 9, 128, 128], P(('groups', 'gx')), parts along dimension 0, may hold values from -1 to 1
- columns: int32 [1024, 9], P(('groups', 'gx')), parts along dimension 0, may hold values from 0 to 127
- colours: int32 [1024], P(('groups', 'gx')), parts along dimension 0, may hold values from 0 to 3
- factor_inv: bfloat16 [1024, 128, 128], P(('groups', 'gx')), parts along dimension 0, may hold values from -1 to 1, as said below
- pivot_diag: float32 [1024, 128], P(('groups', 'gx')), parts along dimension 0, may hold values from -2 to 2, as said below
- pivot_off: float32 [1024, 64], P(('groups', 'gx')), parts along dimension 0, may hold values from -1 to 1
- pivot_pairs: int32 [1024, 64], P(('groups', 'gx')), parts along dimension 0, may hold values 0 or 1
- face_lists: int32 [32, 6, 16], P(('groups', 'gx')), parts along dimension 0, may hold values from 0 to 31, as said below
- rho_prev: float32 [16], P('groups'), parts along dimension 0, may hold values from 0.5 to 2
- tau_prev: float32 [16], P('groups'), parts along dimension 0, may hold values from 0.5 to 2
- theta_prev: float32 [16], P('groups'), parts along dimension 0, may hold values from 0.2 to 2
Outputs:
- x_new: float32 [1024, 8, 128], P(('groups', 'gx')), parts along dimension 0
- r_new: float32 [1024, 8, 128], P(('groups', 'gx')), parts along dimension 0
- q_new: float32 [1024, 8, 128], P(('groups', 'gx')), parts along dimension 0
- d_new: float32 [1024, 8, 128], P(('groups', 'gx')), parts along dimension 0
- step_scalars: float32 [3, 16], P(None, 'groups'), parts along dimension 1
There are 2 independent parts, one for each index of `groups`. A program takes and returns all parts, laid end to end along the dimension named above; each array names one. Nothing has to cross between parts.
Inputs may be any that keep to these rules, and one draw needn't show every extreme that they name: `columns`: column values below 32 name a block of the same tile; a value 32 + f * 16 + s names entry s of face list f of the tile that face f reaches. `face_lists`: each face list holds 16 different local block numbers of its tile. `factor_inv`: unit lower triangular: ones on the diagonal, zeros above it. `pivot_diag`: entries at even positions are positive, at odd positions negative; magnitudes 0.5 to 2.
All inputs are finite; a program needn't handle non-finite values. No bound on the sum of `pivot_pairs` on one device may be relied on, other than what follows from the above.
Results may differ from a plain program's by a relative error of at most 0.0053.
Values may be sent and summed in bfloat16 or wider, within the bound.
No kernel may reach another device: no remote copies, remote signals or barrier semaphores. Data moves between devices by JAX's collectives and lax.ppermute only.
A program may use at most 64 MiB of HBM per device.

v0:
```python
import jax
import jax.numpy as jnp
from jax import lax
from jax.sharding import PartitionSpec as P

OFFSETS = (1, -1, 4, -4, 16, -16)


def passed_along(array, axis, by):
    devices = lax.axis_size(axis)
    pairs = [(i, i + by) for i in range(devices) if 0 <= i + by < devices]
    return lax.ppermute(array, axis, pairs)


def pivot_solve(values, pivot_diag, pivot_off, pivot_pairs):
    rows, count, width = values.shape
    half = width // 2
    pairs = values.reshape(rows, count, half, 2)
    first, second = (pairs[..., 0], pairs[..., 1])
    diag = pivot_diag.reshape(rows, 1, half, 2)
    d_one, d_two = (diag[..., 0], diag[..., 1])
    off = pivot_off[:, None, :]
    paired = pivot_pairs[:, None, :] == 1
    det = d_one * d_two - off * off
    out_one = jnp.where(paired, (d_two * first - off * second) / det, first / d_one)
    out_two = jnp.where(paired, (d_one * second - off * first) / det, second / d_two)
    return jnp.stack([out_one, out_two], axis=-1).reshape(rows, count, width)


def per_device(
    x_vec,
    r_vec,
    q_vec,
    d_vec,
    diag_blocks,
    off_blocks,
    columns,
    colours,
    factor_inv,
    pivot_diag,
    pivot_off,
    pivot_pairs,
    face_lists,
    rho_prev,
    tau_prev,
    theta_prev,
):
    tiles = lax.axis_size("gx")
    place = lax.axis_index("gx")
    tz = place % 4
    ty = place // 4 % 4
    tx = place // 16
    conds = (tz != 0, tz != 3, ty != 0, ty != 3, tx != 0, tx != tiles // 16 - 1)
    present = [cond.astype(jnp.bfloat16) for cond in conds]
    own_lists = face_lists[0]

    def extended(values):
        pieces = [values]
        for face in range(6):
            picked = jnp.take(values, own_lists[face], axis=0)
            arrived = passed_along(picked, "gx", OFFSETS[face])
            pieces.append(arrived * present[face])
        return jnp.concatenate(pieces, axis=0)

    def couple(values):
        gathered = jnp.take(extended(values), columns, axis=0)
        return jnp.einsum(
            "iknb,ikab->ina", gathered, off_blocks, preferred_element_type=jnp.float32
        )

    def apply_dinv(vector):
        first = jnp.einsum(
            "inb,iab->ina",
            vector.astype(jnp.bfloat16),
            factor_inv,
            preferred_element_type=jnp.float32,
        )
        middle = pivot_solve(first, pivot_diag, pivot_off, pivot_pairs).astype(jnp.bfloat16)
        return jnp.einsum("inb,iba->ina", middle, factor_inv, preferred_element_type=jnp.float32)

    count = float(q_vec.shape[0] * q_vec.shape[2] * tiles)
    q_bf = q_vec.astype(jnp.bfloat16)
    image = jnp.einsum(
        "inb,iab->ina", q_bf, diag_blocks, preferred_element_type=jnp.float32
    ) + couple(q_bf)
    local_qt = jnp.sum(q_vec * image, axis=(0, 2))
    first_sums = (local_qt,)
    summed = lax.psum((first_sums[0],), "gx")
    sigma = summed[0] / count
    sigma_safe = jnp.where(sigma >= 0, jnp.maximum(sigma, 0.5), jnp.minimum(sigma, -0.5))
    alpha = rho_prev / sigma_safe
    r_new = r_vec - alpha[None, :, None] * image
    local_sq = jnp.sum(r_new * r_new, axis=(0, 2))
    norm_sq = lax.psum(local_sq, "gx") / count
    sweep = jnp.zeros_like(r_new)
    for colour in range(4):
        chosen = (colours == colour)[:, None, None]
        if colour == 0:
            remaining = r_new
        else:
            remaining = r_new - couple(sweep.astype(jnp.bfloat16))
        sweep = jnp.where(chosen, apply_dinv(remaining), sweep)
    back = jnp.where((colours == 3)[:, None, None], sweep, 0.0)
    for colour in (2, 1, 0):
        chosen = (colours == colour)[:, None, None]
        update = sweep - apply_dinv(couple(back.astype(jnp.bfloat16)))
        back = jnp.where(chosen, update, back)
    local_rho = jnp.sum(r_new * back, axis=(0, 2))
    closing_terms = (local_rho,)
    ended = lax.psum((closing_terms[0],), "gx")
    rho_new = ended[0] / count
    theta = jnp.sqrt(norm_sq + 1e-06) / tau_prev
    csq = 1.0 / (1.0 + theta * theta)
    tau_new = tau_prev * theta * jnp.sqrt(csq)
    d_new = (csq * theta_prev * theta_prev)[None, :, None] * d_vec + (csq * alpha)[
        None, :, None
    ] * q_vec
    x_new = x_vec + d_new
    beta = rho_new / rho_prev
    q_new = back + beta[None, :, None] * q_vec
    return (x_new, r_new, q_new, d_new, jnp.stack([rho_new, tau_new, theta]))


def solution(mesh):
    placed = (
        P(("groups", "gx"), None, None),
        P(("groups", "gx"), None, None),
        P(("groups", "gx"), None, None),
        P(("groups", "gx"), None, None),
        P(("groups", "gx"), None, None),
        P(("groups", "gx"), None, None, None),
        P(("groups", "gx"), None),
        P(("groups", "gx")),
        P(("groups", "gx"), None, None),
        P(("groups", "gx"), None),
        P(("groups", "gx"), None),
        P(("groups", "gx"), None),
        P(("groups", "gx"), None, None),
        P("groups"),
        P("groups"),
        P("groups"),
    )
    return jax.shard_map(
        per_device,
        mesh=mesh,
        in_specs=placed,
        out_specs=(
            P(("groups", "gx"), None, None),
            P(("groups", "gx"), None, None),
            P(("groups", "gx"), None, None),
            P(("groups", "gx"), None, None),
            P(None, "groups"),
        ),
        check_vma=False,
    )
```

profile of v0, /device:TPU:0, one launch (start us, length us, event | category | flops | bytes accessed | tf_op | source)
XLA Modules:
  0.0 258.3 jit_solution(58246147330633298)
XLA Ops:
  0.7 0.9 compare_and_fusion.1
  1.6 0.9 constant_dynamic-update-slice_fusion.6
  3.2 2.4 collective-permute-start
  6.2 1.3 collective-permute-start.1
  8.2 7.7 %collective-permute-start.2 = (bf16[16,8,128]{2,1,0:T(8,128)(2,1)S(1)}, bf16[16,8,128]{2,1,0:T(8,128)(2,1)S(1)}, u32[]{:S(2)}, u32[]{:S(2)}) collective-permute-start(bf16[16,8,128]{2,1,0:T(8,128)(2,1)S(1)} %broadcast_select_fusion.27), channel_id=1, source_target_pairs={{0,4},{1,5},{2,6},{3,7},{4,8},{5,9},{6,10},{7,11},{8,12},{9,13},{1... | collective-permute-start | bytes 98312 | tf_op jit(solution)/shard_map/ppermute | solution.py:12
  16.6 1.3 collective-permute-start.3
  18.6 0.7 collective-permute-start.4
  19.3 0.7 compare_and_fusion
  20.0 0.7 compare_select_fusion
  20.7 0.7 broadcast_compare_fusion.3
  21.4 0.7 broadcast_compare_fusion
  22.3 0.8 copy.37
  23.1 0.8 copy.31
  24.9 0.7 collective-permute-start.5
  25.8 1.9 gather_fusion.6
  27.7 5.4 %convolution_bitcast_fusion.6 = f32[32,8,128]{2,1,0:T(8,128)S(1)} fusion(bf16[32,9,128,128]{3,2,1,0:T(8,128)(2,1)} %param.25, bf16[32,9,8,128]{3,2,1,0:T(8,128)(2,1)S(1)} %bitcast.147, pred[32,9]{1,0:T(8,128)(4,1)S(1)} %copy.28), kind=kOutput, calls=%fused_computation.69 | convolution fusion | flops 75792384 | bytes 10158368 | tf_op jit(solution)/shard_map/iknb,ikab->ina/dot_general | solution.py:67
  33.0 0.8 multiply_reduce_fusion.2
  33.8 32.0 %psum.21 = f32[8]{0:T(128)S(1)} all-reduce(f32[8]{0:T(128)S(1)} %get-tuple-element.77), channel_id=1, replica_groups=mesh['groups'=2,'gx'=16] {'gx'}, use_global_device_ids=true, to_apply=%region_1.4 | all-reduce | flops 8 | bytes 64 | tf_op jit(solution)/shard_map/psum | solution.py:88
  71.6 1.3 collective-permute-start.6
  73.0 1.3 collective-permute-start.7
  74.3 1.3 collective-permute-start.8
  75.6 1.3 collective-permute-start.9
  78.3 3.3 %collective-permute-done.9 = bf16[16,8,128]{2,1,0:T(8,128)(2,1)S(1)} collective-permute-done((bf16[16,8,128]{2,1,0:T(8,128)(2,1)S(1)}, bf16[16,8,128]{2,1,0:T(8,128)(2,1)S(1)}, u32[]{:S(2)}, u32[]{:S(2)}) %collective-permute-start.9) | collective-permute-done | bytes 32800 | tf_op jit(solution)/shard_map/ppermute | solution.py:12
  81.7 1.9 gather_fusion.13
  83.6 5.9 %fusion.17 = f32[32,8,128]{2,1,0:T(8,128)S(1)} fusion(bf16[32,128,128]{2,1,0:T(8,128)(2,1)S(1)} %copy-done, f32[32,8,128]{2,1,0:T(8,128)S(1)} %multiply_subtract_fusion, bf16[32,9,128,128]{3,2,1,0:T(8,128)(2,1)} %param.25, bf16[32,9,8,128]{3,2,1,0:T(8,128)(2,1)S(1)} %bitcast.148, pred[32,9]{1,0:T(8,128)(4,1)S(1)} %copy.28), kind=kOutput, calls=%fused_computation.81 | convolution fusion | flops 84246528 | bytes 11338016 | tf_op jit(solution)/shard_map/inb,iab->ina/dot_general | solution.py:72
  94.5 2.0 collective-permute-start.12
  96.6 1.3 collective-permute-start.13
  97.9 4.6 %collective-permute-start.14 = (bf16[16,8,128]{2,1,0:T(8,128)(2,1)S(1)}, bf16[16,8,128]{2,1,0:T(8,128)(2,1)S(1)}, u32[]{:S(2)}, u32[]{:S(2)}) collective-permute-start(bf16[16,8,128]{2,1,0:T(8,128)(2,1)S(1)} %broadcast_select_fusion.25), channel_id=1, source_target_pairs={{0,4},{1,5},{2,6},{3,7},{4,8},{5,9},{6,10},{7,11},{8,12},{9,13},{1... | collective-permute-start | bytes 98312 | tf_op jit(solution)/shard_map/ppermute | solution.py:12
  102.5 1.3 collective-permute-start.15
  105.2 3.1 %collective-permute-done.15 = bf16[16,8,128]{2,1,0:T(8,128)(2,1)S(1)} collective-permute-done((bf16[16,8,128]{2,1,0:T(8,128)(2,1)S(1)}, bf16[16,8,128]{2,1,0:T(8,128)(2,1)S(1)}, u32[]{:S(2)}, u32[]{:S(2)}) %collective-permute-start.15) | collective-permute-done | bytes 32800 | tf_op jit(solution)/shard_map/ppermute | solution.py:12
  108.4 1.9 gather_fusion.20
  110.3 5.9 %fusion.16 = f32[32,8,128]{2,1,0:T(8,128)S(1)} fusion(bf16[32,128,128]{2,1,0:T(8,128)(2,1)S(1)} %copy-done, f32[32,8,128]{2,1,0:T(8,128)S(1)} %multiply_subtract_fusion, bf16[32,9,128,128]{3,2,1,0:T(8,128)(2,1)} %param.25, bf16[32,9,8,128]{3,2,1,0:T(8,128)(2,1)S(1)} %bitcast.149, pred[32,9]{1,0:T(8,128)(4,1)S(1)} %copy.28), kind=kOutput, calls=%fused_computation.80 | convolution fusion | flops 84246528 | bytes 11338016 | tf_op jit(solution)/shard_map/inb,iab->ina/dot_general | solution.py:72
  121.2 1.3 collective-permute-start.18
  122.6 1.3 collective-permute-start.19
  123.9 6.7 %collective-permute-start.20 = (bf16[16,8,128]{2,1,0:T(8,128)(2,1)S(1)}, bf16[16,8,128]{2,1,0:T(8,128)(2,1)S(1)}, u32[]{:S(2)}, u32[]{:S(2)}) collective-permute-start(bf16[16,8,128]{2,1,0:T(8,128)(2,1)S(1)} %broadcast_select_fusion.24), channel_id=1, source_target_pairs={{0,4},{1,5},{2,6},{3,7},{4,8},{5,9},{6,10},{7,11},{8,12},{9,13},{1... | collective-permute-start | bytes 98312 | tf_op jit(solution)/shard_map/ppermute | solution.py:12
  130.6 1.3 collective-permute-start.21
  131.9 0.8 collective-permute-start.22
  133.5 2.9 %collective-permute-done.21 = bf16[16,8,128]{2,1,0:T(8,128)(2,1)S(1)} collective-permute-done((bf16[16,8,128]{2,1,0:T(8,128)(2,1)S(1)}, bf16[16,8,128]{2,1,0:T(8,128)(2,1)S(1)}, u32[]{:S(2)}, u32[]{:S(2)}) %collective-permute-start.21) | collective-permute-done | bytes 32800 | tf_op jit(solution)/shard_map/ppermute | solution.py:12
  136.5 1.9 gather_fusion.27
  138.3 5.9 %fusion.15 = f32[32,8,128]{2,1,0:T(8,128)S(1)} fusion(bf16[32,128,128]{2,1,0:T(8,128)(2,1)S(1)} %copy-done, f32[32,8,128]{2,1,0:T(8,128)S(1)} %multiply_subtract_fusion, bf16[32,9,128,128]{3,2,1,0:T(8,128)(2,1)} %param.25, bf16[32,9,8,128]{3,2,1,0:T(8,128)(2,1)S(1)} %bitcast.150, pred[32,9]{1,0:T(8,128)(4,1)S(1)} %copy.28), kind=kOutput, calls=%fused_computation.79 | convolution fusion | flops 84246528 | bytes 11338016 | tf_op jit(solution)/shard_map/inb,iab->ina/dot_general | solution.py:72
  149.3 1.3 collective-permute-start.24
  150.6 1.3 collective-permute-start.25
  151.9 6.1 %collective-permute-start.26 = (bf16[16,8,128]{2,1,0:T(8,128)(2,1)S(1)}, bf16[16,8,128]{2,1,0:T(8,128)(2,1)S(1)}, u32[]{:S(2)}, u32[]{:S(2)}) collective-permute-start(bf16[16,8,128]{2,1,0:T(8,128)(2,1)S(1)} %broadcast_select_fusion.23), channel_id=1, source_target_pairs={{0,4},{1,5},{2,6},{3,7},{4,8},{5,9},{6,10},{7,11},{8,12},{9,13},{1... | collective-permute-start | bytes 98312 | tf_op jit(solution)/shard_map/ppermute | solution.py:12
  158.0 1.3 collective-permute-start.27
  160.8 3.1 %collective-permute-done.27 = bf16[16,8,128]{2,1,0:T(8,128)(2,1)S(1)} collective-permute-done((bf16[16,8,128]{2,1,0:T(8,128)(2,1)S(1)}, bf16[16,8,128]{2,1,0:T(8,128)(2,1)S(1)}, u32[]{:S(2)}, u32[]{:S(2)}) %collective-permute-start.27) | collective-permute-done | bytes 32800 | tf_op jit(solution)/shard_map/ppermute | solution.py:12
  163.9 1.9 gather_fusion.34
  165.8 5.9 %fusion.14 = f32[32,8,128]{2,1,0:T(8,128)S(1)} fusion(bf16[32,128,128]{2,1,0:T(8,128)(2,1)S(1)} %copy-done, bf16[32,9,128,128]{3,2,1,0:T(8,128)(2,1)} %param.25, bf16[32,9,8,128]{3,2,1,0:T(8,128)(2,1)S(1)} %bitcast.151, pred[32,9]{1,0:T(8,128)(4,1)S(1)} %copy.28), kind=kOutput, calls=%fused_computation.78 | convolution fusion | flops 84213760 | bytes 11206944 | tf_op jit(solution)/shard_map/inb,iab->ina/dot_general | solution.py:72
  176.7 1.3 collective-permute-start.30
  178.1 1.3 collective-permute-start.31
  179.4 5.8 %collective-permute-start.32 = (bf16[16,8,128]{2,1,0:T(8,128)(2,1)S(1)}, bf16[16,8,128]{2,1,0:T(8,128)(2,1)S(1)}, u32[]{:S(2)}, u32[]{:S(2)}) collective-permute-start(bf16[16,8,128]{2,1,0:T(8,128)(2,1)S(1)} %broadcast_select_fusion.22), channel_id=1, source_target_pairs={{0,4},{1,5},{2,6},{3,7},{4,8},{5,9},{6,10},{7,11},{8,12},{9,13},{1... | collective-permute-start | bytes 98312 | tf_op jit(solution)/shard_map/ppermute | solution.py:12
  185.2 1.3 collective-permute-start.33
  188.0 3.1 %collective-permute-done.33 = bf16[16,8,128]{2,1,0:T(8,128)(2,1)S(1)} collective-permute-done((bf16[16,8,128]{2,1,0:T(8,128)(2,1)S(1)}, bf16[16,8,128]{2,1,0:T(8,128)(2,1)S(1)}, u32[]{:S(2)}, u32[]{:S(2)}) %collective-permute-start.33) | collective-permute-done | bytes 32800 | tf_op jit(solution)/shard_map/ppermute | solution.py:12
  191.1 1.9 gather_fusion.41
  193.0 5.9 %fusion.13 = f32[32,8,128]{2,1,0:T(8,128)S(1)} fusion(bf16[32,128,128]{2,1,0:T(8,128)(2,1)S(1)} %copy-done, bf16[32,9,128,128]{3,2,1,0:T(8,128)(2,1)} %param.25, bf16[32,9,8,128]{3,2,1,0:T(8,128)(2,1)S(1)} %bitcast.152, pred[32,9]{1,0:T(8,128)(4,1)S(1)} %copy.28), kind=kOutput, calls=%fused_computation.77 | convolution fusion | flops 84213760 | bytes 11206944 | tf_op jit(solution)/shard_map/inb,iab->ina/dot_general | solution.py:72
  204.0 1.3 collective-permute-start.36
  205.4 1.3 collective-permute-start.37
  206.7 5.8 %collective-permute-start.38 = (bf16[16,8,128]{2,1,0:T(8,128)(2,1)S(1)}, bf16[16,8,128]{2,1,0:T(8,128)(2,1)S(1)}, u32[]{:S(2)}, u32[]{:S(2)}) collective-permute-start(bf16[16,8,128]{2,1,0:T(8,128)(2,1)S(1)} %broadcast_select_fusion.21), channel_id=1, source_target_pairs={{0,4},{1,5},{2,6},{3,7},{4,8},{5,9},{6,10},{7,11},{8,12},{9,13},{1... | collective-permute-start | bytes 98312 | tf_op jit(solution)/shard_map/ppermute | solution.py:12
  212.5 1.3 collective-permute-start.39
  214.4 0.9 collective-permute-start.41
  215.4 2.9 %collective-permute-done.39 = bf16[16,8,128]{2,1,0:T(8,128)(2,1)S(1)} collective-permute-done((bf16[16,8,128]{2,1,0:T(8,128)(2,1)S(1)}, bf16[16,8,128]{2,1,0:T(8,128)(2,1)S(1)}, u32[]{:S(2)}, u32[]{:S(2)}) %collective-permute-start.39) | collective-permute-done | bytes 32800 | tf_op jit(solution)/shard_map/ppermute | solution.py:12
  218.4 1.9 gather_fusion.48
  220.2 5.9 %fusion.12 = f32[32,8,128]{2,1,0:T(8,128)S(1)} fusion(bf16[32,128,128]{2,1,0:T(8,128)(2,1)S(1)} %copy-done, bf16[32,9,128,128]{3,2,1,0:T(8,128)(2,1)} %param.25, bf16[32,9,8,128]{3,2,1,0:T(8,128)(2,1)S(1)} %bitcast.146, pred[32,9]{1,0:T(8,128)(4,1)S(1)} %copy.28), kind=kOutput, calls=%fused_computation.76 | convolution fusion | flops 84213760 | bytes 11206944 | tf_op jit(solution)/shard_map/inb,iab->ina/dot_general | solution.py:72
  227.4 29.5 %all-reduce = (f32[8]{0:T(128)S(1)}, f32[8]{0:T(128)S(1)}) all-reduce(f32[8]{0:T(128)S(1)} %get-tuple-element.8, f32[8]{0:T(128)S(1)} %get-tuple-element.7), channel_id=1, replica_groups=mesh['groups'=2,'gx'=16] {'gx'}, use_global_device_ids=true, to_apply=%region_3.6 | all-reduce | flops 16 | bytes 128 | tf_op jit(solution)/shard_map/psum | solution.py:94
  257.5 0.8 fusion.73
  (248 shorter events, 44.8 us)
Async XLA Ops:
  0.6 65.3 %copy-start = (bf16[32,128,128]{2,1,0:T(8,128)(2,1)S(1)}, bf16[32,128,128]{2,1,0:T(8,128)(2,1)}, u32[]{:S(2)}) copy-start(bf16[32,128,128]{2,1,0:T(8,128)(2,1)} %param.28) | copy-start | bytes 3145732
  0.6 32.4 %copy-start.2 = (f32[32,8,128]{2,1,0:T(8,128)S(1)}, f32[32,8,128]{2,1,0:T(8,128)}, u32[]{:S(2)}) copy-start(f32[32,8,128]{2,1,0:T(8,128)} %param.22) | copy-start | bytes 393220
  0.7 32.4 %copy-start.3 = (bf16[32,128,128]{2,1,0:T(8,128)(2,1)S(1)}, bf16[32,128,128]{2,1,0:T(8,128)(2,1)}, u32[]{:S(2)}) copy-start(bf16[32,128,128]{2,1,0:T(8,128)(2,1)} %param.24) | copy-start | bytes 3145732
  0.7 65.2 %copy-start.4 = (f32[32,8,128]{2,1,0:T(8,128)S(1)}, f32[32,8,128]{2,1,0:T(8,128)}, u32[]{:S(2)}) copy-start(f32[32,8,128]{2,1,0:T(8,128)} %param.21) | copy-start | bytes 393220
  3.2 21.8 %collective-permute-start = (bf16[16,8,128]{2,1,0:T(8,128)(2,1)S(1)}, bf16[16,8,128]{2,1,0:T(8,128)(2,1)S(1)}, u32[]{:S(2)}, u32[]{:S(2)}) collective-permute-start(bf16[16,8,128]{2,1,0:T(8,128)(2,1)S(1)} %broadcast_select_fusion.41), channel_id=1, source_target_pairs={{0,1},{1,2},{2,3},{3,4},{4,5},{5,6},{6,7},{7,8},{8,9},{9,10},{10,1... | collective-permute-start | bytes 98312 | tf_op jit(solution)/shard_map/ppermute | solution.py:12
  6.2 19.4 %collective-permute-start.1 = (bf16[16,8,128]{2,1,0:T(8,128)(2,1)S(1)}, bf16[16,8,128]{2,1,0:T(8,128)(2,1)S(1)}, u32[]{:S(2)}, u32[]{:S(2)}) collective-permute-start(bf16[16,8,128]{2,1,0:T(8,128)(2,1)S(1)} %broadcast_select_fusion.34), channel_id=1, source_target_pairs={{1,0},{2,1},{3,2},{4,3},{5,4},{6,5},{7,6},{8,7},{9,8},{10,9},{11,1... | collective-permute-start | bytes 98312 | tf_op jit(solution)/shard_map/ppermute | solution.py:12
  8.2 17.5 %collective-permute-start.2 = (bf16[16,8,128]{2,1,0:T(8,128)(2,1)S(1)}, bf16[16,8,128]{2,1,0:T(8,128)(2,1)S(1)}, u32[]{:S(2)}, u32[]{:S(2)}) collective-permute-start(bf16[16,8,128]{2,1,0:T(8,128)(2,1)S(1)} %broadcast_select_fusion.27), channel_id=1, source_target_pairs={{0,4},{1,5},{2,6},{3,7},{4,8},{5,9},{6,10},{7,11},{8,12},{9,13},{1... | collective-permute-start | bytes 98312 | tf_op jit(solution)/shard_map/ppermute | solution.py:12
  16.6 9.1 %collective-permute-start.3 = (bf16[16,8,128]{2,1,0:T(8,128)(2,1)S(1)}, bf16[16,8,128]{2,1,0:T(8,128)(2,1)S(1)}, u32[]{:S(2)}, u32[]{:S(2)}) collective-permute-start(bf16[16,8,128]{2,1,0:T(8,128)(2,1)S(1)} %broadcast_select_fusion.20), channel_id=1, source_target_pairs={{4,0},{5,1},{6,2},{7,3},{8,4},{9,5},{10,6},{11,7},{12,8},{13,9},{1... | collective-permute-start | bytes 98312 | tf_op jit(solution)/shard_map/ppermute | solution.py:12
  18.6 7.1 %collective-permute-start.4 = (bf16[16,8,128]{2,1,0:T(8,128)(2,1)S(1)}, bf16[16,8,128]{2,1,0:T(8,128)(2,1)S(1)}, u32[]{:S(2)}, u32[]{:S(2)}) collective-permute-start(bf16[16,8,128]{2,1,0:T(8,128)(2,1)S(1)} %broadcast_select_fusion.13), channel_id=1, source_target_pairs={} | collective-permute-start | bytes 98312 | tf_op jit(solution)/shard_map/ppermute | solution.py:12
  24.9 0.8 collective-permute-start.5
  25.8 40.0 %copy-start.8 = (f32[8]{0:T(128)S(1)}, f32[8]{0:T(128)}, u32[]{:S(2)}) copy-start(f32[8]{0:T(128)} %param.33) | copy-start | bytes 100
  65.9 160.9 %copy-start.1 = (f32[32,8,128]{2,1,0:T(8,128)}, f32[32,8,128]{2,1,0:T(8,128)S(1)}, u32[]{:S(2)}) copy-start(f32[32,8,128]{2,1,0:T(8,128)S(1)} %multiply_subtract_fusion) | copy-start | bytes 393220
  71.6 6.0 %collective-permute-start.6 = (bf16[16,8,128]{2,1,0:T(8,128)(2,1)S(1)}, bf16[16,8,128]{2,1,0:T(8,128)(2,1)S(1)}, u32[]{:S(2)}, u32[]{:S(2)}) collective-permute-start(bf16[16,8,128]{2,1,0:T(8,128)(2,1)S(1)} %broadcast_select_fusion.40), channel_id=1, source_target_pairs={{0,1},{1,2},{2,3},{3,4},{4,5},{5,6},{6,7},{7,8},{8,9},{9,10},{10,1... | collective-permute-start | bytes 98312 | tf_op jit(solution)/shard_map/ppermute | solution.py:12
  73.0 5.3 %collective-permute-start.7 = (bf16[16,8,128]{2,1,0:T(8,128)(2,1)S(1)}, bf16[16,8,128]{2,1,0:T(8,128)(2,1)S(1)}, u32[]{:S(2)}, u32[]{:S(2)}) collective-permute-start(bf16[16,8,128]{2,1,0:T(8,128)(2,1)S(1)} %broadcast_select_fusion.33), channel_id=1, source_target_pairs={{1,0},{2,1},{3,2},{4,3},{5,4},{6,5},{7,6},{8,7},{9,8},{10,9},{11,1... | collective-permute-start | bytes 98312 | tf_op jit(solution)/shard_map/ppermute | solution.py:12
  74.3 4.0 %collective-permute-start.8 = (bf16[16,8,128]{2,1,0:T(8,128)(2,1)S(1)}, bf16[16,8,128]{2,1,0:T(8,128)(2,1)S(1)}, u32[]{:S(2)}, u32[]{:S(2)}) collective-permute-start(bf16[16,8,128]{2,1,0:T(8,128)(2,1)S(1)} %broadcast_select_fusion.26), channel_id=1, source_target_pairs={{0,4},{1,5},{2,6},{3,7},{4,8},{5,9},{6,10},{7,11},{8,12},{9,13},{1... | collective-permute-start | bytes 98312 | tf_op jit(solution)/shard_map/ppermute | solution.py:12
  75.6 6.0 %collective-permute-start.9 = (bf16[16,8,128]{2,1,0:T(8,128)(2,1)S(1)}, bf16[16,8,128]{2,1,0:T(8,128)(2,1)S(1)}, u32[]{:S(2)}, u32[]{:S(2)}) collective-permute-start(bf16[16,8,128]{2,1,0:T(8,128)(2,1)S(1)} %broadcast_select_fusion.19), channel_id=1, source_target_pairs={{4,0},{5,1},{6,2},{7,3},{8,4},{9,5},{10,6},{11,7},{12,8},{13,9},{1... | collective-permute-start | bytes 98312 | tf_op jit(solution)/shard_map/ppermute | solution.py:12
  76.9 4.7 %collective-permute-start.10 = (bf16[16,8,128]{2,1,0:T(8,128)(2,1)S(1)}, bf16[16,8,128]{2,1,0:T(8,128)(2,1)S(1)}, u32[]{:S(2)}, u32[]{:S(2)}) collective-permute-start(bf16[16,8,128]{2,1,0:T(8,128)(2,1)S(1)} %broadcast_select_fusion.12), channel_id=1, source_target_pairs={} | collective-permute-start | bytes 98312 | tf_op jit(solution)/shard_map/ppermute | solution.py:12
  77.6 4.1 %collective-permute-start.11 = (bf16[16,8,128]{2,1,0:T(8,128)(2,1)S(1)}, bf16[16,8,128]{2,1,0:T(8,128)(2,1)S(1)}, u32[]{:S(2)}, u32[]{:S(2)}) collective-permute-start(bf16[16,8,128]{2,1,0:T(8,128)(2,1)S(1)} %broadcast_select_fusion.5), channel_id=1, source_target_pairs={} | collective-permute-start | bytes 98312 | tf_op jit(solution)/shard_map/ppermute | solution.py:12
  94.5 10.0 %collective-permute-start.12 = (bf16[16,8,128]{2,1,0:T(8,128)(2,1)S(1)}, bf16[16,8,128]{2,1,0:T(8,128)(2,1)S(1)}, u32[]{:S(2)}, u32[]{:S(2)}) collective-permute-start(bf16[16,8,128]{2,1,0:T(8,128)(2,1)S(1)} %broadcast_select_fusion.39), channel_id=1, source_target_pairs={{0,1},{1,2},{2,3},{3,4},{4,5},{5,6},{6,7},{7,8},{8,9},{9,10},{10,1... | collective-permute-start | bytes 98312 | tf_op jit(solution)/shard_map/ppermute | solution.py:12
  96.6 8.6 %collective-permute-start.13 = (bf16[16,8,128]{2,1,0:T(8,128)(2,1)S(1)}, bf16[16,8,128]{2,1,0:T(8,128)(2,1)S(1)}, u32[]{:S(2)}, u32[]{:S(2)}) collective-permute-start(bf16[16,8,128]{2,1,0:T(8,128)(2,1)S(1)} %broadcast_select_fusion.32), channel_id=1, source_target_pairs={{1,0},{2,1},{3,2},{4,3},{5,4},{6,5},{7,6},{8,7},{9,8},{10,9},{11,1... | collective-permute-start | bytes 98312 | tf_op jit(solution)/shard_map/ppermute | solution.py:12
  97.9 7.3 %collective-permute-start.14 = (bf16[16,8,128]{2,1,0:T(8,128)(2,1)S(1)}, bf16[16,8,128]{2,1,0:T(8,128)(2,1)S(1)}, u32[]{:S(2)}, u32[]{:S(2)}) collective-permute-start(bf16[16,8,128]{2,1,0:T(8,128)(2,1)S(1)} %broadcast_select_fusion.25), channel_id=1, source_target_pairs={{0,4},{1,5},{2,6},{3,7},{4,8},{5,9},{6,10},{7,11},{8,12},{9,13},{1... | collective-permute-start | bytes 98312 | tf_op jit(solution)/shard_map/ppermute | solution.py:12
  102.5 5.8 %collective-permute-start.15 = (bf16[16,8,128]{2,1,0:T(8,128)(2,1)S(1)}, bf16[16,8,128]{2,1,0:T(8,128)(2,1)S(1)}, u32[]{:S(2)}, u32[]{:S(2)}) collective-permute-start(bf16[16,8,128]{2,1,0:T(8,128)(2,1)S(1)} %broadcast_select_fusion.18), channel_id=1, source_target_pairs={{4,0},{5,1},{6,2},{7,3},{8,4},{9,5},{10,6},{11,7},{12,8},{13,9},{1... | collective-permute-start | bytes 98312 | tf_op jit(solution)/shard_map/ppermute | solution.py:12
  103.8 4.5 %collective-permute-start.16 = (bf16[16,8,128]{2,1,0:T(8,128)(2,1)S(1)}, bf16[16,8,128]{2,1,0:T(8,128)(2,1)S(1)}, u32[]{:S(2)}, u32[]{:S(2)}) collective-permute-start(bf16[16,8,128]{2,1,0:T(8,128)(2,1)S(1)} %broadcast_select_fusion.11), channel_id=1, source_target_pairs={} | collective-permute-start | bytes 98312 | tf_op jit(solution)/shard_map/ppermute | solution.py:12
  104.5 3.9 %collective-permute-start.17 = (bf16[16,8,128]{2,1,0:T(8,128)(2,1)S(1)}, bf16[16,8,128]{2,1,0:T(8,128)(2,1)S(1)}, u32[]{:S(2)}, u32[]{:S(2)}) collective-permute-start(bf16[16,8,128]{2,1,0:T(8,128)(2,1)S(1)} %broadcast_select_fusion.4), channel_id=1, source_target_pairs={} | collective-permute-start | bytes 98312 | tf_op jit(solution)/shard_map/ppermute | solution.py:12
  121.2 11.5 %collective-permute-start.18 = (bf16[16,8,128]{2,1,0:T(8,128)(2,1)S(1)}, bf16[16,8,128]{2,1,0:T(8,128)(2,1)S(1)}, u32[]{:S(2)}, u32[]{:S(2)}) collective-permute-start(bf16[16,8,128]{2,1,0:T(8,128)(2,1)S(1)} %broadcast_select_fusion.38), channel_id=1, source_target_pairs={{0,1},{1,2},{2,3},{3,4},{4,5},{5,6},{6,7},{7,8},{8,9},{9,10},{10,1... | collective-permute-start | bytes 98312 | tf_op jit(solution)/shard_map/ppermute | solution.py:12
  122.6 10.8 %collective-permute-start.19 = (bf16[16,8,128]{2,1,0:T(8,128)(2,1)S(1)}, bf16[16,8,128]{2,1,0:T(8,128)(2,1)S(1)}, u32[]{:S(2)}, u32[]{:S(2)}) collective-permute-start(bf16[16,8,128]{2,1,0:T(8,128)(2,1)S(1)} %broadcast_select_fusion.31), channel_id=1, source_target_pairs={{1,0},{2,1},{3,2},{4,3},{5,4},{6,5},{7,6},{8,7},{9,8},{10,9},{11,1... | collective-permute-start | bytes 98312 | tf_op jit(solution)/shard_map/ppermute | solution.py:12
  123.9 9.6 %collective-permute-start.20 = (bf16[16,8,128]{2,1,0:T(8,128)(2,1)S(1)}, bf16[16,8,128]{2,1,0:T(8,128)(2,1)S(1)}, u32[]{:S(2)}, u32[]{:S(2)}) collective-permute-start(bf16[16,8,128]{2,1,0:T(8,128)(2,1)S(1)} %broadcast_select_fusion.24), channel_id=1, source_target_pairs={{0,4},{1,5},{2,6},{3,7},{4,8},{5,9},{6,10},{7,11},{8,12},{9,13},{1... | collective-permute-start | bytes 98312 | tf_op jit(solution)/shard_map/ppermute | solution.py:12
  130.6 5.8 %collective-permute-start.21 = (bf16[16,8,128]{2,1,0:T(8,128)(2,1)S(1)}, bf16[16,8,128]{2,1,0:T(8,128)(2,1)S(1)}, u32[]{:S(2)}, u32[]{:S(2)}) collective-permute-start(bf16[16,8,128]{2,1,0:T(8,128)(2,1)S(1)} %broadcast_select_fusion.17), channel_id=1, source_target_pairs={{4,0},{5,1},{6,2},{7,3},{8,4},{9,5},{10,6},{11,7},{12,8},{13,9},{1... | collective-permute-start | bytes 98312 | tf_op jit(solution)/shard_map/ppermute | solution.py:12
  131.9 4.5 %collective-permute-start.22 = (bf16[16,8,128]{2,1,0:T(8,128)(2,1)S(1)}, bf16[16,8,128]{2,1,0:T(8,128)(2,1)S(1)}, u32[]{:S(2)}, u32[]{:S(2)}) collective-permute-start(bf16[16,8,128]{2,1,0:T(8,128)(2,1)S(1)} %broadcast_select_fusion.10), channel_id=1, source_target_pairs={} | collective-permute-start | bytes 98312 | tf_op jit(solution)/shard_map/ppermute | solution.py:12
  132.7 3.7 %collective-permute-start.23 = (bf16[16,8,128]{2,1,0:T(8,128)(2,1)S(1)}, bf16[16,8,128]{2,1,0:T(8,128)(2,1)S(1)}, u32[]{:S(2)}, u32[]{:S(2)}) collective-permute-start(bf16[16,8,128]{2,1,0:T(8,128)(2,1)S(1)} %broadcast_select_fusion.3), channel_id=1, source_target_pairs={} | collective-permute-start | bytes 98312 | tf_op jit(solution)/shard_map/ppermute | solution.py:12
  149.3 10.7 %collective-permute-start.24 = (bf16[16,8,128]{2,1,0:T(8,128)(2,1)S(1)}, bf16[16,8,128]{2,1,0:T(8,128)(2,1)S(1)}, u32[]{:S(2)}, u32[]{:S(2)}) collective-permute-start(bf16[16,8,128]{2,1,0:T(8,128)(2,1)S(1)} %broadcast_select_fusion.37), channel_id=1, source_target_pairs={{0,1},{1,2},{2,3},{3,4},{4,5},{5,6},{6,7},{7,8},{8,9},{9,10},{10,1... | collective-permute-start | bytes 98312 | tf_op jit(solution)/shard_map/ppermute | solution.py:12
  150.6 10.1 %collective-permute-start.25 = (bf16[16,8,128]{2,1,0:T(8,128)(2,1)S(1)}, bf16[16,8,128]{2,1,0:T(8,128)(2,1)S(1)}, u32[]{:S(2)}, u32[]{:S(2)}) collective-permute-start(bf16[16,8,128]{2,1,0:T(8,128)(2,1)S(1)} %broadcast_select_fusion.30), channel_id=1, source_target_pairs={{1,0},{2,1},{3,2},{4,3},{5,4},{6,5},{7,6},{8,7},{9,8},{10,9},{11,1... | collective-permute-start | bytes 98312 | tf_op jit(solution)/shard_map/ppermute | solution.py:12
  151.9 8.8 %collective-permute-start.26 = (bf16[16,8,128]{2,1,0:T(8,128)(2,1)S(1)}, bf16[16,8,128]{2,1,0:T(8,128)(2,1)S(1)}, u32[]{:S(2)}, u32[]{:S(2)}) collective-permute-start(bf16[16,8,128]{2,1,0:T(8,128)(2,1)S(1)} %broadcast_select_fusion.23), channel_id=1, source_target_pairs={{0,4},{1,5},{2,6},{3,7},{4,8},{5,9},{6,10},{7,11},{8,12},{9,13},{1... | collective-permute-start | bytes 98312 | tf_op jit(solution)/shard_map/ppermute | solution.py:12
  158.0 5.8 %collective-permute-start.27 = (bf16[16,8,128]{2,1,0:T(8,128)(2,1)S(1)}, bf16[16,8,128]{2,1,0:T(8,128)(2,1)S(1)}, u32[]{:S(2)}, u32[]{:S(2)}) collective-permute-start(bf16[16,8,128]{2,1,0:T(8,128)(2,1)S(1)} %broadcast_select_fusion.16), channel_id=1, source_target_pairs={{4,0},{5,1},{6,2},{7,3},{8,4},{9,5},{10,6},{11,7},{12,8},{13,9},{1... | collective-permute-start | bytes 98312 | tf_op jit(solution)/shard_map/ppermute | solution.py:12
  159.3 4.5 %collective-permute-start.28 = (bf16[16,8,128]{2,1,0:T(8,128)(2,1)S(1)}, bf16[16,8,128]{2,1,0:T(8,128)(2,1)S(1)}, u32[]{:S(2)}, u32[]{:S(2)}) collective-permute-start(bf16[16,8,128]{2,1,0:T(8,128)(2,1)S(1)} %broadcast_select_fusion.9), channel_id=1, source_target_pairs={} | collective-permute-start | bytes 98312 | tf_op jit(solution)/shard_map/ppermute | solution.py:12
  160.0 3.9 %collective-permute-start.29 = (bf16[16,8,128]{2,1,0:T(8,128)(2,1)S(1)}, bf16[16,8,128]{2,1,0:T(8,128)(2,1)S(1)}, u32[]{:S(2)}, u32[]{:S(2)}) collective-permute-start(bf16[16,8,128]{2,1,0:T(8,128)(2,1)S(1)} %broadcast_select_fusion.2), channel_id=1, source_target_pairs={} | collective-permute-start | bytes 98312 | tf_op jit(solution)/shard_map/ppermute | solution.py:12
  176.7 10.5 %collective-permute-start.30 = (bf16[16,8,128]{2,1,0:T(8,128)(2,1)S(1)}, bf16[16,8,128]{2,1,0:T(8,128)(2,1)S(1)}, u32[]{:S(2)}, u32[]{:S(2)}) collective-permute-start(bf16[16,8,128]{2,1,0:T(8,128)(2,1)S(1)} %broadcast_select_fusion.36), channel_id=1, source_target_pairs={{0,1},{1,2},{2,3},{3,4},{4,5},{5,6},{6,7},{7,8},{8,9},{9,10},{10,1... | collective-permute-start | bytes 98312 | tf_op jit(solution)/shard_map/ppermute | solution.py:12
  178.1 9.8 %collective-permute-start.31 = (bf16[16,8,128]{2,1,0:T(8,128)(2,1)S(1)}, bf16[16,8,128]{2,1,0:T(8,128)(2,1)S(1)}, u32[]{:S(2)}, u32[]{:S(2)}) collective-permute-start(bf16[16,8,128]{2,1,0:T(8,128)(2,1)S(1)} %broadcast_select_fusion.29), channel_id=1, source_target_pairs={{1,0},{2,1},{3,2},{4,3},{5,4},{6,5},{7,6},{8,7},{9,8},{10,9},{11,1... | collective-permute-start | bytes 98312 | tf_op jit(solution)/shard_map/ppermute | solution.py:12
  179.4 8.5 %collective-permute-start.32 = (bf16[16,8,128]{2,1,0:T(8,128)(2,1)S(1)}, bf16[16,8,128]{2,1,0:T(8,128)(2,1)S(1)}, u32[]{:S(2)}, u32[]{:S(2)}) collective-permute-start(bf16[16,8,128]{2,1,0:T(8,128)(2,1)S(1)} %broadcast_select_fusion.22), channel_id=1, source_target_pairs={{0,4},{1,5},{2,6},{3,7},{4,8},{5,9},{6,10},{7,11},{8,12},{9,13},{1... | collective-permute-start | bytes 98312 | tf_op jit(solution)/shard_map/ppermute | solution.py:12
  185.2 5.8 %collective-permute-start.33 = (bf16[16,8,128]{2,1,0:T(8,128)(2,1)S(1)}, bf16[16,8,128]{2,1,0:T(8,128)(2,1)S(1)}, u32[]{:S(2)}, u32[]{:S(2)}) collective-permute-start(bf16[16,8,128]{2,1,0:T(8,128)(2,1)S(1)} %broadcast_select_fusion.15), channel_id=1, source_target_pairs={{4,0},{5,1},{6,2},{7,3},{8,4},{9,5},{10,6},{11,7},{12,8},{13,9},{1... | collective-permute-start | bytes 98312 | tf_op jit(solution)/shard_map/ppermute | solution.py:12
  186.5 4.5 %collective-permute-start.34 = (bf16[16,8,128]{2,1,0:T(8,128)(2,1)S(1)}, bf16[16,8,128]{2,1,0:T(8,128)(2,1)S(1)}, u32[]{:S(2)}, u32[]{:S(2)}) collective-permute-start(bf16[16,8,128]{2,1,0:T(8,128)(2,1)S(1)} %broadcast_select_fusion.8), channel_id=1, source_target_pairs={} | collective-permute-start | bytes 98312 | tf_op jit(solution)/shard_map/ppermute | solution.py:12
  187.2 3.9 %collective-permute-start.35 = (bf16[16,8,128]{2,1,0:T(8,128)(2,1)S(1)}, bf16[16,8,128]{2,1,0:T(8,128)(2,1)S(1)}, u32[]{:S(2)}, u32[]{:S(2)}) collective-permute-start(bf16[16,8,128]{2,1,0:T(8,128)(2,1)S(1)} %broadcast_select_fusion.1), channel_id=1, source_target_pairs={} | collective-permute-start | bytes 98312 | tf_op jit(solution)/shard_map/ppermute | solution.py:12
  199.6 57.3 %copy-start.7 = (f32[8]{0:T(128)S(1)}, f32[8]{0:T(128)}, u32[]{:S(2)}) copy-start(f32[8]{0:T(128)} %param.34) | copy-start | bytes 100
  199.6 57.2 %copy-start.9 = (f32[8]{0:T(128)S(1)}, f32[8]{0:T(128)}, u32[]{:S(2)}) copy-start(f32[8]{0:T(128)} %param.33) | copy-start | bytes 100
  199.6 57.3 %copy-start.10 = (f32[8]{0:T(128)S(1)}, f32[8]{0:T(128)}, u32[]{:S(2)}) copy-start(f32[8]{0:T(128)} %param.35) | copy-start | bytes 100
  199.6 57.9 %copy-start.5 = (f32[32,8,128]{2,1,0:T(8,128)S(1)}, f32[32,8,128]{2,1,0:T(8,128)}, u32[]{:S(2)}) copy-start(f32[32,8,128]{2,1,0:T(8,128)} %param.20) | copy-start | bytes 393220
  199.7 57.8 %copy-start.6 = (f32[32,8,128]{2,1,0:T(8,128)S(1)}, f32[32,8,128]{2,1,0:T(8,128)}, u32[]{:S(2)}) copy-start(f32[32,8,128]{2,1,0:T(8,128)} %param.23) | copy-start | bytes 393220
  204.0 10.5 %collective-permute-start.36 = (bf16[16,8,128]{2,1,0:T(8,128)(2,1)S(1)}, bf16[16,8,128]{2,1,0:T(8,128)(2,1)S(1)}, u32[]{:S(2)}, u32[]{:S(2)}) collective-permute-start(bf16[16,8,128]{2,1,0:T(8,128)(2,1)S(1)} %broadcast_select_fusion.35), channel_id=1, source_target_pairs={{0,1},{1,2},{2,3},{3,4},{4,5},{5,6},{6,7},{7,8},{8,9},{9,10},{10,1... | collective-permute-start | bytes 98312 | tf_op jit(solution)/shard_map/ppermute | solution.py:12
  205.4 10.0 %collective-permute-start.37 = (bf16[16,8,128]{2,1,0:T(8,128)(2,1)S(1)}, bf16[16,8,128]{2,1,0:T(8,128)(2,1)S(1)}, u32[]{:S(2)}, u32[]{:S(2)}) collective-permute-start(bf16[16,8,128]{2,1,0:T(8,128)(2,1)S(1)} %broadcast_select_fusion.28), channel_id=1, source_target_pairs={{1,0},{2,1},{3,2},{4,3},{5,4},{6,5},{7,6},{8,7},{9,8},{10,9},{11,1... | collective-permute-start | bytes 98312 | tf_op jit(solution)/shard_map/ppermute | solution.py:12
  206.7 8.7 %collective-permute-start.38 = (bf16[16,8,128]{2,1,0:T(8,128)(2,1)S(1)}, bf16[16,8,128]{2,1,0:T(8,128)(2,1)S(1)}, u32[]{:S(2)}, u32[]{:S(2)}) collective-permute-start(bf16[16,8,128]{2,1,0:T(8,128)(2,1)S(1)} %broadcast_select_fusion.21), channel_id=1, source_target_pairs={{0,4},{1,5},{2,6},{3,7},{4,8},{5,9},{6,10},{7,11},{8,12},{9,13},{1... | collective-permute-start | bytes 98312 | tf_op jit(solution)/shard_map/ppermute | solution.py:12
  212.5 5.8 %collective-permute-start.39 = (bf16[16,8,128]{2,1,0:T(8,128)(2,1)S(1)}, bf16[16,8,128]{2,1,0:T(8,128)(2,1)S(1)}, u32[]{:S(2)}, u32[]{:S(2)}) collective-permute-start(bf16[16,8,128]{2,1,0:T(8,128)(2,1)S(1)} %broadcast_select_fusion.14), channel_id=1, source_target_pairs={{4,0},{5,1},{6,2},{7,3},{8,4},{9,5},{10,6},{11,7},{12,8},{13,9},{1... | collective-permute-start | bytes 98312 | tf_op jit(solution)/shard_map/ppermute | solution.py:12
  213.8 4.5 %collective-permute-start.40 = (bf16[16,8,128]{2,1,0:T(8,128)(2,1)S(1)}, bf16[16,8,128]{2,1,0:T(8,128)(2,1)S(1)}, u32[]{:S(2)}, u32[]{:S(2)}) collective-permute-start(bf16[16,8,128]{2,1,0:T(8,128)(2,1)S(1)} %broadcast_select_fusion.7), channel_id=1, source_target_pairs={} | collective-permute-start | bytes 98312 | tf_op jit(solution)/shard_map/ppermute | solution.py:12
  214.4 3.9 %collective-permute-start.41 = (bf16[16,8,128]{2,1,0:T(8,128)(2,1)S(1)}, bf16[16,8,128]{2,1,0:T(8,128)(2,1)S(1)}, u32[]{:S(2)}, u32[]{:S(2)}) collective-permute-start(bf16[16,8,128]{2,1,0:T(8,128)(2,1)S(1)} %broadcast_select_fusion), channel_id=1, source_target_pairs={} | collective-permute-start | bytes 98312 | tf_op jit(solution)/shard_map/ppermute | solution.py:12
where the time goes:
time: 260 us; the launch traced here: 258 us
  starting transfers between devices  76.5 us (29%)
  blocking collectives  61.5 us (24%)
  matrix products  44.9 us (17%)
  local copies, waits for them, and re-layouts  42.6 us (16%)
  waiting for transfers between devices  18.4 us (7%)
  other arithmetic  12.2 us (5%)
    ppermute x42, starting transfers between devices, passed_along(): return lax.ppermute(array, axis, pairs)  76.5 us
    dot_general x7, matrix products, apply_dinv(): jnp.einsum('inb,iab->ina', vector.astype(jnp.bfloat16), factor_inv, prefe...  36 us
    psum x1, blocking collectives, per_device(): summed = lax.psum((first_sums[0],), 'gx')  32 us
    psum x1, blocking collectives, per_device(): norm_sq = lax.psum(local_sq, 'gx') / count  29.5 us
    gather x42, local copies, waits for them, and re-layouts, extended(): picked = jnp.take(values, own_lists[face], axis=0)  24.1 us
    ppermute x42, waiting for transfers between devices, passed_along(): return lax.ppermute(array, axis, pairs)  18.4 us
    gather x7, local copies, waits for them, and re-layouts, couple(): gathered = jnp.take(extended(values), columns, axis=0)  13 us
    dot_general x1, matrix products, couple(): jnp.einsum('iknb,ikab->ina', gathered, off_blocks, preferred_element_type...  5.35 us
  transfers between devices with their start and end apart: 42, of which 6 were waited for; matrix products, arithmetic and copies ran while one was open for 4% of the time, Pallas kernels for 0%

commit v1 on v0

v1 whole, which is shorter than its diff:
```python
import functools

import jax
import jax.numpy as jnp
from jax import lax
from jax.experimental import pallas as pl
from jax.experimental.pallas import tpu as pltpu
from jax.sharding import PartitionSpec as P

F32 = jnp.float32
BF16 = jnp.bfloat16
VMEM = pltpu.VMEM
SMEM = pltpu.SMEM
SIDE = 4
UNROLL = 4


def swap_pairs(stride, extent, phase, tiles):
    pairs = []
    for tile in range(tiles):
        place = tile // stride % extent
        if place % 2 == phase and place + 1 < extent:
            pairs += [(tile, tile + stride), (tile + stride, tile)]
    return pairs


def swaps_of(tiles):
    swaps = []
    for axis, (stride, extent) in enumerate(((1, SIDE), (SIDE, SIDE), (16, tiles // 16))):
        for phase in range(2):
            pairs = swap_pairs(stride, extent, phase, tiles)
            if pairs:
                swaps.append((axis, phase, pairs))
    return swaps


def going_up(axis, phase):
    place = lax.axis_index("gx") // (1, SIDE, 16)[axis]
    return jnp.where(lax.rem(place, 2) == phase, 1, 0)


def send_faces(swaps, state, faces, sent):
    for (axis, phase, _), out in zip(swaps, sent):
        face = 2 * axis + 1 - going_up(axis, phase)
        for slot in range(0, 16, 2):
            two = [state[faces[0, face, slot + j]] for j in range(2)]
            rows = pl.ds(slot * 8, 16)
            out[rows, :] = jnp.concatenate(two, axis=0).astype(BF16)


def take_faces(swaps, arrived, extended):
    for (axis, phase, _), piece in zip(swaps, arrived):
        face = 2 * axis + going_up(axis, phase)
        extended[pl.ds(32 + face * 16, 16)] = piece[...].astype(F32).reshape(16, 8, 128)


def dot_t(left, right):
    return lax.dot_general(left, right, (((1,), (1,)), ((), ())), preferred_element_type=F32)


def coupled(block, extended, off, columns):
    total = None
    for k in range(9):
        term = dot_t(extended[columns[block, k]].astype(BF16), off[block, k])
        total = term if total is None else total + term
    return total


def solved(block, vector, factor, straight, crossed):
    matrix = factor[block]
    first = dot_t(vector.astype(BF16), matrix)
    lane = lax.broadcasted_iota(jnp.int32, first.shape, 1)
    other = jnp.where(lane % 2 == 0, pltpu.roll(first, 127, 1), pltpu.roll(first, 1, 1))
    row = pl.ds(block, 1)
    middle = straight[row, :] * first + crossed[row, :] * other
    return jnp.dot(middle.astype(BF16), matrix, preferred_element_type=F32)


def for_colour(colour, tables, body):
    count = tables[4, colour]

    def step(group, carry):
        body([tables[colour, group * UNROLL + j] for j in range(UNROLL)])
        return carry

    lax.fori_loop(0, (count + UNROLL - 1) // UNROLL, step, 0)


def first_kernel(swaps, q_ref, faces_in, faces, *sent):
    for face in range(6):
        for slot in range(16):
            faces[0, face, slot] = faces_in[0, face, slot]
    send_faces(swaps, q_ref, faces_in, sent)


def setup_kernel(columns_in, colours_in, diag_ref, off_ref, pairs_ref, columns, tables, straight, crossed):
    def copy_row(row, carry):
        for k in range(9):
            columns[row, k] = columns_in[row, k]
        return carry

    lax.fori_loop(0, 32, copy_row, 0)
    for colour in range(4):
        count = jnp.int32(0)
        for block in range(32):
            tables[colour, count] = block
            count = count + jnp.where(colours_in[block] == colour, 1, 0)
        last = tables[colour, jnp.maximum(count - 1, 0)]
        for j in range(UNROLL):
            tables[colour, count + j] = last
        tables[4, colour] = count
    half = lax.broadcasted_iota(jnp.int32, (64, 128), 0)
    lane = lax.broadcasted_iota(jnp.int32, (64, 128), 1)
    spread = jnp.where(lane // 2 == half, 1.0, 0.0).astype(F32)
    off = jnp.dot(off_ref[...], spread, precision=lax.Precision.HIGHEST, preferred_element_type=F32)
    paired = jnp.dot(
        pairs_ref[...].astype(F32), spread, precision=lax.Precision.HIGHEST, preferred_element_type=F32
    )
    own = diag_ref[...]
    even = lax.broadcasted_iota(jnp.int32, own.shape, 1) % 2 == 0
    other = jnp.where(even, pltpu.roll(own, 127, 1), pltpu.roll(own, 1, 1))
    det = own * other - off * off
    straight[...] = jnp.where(paired > 0.5, other / det, 1.0 / own)
    crossed[...] = jnp.where(paired > 0.5, -off / det, 0.0)


def image_kernel(swaps, tiles, q_ref, diag, off, columns, *refs):
    arrived, (image, partial, extended) = refs[: len(swaps)], refs[len(swaps) :]
    extended[pl.ds(0, 32)] = q_ref[...].astype(BF16).astype(F32)
    extended[pl.ds(32, 96)] = jnp.zeros((96, 8, 128), F32)
    take_faces(swaps, arrived, extended)

    def step(group, total):
        for j in range(UNROLL):
            block = group * UNROLL + j
            value = dot_t(extended[block].astype(BF16), diag[block])
            value = value + coupled(block, extended, off, columns)
            image[block] = value
            total = total + q_ref[block] * value
        return total

    total = lax.fori_loop(0, 32 // UNROLL, step, jnp.zeros((8, 128), F32))
    for tile in range(tiles):
        partial[tile] = total


def column_of(values):
    row = lax.broadcasted_iota(jnp.int32, (8, 128), 0)
    out = jnp.zeros((8, 128), F32)
    for n in range(8):
        out = jnp.where(row == n, values[n], out)
    return out


def start_kernel(
    swaps, count, sums, r_ref, image, rho, factor, straight, crossed, tables, faces, r_new, w, norm, alpha, *sent
):
    sigma = jnp.sum(jnp.sum(sums[...], axis=0), axis=1, keepdims=True) / count
    sigma = jnp.where(sigma >= 0, jnp.maximum(sigma, 0.5), jnp.minimum(sigma, -0.5))
    step_size = column_of(rho) / sigma
    alpha[...] = step_size
    new = r_ref[...] - step_size[None] * image[...]
    r_new[...] = new
    norm[...] = jnp.sum(new * new, axis=0)
    w[...] = jnp.zeros_like(w)

    def body(blocks):
        values = [solved(b, r_new[b], factor, straight, crossed) for b in blocks]
        for b, value in zip(blocks, values):
            w[b] = value

    for_colour(0, tables, body)
    send_faces(swaps, w, faces, sent)


def forward_kernel(swaps, colour, r_new, w_in, off, factor, straight, crossed, columns, tables, faces, *refs):
    n = len(swaps)
    arrived, w, sent, extended = refs[:n], refs[n], refs[n + 1 : -1], refs[-1]
    w[...] = w_in[...]
    extended[pl.ds(0, 32)] = w_in[...].astype(BF16).astype(F32)
    extended[pl.ds(32, 96)] = jnp.zeros((96, 8, 128), F32)
    take_faces(swaps, arrived, extended)

    def body(blocks):
        rest = [r_new[b] - coupled(b, extended, off, columns) for b in blocks]
        values = [solved(b, s, factor, straight, crossed) for b, s in zip(blocks, rest)]
        for b, value in zip(blocks, values):
            w[b] = value

    for_colour(colour, tables, body)
    if colour == 3:
        z = sent[0]
        z[...] = jnp.zeros_like(z)

        def copy(blocks):
            for b in blocks:
                z[b] = w[b]

        for_colour(3, tables, copy)
        send_faces(swaps, z, faces, sent[1:])
    else:
        send_faces(swaps, w, faces, sent)


def backward_kernel(swaps, tiles, colour, w, z_in, off, factor, straight, crossed, columns, tables, faces, *refs):
    n = len(swaps)
    arrived, rest = refs[:n], refs[n:]
    if colour == 0:
        r_new, norm, z, partial, extended = rest
    else:
        z, sent, extended = rest[0], rest[1:-1], rest[-1]
    z[...] = z_in[...]
    extended[pl.ds(0, 32)] = z_in[...].astype(BF16).astype(F32)
    extended[pl.ds(32, 96)] = jnp.zeros((96, 8, 128), F32)
    take_faces(swaps, arrived, extended)

    def body(blocks):
        sums = [coupled(b, extended, off, columns) for b in blocks]
        values = [w[b] - solved(b, s, factor, straight, crossed) for b, s in zip(blocks, sums)]
        for b, value in zip(blocks, values):
            z[b] = value

    for_colour(colour, tables, body)
    if colour == 0:
        rho = jnp.sum(r_new[...] * z[...], axis=0)
        both = jnp.concatenate([rho, norm[...]], axis=0)
        for tile in range(tiles):
            partial[tile] = both
    else:
        send_faces(swaps, z, faces, sent)


def last_kernel(count, sums, z, q_ref, x_ref, d_ref, alpha, rho, tau, theta_in, x_new, q_new, d_new, scalars):
    both = jnp.sum(jnp.sum(sums[...], axis=0), axis=1, keepdims=True) / count
    rho_new = both[:8] + jnp.zeros((8, 128), F32)
    norm = both[8:]
    tau_old = column_of(tau)
    theta_old = column_of(theta_in)
    theta = jnp.sqrt(norm + 1e-06) / tau_old
    csq = 1.0 / (1.0 + theta * theta)
    tau_new = tau_old * theta * jnp.sqrt(csq)
    beta = rho_new / column_of(rho)
    q_old = q_ref[...]
    d = (csq * theta_old * theta_old)[None] * d_ref[...] + (csq * alpha[...])[None] * q_old
    d_new[...] = d
    x_new[...] = x_ref[...] + d
    q_new[...] = z[...] + beta[None] * q_old
    row = lax.broadcasted_iota(jnp.int32, (8, 128), 0)
    lane = lax.broadcasted_iota(jnp.int32, (8, 128), 1)
    for index, value in enumerate((rho_new, tau_new, theta)):
        line = jnp.sum(jnp.where(row == lane, value, 0.0), axis=0, keepdims=True)
        scalars[pl.ds(index, 1), :] = line[:, :8]


def vec(*shape, dtype=F32):
    return jax.ShapeDtypeStruct(shape, dtype)


def call(body, outs, places, scratch=()):
    return pl.pallas_call(
        body,
        out_shape=outs,
        in_specs=[pl.BlockSpec(memory_space=place) for place in places],
        out_specs=[pl.BlockSpec(memory_space=getattr(out, "memory_space", VMEM)) for out in outs],
        scratch_shapes=list(scratch),
        compiler_params=pltpu.CompilerParams(vmem_limit_bytes=16 * 2**20),
    )


def per_device(
    x_vec,
    r_vec,
    q_vec,
    d_vec,
    diag_blocks,
    off_blocks,
    columns,
    colours,
    factor_inv,
    pivot_diag,
    pivot_off,
    pivot_pairs,
    face_lists,
    rho_prev,
    tau_prev,
    theta_prev,
):
    tiles = lax.axis_size("gx")
    swaps = swaps_of(tiles)
    n = len(swaps)
    count = float(q_vec.shape[0] * q_vec.shape[2] * tiles)
    block_vec = vec(32, 8, 128)
    pieces = [vec(128, 128, dtype=BF16)] * n
    scratch = [VMEM((128, 8, 128), F32)]

    def exchange(sent):
        return [lax.ppermute(piece, "gx", pairs) for piece, (_, _, pairs) in zip(sent, swaps)]

    faces, *sent = call(
        functools.partial(first_kernel, swaps),
        [SMEM((1, 6, 16), jnp.int32)] + pieces,
        [VMEM, SMEM],
    )(q_vec, face_lists)
    arrived = exchange(sent)
    columns, tables, straight, crossed = call(
        setup_kernel,
        [SMEM((32, 9), jnp.int32), SMEM((8, 128), jnp.int32), vec(32, 128), vec(32, 128)],
        [SMEM, SMEM, VMEM, VMEM, VMEM],
    )(columns, colours, pivot_diag, pivot_off, pivot_pairs)
    image, partial = call(
        functools.partial(image_kernel, swaps, tiles),
        [block_vec, vec(tiles, 8, 128)],
        [VMEM] * 3 + [SMEM] + [VMEM] * n,
        scratch,
    )(q_vec, diag_blocks, off_blocks, columns, *arrived)
    sums = lax.all_to_all(partial, "gx", 0, 0, tiled=True)
    r_new, w, norm, alpha, *sent = call(
        functools.partial(start_kernel, swaps, count),
        [block_vec, block_vec, vec(8, 128), vec(8, 128)] + pieces,
        [VMEM] * 3 + [SMEM] + [VMEM] * 3 + [SMEM] * 2,
    )(sums, r_vec, image, rho_prev, factor_inv, straight, crossed, tables, faces)
    fixed = (off_blocks, factor_inv, straight, crossed, columns, tables, faces)
    fixed_places = [VMEM] * 4 + [SMEM] * 3
    for colour in (1, 2, 3):
        w, *sent = call(
            functools.partial(forward_kernel, swaps, colour),
            [block_vec] * (2 if colour == 3 else 1) + pieces,
            [VMEM] * 2 + fixed_places + [VMEM] * n,
            scratch,
        )(r_new, w, *fixed, *exchange(sent))
    z, *sent = sent
    for colour in (2, 1):
        z, *sent = call(
            functools.partial(backward_kernel, swaps, tiles, colour),
            [block_vec] + pieces,
            [VMEM] * 2 + fixed_places + [VMEM] * n,
            scratch,
        )(w, z, *fixed, *exchange(sent))
    z, partial = call(
        functools.partial(backward_kernel, swaps, tiles, 0),
        [block_vec, vec(tiles, 16, 128)],
        [VMEM] * 2 + fixed_places + [VMEM] * (n + 2),
        scratch,
    )(w, z, *fixed, *exchange(sent), r_new, norm)
    sums = lax.all_to_all(partial, "gx", 0, 0, tiled=True)
    x_new, q_new, d_new, scalars = call(
        functools.partial(last_kernel, count),
        [block_vec] * 3 + [vec(3, 8)],
        [VMEM] * 6 + [SMEM] * 3,
    )(sums, z, q_vec, x_vec, d_vec, alpha, rho_prev, tau_prev, theta_prev)
    return (x_new, r_new, q_new, d_new, scalars)


def solution(mesh):
    blocks = P(("groups", "gx"))
    return jax.shard_map(
        per_device,
        mesh=mesh,
        in_specs=(blocks,) * 13 + (P("groups"),) * 3,
        out_specs=(blocks,) * 4 + (P(None, "groups"),),
        check_vma=False,
    )
```

time: 260 us -> 139 us (0.53)
  matrix products: 44.9 us -> 0 us
  Pallas kernels: 0 us -> 35.9 us
  starting transfers between devices: 76.5 us -> 43.9 us
  local copies, waits for them, and re-layouts: 42.6 us -> 11.9 us
  blocking collectives: 61.5 us -> 37.3 us
  other arithmetic: 12.2 us -> 0 us
  waiting for transfers between devices: 18.4 us -> 7.69 us
    psum x2 -> x0, blocking collectives: 61.5 us -> none  [the longest x1 32 us: per_device(): summed = lax.psum((first_sums[0],), 'gx')]
    dot_general x16 -> x0, matrix products: 44.9 us -> none  [the longest x7 36 us: apply_dinv(): jnp.einsum('inb,iab->ina', vector.astype(jnp.bfloat16), factor_inv, prefe...]
    all_to_all x0 -> x2, blocking collectives: none -> 37.3 us  [per_device(): sums = lax.all_to_all(partial, 'gx', 0, 0, tiled=True)]
    gather x49 -> x0, local copies, waits for them, and re-layouts: 37.1 us -> none  [the longest x42 24.1 us: extended(): picked = jnp.take(values, own_lists[face], axis=0)]
    pallas_call x0 -> x11, Pallas kernels: none -> 35.9 us  [the longest x3 13.2 us: per_device(): call(functools.partial(forward_kernel, swaps, colour), [block_vec] * (2 i...]
    ppermute x42 -> x28, starting transfers between devices: 76.5 us -> 43.9 us  [exchange(): lax.ppermute(piece, 'gx', pairs)]
    ppermute x42 -> x28, waiting for transfers between devices: 18.4 us -> 7.69 us  [exchange(): lax.ppermute(piece, 'gx', pairs)]
    unnamed x24 -> x40, local copies, waits for them, and re-layouts: 1.69 us -> 11.9 us
  transfers between devices with their start and end apart: 42 -> 28, of which waited for: 6 -> 6; matrix products, arithmetic and copies ran while one was open for 4% -> 1% of each run, Pallas kernels for 0% -> 1%
where the time goes in v1:
time: 139 us; the launch traced here: 138 us
  starting transfers between devices  43.9 us (32%)
  blocking collectives  37.3 us (27%)
  Pallas kernels  35.9 us (26%)
  local copies, waits for them, and re-layouts  11.9 us (9%)
  waiting for transfers between devices  7.69 us (6%)
    ppermute x28, starting transfers between devices, exchange(): lax.ppermute(piece, 'gx', pairs)  43.9 us
    all_to_all x2, blocking collectives, per_device(): sums = lax.all_to_all(partial, 'gx', 0, 0, tiled=True)  37.3 us
    pallas_call x3, Pallas kernels, per_device(): call(functools.partial(forward_kernel, swaps, colour), [block_vec] * (2 i...  13.2 us
    unnamed x40, local copies, waits for them, and re-layouts  11.9 us
    pallas_call x2, Pallas kernels, per_device(): call(functools.partial(backward_kernel, swaps, tiles, colour), [block_vec...  8.26 us
    ppermute x28, waiting for transfers between devices, exchange(): lax.ppermute(piece, 'gx', pairs)  7.69 us
    pallas_call x1, Pallas kernels, per_device(): call(functools.partial(image_kernel, swaps, tiles), [block_vec, vec(tiles...  6.4 us
  transfers between devices with their start and end apart: 28, of which 6 were waited for; matrix products, arithmetic and copies ran while one was open for 1% of the time, Pallas kernels for 1%

profile of v1, /device:TPU:0, one launch (start us, length us, event | category | flops | bytes accessed | tf_op | source)
XLA Modules:
  0.0 137.7 jit_solution(17600227962656853728)
XLA Ops:
  0.6 0.7 copy.22.faces_in
  1.3 0.9 copy-done.5
  2.2 0.8 shard_map.192
  3.0 0.5 collective-permute-start
  3.5 0.7 collective-permute-start.1
  4.2 2.7 %collective-permute-start.2 = (bf16[128,128]{1,0:T(8,128)(2,1)S(1)}, bf16[128,128]{1,0:T(8,128)(2,1)S(1)}, u32[]{:S(2)}, u32[]{:S(2)}) collective-permute-start(bf16[128,128]{1,0:T(8,128)(2,1)S(1)} %get-tuple-element.59), channel_id=1, source_target_pairs={{0,4},{4,0},{1,5},{5,1},{2,6},{6,2},{3,7},{7,3},{8,12},{12,8},{9,1... | collective-permute-start | bytes 98312 | tf_op jit(solution)/shard_map/ppermute | solution.py:297
  6.9 0.7 collective-permute-start.3
  7.5 0.8 copy.21.columns_in
  8.3 0.7 copy-done.12
  9.0 0.7 copy-done.13
  9.7 0.7 copy-done.14
  10.4 0.7 copy-done.16
  11.1 1.7 %shard_map.191 = (s32[32,9]{1,0:T(8,128)S(4)}, s32[8,128]{1,0:T(8,128)S(4)}, f32[32,128]{1,0:T(8,128)S(1)}, f32[32,128]{1,0:T(8,128)S(1)}) custom-call(s32[32,9]{1,0:T(8,128)S(1)} %copy.21.columns_in, s32[32]{0:T(128)S(1)} %copy-done.16, f32[32,128]{1,0:T(8,128)S(1)} %copy-done.12, f32[32,64]{1,0:T(8,128)S(1)} %copy-done.13, s32[32,64]{1,0:T(8,128)S(1)} %copy-done.14), custom_call_target="tpu_custom_call" | custom-call | tf_op jit(solution)/shard_map/pallas_call | solution.py:305
  12.9 0.0 collective-permute-done.2.refs_2_
  12.9 0.0 copy-start
  12.9 3.7 %copy-done = bf16[32,9,128,128]{3,2,1,0:T(8,128)(2,1)S(1)} copy-done((bf16[32,9,128,128]{3,2,1,0:T(8,128)(2,1)S(1)}, bf16[32,9,128,128]{3,2,1,0:T(8,128)(2,1)}, u32[]{:S(2)}) %copy-start) | copy-done | bytes 9437208
  16.6 0.9 copy-done.6
  17.5 1.2 copy-done.8
  18.7 6.4 %shard_map.193 = (f32[32,8,128]{2,1,0:T(8,128)S(1)}, f32[16,8,128]{2,1,0:T(8,128)S(1)}) custom-call(f32[32,8,128]{2,1,0:T(8,128)S(1)} %copy-done.6, bf16[32,128,128]{2,1,0:T(8,128)(2,1)S(1)} %copy-done.8, bf16[32,9,128,128]{3,2,1,0:T(8,128)(2,1)S(1)} %copy-done, s32[32,9]{1,0:T(8,128)S(4)} %get-tuple-element.56.columns, ...), custom_call_target="tpu_custom_call" | custom-call | tf_op jit(solution)/shard_map/pallas_call | solution.py:310
  25.1 15.3 %all_to_all.10.sums = f32[16,8,128]{2,1,0:T(8,128)S(1)} all-to-all(f32[16,8,128]{2,1,0:T(8,128)S(1)} %get-tuple-element.61), channel_id=1, replica_groups=mesh['groups'=2,'gx'=16] {'gx'}, dimensions={0} | all-to-all | bytes 131072 | tf_op jit(solution)/shard_map/all_to_all | solution.py:316
  40.4 2.4 %shard_map.194 = (f32[32,8,128]{2,1,0:T(8,128)}, f32[32,8,128]{2,1,0:T(8,128)S(1)}, f32[8,128]{1,0:T(8,128)S(1)}, f32[8,128]{1,0:T(8,128)S(1)}, bf16[128,128]{1,...) custom-call(f32[16,8,128]{2,1,0:T(8,128)S(1)} %all_to_all.10.sums, ...), custom_call_target="tpu_custom_call" | custom-call | tf_op jit(solution)/shard_map/pallas_call | solution.py:317
  42.8 0.6 collective-permute-start.4
  43.3 0.7 collective-permute-start.5
  44.0 1.7 %collective-permute-start.6 = (bf16[128,128]{1,0:T(8,128)(2,1)S(1)}, bf16[128,128]{1,0:T(8,128)(2,1)S(1)}, u32[]{:S(2)}, u32[]{:S(2)}) collective-permute-start(bf16[128,128]{1,0:T(8,128)(2,1)S(1)} %get-tuple-element.71), channel_id=1, source_target_pairs={{0,4},{4,0},{1,5},{5,1},{2,6},{6,2},{3,7},{7,3},{8,12},{12,8},{9,1... | collective-permute-start | bytes 98312 | tf_op jit(solution)/shard_map/ppermute | solution.py:297
  45.7 0.7 collective-permute-start.7
  46.4 0.0 collective-permute-done.4.refs_0_
  46.4 1.6 %collective-permute-done.6.refs_2_ = bf16[128,128]{1,0:T(8,128)(2,1)S(1)} collective-permute-done((bf16[128,128]{1,0:T(8,128)(2,1)S(1)}, bf16[128,128]{1,0:T(8,128)(2,1)S(1)}, u32[]{:S(2)}, u32[]{:S(2)}) %collective-permute-start.6) | collective-permute-done | bytes 32800 | tf_op jit(solution)/shard_map/ppermute | solution.py:297
  48.0 0.9 copy-done.3
  48.9 3.3 %shard_map.195 = (f32[32,8,128]{2,1,0:T(8,128)S(1)}, bf16[128,128]{1,0:T(8,128)(2,1)S(1)}, bf16[128,128]{1,0:T(8,128)(2,1)S(1)}, bf16[128,128]{1,0:T(8,128)(2,1)S(1)}, bf16[128,128]{1,0:T(8,128)(2,1)S(1)}) custom-call(f32[32,8,128]{2,1,0:T(8,128)S(1)} %copy-done.3, f32[32,8,128]{2,1,0:T(8,128)S(1)} %get-tuple-element.68.w_in, ...), custom_call_target="tpu_custom_call" | custom-call | tf_op jit(solution)/shard_map/pallas_call | solution.py:325
  52.2 0.2 collective-permute-start.8
  52.4 0.7 collective-permute-start.9
  53.1 5.3 %collective-permute-start.10 = (bf16[128,128]{1,0:T(8,128)(2,1)S(1)}, bf16[128,128]{1,0:T(8,128)(2,1)S(1)}, u32[]{:S(2)}, u32[]{:S(2)}) collective-permute-start(bf16[128,128]{1,0:T(8,128)(2,1)S(1)} %get-tuple-element.76), channel_id=1, source_target_pairs={{0,4},{4,0},{1,5},{5,1},{2,6},{6,2},{3,7},{7,3},{8,12},{12,8},{9,1... | collective-permute-start | bytes 98312 | tf_op jit(solution)/shard_map/ppermute | solution.py:297
  58.4 0.7 collective-permute-start.11
  59.1 0.0 collective-permute-done.9.refs_1_
  59.1 1.2 collective-permute-done.10.refs_2_
  60.3 4.9 %shard_map.196 = (f32[32,8,128]{2,1,0:T(8,128)S(1)}, bf16[128,128]{1,0:T(8,128)(2,1)S(1)}, bf16[128,128]{1,0:T(8,128)(2,1)S(1)}, bf16[128,128]{1,0:T(8,128)(2,1)S(1)}, bf16[128,128]{1,0:T(8,128)(2,1)S(1)}) custom-call(f32[32,8,128]{2,1,0:T(8,128)S(1)} %copy-done.3, f32[32,8,128]{2,1,0:T(8,128)S(1)} %get-tuple-element.73.w_in, ...), custom_call_target="tpu_custom_call" | custom-call | tf_op jit(solution)/shard_map/pallas_call | solution.py:325
  65.2 3.6 %collective-permute-start.12 = (bf16[128,128]{1,0:T(8,128)(2,1)S(1)}, bf16[128,128]{1,0:T(8,128)(2,1)S(1)}, u32[]{:S(2)}, u32[]{:S(2)}) collective-permute-start(bf16[128,128]{1,0:T(8,128)(2,1)S(1)} %get-tuple-element.79), channel_id=1, source_target_pairs={{0,1},{1,0},{2,3},{3,2},{4,5},{5,4},{6,7},{7,6},{8,9},{9,8},{10,11... | collective-permute-start | bytes 98312 | tf_op jit(solution)/shard_map/ppermute | solution.py:297
  68.8 0.7 collective-permute-start.13
  69.4 2.1 %collective-permute-start.14 = (bf16[128,128]{1,0:T(8,128)(2,1)S(1)}, bf16[128,128]{1,0:T(8,128)(2,1)S(1)}, u32[]{:S(2)}, u32[]{:S(2)}) collective-permute-start(bf16[128,128]{1,0:T(8,128)(2,1)S(1)} %get-tuple-element.81), channel_id=1, source_target_pairs={{0,4},{4,0},{1,5},{5,1},{2,6},{6,2},{3,7},{7,3},{8,12},{12,8},{9,1... | collective-permute-start | bytes 98312 | tf_op jit(solution)/shard_map/ppermute | solution.py:297
  71.5 0.7 collective-permute-start.15
  72.2 1.2 collective-permute-done.14.refs_2_
  73.4 5.0 %shard_map.197 = (f32[32,8,128]{2,1,0:T(8,128)S(1)}, f32[32,8,128]{2,1,0:T(8,128)S(1)}, bf16[128,128]{1,0:T(8,128)(2,1)S(1)}, bf16[128,128]{1,0:T(8,128)(2,1)S(1...) custom-call(f32[32,8,128]{2,1,0:T(8,128)S(1)} %copy-done.4, f32[32,8,128]{2,1,0:T(8,128)S(1)} %get-tuple-element.78.w_in, ...), custom_call_target="tpu_custom_call" | custom-call | tf_op jit(solution)/shard_map/pallas_call | solution.py:325
  78.4 1.6 %collective-permute-start.16 = (bf16[128,128]{1,0:T(8,128)(2,1)S(1)}, bf16[128,128]{1,0:T(8,128)(2,1)S(1)}, u32[]{:S(2)}, u32[]{:S(2)}) collective-permute-start(bf16[128,128]{1,0:T(8,128)(2,1)S(1)} %get-tuple-element.85), channel_id=1, source_target_pairs={{0,1},{1,0},{2,3},{3,2},{4,5},{5,4},{6,7},{7,6},{8,9},{9,8},{10,11... | collective-permute-start | bytes 98312 | tf_op jit(solution)/shard_map/ppermute | solution.py:297
  80.1 0.7 collective-permute-start.17
  80.7 5.3 %collective-permute-start.18 = (bf16[128,128]{1,0:T(8,128)(2,1)S(1)}, bf16[128,128]{1,0:T(8,128)(2,1)S(1)}, u32[]{:S(2)}, u32[]{:S(2)}) collective-permute-start(bf16[128,128]{1,0:T(8,128)(2,1)S(1)} %get-tuple-element.87), channel_id=1, source_target_pairs={{0,4},{4,0},{1,5},{5,1},{2,6},{6,2},{3,7},{7,3},{8,12},{12,8},{9,1... | collective-permute-start | bytes 98312 | tf_op jit(solution)/shard_map/ppermute | solution.py:297
  86.0 0.7 collective-permute-start.19
  86.7 1.2 collective-permute-done.18.refs_2_
  87.9 4.9 %shard_map.198 = (f32[32,8,128]{2,1,0:T(8,128)S(1)}, bf16[128,128]{1,0:T(8,128)(2,1)S(1)}, bf16[128,128]{1,0:T(8,128)(2,1)S(1)}, bf16[128,128]{1,0:T(8,128)(2,1)S(1)}, bf16[128,128]{1,0:T(8,128)(2,1)S(1)}) custom-call(f32[32,8,128]{2,1,0:T(8,128)S(1)} %get-tuple-element.83.w, f32[32,8,128]{2,1,0:T(8,128)S(1)} %get-tuple-element.84.z_in, ...), custom_call_target="tpu_custom_call" | custom-call | tf_op jit(solution)/shard_map/pallas_call | solution.py:333
  92.8 0.5 collective-permute-start.20
  93.3 0.7 collective-permute-start.21
  94.0 3.8 %collective-permute-start.22 = (bf16[128,128]{1,0:T(8,128)(2,1)S(1)}, bf16[128,128]{1,0:T(8,128)(2,1)S(1)}, u32[]{:S(2)}, u32[]{:S(2)}) collective-permute-start(bf16[128,128]{1,0:T(8,128)(2,1)S(1)} %get-tuple-element.92), channel_id=1, source_target_pairs={{0,4},{4,0},{1,5},{5,1},{2,6},{6,2},{3,7},{7,3},{8,12},{12,8},{9,1... | collective-permute-start | bytes 98312 | tf_op jit(solution)/shard_map/ppermute | solution.py:297
  97.8 0.7 collective-permute-start.23
  98.4 1.2 collective-permute-done.22.refs_2_
  99.7 0.0 copy-start.17
  99.7 0.0 copy-start.18
  99.7 3.3 %shard_map.199 = (f32[32,8,128]{2,1,0:T(8,128)S(1)}, bf16[128,128]{1,0:T(8,128)(2,1)S(1)}, bf16[128,128]{1,0:T(8,128)(2,1)S(1)}, bf16[128,128]{1,0:T(8,128)(2,1)S(1)}, bf16[128,128]{1,0:T(8,128)(2,1)S(1)}) custom-call(f32[32,8,128]{2,1,0:T(8,128)S(1)} %get-tuple-element.83.w, f32[32,8,128]{2,1,0:T(8,128)S(1)} %get-tuple-element.89.z_in, ...), custom_call_target="tpu_custom_call" | custom-call | tf_op jit(solution)/shard_map/pallas_call | solution.py:333
  103.0 0.1 collective-permute-start.24
  103.1 0.7 collective-permute-start.25
  103.8 6.8 %collective-permute-start.26 = (bf16[128,128]{1,0:T(8,128)(2,1)S(1)}, bf16[128,128]{1,0:T(8,128)(2,1)S(1)}, u32[]{:S(2)}, u32[]{:S(2)}) collective-permute-start(bf16[128,128]{1,0:T(8,128)(2,1)S(1)} %get-tuple-element.97), channel_id=1, source_target_pairs={{0,4},{4,0},{1,5},{5,1},{2,6},{6,2},{3,7},{7,3},{8,12},{12,8},{9,1... | collective-permute-start | bytes 98312 | tf_op jit(solution)/shard_map/ppermute | solution.py:297
  110.6 0.7 collective-permute-start.27
  111.3 1.2 collective-permute-done.26.refs_2_
  112.5 1.7 %shard_map.200 = (f32[32,8,128]{2,1,0:T(8,128)S(1)}, f32[16,16,128]{2,1,0:T(8,128)S(1)}) custom-call(f32[32,8,128]{2,1,0:T(8,128)S(1)} %get-tuple-element.83.w, f32[32,8,128]{2,1,0:T(8,128)S(1)} %get-tuple-element.94.z_in, bf16[32,9,128,128]{3,2,1,0:T(8,128)(2,1)S(1)} %copy-done.1, bf16[32,128,128]{2,1,0:T(8,128)(2,1)S(1)} %copy-done.2, ...), custom_call_target="tpu_custom_call" | custom-call | tf_op jit(solution)/shard_map/pallas_call | solution.py:339
  114.2 22.0 %all_to_all.11.sums = f32[16,16,128]{2,1,0:T(8,128)S(1)} all-to-all(f32[16,16,128]{2,1,0:T(8,128)S(1)} %get-tuple-element.100), channel_id=1, replica_groups=mesh['groups'=2,'gx'=16] {'gx'}, dimensions={0} | all-to-all | bytes 262144 | tf_op jit(solution)/shard_map/all_to_all | solution.py:345
  136.3 1.4 %shard_map.201 = (f32[32,8,128]{2,1,0:T(8,128)}, f32[32,8,128]{2,1,0:T(8,128)}, f32[32,8,128]{2,1,0:T(8,128)}, f32[3,8]{1,0:T(4,128)}) custom-call(f32[16,16,128]{2,1,0:T(8,128)S(1)} %all_to_all.11.sums, f32[32,8,128]{2,1,0:T(8,128)S(1)} %get-tuple-element.101.z, f32[32,8,128]{2,1,0:T(8,128)S(1)} %copy-done.7, f32[32,8,128]{2,1,0:T(8,128)S(1)} %copy-done.10, ...), custom_call_target="tpu_custom_call" | custom-call | tf_op jit(solution)/shard_map/pallas_call | solution.py:346
  (45 shorter events, 0.1 us)
Async XLA Ops:
  0.6 39.8 %copy-start.15 = (f32[8]{0:T(128)S(1)}, f32[8]{0:T(128)}, u32[]{:S(2)}) copy-start(f32[8]{0:T(128)} %rho.3) | copy-start | bytes 100
  1.3 0.9 copy-start.5
  2.2 38.1 %copy-start.9 = (f32[32,8,128]{2,1,0:T(8,128)S(1)}, f32[32,8,128]{2,1,0:T(8,128)}, u32[]{:S(2)}) copy-start(f32[32,8,128]{2,1,0:T(8,128)} %r_ref.1) | copy-start | bytes 393220
  3.0 9.8 %collective-permute-start = (bf16[128,128]{1,0:T(8,128)(2,1)S(1)}, bf16[128,128]{1,0:T(8,128)(2,1)S(1)}, u32[]{:S(2)}, u32[]{:S(2)}) collective-permute-start(bf16[128,128]{1,0:T(8,128)(2,1)S(1)} %get-tuple-element.57), channel_id=1, source_target_pairs={{0,1},{1,0},{2,3},{3,2},{4,5},{5,4},{6,7},{7,6},{8,9},{9,8},{10,11... | collective-permute-start | bytes 98312 | tf_op jit(solution)/shard_map/ppermute | solution.py:297
  3.5 9.3 %collective-permute-start.1 = (bf16[128,128]{1,0:T(8,128)(2,1)S(1)}, bf16[128,128]{1,0:T(8,128)(2,1)S(1)}, u32[]{:S(2)}, u32[]{:S(2)}) collective-permute-start(bf16[128,128]{1,0:T(8,128)(2,1)S(1)} %get-tuple-element.58), channel_id=1, source_target_pairs={{1,2},{2,1},{5,6},{6,5},{9,10},{10,9},{13,14},{14,13},{17,18},{18,... | collective-permute-start | bytes 98312 | tf_op jit(solution)/shard_map/ppermute | solution.py:297
  4.2 8.7 %collective-permute-start.2 = (bf16[128,128]{1,0:T(8,128)(2,1)S(1)}, bf16[128,128]{1,0:T(8,128)(2,1)S(1)}, u32[]{:S(2)}, u32[]{:S(2)}) collective-permute-start(bf16[128,128]{1,0:T(8,128)(2,1)S(1)} %get-tuple-element.59), channel_id=1, source_target_pairs={{0,4},{4,0},{1,5},{5,1},{2,6},{6,2},{3,7},{7,3},{8,12},{12,8},{9,1... | collective-permute-start | bytes 98312 | tf_op jit(solution)/shard_map/ppermute | solution.py:297
  6.9 6.0 %collective-permute-start.3 = (bf16[128,128]{1,0:T(8,128)(2,1)S(1)}, bf16[128,128]{1,0:T(8,128)(2,1)S(1)}, u32[]{:S(2)}, u32[]{:S(2)}) collective-permute-start(bf16[128,128]{1,0:T(8,128)(2,1)S(1)} %get-tuple-element.60), channel_id=1, source_target_pairs={{4,8},{8,4},{5,9},{9,5},{6,10},{10,6},{7,11},{11,7},{20,24},{24,20... | collective-permute-start | bytes 98312 | tf_op jit(solution)/shard_map/ppermute | solution.py:297
  8.3 0.7 copy-start.12
  9.0 0.7 copy-start.13
  9.7 0.7 copy-start.14
  10.4 0.7 copy-start.16
  12.9 3.7 %copy-start = (bf16[32,9,128,128]{3,2,1,0:T(8,128)(2,1)S(1)}, bf16[32,9,128,128]{3,2,1,0:T(8,128)(2,1)}, u32[]{:S(2)}) copy-start(bf16[32,9,128,128]{3,2,1,0:T(8,128)(2,1)} %off.13) | copy-start | bytes 28311556
  16.6 0.9 copy-start.6
  17.5 1.2 copy-start.8
  18.7 21.7 %copy-start.2 = (bf16[32,128,128]{2,1,0:T(8,128)(2,1)S(1)}, bf16[32,128,128]{2,1,0:T(8,128)(2,1)}, u32[]{:S(2)}) copy-start(bf16[32,128,128]{2,1,0:T(8,128)(2,1)} %factor.13) | copy-start | bytes 3145732
  18.7 29.3 %copy-start.1 = (bf16[32,9,128,128]{3,2,1,0:T(8,128)(2,1)S(1)}, bf16[32,9,128,128]{3,2,1,0:T(8,128)(2,1)}, u32[]{:S(2)}) copy-start(bf16[32,9,128,128]{3,2,1,0:T(8,128)(2,1)} %off.13) | copy-start | bytes 28311556
  42.8 3.6 %collective-permute-start.4 = (bf16[128,128]{1,0:T(8,128)(2,1)S(1)}, bf16[128,128]{1,0:T(8,128)(2,1)S(1)}, u32[]{:S(2)}, u32[]{:S(2)}) collective-permute-start(bf16[128,128]{1,0:T(8,128)(2,1)S(1)} %get-tuple-element.69), channel_id=1, source_target_pairs={{0,1},{1,0},{2,3},{3,2},{4,5},{5,4},{6,7},{7,6},{8,9},{9,8},{10,11... | collective-permute-start | bytes 98312 | tf_op jit(solution)/shard_map/ppermute | solution.py:297
  43.3 3.1 %collective-permute-start.5 = (bf16[128,128]{1,0:T(8,128)(2,1)S(1)}, bf16[128,128]{1,0:T(8,128)(2,1)S(1)}, u32[]{:S(2)}, u32[]{:S(2)}) collective-permute-start(bf16[128,128]{1,0:T(8,128)(2,1)S(1)} %get-tuple-element.70), channel_id=1, source_target_pairs={{1,2},{2,1},{5,6},{6,5},{9,10},{10,9},{13,14},{14,13},{17,18},{18,... | collective-permute-start | bytes 98312 | tf_op jit(solution)/shard_map/ppermute | solution.py:297
  44.0 4.0 %collective-permute-start.6 = (bf16[128,128]{1,0:T(8,128)(2,1)S(1)}, bf16[128,128]{1,0:T(8,128)(2,1)S(1)}, u32[]{:S(2)}, u32[]{:S(2)}) collective-permute-start(bf16[128,128]{1,0:T(8,128)(2,1)S(1)} %get-tuple-element.71), channel_id=1, source_target_pairs={{0,4},{4,0},{1,5},{5,1},{2,6},{6,2},{3,7},{7,3},{8,12},{12,8},{9,1... | collective-permute-start | bytes 98312 | tf_op jit(solution)/shard_map/ppermute | solution.py:297
  45.7 2.2 %collective-permute-start.7 = (bf16[128,128]{1,0:T(8,128)(2,1)S(1)}, bf16[128,128]{1,0:T(8,128)(2,1)S(1)}, u32[]{:S(2)}, u32[]{:S(2)}) collective-permute-start(bf16[128,128]{1,0:T(8,128)(2,1)S(1)} %get-tuple-element.72), channel_id=1, source_target_pairs={{4,8},{8,4},{5,9},{9,5},{6,10},{10,6},{7,11},{11,7},{20,24},{24,20... | collective-permute-start | bytes 98312 | tf_op jit(solution)/shard_map/ppermute | solution.py:297
  48.0 0.9 copy-start.3
  48.9 24.6 %copy-start.4 = (f32[32,8,128]{2,1,0:T(8,128)S(1)}, f32[32,8,128]{2,1,0:T(8,128)}, u32[]{:S(2)}) copy-start(f32[32,8,128]{2,1,0:T(8,128)} %get-tuple-element.52.r_new.refs_4_) | copy-start | bytes 393220
  52.2 6.8 %collective-permute-start.8 = (bf16[128,128]{1,0:T(8,128)(2,1)S(1)}, bf16[128,128]{1,0:T(8,128)(2,1)S(1)}, u32[]{:S(2)}, u32[]{:S(2)}) collective-permute-start(bf16[128,128]{1,0:T(8,128)(2,1)S(1)} %get-tuple-element.74), channel_id=1, source_target_pairs={{0,1},{1,0},{2,3},{3,2},{4,5},{5,4},{6,7},{7,6},{8,9},{9,8},{10,11... | collective-permute-start | bytes 98312 | tf_op jit(solution)/shard_map/ppermute | solution.py:297
  52.4 6.6 %collective-permute-start.9 = (bf16[128,128]{1,0:T(8,128)(2,1)S(1)}, bf16[128,128]{1,0:T(8,128)(2,1)S(1)}, u32[]{:S(2)}, u32[]{:S(2)}) collective-permute-start(bf16[128,128]{1,0:T(8,128)(2,1)S(1)} %get-tuple-element.75), channel_id=1, source_target_pairs={{1,2},{2,1},{5,6},{6,5},{9,10},{10,9},{13,14},{14,13},{17,18},{18,... | collective-permute-start | bytes 98312 | tf_op jit(solution)/shard_map/ppermute | solution.py:297
  53.1 7.2 %collective-permute-start.10 = (bf16[128,128]{1,0:T(8,128)(2,1)S(1)}, bf16[128,128]{1,0:T(8,128)(2,1)S(1)}, u32[]{:S(2)}, u32[]{:S(2)}) collective-permute-start(bf16[128,128]{1,0:T(8,128)(2,1)S(1)} %get-tuple-element.76), channel_id=1, source_target_pairs={{0,4},{4,0},{1,5},{5,1},{2,6},{6,2},{3,7},{7,3},{8,12},{12,8},{9,1... | collective-permute-start | bytes 98312 | tf_op jit(solution)/shard_map/ppermute | solution.py:297
  58.4 1.9 %collective-permute-start.11 = (bf16[128,128]{1,0:T(8,128)(2,1)S(1)}, bf16[128,128]{1,0:T(8,128)(2,1)S(1)}, u32[]{:S(2)}, u32[]{:S(2)}) collective-permute-start(bf16[128,128]{1,0:T(8,128)(2,1)S(1)} %get-tuple-element.77), channel_id=1, source_target_pairs={{4,8},{8,4},{5,9},{9,5},{6,10},{10,6},{7,11},{11,7},{20,24},{24,20... | collective-permute-start | bytes 98312 | tf_op jit(solution)/shard_map/ppermute | solution.py:297
  65.2 7.0 %collective-permute-start.12 = (bf16[128,128]{1,0:T(8,128)(2,1)S(1)}, bf16[128,128]{1,0:T(8,128)(2,1)S(1)}, u32[]{:S(2)}, u32[]{:S(2)}) collective-permute-start(bf16[128,128]{1,0:T(8,128)(2,1)S(1)} %get-tuple-element.79), channel_id=1, source_target_pairs={{0,1},{1,0},{2,3},{3,2},{4,5},{5,4},{6,7},{7,6},{8,9},{9,8},{10,11... | collective-permute-start | bytes 98312 | tf_op jit(solution)/shard_map/ppermute | solution.py:297
  68.8 3.4 %collective-permute-start.13 = (bf16[128,128]{1,0:T(8,128)(2,1)S(1)}, bf16[128,128]{1,0:T(8,128)(2,1)S(1)}, u32[]{:S(2)}, u32[]{:S(2)}) collective-permute-start(bf16[128,128]{1,0:T(8,128)(2,1)S(1)} %get-tuple-element.80), channel_id=1, source_target_pairs={{1,2},{2,1},{5,6},{6,5},{9,10},{10,9},{13,14},{14,13},{17,18},{18,... | collective-permute-start | bytes 98312 | tf_op jit(solution)/shard_map/ppermute | solution.py:297
  69.4 4.0 %collective-permute-start.14 = (bf16[128,128]{1,0:T(8,128)(2,1)S(1)}, bf16[128,128]{1,0:T(8,128)(2,1)S(1)}, u32[]{:S(2)}, u32[]{:S(2)}) collective-permute-start(bf16[128,128]{1,0:T(8,128)(2,1)S(1)} %get-tuple-element.81), channel_id=1, source_target_pairs={{0,4},{4,0},{1,5},{5,1},{2,6},{6,2},{3,7},{7,3},{8,12},{12,8},{9,1... | collective-permute-start | bytes 98312 | tf_op jit(solution)/shard_map/ppermute | solution.py:297
  71.5 1.9 %collective-permute-start.15 = (bf16[128,128]{1,0:T(8,128)(2,1)S(1)}, bf16[128,128]{1,0:T(8,128)(2,1)S(1)}, u32[]{:S(2)}, u32[]{:S(2)}) collective-permute-start(bf16[128,128]{1,0:T(8,128)(2,1)S(1)} %get-tuple-element.82), channel_id=1, source_target_pairs={{4,8},{8,4},{5,9},{9,5},{6,10},{10,6},{7,11},{11,7},{20,24},{24,20... | collective-permute-start | bytes 98312 | tf_op jit(solution)/shard_map/ppermute | solution.py:297
  78.4 8.2 %collective-permute-start.16 = (bf16[128,128]{1,0:T(8,128)(2,1)S(1)}, bf16[128,128]{1,0:T(8,128)(2,1)S(1)}, u32[]{:S(2)}, u32[]{:S(2)}) collective-permute-start(bf16[128,128]{1,0:T(8,128)(2,1)S(1)} %get-tuple-element.85), channel_id=1, source_target_pairs={{0,1},{1,0},{2,3},{3,2},{4,5},{5,4},{6,7},{7,6},{8,9},{9,8},{10,11... | collective-permute-start | bytes 98312 | tf_op jit(solution)/shard_map/ppermute | solution.py:297
  80.1 6.6 %collective-permute-start.17 = (bf16[128,128]{1,0:T(8,128)(2,1)S(1)}, bf16[128,128]{1,0:T(8,128)(2,1)S(1)}, u32[]{:S(2)}, u32[]{:S(2)}) collective-permute-start(bf16[128,128]{1,0:T(8,128)(2,1)S(1)} %get-tuple-element.86), channel_id=1, source_target_pairs={{1,2},{2,1},{5,6},{6,5},{9,10},{10,9},{13,14},{14,13},{17,18},{18,... | collective-permute-start | bytes 98312 | tf_op jit(solution)/shard_map/ppermute | solution.py:297
  80.7 7.2 %collective-permute-start.18 = (bf16[128,128]{1,0:T(8,128)(2,1)S(1)}, bf16[128,128]{1,0:T(8,128)(2,1)S(1)}, u32[]{:S(2)}, u32[]{:S(2)}) collective-permute-start(bf16[128,128]{1,0:T(8,128)(2,1)S(1)} %get-tuple-element.87), channel_id=1, source_target_pairs={{0,4},{4,0},{1,5},{5,1},{2,6},{6,2},{3,7},{7,3},{8,12},{12,8},{9,1... | collective-permute-start | bytes 98312 | tf_op jit(solution)/shard_map/ppermute | solution.py:297
  86.0 1.9 %collective-permute-start.19 = (bf16[128,128]{1,0:T(8,128)(2,1)S(1)}, bf16[128,128]{1,0:T(8,128)(2,1)S(1)}, u32[]{:S(2)}, u32[]{:S(2)}) collective-permute-start(bf16[128,128]{1,0:T(8,128)(2,1)S(1)} %get-tuple-element.88), channel_id=1, source_target_pairs={{4,8},{8,4},{5,9},{9,5},{6,10},{10,6},{7,11},{11,7},{20,24},{24,20... | collective-permute-start | bytes 98312 | tf_op jit(solution)/shard_map/ppermute | solution.py:297
  92.8 5.6 %collective-permute-start.20 = (bf16[128,128]{1,0:T(8,128)(2,1)S(1)}, bf16[128,128]{1,0:T(8,128)(2,1)S(1)}, u32[]{:S(2)}, u32[]{:S(2)}) collective-permute-start(bf16[128,128]{1,0:T(8,128)(2,1)S(1)} %get-tuple-element.90), channel_id=1, source_target_pairs={{0,1},{1,0},{2,3},{3,2},{4,5},{5,4},{6,7},{7,6},{8,9},{9,8},{10,11... | collective-permute-start | bytes 98312 | tf_op jit(solution)/shard_map/ppermute | solution.py:297
  93.3 5.1 %collective-permute-start.21 = (bf16[128,128]{1,0:T(8,128)(2,1)S(1)}, bf16[128,128]{1,0:T(8,128)(2,1)S(1)}, u32[]{:S(2)}, u32[]{:S(2)}) collective-permute-start(bf16[128,128]{1,0:T(8,128)(2,1)S(1)} %get-tuple-element.91), channel_id=1, source_target_pairs={{1,2},{2,1},{5,6},{6,5},{9,10},{10,9},{13,14},{14,13},{17,18},{18,... | collective-permute-start | bytes 98312 | tf_op jit(solution)/shard_map/ppermute | solution.py:297
  94.0 5.7 %collective-permute-start.22 = (bf16[128,128]{1,0:T(8,128)(2,1)S(1)}, bf16[128,128]{1,0:T(8,128)(2,1)S(1)}, u32[]{:S(2)}, u32[]{:S(2)}) collective-permute-start(bf16[128,128]{1,0:T(8,128)(2,1)S(1)} %get-tuple-element.92), channel_id=1, source_target_pairs={{0,4},{4,0},{1,5},{5,1},{2,6},{6,2},{3,7},{7,3},{8,12},{12,8},{9,1... | collective-permute-start | bytes 98312 | tf_op jit(solution)/shard_map/ppermute | solution.py:297
  97.8 1.9 %collective-permute-start.23 = (bf16[128,128]{1,0:T(8,128)(2,1)S(1)}, bf16[128,128]{1,0:T(8,128)(2,1)S(1)}, u32[]{:S(2)}, u32[]{:S(2)}) collective-permute-start(bf16[128,128]{1,0:T(8,128)(2,1)S(1)} %get-tuple-element.93), channel_id=1, source_target_pairs={{4,8},{8,4},{5,9},{9,5},{6,10},{10,6},{7,11},{11,7},{20,24},{24,20... | collective-permute-start | bytes 98312 | tf_op jit(solution)/shard_map/ppermute | solution.py:297
  99.7 36.6 %copy-start.7 = (f32[32,8,128]{2,1,0:T(8,128)S(1)}, f32[32,8,128]{2,1,0:T(8,128)}, u32[]{:S(2)}) copy-start(f32[32,8,128]{2,1,0:T(8,128)} %q_ref.5) | copy-start | bytes 393220
  99.7 36.6 %copy-start.10 = (f32[32,8,128]{2,1,0:T(8,128)S(1)}, f32[32,8,128]{2,1,0:T(8,128)}, u32[]{:S(2)}) copy-start(f32[32,8,128]{2,1,0:T(8,128)} %x_ref.1) | copy-start | bytes 393220
  99.7 36.6 %copy-start.11 = (f32[32,8,128]{2,1,0:T(8,128)S(1)}, f32[32,8,128]{2,1,0:T(8,128)}, u32[]{:S(2)}) copy-start(f32[32,8,128]{2,1,0:T(8,128)} %d_ref.1) | copy-start | bytes 393220
  99.7 36.6 %copy-start.17 = (f32[8]{0:T(128)S(1)}, f32[8]{0:T(128)}, u32[]{:S(2)}) copy-start(f32[8]{0:T(128)} %tau.1) | copy-start | bytes 100
  99.7 36.6 %copy-start.18 = (f32[8]{0:T(128)S(1)}, f32[8]{0:T(128)}, u32[]{:S(2)}) copy-start(f32[8]{0:T(128)} %theta_in.1) | copy-start | bytes 100
  103.0 8.3 %collective-permute-start.24 = (bf16[128,128]{1,0:T(8,128)(2,1)S(1)}, bf16[128,128]{1,0:T(8,128)(2,1)S(1)}, u32[]{:S(2)}, u32[]{:S(2)}) collective-permute-start(bf16[128,128]{1,0:T(8,128)(2,1)S(1)} %get-tuple-element.95), channel_id=1, source_target_pairs={{0,1},{1,0},{2,3},{3,2},{4,5},{5,4},{6,7},{7,6},{8,9},{9,8},{10,11... | collective-permute-start | bytes 98312 | tf_op jit(solution)/shard_map/ppermute | solution.py:297
  103.1 8.2 %collective-permute-start.25 = (bf16[128,128]{1,0:T(8,128)(2,1)S(1)}, bf16[128,128]{1,0:T(8,128)(2,1)S(1)}, u32[]{:S(2)}, u32[]{:S(2)}) collective-permute-start(bf16[128,128]{1,0:T(8,128)(2,1)S(1)} %get-tuple-element.96), channel_id=1, source_target_pairs={{1,2},{2,1},{5,6},{6,5},{9,10},{10,9},{13,14},{14,13},{17,18},{18,... | collective-permute-start | bytes 98312 | tf_op jit(solution)/shard_map/ppermute | solution.py:297
  103.8 8.7 %collective-permute-start.26 = (bf16[128,128]{1,0:T(8,128)(2,1)S(1)}, bf16[128,128]{1,0:T(8,128)(2,1)S(1)}, u32[]{:S(2)}, u32[]{:S(2)}) collective-permute-start(bf16[128,128]{1,0:T(8,128)(2,1)S(1)} %get-tuple-element.97), channel_id=1, source_target_pairs={{0,4},{4,0},{1,5},{5,1},{2,6},{6,2},{3,7},{7,3},{8,12},{12,8},{9,1... | collective-permute-start | bytes 98312 | tf_op jit(solution)/shard_map/ppermute | solution.py:297
  110.6 1.9 %collective-permute-start.27 = (bf16[128,128]{1,0:T(8,128)(2,1)S(1)}, bf16[128,128]{1,0:T(8,128)(2,1)S(1)}, u32[]{:S(2)}, u32[]{:S(2)}) collective-permute-start(bf16[128,128]{1,0:T(8,128)(2,1)S(1)} %get-tuple-element.98), channel_id=1, source_target_pairs={{4,8},{8,4},{5,9},{9,5},{6,10},{10,6},{7,11},{11,7},{20,24},{24,20... | collective-permute-start | bytes 98312 | tf_op jit(solution)/shard_map/ppermute | solution.py:297

commit v2 on v1

v2 whole, which is shorter than its diff:
```python
import functools

import jax
import jax.numpy as jnp
from jax import lax
from jax.experimental import pallas as pl
from jax.experimental.pallas import tpu as pltpu
from jax.sharding import PartitionSpec as P

F32 = jnp.float32
BF16 = jnp.bfloat16
VMEM = pltpu.VMEM
SMEM = pltpu.SMEM
HBM = pltpu.HBM
SIDE = 4
COUPLE = 4
SOLVE = 16


def swap_pairs(axis, stride, extent, phase, tiles):
    pairs = []
    for tile in range(tiles):
        place = tile // stride % extent
        up = place % 2 == phase
        other = place + 1 if up else place - 1
        if 0 <= other < extent:
            pairs.append((tile, tile + (other - place) * stride))
        elif axis == 0:
            pairs.append((tile, tile + (extent - 1 - 2 * place) * stride))
        else:
            pairs.append((tile, tile ^ 1))
    return pairs


def swaps_of(tiles):
    swaps = []
    for axis, (stride, extent) in enumerate(((1, SIDE), (SIDE, SIDE), (16, tiles // 16))):
        for phase in range(2 if extent > 2 else extent - 1):
            swaps.append((axis, phase, extent, swap_pairs(axis, stride, extent, phase, tiles)))
    return swaps


def partner(axis, phase, extent):
    place = lax.rem(lax.axis_index("gx") // (1, SIDE, 16)[axis], extent)
    up = jnp.where(lax.rem(place, 2) == phase, 1, 0)
    other = place + 2 * up - 1
    return up, (other >= 0) & (other < extent)


def send_faces(swaps, state, faces, sent):
    for (axis, phase, extent, _), out in zip(swaps, sent):
        up, _ = partner(axis, phase, extent)
        face = 2 * axis + 1 - up
        for slot in range(0, 16, 2):
            two = [state[faces[face, 0, slot + j]] for j in range(2)]
            out[pl.ds(slot * 8, 16), :] = jnp.concatenate(two, axis=0).astype(BF16)


def extend(swaps, state, arrived, extended):
    extended[pl.ds(0, 32)] = state[...].astype(BF16).astype(F32)
    zeros = jnp.zeros((16, 8, 128), F32)
    reached = set()
    for (axis, phase, extent, _), piece in zip(swaps, arrived):
        up, real = partner(axis, phase, extent)
        value = piece[...].astype(F32).reshape(16, 8, 128)
        extended[pl.ds(32 + (2 * axis + up) * 16, 16)] = jnp.where(real, value, zeros)
        reached.add((axis, phase))
    for axis in range(3):
        if (axis, 0) not in reached:
            extended[pl.ds(32 + axis * 32, 32)] = jnp.zeros((32, 8, 128), F32)
        elif (axis, 1) not in reached:
            up, _ = partner(axis, 1, 2)
            extended[pl.ds(32 + (2 * axis + up) * 16, 16)] = zeros


def dot_t(left, right):
    return lax.dot_general(left, right, (((1,), (1,)), ((), ())), preferred_element_type=F32)


def coupled(block, extended, off, columns, first=()):
    vectors = [pair[0] for pair in first] + [extended[columns[k, block]] for k in range(9)]
    matrices = [pair[1] for pair in first] + [off[block, k] for k in range(9)]
    return dot_t(jnp.concatenate(vectors, axis=1).astype(BF16), jnp.concatenate(matrices, axis=1))


def solved(blocks, vectors, factor, straight, crossed):
    matrices = [factor[b] for b in blocks]
    firsts = [dot_t(v.astype(BF16), m) for v, m in zip(vectors, matrices)]
    even = lax.broadcasted_iota(jnp.int32, (8, 128), 1) % 2 == 0
    middles = []
    for b, first in zip(blocks, firsts):
        other = jnp.where(even, pltpu.roll(first, 127, 1), pltpu.roll(first, 1, 1))
        row = pl.ds(b, 1)
        middles.append((straight[row, :] * first + crossed[row, :] * other).astype(BF16))
    return [jnp.dot(v, m, preferred_element_type=F32) for v, m in zip(middles, matrices)]


def for_colour(colour, tables, size, body):
    def step(group, carry):
        body([tables[colour, group * size + j] for j in range(size)])
        return carry

    lax.fori_loop(0, (tables[4, colour] + size - 1) // size, step, 0)


def first_kernel(swaps, q_hbm, faces_hbm, q, faces, *refs):
    sent, sems = refs[:-1], refs[-1]
    copies = [
        pltpu.make_async_copy(faces_hbm, faces, sems.at[0]),
        pltpu.make_async_copy(q_hbm, q, sems.at[1]),
    ]
    for copy in copies:
        copy.start()
    for copy in copies:
        copy.wait()
    send_faces(swaps, q, faces, sent)


def setup_kernel(
    off_hbm, columns_hbm, colours_hbm, diag_ref, off_ref, pairs_ref, off, columns, tables, straight, crossed, colours, sems
):
    half = off_hbm.shape[0] // 2
    loads = [
        pltpu.make_async_copy(colours_hbm, colours, sems.at[0]),
        pltpu.make_async_copy(columns_hbm, columns, sems.at[1]),
        pltpu.make_async_copy(off_hbm.at[pl.ds(0, half)], off.at[pl.ds(0, half)], sems.at[2]),
    ]
    for load in loads:
        load.start()
    pair = lax.broadcasted_iota(jnp.int32, (64, 128), 0)
    lane = lax.broadcasted_iota(jnp.int32, (64, 128), 1)
    spread = jnp.where(lane // 2 == pair, 1.0, 0.0).astype(F32)
    cross = jnp.dot(off_ref[...], spread, precision=lax.Precision.HIGHEST, preferred_element_type=F32)
    paired = jnp.dot(pairs_ref[...].astype(F32), spread, precision=lax.Precision.HIGHEST, preferred_element_type=F32)
    own = diag_ref[...]
    even = lax.broadcasted_iota(jnp.int32, own.shape, 1) % 2 == 0
    other = jnp.where(even, pltpu.roll(own, 127, 1), pltpu.roll(own, 1, 1))
    det = own * other - cross * cross
    straight[...] = jnp.where(paired > 0.5, other / det, 1.0 / own)
    crossed[...] = jnp.where(paired > 0.5, -cross / det, 0.0)
    loads[0].wait()
    for colour in range(4):
        count = jnp.int32(0)
        for block in range(32):
            tables[colour, count] = block
            count = count + jnp.where(colours[block] == colour, 1, 0)
        last = tables[colour, jnp.maximum(count - 1, 0)]
        for j in range(16):
            tables[colour, count + j] = last
        tables[4, colour] = count
    for load in loads[1:]:
        load.wait()


def image_kernel(swaps, tiles, q, diag, off_hbm, off_in, columns, *refs):
    n = len(swaps)
    arrived, (off, image, partial, extended, sems) = refs[:n], refs[n:]
    half, part = off_hbm.shape[0] // 2, 4
    loads = []
    for index in range(half // part):
        rows = pl.ds(half + index * part, part)
        loads.append(pltpu.make_async_copy(off_hbm.at[rows], off.at[rows], sems.at[index]))
        loads[-1].start()
    extend(swaps, q, arrived, extended)

    def step(group, total):
        blocks = [group * part + j for j in range(part)]
        values = [coupled(b, extended, off, columns, [(extended[b], diag[b])]) for b in blocks]
        for b, value in zip(blocks, values):
            image[b] = value
            total = total + q[b] * value
        return total

    total = lax.fori_loop(0, half // part, step, jnp.zeros((8, 128), F32))
    for index, load in enumerate(loads):
        load.wait()
        total = step(half // part + index, total)
    for tile in range(tiles):
        partial[tile] = total


def column_of(values):
    row = lax.broadcasted_iota(jnp.int32, (8, 128), 0)
    out = jnp.zeros((8, 128), F32)
    for n in range(8):
        out = jnp.where(row == n, values[n], out)
    return out


def start_kernel(
    swaps, count, sums, r_ref, image, rho, factor, straight, crossed, tables, faces, r_new, w, norm, alpha, *sent
):
    sigma = jnp.sum(jnp.sum(sums[...], axis=0), axis=1, keepdims=True) / count
    sigma = jnp.where(sigma >= 0, jnp.maximum(sigma, 0.5), jnp.minimum(sigma, -0.5))
    step_size = column_of(rho) / sigma
    alpha[...] = step_size
    new = r_ref[...] - step_size[None] * image[...]
    r_new[...] = new
    norm[...] = jnp.sum(new * new, axis=0)
    w[...] = jnp.zeros_like(w)

    def body(blocks):
        for b, value in zip(blocks, solved(blocks, [r_new[b] for b in blocks], factor, straight, crossed)):
            w[b] = value

    for_colour(0, tables, SOLVE, body)
    send_faces(swaps, w, faces, sent)


def forward_kernel(swaps, colour, r_new, w_in, off, factor, straight, crossed, columns, tables, faces, *refs):
    n = len(swaps)
    arrived, w, sent, (extended, rest) = refs[:n], refs[n], refs[n + 1 : -2], refs[-2:]
    w[...] = w_in[...]
    extend(swaps, w_in, arrived, extended)

    def couple(blocks):
        for b, value in zip(blocks, [coupled(b, extended, off, columns) for b in blocks]):
            rest[b] = r_new[b] - value

    def solve(blocks):
        for b, value in zip(blocks, solved(blocks, [rest[b] for b in blocks], factor, straight, crossed)):
            w[b] = value

    for_colour(colour, tables, COUPLE, couple)
    for_colour(colour, tables, SOLVE, solve)
    if colour == 3:
        z = sent[0]
        z[...] = jnp.zeros_like(z)

        def copy(blocks):
            for b in blocks:
                z[b] = w[b]

        for_colour(3, tables, COUPLE, copy)
        send_faces(swaps, z, faces, sent[1:])
    else:
        send_faces(swaps, w, faces, sent)


def backward_kernel(swaps, tiles, colour, w, z_in, off, factor, straight, crossed, columns, tables, faces, *refs):
    n = len(swaps)
    arrived, others, (extended, rest) = refs[:n], refs[n:-2], refs[-2:]
    if colour == 0:
        r_new, norm, z, partial = others
    else:
        z, sent = others[0], others[1:]
    z[...] = z_in[...]
    extend(swaps, z_in, arrived, extended)

    def couple(blocks):
        for b, value in zip(blocks, [coupled(b, extended, off, columns) for b in blocks]):
            rest[b] = value

    def solve(blocks):
        for b, value in zip(blocks, solved(blocks, [rest[b] for b in blocks], factor, straight, crossed)):
            z[b] = w[b] - value

    for_colour(colour, tables, COUPLE, couple)
    for_colour(colour, tables, SOLVE, solve)
    if colour == 0:
        rho = jnp.sum(r_new[...] * z[...], axis=0)
        both = jnp.concatenate([rho, norm[...]], axis=0)
        for tile in range(tiles):
            partial[tile] = both
    else:
        send_faces(swaps, z, faces, sent)


def last_kernel(count, sums, z, q_ref, x_ref, d_ref, alpha, rho, tau, theta_in, x_new, q_new, d_new, scalars):
    both = jnp.sum(jnp.sum(sums[...], axis=0), axis=1, keepdims=True) / count
    rho_new = both[:8] + jnp.zeros((8, 128), F32)
    norm = both[8:]
    tau_old = column_of(tau)
    theta_old = column_of(theta_in)
    theta = jnp.sqrt(norm + 1e-06) / tau_old
    csq = 1.0 / (1.0 + theta * theta)
    tau_new = tau_old * theta * jnp.sqrt(csq)
    beta = rho_new / column_of(rho)
    q_old = q_ref[...]
    d = (csq * theta_old * theta_old)[None] * d_ref[...] + (csq * alpha[...])[None] * q_old
    d_new[...] = d
    x_new[...] = x_ref[...] + d
    q_new[...] = z[...] + beta[None] * q_old
    row = lax.broadcasted_iota(jnp.int32, (8, 128), 0)
    lane = lax.broadcasted_iota(jnp.int32, (8, 128), 1)
    for index, value in enumerate((rho_new, tau_new, theta)):
        line = jnp.sum(jnp.where(row == lane, value, 0.0), axis=0, keepdims=True)
        scalars[pl.ds(index, 1), :] = line[:, :8]


def vec(*shape, dtype=F32):
    return jax.ShapeDtypeStruct(shape, dtype)


def call(body, outs, places, scratch=(), cost=0, aliases=None):
    return pl.pallas_call(
        body,
        out_shape=outs,
        in_specs=[pl.BlockSpec(memory_space=place) for place in places],
        out_specs=[pl.BlockSpec(memory_space=getattr(out, "memory_space", VMEM)) for out in outs],
        scratch_shapes=list(scratch),
        input_output_aliases=aliases or {},
        cost_estimate=pl.CostEstimate(flops=cost, bytes_accessed=0, transcendentals=0) if cost else None,
        compiler_params=pltpu.CompilerParams(vmem_limit_bytes=8 * 2**20),
    )


def in_hbm(array):
    return pltpu.with_memory_space_constraint(array, HBM)


def per_device(
    x_vec,
    r_vec,
    q_vec,
    d_vec,
    diag_blocks,
    off_blocks,
    columns,
    colours,
    factor_inv,
    pivot_diag,
    pivot_off,
    pivot_pairs,
    face_lists,
    rho_prev,
    tau_prev,
    theta_prev,
):
    tiles = lax.axis_size("gx")
    swaps = swaps_of(tiles)
    n = len(swaps)
    count = float(q_vec.shape[0] * q_vec.shape[2] * tiles)
    kept = VMEM((32, 8, 128), F32)
    pieces = [vec(128, 128, dtype=BF16)] * n
    scratch = [VMEM((128, 8, 128), F32), VMEM((32, 8, 128), F32)]
    off_kept = VMEM(off_blocks.shape, BF16)

    def exchange(sent):
        return [lax.ppermute(piece, "gx", swap[-1]) for piece, swap in zip(sent, swaps)]

    q, faces, *sent = call(
        functools.partial(first_kernel, swaps),
        [kept, SMEM((6, 1, 16), jnp.int32)] + pieces,
        [HBM, HBM],
        [pltpu.SemaphoreType.DMA((2,))],
        cost=10**10,
    )(in_hbm(q_vec), in_hbm(face_lists.transpose(1, 0, 2)))
    arrived = exchange(sent)
    off, columns, tables, straight, crossed = call(
        setup_kernel,
        [off_kept, SMEM((9, 32), jnp.int32), SMEM((8, 128), jnp.int32), vec(32, 128), vec(32, 128)],
        [HBM, HBM, HBM, VMEM, VMEM, VMEM],
        [SMEM((32,), jnp.int32), pltpu.SemaphoreType.DMA((3,))],
    )(in_hbm(off_blocks), in_hbm(columns.T), in_hbm(colours), pivot_diag, pivot_off, pivot_pairs)
    off, image, partial = call(
        functools.partial(image_kernel, swaps, tiles),
        [off_kept, kept, vec(tiles, 8, 128)],
        [VMEM, VMEM, HBM, VMEM, SMEM] + [VMEM] * n,
        [scratch[0], pltpu.SemaphoreType.DMA((4,))],
        aliases={3: 0},
    )(q, diag_blocks, in_hbm(off_blocks), off, columns, *arrived)
    sums = lax.all_to_all(partial, "gx", 0, 0, tiled=True)
    r_new, w, norm, alpha, *sent = call(
        functools.partial(start_kernel, swaps, count),
        [kept, kept, vec(8, 128), vec(8, 128)] + pieces,
        [VMEM] * 3 + [SMEM] + [VMEM] * 3 + [SMEM] * 2,
    )(sums, r_vec, image, rho_prev, factor_inv, straight, crossed, tables, faces)
    fixed = (off, factor_inv, straight, crossed, columns, tables, faces)
    fixed_places = [VMEM] * 4 + [SMEM] * 3
    for colour in (1, 2, 3):
        w, *sent = call(
            functools.partial(forward_kernel, swaps, colour),
            [kept] * (2 if colour == 3 else 1) + pieces,
            [VMEM] * 2 + fixed_places + [VMEM] * n,
            scratch,
        )(r_new, w, *fixed, *exchange(sent))
    z, *sent = sent
    for colour in (2, 1):
        z, *sent = call(
            functools.partial(backward_kernel, swaps, tiles, colour),
            [kept] + pieces,
            [VMEM] * 2 + fixed_places + [VMEM] * n,
            scratch,
        )(w, z, *fixed, *exchange(sent))
    z, partial = call(
        functools.partial(backward_kernel, swaps, tiles, 0),
        [kept, vec(tiles, 16, 128)],
        [VMEM] * 2 + fixed_places + [VMEM] * (n + 2),
        scratch,
    )(w, z, *fixed, *exchange(sent), r_new, norm)
    sums = lax.all_to_all(partial, "gx", 0, 0, tiled=True)
    block_vec = vec(32, 8, 128)
    x_new, q_new, d_new, scalars = call(
        functools.partial(last_kernel, count),
        [block_vec] * 3 + [vec(3, 8)],
        [VMEM] * 6 + [SMEM] * 3,
    )(sums, z, q, x_vec, d_vec, alpha, rho_prev, tau_prev, theta_prev)
    return (x_new, r_new, q_new, d_new, scalars)


def solution(mesh):
    blocks = P(("groups", "gx"))
    return jax.shard_map(
        per_device,
        mesh=mesh,
        in_specs=(blocks,) * 13 + (P("groups"),) * 3,
        out_specs=(blocks,) * 4 + (P(None, "groups"),),
        check_vma=False,
    )
```

time: 139 us -> 82.5 us (0.59)
  blocking collectives: 37.3 us -> 12.1 us
  starting transfers between devices: 43.9 us -> 27.3 us
  Pallas kernels: 35.9 us -> 21.1 us
  waiting for transfers between devices: 7.69 us -> 20.3 us
  local copies, waits for them, and re-layouts: 11.9 us -> 0.71 us
    all_to_all x2 -> x1, blocking collectives: 37.3 us -> 12.1 us  [per_device(): sums = lax.all_to_all(partial, 'gx', 0, 0, tiled=True)]
    ppermute x28, starting transfers between devices: 43.9 us -> 23.7 us  [exchange(): lax.ppermute(piece, 'gx', swap[-1])]
    pallas_call x10, Pallas kernels: 34.5 us -> 19.7 us  [the longest x3 4.85 us: per_device(): call(functools.partial(forward_kernel, swaps, colour), [kept] * (2 if col...]
    unnamed x40 -> x23, local copies, waits for them, and re-layouts: 11.9 us -> 0.71 us
    all_to_all x0 -> x1, waiting for transfers between devices: none -> 7.24 us  [per_device(): sums = lax.all_to_all(partial, 'gx', 0, 0, tiled=True)]
    ppermute x28, waiting for transfers between devices: 7.69 us -> 13.1 us  [exchange(): lax.ppermute(piece, 'gx', swap[-1])]
    all_to_all x0 -> x1, starting transfers between devices: none -> 3.51 us  [per_device(): sums = lax.all_to_all(partial, 'gx', 0, 0, tiled=True)]
  transfers between devices with their start and end apart: 28 -> 29, of which waited for: 6 -> 11; matrix products, arithmetic and copies ran while one was open for 1% -> 1% of each run, Pallas kernels for 1% -> 3%
where the time goes in v2:
time: 82.5 us; the launch traced here: 82.4 us
  starting transfers between devices  27.3 us (33%)
  Pallas kernels  21.1 us (26%)
  waiting for transfers between devices  20.3 us (25%)
  blocking collectives  12.1 us (15%)
  between operations  0.91 us (1%)
    ppermute x28, starting transfers between devices, exchange(): lax.ppermute(piece, 'gx', swap[-1])  23.7 us
    ppermute x28, waiting for transfers between devices, exchange(): lax.ppermute(piece, 'gx', swap[-1])  13.1 us
    all_to_all x1, blocking collectives, per_device(): sums = lax.all_to_all(partial, 'gx', 0, 0, tiled=True)  12.1 us
    all_to_all x1, waiting for transfers between devices, per_device(): sums = lax.all_to_all(partial, 'gx', 0, 0, tiled=True)  7.24 us
    pallas_call x3, Pallas kernels, per_device(): call(functools.partial(forward_kernel, swaps, colour), [kept] * (2 if col...  4.85 us
    pallas_call x1, Pallas kernels, per_device(): call(functools.partial(image_kernel, swaps, tiles), [off_kept, kept, vec(...  3.75 us
    pallas_call x2, Pallas kernels, per_device(): call(functools.partial(backward_kernel, swaps, tiles, colour), [kept] + p...  3.67 us
    all_to_all x1, starting transfers between devices, per_device(): sums = lax.all_to_all(partial, 'gx', 0, 0, tiled=True)  3.51 us
  transfers between devices with their start and end apart: 29, of which 11 were waited for; matrix products, arithmetic and copies ran while one was open for 1% of the time, Pallas kernels for 3%

profile of v2, /device:TPU:0, one launch (start us, length us, event | category | flops | bytes accessed | tf_op | source)
XLA Modules:
  0.0 82.4 jit_solution(2208087590555441411)
XLA Ops:
  0.7 1.0 %shard_map.191 = (f32[32,8,128]{2,1,0:T(8,128)S(1)}, s32[6,1,16]{2,1,0:T(1,128)S(4)}, bf16[128,128]{1,0:T(8,128)(2,1)S(1)}, bf16[128,128]{1,0:T(8,128)(2,1)S(1)}...) custom-call(f32[32,8,128]{2,1,0:T(8,128)} %q_hbm.1, s32[6,1,16]{2,1,0:T(1,128)} %bitcast.3), custom_call_target="tpu_custom_call" | custom-call | flops 10000000000 | tf_op jit(solution)/shard_map/pallas_call | solution.py:342
  1.7 0.0 copy-start.1
  1.7 0.5 collective-permute-start
  2.2 2.6 %collective-permute-start.1 = (bf16[128,128]{1,0:T(8,128)(2,1)S(1)}, bf16[128,128]{1,0:T(8,128)(2,1)S(1)}, u32[]{:S(2)}, u32[]{:S(2)}) collective-permute-start(bf16[128,128]{1,0:T(8,128)(2,1)S(1)} %get-tuple-element.63), channel_id=1, source_target_pairs={{0,3},{1,2},{2,1},{3,0},{4,7},{5,6},{6,5},{7,4},{8,11},{9,10},{10,... | collective-permute-start | bytes 98312 | tf_op jit(solution)/shard_map/ppermute | solution.py:340
  4.8 1.6 %collective-permute-start.2 = (bf16[128,128]{1,0:T(8,128)(2,1)S(1)}, bf16[128,128]{1,0:T(8,128)(2,1)S(1)}, u32[]{:S(2)}, u32[]{:S(2)}) collective-permute-start(bf16[128,128]{1,0:T(8,128)(2,1)S(1)} %get-tuple-element.64), channel_id=1, source_target_pairs={{0,4},{1,5},{2,6},{3,7},{4,0},{5,1},{6,2},{7,3},{8,12},{9,13},{10,... | collective-permute-start | bytes 98312 | tf_op jit(solution)/shard_map/ppermute | solution.py:340
  6.4 0.0 collective-permute-start.3
  6.4 2.4 %shard_map.192 = (bf16[32,9,128,128]{3,2,1,0:T(8,128)(2,1)S(1)}, s32[9,32]{1,0:T(8,128)S(4)}, s32[8,128]{1,0:T(8,128)S(4)}, f32[32,128]{1,0:T(8,128)S(1)}, f32[32,128]{1,0:T(8,128)S(1)}) custom-call(bf16[32,9,128,128]{3,2,1,0:T(8,128)(2,1)} %off_hbm.3, s32[9,32]{1,0:T(8,128)} %bitcast.2, s32[32]{0:T(128)} %colours_hbm.1, f32[32,128]{1,0:T(8,128)S(1)} %copy-done.5, ...), custom_call_target="tpu_custom_call" | custom-call | tf_op jit(solution)/shard_map/pallas_call | solution.py:350
  8.8 0.0 collective-permute-done.refs_0_
  8.8 0.0 collective-permute-done.1.refs_1_
  8.8 0.0 collective-permute-done.2.refs_2_
  8.8 0.0 collective-permute-done.3.refs_3_
  8.9 0.0 copy-start
  8.9 0.0 copy-start.2
  8.9 0.0 copy-start.8
  8.9 3.8 %shard_map.193 = (bf16[32,9,128,128]{3,2,1,0:T(8,128)(2,1)S(1)}, f32[32,8,128]{2,1,0:T(8,128)S(1)}, f32[16,8,128]{2,1,0:T(8,128)S(1)}) custom-call(f32[32,8,128]{2,1,0:T(8,128)S(1)} %get-tuple-element.59.q.q_ref, bf16[32,128,128]{2,1,0:T(8,128)(2,1)S(1)} %copy-done.1, bf16[32,9,128,128]{3,2,1,0:T(8,128)(2,1)} %off_hbm.3, ...), custom_call_target="tpu_custom_call", output_to_operand_aliasing={{0}: (3, {})} | custom-call | tf_op jit(solution)/shard_map/pallas_call | solution.py:356
  12.7 12.1 %all_to_all.10.sums = f32[16,8,128]{2,1,0:T(8,128)S(1)} all-to-all(f32[16,8,128]{2,1,0:T(8,128)S(1)} %get-tuple-element.66), channel_id=1, replica_groups=mesh['groups'=2,'gx'=16] {'gx'}, dimensions={0} | all-to-all | bytes 131072 | tf_op jit(solution)/shard_map/all_to_all | solution.py:363
  24.8 1.3 %shard_map.194 = (f32[32,8,128]{2,1,0:T(8,128)S(1)}, f32[32,8,128]{2,1,0:T(8,128)S(1)}, f32[8,128]{1,0:T(8,128)S(1)}, f32[8,128]{1,0:T(8,128)S(1)}, bf16[128,128...) custom-call(f32[16,8,128]{2,1,0:T(8,128)S(1)} %all_to_all.10.sums, ...), custom_call_target="tpu_custom_call" | custom-call | tf_op jit(solution)/shard_map/pallas_call | solution.py:364
  26.1 0.1 collective-permute-start.4
  26.2 0.2 collective-permute-start.5
  26.4 0.7 collective-permute-start.6
  27.1 0.3 collective-permute-done.4.refs_0_
  27.4 2.2 %collective-permute-done.5.refs_1_ = bf16[128,128]{1,0:T(8,128)(2,1)S(1)} collective-permute-done((bf16[128,128]{1,0:T(8,128)(2,1)S(1)}, bf16[128,128]{1,0:T(8,128)(2,1)S(1)}, u32[]{:S(2)}, u32[]{:S(2)}) %collective-permute-start.5) | collective-permute-done | bytes 32800 | tf_op jit(solution)/shard_map/ppermute | solution.py:340
  29.6 0.7 collective-permute-done.6.refs_2_
  30.4 1.1 %shard_map.195 = (f32[32,8,128]{2,1,0:T(8,128)S(1)}, bf16[128,128]{1,0:T(8,128)(2,1)S(1)}, bf16[128,128]{1,0:T(8,128)(2,1)S(1)}, bf16[128,128]{1,0:T(8,128)(2,1)S(1)}, bf16[128,128]{1,0:T(8,128)(2,1)S(1)}) custom-call(f32[32,8,128]{2,1,0:T(8,128)S(1)} %get-tuple-element.114.r_new.refs_4_, f32[32,8,128]{2,1,0:T(8,128)S(1)} %get-tuple-element.73.w_in, ...), custom_call_target="tpu_custom_call" | custom-call | tf_op jit(solution)/shard_map/pallas_call | solution.py:372
  31.5 0.5 collective-permute-start.8
  32.0 2.0 %collective-permute-start.9 = (bf16[128,128]{1,0:T(8,128)(2,1)S(1)}, bf16[128,128]{1,0:T(8,128)(2,1)S(1)}, u32[]{:S(2)}, u32[]{:S(2)}) collective-permute-start(bf16[128,128]{1,0:T(8,128)(2,1)S(1)} %get-tuple-element.81), channel_id=1, source_target_pairs={{0,3},{1,2},{2,1},{3,0},{4,7},{5,6},{6,5},{7,4},{8,11},{9,10},{10,... | collective-permute-start | bytes 98312 | tf_op jit(solution)/shard_map/ppermute | solution.py:340
  34.1 2.0 %collective-permute-start.10 = (bf16[128,128]{1,0:T(8,128)(2,1)S(1)}, bf16[128,128]{1,0:T(8,128)(2,1)S(1)}, u32[]{:S(2)}, u32[]{:S(2)}) collective-permute-start(bf16[128,128]{1,0:T(8,128)(2,1)S(1)} %get-tuple-element.82), channel_id=1, source_target_pairs={{0,4},{1,5},{2,6},{3,7},{4,0},{5,1},{6,2},{7,3},{8,12},{9,13},{10,... | collective-permute-start | bytes 98312 | tf_op jit(solution)/shard_map/ppermute | solution.py:340
  36.1 0.0 collective-permute-start.11
  36.1 0.0 collective-permute-done.8.refs_0_
  36.1 0.0 collective-permute-done.9.refs_1_
  36.1 1.9 %collective-permute-done.10.refs_2_ = bf16[128,128]{1,0:T(8,128)(2,1)S(1)} collective-permute-done((bf16[128,128]{1,0:T(8,128)(2,1)S(1)}, bf16[128,128]{1,0:T(8,128)(2,1)S(1)}, u32[]{:S(2)}, u32[]{:S(2)}) %collective-permute-start.10) | collective-permute-done | bytes 32800 | tf_op jit(solution)/shard_map/ppermute | solution.py:340
  38.0 2.5 %shard_map.196 = (f32[32,8,128]{2,1,0:T(8,128)S(1)}, bf16[128,128]{1,0:T(8,128)(2,1)S(1)}, bf16[128,128]{1,0:T(8,128)(2,1)S(1)}, bf16[128,128]{1,0:T(8,128)(2,1)S(1)}, bf16[128,128]{1,0:T(8,128)(2,1)S(1)}) custom-call(f32[32,8,128]{2,1,0:T(8,128)S(1)} %get-tuple-element.114.r_new.refs_4_, f32[32,8,128]{2,1,0:T(8,128)S(1)} %get-tuple-element.79.w_in, ...), custom_call_target="tpu_custom_call" | custom-call | tf_op jit(solution)/shard_map/pallas_call | solution.py:372
  40.5 0.1 collective-permute-start.12
  40.6 0.1 collective-permute-start.13
  40.7 1.7 %collective-permute-start.14 = (bf16[128,128]{1,0:T(8,128)(2,1)S(1)}, bf16[128,128]{1,0:T(8,128)(2,1)S(1)}, u32[]{:S(2)}, u32[]{:S(2)}) collective-permute-start(bf16[128,128]{1,0:T(8,128)(2,1)S(1)} %get-tuple-element.87), channel_id=1, source_target_pairs={{0,4},{1,5},{2,6},{3,7},{4,0},{5,1},{6,2},{7,3},{8,12},{9,13},{10,... | collective-permute-start | bytes 98312 | tf_op jit(solution)/shard_map/ppermute | solution.py:340
  42.4 1.6 %collective-permute-done.13.refs_1_ = bf16[128,128]{1,0:T(8,128)(2,1)S(1)} collective-permute-done((bf16[128,128]{1,0:T(8,128)(2,1)S(1)}, bf16[128,128]{1,0:T(8,128)(2,1)S(1)}, u32[]{:S(2)}, u32[]{:S(2)}) %collective-permute-start.13) | collective-permute-done | bytes 32800 | tf_op jit(solution)/shard_map/ppermute | solution.py:340
  44.0 0.7 collective-permute-done.14.refs_2_
  44.7 1.2 %shard_map.197 = (f32[32,8,128]{2,1,0:T(8,128)S(1)}, f32[32,8,128]{2,1,0:T(8,128)S(1)}, bf16[128,128]{1,0:T(8,128)(2,1)S(1)}, bf16[128,128]{1,0:T(8,128)(2,1)S(1...) custom-call(f32[32,8,128]{2,1,0:T(8,128)S(1)} %get-tuple-element.114.r_new.refs_4_, ...), custom_call_target="tpu_custom_call" | custom-call | tf_op jit(solution)/shard_map/pallas_call | solution.py:372
  45.9 0.6 collective-permute-start.16
  46.5 2.0 %collective-permute-start.17 = (bf16[128,128]{1,0:T(8,128)(2,1)S(1)}, bf16[128,128]{1,0:T(8,128)(2,1)S(1)}, u32[]{:S(2)}, u32[]{:S(2)}) collective-permute-start(bf16[128,128]{1,0:T(8,128)(2,1)S(1)} %get-tuple-element.92), channel_id=1, source_target_pairs={{0,3},{1,2},{2,1},{3,0},{4,7},{5,6},{6,5},{7,4},{8,11},{9,10},{10,... | collective-permute-start | bytes 98312 | tf_op jit(solution)/shard_map/ppermute | solution.py:340
  48.5 2.0 %collective-permute-start.18 = (bf16[128,128]{1,0:T(8,128)(2,1)S(1)}, bf16[128,128]{1,0:T(8,128)(2,1)S(1)}, u32[]{:S(2)}, u32[]{:S(2)}) collective-permute-start(bf16[128,128]{1,0:T(8,128)(2,1)S(1)} %get-tuple-element.93), channel_id=1, source_target_pairs={{0,4},{1,5},{2,6},{3,7},{4,0},{5,1},{6,2},{7,3},{8,12},{9,13},{10,... | collective-permute-start | bytes 98312 | tf_op jit(solution)/shard_map/ppermute | solution.py:340
  50.5 0.0 collective-permute-done.17.refs_1_
  50.6 1.9 %collective-permute-done.18.refs_2_ = bf16[128,128]{1,0:T(8,128)(2,1)S(1)} collective-permute-done((bf16[128,128]{1,0:T(8,128)(2,1)S(1)}, bf16[128,128]{1,0:T(8,128)(2,1)S(1)}, u32[]{:S(2)}, u32[]{:S(2)}) %collective-permute-start.18) | collective-permute-done | bytes 32800 | tf_op jit(solution)/shard_map/ppermute | solution.py:340
  52.4 2.5 %shard_map.198 = (f32[32,8,128]{2,1,0:T(8,128)S(1)}, bf16[128,128]{1,0:T(8,128)(2,1)S(1)}, bf16[128,128]{1,0:T(8,128)(2,1)S(1)}, bf16[128,128]{1,0:T(8,128)(2,1)S(1)}, bf16[128,128]{1,0:T(8,128)(2,1)S(1)}) custom-call(f32[32,8,128]{2,1,0:T(8,128)S(1)} %get-tuple-element.89.w, f32[32,8,128]{2,1,0:T(8,128)S(1)} %get-tuple-element.90.z_in, ...), custom_call_target="tpu_custom_call" | custom-call | tf_op jit(solution)/shard_map/pallas_call | solution.py:380
  55.0 0.1 collective-permute-start.20
  55.0 0.2 collective-permute-start.21
  55.2 2.0 %collective-permute-start.22 = (bf16[128,128]{1,0:T(8,128)(2,1)S(1)}, bf16[128,128]{1,0:T(8,128)(2,1)S(1)}, u32[]{:S(2)}, u32[]{:S(2)}) collective-permute-start(bf16[128,128]{1,0:T(8,128)(2,1)S(1)} %get-tuple-element.98), channel_id=1, source_target_pairs={{0,4},{1,5},{2,6},{3,7},{4,0},{5,1},{6,2},{7,3},{8,12},{9,13},{10,... | collective-permute-start | bytes 98312 | tf_op jit(solution)/shard_map/ppermute | solution.py:340
  57.2 0.0 collective-permute-start.23
  57.2 0.0 collective-permute-done.20.refs_0_
  57.2 1.2 %collective-permute-done.21.refs_1_ = bf16[128,128]{1,0:T(8,128)(2,1)S(1)} collective-permute-done((bf16[128,128]{1,0:T(8,128)(2,1)S(1)}, bf16[128,128]{1,0:T(8,128)(2,1)S(1)}, u32[]{:S(2)}, u32[]{:S(2)}) %collective-permute-start.21) | collective-permute-done | bytes 32800 | tf_op jit(solution)/shard_map/ppermute | solution.py:340
  58.4 0.7 collective-permute-done.22.refs_2_
  59.1 0.0 collective-permute-done.23.refs_3_
  59.1 0.0 copy-start.10
  59.1 1.2 %shard_map.199 = (f32[32,8,128]{2,1,0:T(8,128)S(1)}, bf16[128,128]{1,0:T(8,128)(2,1)S(1)}, bf16[128,128]{1,0:T(8,128)(2,1)S(1)}, bf16[128,128]{1,0:T(8,128)(2,1)S(1)}, bf16[128,128]{1,0:T(8,128)(2,1)S(1)}) custom-call(f32[32,8,128]{2,1,0:T(8,128)S(1)} %get-tuple-element.89.w, f32[32,8,128]{2,1,0:T(8,128)S(1)} %get-tuple-element.95.z_in, ...), custom_call_target="tpu_custom_call" | custom-call | tf_op jit(solution)/shard_map/pallas_call | solution.py:380
  60.3 0.6 collective-permute-start.24
  60.9 2.0 %collective-permute-start.25 = (bf16[128,128]{1,0:T(8,128)(2,1)S(1)}, bf16[128,128]{1,0:T(8,128)(2,1)S(1)}, u32[]{:S(2)}, u32[]{:S(2)}) collective-permute-start(bf16[128,128]{1,0:T(8,128)(2,1)S(1)} %get-tuple-element.102), channel_id=1, source_target_pairs={{0,3},{1,2},{2,1},{3,0},{4,7},{5,6},{6,5},{7,4},{8,11},{9,10},{10,... | collective-permute-start | bytes 98312 | tf_op jit(solution)/shard_map/ppermute | solution.py:340
  62.9 2.0 %collective-permute-start.26 = (bf16[128,128]{1,0:T(8,128)(2,1)S(1)}, bf16[128,128]{1,0:T(8,128)(2,1)S(1)}, u32[]{:S(2)}, u32[]{:S(2)}) collective-permute-start(bf16[128,128]{1,0:T(8,128)(2,1)S(1)} %get-tuple-element.103), channel_id=1, source_target_pairs={{0,4},{1,5},{2,6},{3,7},{4,0},{5,1},{6,2},{7,3},{8,12},{9,13},{10,... | collective-permute-start | bytes 98312 | tf_op jit(solution)/shard_map/ppermute | solution.py:340
  65.0 1.9 %collective-permute-done.26.refs_2_ = bf16[128,128]{1,0:T(8,128)(2,1)S(1)} collective-permute-done((bf16[128,128]{1,0:T(8,128)(2,1)S(1)}, bf16[128,128]{1,0:T(8,128)(2,1)S(1)}, u32[]{:S(2)}, u32[]{:S(2)}) %collective-permute-start.26) | collective-permute-done | bytes 32800 | tf_op jit(solution)/shard_map/ppermute | solution.py:340
  66.9 0.0 collective-permute-done.27.refs_3_
  66.9 2.7 %shard_map.200 = (f32[32,8,128]{2,1,0:T(8,128)S(1)}, f32[16,16,128]{2,1,0:T(8,128)}) custom-call(f32[32,8,128]{2,1,0:T(8,128)S(1)} %get-tuple-element.89.w, f32[32,8,128]{2,1,0:T(8,128)S(1)} %get-tuple-element.100.z_in, bf16[32,9,128,128]{3,2,1,0:T(8,128)(2,1)S(1)} %get-tuple-element.74.off, bf16[32,128,128]{2,1,0:T(8,128)(2,1)S(1)} %copy-done, ...), custom_call_target="tpu_custom_call" | custom-call | tf_op jit(solution)/shard_map/pallas_call | solution.py:386
  69.5 3.5 %all-to-all-start.1 = ((f32[16,16,128]{2,1,0:T(8,128)}), f32[16,16,128]{2,1,0:T(8,128)S(1)}, u32[]{:S(2)}, u32[]{:S(2)}) async-start(f32[16,16,128]{2,1,0:T(8,128)} %get-tuple-element.106), calls=%async_computation.1 | async-start | bytes 262144 | tf_op jit(solution)/shard_map/all_to_all | solution.py:392
  73.1 0.7 copy.23
  73.7 7.2 %all-to-all-done.1.sums = f32[16,16,128]{2,1,0:T(8,128)S(1)} async-done(((f32[16,16,128]{2,1,0:T(8,128)}), f32[16,16,128]{2,1,0:T(8,128)S(1)}, u32[]{:S(2)}, u32[]{:S(2)}) %all-to-all-start.1) | async-done | bytes 131104 | tf_op jit(solution)/shard_map/all_to_all | solution.py:392
  81.0 1.4 %shard_map.201 = (f32[32,8,128]{2,1,0:T(8,128)}, f32[32,8,128]{2,1,0:T(8,128)}, f32[32,8,128]{2,1,0:T(8,128)}, f32[3,8]{1,0:T(4,128)}) custom-call(f32[16,16,128]{2,1,0:T(8,128)S(1)} %all-to-all-done.1.sums, f32[32,8,128]{2,1,0:T(8,128)S(1)} %get-tuple-element.107.z, f32[32,8,128]{2,1,0:T(8,128)S(1)} %get-tuple-element.59.q.q_ref, ...), custom_call_target="tpu_custom_call" | custom-call | tf_op jit(solution)/shard_map/pallas_call | solution.py:394
  (29 shorter events, 0.1 us)
Async XLA Ops:
  0.6 5.8 %copy-start.5 = (f32[32,128]{1,0:T(8,128)S(1)}, f32[32,128]{1,0:T(8,128)}, u32[]{:S(2)}) copy-start(f32[32,128]{1,0:T(8,128)} %diag_ref.1) | copy-start | bytes 49156
  0.6 5.8 %copy-start.6 = (f32[32,64]{1,0:T(8,128)S(1)}, f32[32,64]{1,0:T(8,128)}, u32[]{:S(2)}) copy-start(f32[32,64]{1,0:T(8,128)} %off_ref.1) | copy-start | bytes 24580
  0.7 5.8 %copy-start.7 = (s32[32,64]{1,0:T(8,128)S(1)}, s32[32,64]{1,0:T(8,128)}, u32[]{:S(2)}) copy-start(s32[32,64]{1,0:T(8,128)} %pairs_ref.1) | copy-start | bytes 24580
  1.7 7.2 %copy-start.1 = (bf16[32,128,128]{2,1,0:T(8,128)(2,1)S(1)}, bf16[32,128,128]{2,1,0:T(8,128)(2,1)}, u32[]{:S(2)}) copy-start(bf16[32,128,128]{2,1,0:T(8,128)(2,1)} %diag.1) | copy-start | bytes 3145732
  1.7 7.1 %collective-permute-start = (bf16[128,128]{1,0:T(8,128)(2,1)S(1)}, bf16[128,128]{1,0:T(8,128)(2,1)S(1)}, u32[]{:S(2)}, u32[]{:S(2)}) collective-permute-start(bf16[128,128]{1,0:T(8,128)(2,1)S(1)} %get-tuple-element.62), channel_id=1, source_target_pairs={{0,1},{1,0},{2,3},{3,2},{4,5},{5,4},{6,7},{7,6},{8,9},{9,8},{10,11... | collective-permute-start | bytes 98312 | tf_op jit(solution)/shard_map/ppermute | solution.py:340
  2.2 6.6 %collective-permute-start.1 = (bf16[128,128]{1,0:T(8,128)(2,1)S(1)}, bf16[128,128]{1,0:T(8,128)(2,1)S(1)}, u32[]{:S(2)}, u32[]{:S(2)}) collective-permute-start(bf16[128,128]{1,0:T(8,128)(2,1)S(1)} %get-tuple-element.63), channel_id=1, source_target_pairs={{0,3},{1,2},{2,1},{3,0},{4,7},{5,6},{6,5},{7,4},{8,11},{9,10},{10,... | collective-permute-start | bytes 98312 | tf_op jit(solution)/shard_map/ppermute | solution.py:340
  4.8 4.0 %collective-permute-start.2 = (bf16[128,128]{1,0:T(8,128)(2,1)S(1)}, bf16[128,128]{1,0:T(8,128)(2,1)S(1)}, u32[]{:S(2)}, u32[]{:S(2)}) collective-permute-start(bf16[128,128]{1,0:T(8,128)(2,1)S(1)} %get-tuple-element.64), channel_id=1, source_target_pairs={{0,4},{1,5},{2,6},{3,7},{4,0},{5,1},{6,2},{7,3},{8,12},{9,13},{10,... | collective-permute-start | bytes 98312 | tf_op jit(solution)/shard_map/ppermute | solution.py:340
  6.4 2.4 %collective-permute-start.3 = (bf16[128,128]{1,0:T(8,128)(2,1)S(1)}, bf16[128,128]{1,0:T(8,128)(2,1)S(1)}, u32[]{:S(2)}, u32[]{:S(2)}) collective-permute-start(bf16[128,128]{1,0:T(8,128)(2,1)S(1)} %get-tuple-element.65), channel_id=1, source_target_pairs={{0,1},{1,0},{2,3},{3,2},{4,8},{5,9},{6,10},{7,11},{8,4},{9,5},{10,... | collective-permute-start | bytes 98312 | tf_op jit(solution)/shard_map/ppermute | solution.py:340
  8.9 15.9 %copy-start = (bf16[32,128,128]{2,1,0:T(8,128)(2,1)S(1)}, bf16[32,128,128]{2,1,0:T(8,128)(2,1)}, u32[]{:S(2)}) copy-start(bf16[32,128,128]{2,1,0:T(8,128)(2,1)} %factor.13) | copy-start | bytes 3145732
  8.9 15.9 %copy-start.2 = (f32[32,8,128]{2,1,0:T(8,128)S(1)}, f32[32,8,128]{2,1,0:T(8,128)}, u32[]{:S(2)}) copy-start(f32[32,8,128]{2,1,0:T(8,128)} %r_ref.1) | copy-start | bytes 393220
  8.9 15.9 %copy-start.8 = (f32[8]{0:T(128)S(1)}, f32[8]{0:T(128)}, u32[]{:S(2)}) copy-start(f32[8]{0:T(128)} %rho.3) | copy-start | bytes 100
  26.1 1.3 %collective-permute-start.4 = (bf16[128,128]{1,0:T(8,128)(2,1)S(1)}, bf16[128,128]{1,0:T(8,128)(2,1)S(1)}, u32[]{:S(2)}, u32[]{:S(2)}) collective-permute-start(bf16[128,128]{1,0:T(8,128)(2,1)S(1)} %get-tuple-element.75), channel_id=1, source_target_pairs={{0,1},{1,0},{2,3},{3,2},{4,5},{5,4},{6,7},{7,6},{8,9},{9,8},{10,11... | collective-permute-start | bytes 98312 | tf_op jit(solution)/shard_map/ppermute | solution.py:340
  26.2 3.4 %collective-permute-start.5 = (bf16[128,128]{1,0:T(8,128)(2,1)S(1)}, bf16[128,128]{1,0:T(8,128)(2,1)S(1)}, u32[]{:S(2)}, u32[]{:S(2)}) collective-permute-start(bf16[128,128]{1,0:T(8,128)(2,1)S(1)} %get-tuple-element.76), channel_id=1, source_target_pairs={{0,3},{1,2},{2,1},{3,0},{4,7},{5,6},{6,5},{7,4},{8,11},{9,10},{10,... | collective-permute-start | bytes 98312 | tf_op jit(solution)/shard_map/ppermute | solution.py:340
  26.4 3.9 %collective-permute-start.6 = (bf16[128,128]{1,0:T(8,128)(2,1)S(1)}, bf16[128,128]{1,0:T(8,128)(2,1)S(1)}, u32[]{:S(2)}, u32[]{:S(2)}) collective-permute-start(bf16[128,128]{1,0:T(8,128)(2,1)S(1)} %get-tuple-element.77), channel_id=1, source_target_pairs={{0,4},{1,5},{2,6},{3,7},{4,0},{5,1},{6,2},{7,3},{8,12},{9,13},{10,... | collective-permute-start | bytes 98312 | tf_op jit(solution)/shard_map/ppermute | solution.py:340
  27.1 3.2 %collective-permute-start.7 = (bf16[128,128]{1,0:T(8,128)(2,1)S(1)}, bf16[128,128]{1,0:T(8,128)(2,1)S(1)}, u32[]{:S(2)}, u32[]{:S(2)}) collective-permute-start(bf16[128,128]{1,0:T(8,128)(2,1)S(1)} %get-tuple-element.78), channel_id=1, source_target_pairs={{0,1},{1,0},{2,3},{3,2},{4,8},{5,9},{6,10},{7,11},{8,4},{9,5},{10,... | collective-permute-start | bytes 98312 | tf_op jit(solution)/shard_map/ppermute | solution.py:340
  31.5 4.6 %collective-permute-start.8 = (bf16[128,128]{1,0:T(8,128)(2,1)S(1)}, bf16[128,128]{1,0:T(8,128)(2,1)S(1)}, u32[]{:S(2)}, u32[]{:S(2)}) collective-permute-start(bf16[128,128]{1,0:T(8,128)(2,1)S(1)} %get-tuple-element.80), channel_id=1, source_target_pairs={{0,1},{1,0},{2,3},{3,2},{4,5},{5,4},{6,7},{7,6},{8,9},{9,8},{10,11... | collective-permute-start | bytes 98312 | tf_op jit(solution)/shard_map/ppermute | solution.py:340
  32.0 4.1 %collective-permute-start.9 = (bf16[128,128]{1,0:T(8,128)(2,1)S(1)}, bf16[128,128]{1,0:T(8,128)(2,1)S(1)}, u32[]{:S(2)}, u32[]{:S(2)}) collective-permute-start(bf16[128,128]{1,0:T(8,128)(2,1)S(1)} %get-tuple-element.81), channel_id=1, source_target_pairs={{0,3},{1,2},{2,1},{3,0},{4,7},{5,6},{6,5},{7,4},{8,11},{9,10},{10,... | collective-permute-start | bytes 98312 | tf_op jit(solution)/shard_map/ppermute | solution.py:340
  34.1 3.9 %collective-permute-start.10 = (bf16[128,128]{1,0:T(8,128)(2,1)S(1)}, bf16[128,128]{1,0:T(8,128)(2,1)S(1)}, u32[]{:S(2)}, u32[]{:S(2)}) collective-permute-start(bf16[128,128]{1,0:T(8,128)(2,1)S(1)} %get-tuple-element.82), channel_id=1, source_target_pairs={{0,4},{1,5},{2,6},{3,7},{4,0},{5,1},{6,2},{7,3},{8,12},{9,13},{10,... | collective-permute-start | bytes 98312 | tf_op jit(solution)/shard_map/ppermute | solution.py:340
  36.1 1.9 %collective-permute-start.11 = (bf16[128,128]{1,0:T(8,128)(2,1)S(1)}, bf16[128,128]{1,0:T(8,128)(2,1)S(1)}, u32[]{:S(2)}, u32[]{:S(2)}) collective-permute-start(bf16[128,128]{1,0:T(8,128)(2,1)S(1)} %get-tuple-element.83), channel_id=1, source_target_pairs={{0,1},{1,0},{2,3},{3,2},{4,8},{5,9},{6,10},{7,11},{8,4},{9,5},{10,... | collective-permute-start | bytes 98312 | tf_op jit(solution)/shard_map/ppermute | solution.py:340
  40.5 1.9 %collective-permute-start.12 = (bf16[128,128]{1,0:T(8,128)(2,1)S(1)}, bf16[128,128]{1,0:T(8,128)(2,1)S(1)}, u32[]{:S(2)}, u32[]{:S(2)}) collective-permute-start(bf16[128,128]{1,0:T(8,128)(2,1)S(1)} %get-tuple-element.85), channel_id=1, source_target_pairs={{0,1},{1,0},{2,3},{3,2},{4,5},{5,4},{6,7},{7,6},{8,9},{9,8},{10,11... | collective-permute-start | bytes 98312 | tf_op jit(solution)/shard_map/ppermute | solution.py:340
  40.6 3.4 %collective-permute-start.13 = (bf16[128,128]{1,0:T(8,128)(2,1)S(1)}, bf16[128,128]{1,0:T(8,128)(2,1)S(1)}, u32[]{:S(2)}, u32[]{:S(2)}) collective-permute-start(bf16[128,128]{1,0:T(8,128)(2,1)S(1)} %get-tuple-element.86), channel_id=1, source_target_pairs={{0,3},{1,2},{2,1},{3,0},{4,7},{5,6},{6,5},{7,4},{8,11},{9,10},{10,... | collective-permute-start | bytes 98312 | tf_op jit(solution)/shard_map/ppermute | solution.py:340
  40.7 4.0 %collective-permute-start.14 = (bf16[128,128]{1,0:T(8,128)(2,1)S(1)}, bf16[128,128]{1,0:T(8,128)(2,1)S(1)}, u32[]{:S(2)}, u32[]{:S(2)}) collective-permute-start(bf16[128,128]{1,0:T(8,128)(2,1)S(1)} %get-tuple-element.87), channel_id=1, source_target_pairs={{0,4},{1,5},{2,6},{3,7},{4,0},{5,1},{6,2},{7,3},{8,12},{9,13},{10,... | collective-permute-start | bytes 98312 | tf_op jit(solution)/shard_map/ppermute | solution.py:340
  42.4 2.3 %collective-permute-start.15 = (bf16[128,128]{1,0:T(8,128)(2,1)S(1)}, bf16[128,128]{1,0:T(8,128)(2,1)S(1)}, u32[]{:S(2)}, u32[]{:S(2)}) collective-permute-start(bf16[128,128]{1,0:T(8,128)(2,1)S(1)} %get-tuple-element.88), channel_id=1, source_target_pairs={{0,1},{1,0},{2,3},{3,2},{4,8},{5,9},{6,10},{7,11},{8,4},{9,5},{10,... | collective-permute-start | bytes 98312 | tf_op jit(solution)/shard_map/ppermute | solution.py:340
  45.9 4.7 %collective-permute-start.16 = (bf16[128,128]{1,0:T(8,128)(2,1)S(1)}, bf16[128,128]{1,0:T(8,128)(2,1)S(1)}, u32[]{:S(2)}, u32[]{:S(2)}) collective-permute-start(bf16[128,128]{1,0:T(8,128)(2,1)S(1)} %get-tuple-element.91), channel_id=1, source_target_pairs={{0,1},{1,0},{2,3},{3,2},{4,5},{5,4},{6,7},{7,6},{8,9},{9,8},{10,11... | collective-permute-start | bytes 98312 | tf_op jit(solution)/shard_map/ppermute | solution.py:340
  46.5 4.1 %collective-permute-start.17 = (bf16[128,128]{1,0:T(8,128)(2,1)S(1)}, bf16[128,128]{1,0:T(8,128)(2,1)S(1)}, u32[]{:S(2)}, u32[]{:S(2)}) collective-permute-start(bf16[128,128]{1,0:T(8,128)(2,1)S(1)} %get-tuple-element.92), channel_id=1, source_target_pairs={{0,3},{1,2},{2,1},{3,0},{4,7},{5,6},{6,5},{7,4},{8,11},{9,10},{10,... | collective-permute-start | bytes 98312 | tf_op jit(solution)/shard_map/ppermute | solution.py:340
  48.5 3.9 %collective-permute-start.18 = (bf16[128,128]{1,0:T(8,128)(2,1)S(1)}, bf16[128,128]{1,0:T(8,128)(2,1)S(1)}, u32[]{:S(2)}, u32[]{:S(2)}) collective-permute-start(bf16[128,128]{1,0:T(8,128)(2,1)S(1)} %get-tuple-element.93), channel_id=1, source_target_pairs={{0,4},{1,5},{2,6},{3,7},{4,0},{5,1},{6,2},{7,3},{8,12},{9,13},{10,... | collective-permute-start | bytes 98312 | tf_op jit(solution)/shard_map/ppermute | solution.py:340
  50.5 1.9 %collective-permute-start.19 = (bf16[128,128]{1,0:T(8,128)(2,1)S(1)}, bf16[128,128]{1,0:T(8,128)(2,1)S(1)}, u32[]{:S(2)}, u32[]{:S(2)}) collective-permute-start(bf16[128,128]{1,0:T(8,128)(2,1)S(1)} %get-tuple-element.94), channel_id=1, source_target_pairs={{0,1},{1,0},{2,3},{3,2},{4,8},{5,9},{6,10},{7,11},{8,4},{9,5},{10,... | collective-permute-start | bytes 98312 | tf_op jit(solution)/shard_map/ppermute | solution.py:340
  55.0 2.3 %collective-permute-start.20 = (bf16[128,128]{1,0:T(8,128)(2,1)S(1)}, bf16[128,128]{1,0:T(8,128)(2,1)S(1)}, u32[]{:S(2)}, u32[]{:S(2)}) collective-permute-start(bf16[128,128]{1,0:T(8,128)(2,1)S(1)} %get-tuple-element.96), channel_id=1, source_target_pairs={{0,1},{1,0},{2,3},{3,2},{4,5},{5,4},{6,7},{7,6},{8,9},{9,8},{10,11... | collective-permute-start | bytes 98312 | tf_op jit(solution)/shard_map/ppermute | solution.py:340
  55.0 3.4 %collective-permute-start.21 = (bf16[128,128]{1,0:T(8,128)(2,1)S(1)}, bf16[128,128]{1,0:T(8,128)(2,1)S(1)}, u32[]{:S(2)}, u32[]{:S(2)}) collective-permute-start(bf16[128,128]{1,0:T(8,128)(2,1)S(1)} %get-tuple-element.97), channel_id=1, source_target_pairs={{0,3},{1,2},{2,1},{3,0},{4,7},{5,6},{6,5},{7,4},{8,11},{9,10},{10,... | collective-permute-start | bytes 98312 | tf_op jit(solution)/shard_map/ppermute | solution.py:340
  55.2 3.9 %collective-permute-start.22 = (bf16[128,128]{1,0:T(8,128)(2,1)S(1)}, bf16[128,128]{1,0:T(8,128)(2,1)S(1)}, u32[]{:S(2)}, u32[]{:S(2)}) collective-permute-start(bf16[128,128]{1,0:T(8,128)(2,1)S(1)} %get-tuple-element.98), channel_id=1, source_target_pairs={{0,4},{1,5},{2,6},{3,7},{4,0},{5,1},{6,2},{7,3},{8,12},{9,13},{10,... | collective-permute-start | bytes 98312 | tf_op jit(solution)/shard_map/ppermute | solution.py:340
  57.2 1.9 %collective-permute-start.23 = (bf16[128,128]{1,0:T(8,128)(2,1)S(1)}, bf16[128,128]{1,0:T(8,128)(2,1)S(1)}, u32[]{:S(2)}, u32[]{:S(2)}) collective-permute-start(bf16[128,128]{1,0:T(8,128)(2,1)S(1)} %get-tuple-element.99), channel_id=1, source_target_pairs={{0,1},{1,0},{2,3},{3,2},{4,8},{5,9},{6,10},{7,11},{8,4},{9,5},{10,... | collective-permute-start | bytes 98312 | tf_op jit(solution)/shard_map/ppermute | solution.py:340
  59.1 21.8 %copy-start.3 = (f32[32,8,128]{2,1,0:T(8,128)S(1)}, f32[32,8,128]{2,1,0:T(8,128)}, u32[]{:S(2)}) copy-start(f32[32,8,128]{2,1,0:T(8,128)} %x_ref.1) | copy-start | bytes 393220
  59.1 21.8 %copy-start.4 = (f32[32,8,128]{2,1,0:T(8,128)S(1)}, f32[32,8,128]{2,1,0:T(8,128)}, u32[]{:S(2)}) copy-start(f32[32,8,128]{2,1,0:T(8,128)} %d_ref.1) | copy-start | bytes 393220
  59.1 21.8 %copy-start.9 = (f32[8]{0:T(128)S(1)}, f32[8]{0:T(128)}, u32[]{:S(2)}) copy-start(f32[8]{0:T(128)} %tau.1) | copy-start | bytes 100
  59.1 21.8 %copy-start.10 = (f32[8]{0:T(128)S(1)}, f32[8]{0:T(128)}, u32[]{:S(2)}) copy-start(f32[8]{0:T(128)} %theta_in.1) | copy-start | bytes 100
  60.3 4.6 %collective-permute-start.24 = (bf16[128,128]{1,0:T(8,128)(2,1)S(1)}, bf16[128,128]{1,0:T(8,128)(2,1)S(1)}, u32[]{:S(2)}, u32[]{:S(2)}) collective-permute-start(bf16[128,128]{1,0:T(8,128)(2,1)S(1)} %get-tuple-element.101), channel_id=1, source_target_pairs={{0,1},{1,0},{2,3},{3,2},{4,5},{5,4},{6,7},{7,6},{8,9},{9,8},{10,11... | collective-permute-start | bytes 98312 | tf_op jit(solution)/shard_map/ppermute | solution.py:340
  60.9 4.0 %collective-permute-start.25 = (bf16[128,128]{1,0:T(8,128)(2,1)S(1)}, bf16[128,128]{1,0:T(8,128)(2,1)S(1)}, u32[]{:S(2)}, u32[]{:S(2)}) collective-permute-start(bf16[128,128]{1,0:T(8,128)(2,1)S(1)} %get-tuple-element.102), channel_id=1, source_target_pairs={{0,3},{1,2},{2,1},{3,0},{4,7},{5,6},{6,5},{7,4},{8,11},{9,10},{10,... | collective-permute-start | bytes 98312 | tf_op jit(solution)/shard_map/ppermute | solution.py:340
  62.9 3.9 %collective-permute-start.26 = (bf16[128,128]{1,0:T(8,128)(2,1)S(1)}, bf16[128,128]{1,0:T(8,128)(2,1)S(1)}, u32[]{:S(2)}, u32[]{:S(2)}) collective-permute-start(bf16[128,128]{1,0:T(8,128)(2,1)S(1)} %get-tuple-element.103), channel_id=1, source_target_pairs={{0,4},{1,5},{2,6},{3,7},{4,0},{5,1},{6,2},{7,3},{8,12},{9,13},{10,... | collective-permute-start | bytes 98312 | tf_op jit(solution)/shard_map/ppermute | solution.py:340
  64.9 1.9 %collective-permute-start.27 = (bf16[128,128]{1,0:T(8,128)(2,1)S(1)}, bf16[128,128]{1,0:T(8,128)(2,1)S(1)}, u32[]{:S(2)}, u32[]{:S(2)}) collective-permute-start(bf16[128,128]{1,0:T(8,128)(2,1)S(1)} %get-tuple-element.104), channel_id=1, source_target_pairs={{0,1},{1,0},{2,3},{3,2},{4,8},{5,9},{6,10},{7,11},{8,4},{9,5},{10,... | collective-permute-start | bytes 98312 | tf_op jit(solution)/shard_map/ppermute | solution.py:340
  69.5 11.4 %all-to-all-start.1 = ((f32[16,16,128]{2,1,0:T(8,128)}), f32[16,16,128]{2,1,0:T(8,128)S(1)}, u32[]{:S(2)}, u32[]{:S(2)}) async-start(f32[16,16,128]{2,1,0:T(8,128)} %get-tuple-element.106), calls=%async_computation.1 | async-start | bytes 262144 | tf_op jit(solution)/shard_map/all_to_all | solution.py:392

commit v3 on v2

--- a/solution.py
+++ b/solution.py
@@ -62,7 +62,7 @@
     reached = set()
     for (axis, phase, extent, _), piece in zip(swaps, arrived):
         up, real = partner(axis, phase, extent)
-        value = piece[...].astype(F32).reshape(16, 8, 128)
+        value = piece[pl.ds(0, 128), :].astype(F32).reshape(16, 8, 128)
         extended[pl.ds(32 + (2 * axis + up) * 16, 16)] = jnp.where(real, value, zeros)
         reached.add((axis, phase))
     for axis in range(3):
@@ -188,7 +188,7 @@
 
 
 def start_kernel(
-    swaps, count, sums, r_ref, image, rho, factor, straight, crossed, tables, faces, r_new, w, norm, alpha, *sent
+    swaps, count, sums, r_ref, image, rho, factor, straight, crossed, tables, faces, r_new, w, alpha, *sent
 ):
     sigma = jnp.sum(jnp.sum(sums[...], axis=0), axis=1, keepdims=True) / count
     sigma = jnp.where(sigma >= 0, jnp.maximum(sigma, 0.5), jnp.minimum(sigma, -0.5))
@@ -196,7 +196,6 @@
     alpha[...] = step_size
     new = r_ref[...] - step_size[None] * image[...]
     r_new[...] = new
-    norm[...] = jnp.sum(new * new, axis=0)
     w[...] = jnp.zeros_like(w)
 
     def body(blocks):
@@ -207,9 +206,52 @@
     send_faces(swaps, w, faces, sent)
 
 
+def adjoint_kernel(r_new, w, off, columns, tables, adjoint, terms):
+    new = r_new[...]
+    terms[pl.ds(0, 8), :] = jnp.sum(new * w[...], axis=0)
+    terms[pl.ds(8, 8), :] = jnp.sum(new * new, axis=0)
+    adjoint[...] = jnp.zeros_like(adjoint)
+    count = tables[4, 0]
+
+    def step(group, carry):
+        products = []
+        for j in range(COUPLE):
+            place = group * COUPLE + j
+            block = tables[0, place]
+            vector = jnp.where(place < count, w[block], 0.0)
+            high = vector.astype(BF16)
+            low = (vector - high.astype(F32)).astype(BF16)
+            matrix = jnp.concatenate([off[block, k] for k in range(9)], axis=1)
+            both = jnp.dot(jnp.concatenate([high, low], axis=0), matrix, preferred_element_type=F32)
+            products.append((block, both[:8] + both[8:]))
+        for block, product in products:
+            for k in range(9):
+                column = columns[k, block]
+                adjoint[column] = adjoint[column] + product[:, k * 128 : k * 128 + 128]
+        return carry
+
+    lax.fori_loop(0, (count + COUPLE - 1) // COUPLE, step, 0)
+
+
+def gather_kernel(swaps, adjoint, faces, *refs):
+    arrived, total = refs[:-1], refs[-1]
+    total[...] = adjoint[pl.ds(0, 32)]
+    for (axis, phase, extent, _), piece in zip(swaps, arrived):
+        up, real = partner(axis, phase, extent)
+        face = 2 * axis + 1 - up
+        value = piece[pl.ds(128, 128), :].astype(F32).reshape(16, 8, 128)
+        value = jnp.where(real, value, 0.0)
+        for slot in range(16):
+            block = faces[face, 0, slot]
+            total[block] = total[block] + value[slot]
+
+
 def forward_kernel(swaps, colour, r_new, w_in, off, factor, straight, crossed, columns, tables, faces, *refs):
     n = len(swaps)
-    arrived, w, sent, (extended, rest) = refs[:n], refs[n], refs[n + 1 : -2], refs[-2:]
+    arrived, others, (extended, rest) = refs[:n], refs[n:-2], refs[-2:]
+    if colour == 1:
+        adjoint, others = others[0], others[1:]
+    w, sent = others[0], others[1:]
     w[...] = w_in[...]
     extend(swaps, w_in, arrived, extended)
 
@@ -235,15 +277,20 @@
         send_faces(swaps, z, faces, sent[1:])
     else:
         send_faces(swaps, w, faces, sent)
+    if colour == 1:
+        for (axis, phase, extent, _), out in zip(swaps, sent):
+            up, _ = partner(axis, phase, extent)
+            value = adjoint[pl.ds(32 + (2 * axis + up) * 16, 16)]
+            out[pl.ds(128, 128), :] = value.reshape(128, 128).astype(BF16)
 
 
 def backward_kernel(swaps, tiles, colour, w, z_in, off, factor, straight, crossed, columns, tables, faces, *refs):
     n = len(swaps)
     arrived, others, (extended, rest) = refs[:n], refs[n:-2], refs[-2:]
-    if colour == 0:
-        r_new, norm, z, partial = others
-    else:
-        z, sent = others[0], others[1:]
+    if colour == 1:
+        r_new, total, terms, partial = others[0], others[1], others[2], others[-1]
+        others = others[3:-1]
+    z, sent = others[0], others[1:]
     z[...] = z_in[...]
     extend(swaps, z_in, arrived, extended)
 
@@ -257,12 +304,13 @@
 
     for_colour(colour, tables, COUPLE, couple)
     for_colour(colour, tables, SOLVE, solve)
-    if colour == 0:
-        rho = jnp.sum(r_new[...] * z[...], axis=0)
-        both = jnp.concatenate([rho, norm[...]], axis=0)
+    if colour == 1:
+        new = z[...]
+        rho = terms[pl.ds(0, 8), :] + jnp.sum(r_new[...] * new - total[...] * new.astype(BF16).astype(F32), axis=0)
+        both = jnp.concatenate([rho, terms[pl.ds(8, 8), :]], axis=0)
         for tile in range(tiles):
             partial[tile] = both
-    else:
+    if colour > 0:
         send_faces(swaps, z, faces, sent)
 
 
@@ -361,35 +409,52 @@
         aliases={3: 0},
     )(q, diag_blocks, in_hbm(off_blocks), off, columns, *arrived)
     sums = lax.all_to_all(partial, "gx", 0, 0, tiled=True)
-    r_new, w, norm, alpha, *sent = call(
+    r_new, w, alpha, *sent = call(
         functools.partial(start_kernel, swaps, count),
-        [kept, kept, vec(8, 128), vec(8, 128)] + pieces,
+        [kept, kept, vec(8, 128)] + pieces,
         [VMEM] * 3 + [SMEM] + [VMEM] * 3 + [SMEM] * 2,
     )(sums, r_vec, image, rho_prev, factor_inv, straight, crossed, tables, faces)
     fixed = (off, factor_inv, straight, crossed, columns, tables, faces)
     fixed_places = [VMEM] * 4 + [SMEM] * 3
+    adjoint, terms = call(
+        adjoint_kernel,
+        [VMEM((128, 8, 128), F32), VMEM((16, 128), F32)],
+        [VMEM] * 3 + [SMEM] * 2,
+        cost=10**8,
+    )(r_new, w, off, columns, tables)
     for colour in (1, 2, 3):
+        arrived = exchange(sent)
+        if colour == 2:
+            total = call(functools.partial(gather_kernel, swaps), [kept], [VMEM, SMEM] + [VMEM] * n, cost=10**8)(
+                adjoint, faces, *arrived
+            )[0]
         w, *sent = call(
             functools.partial(forward_kernel, swaps, colour),
-            [kept] * (2 if colour == 3 else 1) + pieces,
-            [VMEM] * 2 + fixed_places + [VMEM] * n,
+            [kept] * (2 if colour == 3 else 1) + ([vec(256, 128, dtype=BF16)] * n if colour == 1 else pieces),
+            [VMEM] * 2 + fixed_places + [VMEM] * (n + 1 if colour == 1 else n),
             scratch,
-        )(r_new, w, *fixed, *exchange(sent))
+        )(r_new, w, *fixed, *arrived, *([adjoint] if colour == 1 else []))
     z, *sent = sent
-    for colour in (2, 1):
-        z, *sent = call(
-            functools.partial(backward_kernel, swaps, tiles, colour),
-            [kept] + pieces,
-            [VMEM] * 2 + fixed_places + [VMEM] * n,
-            scratch,
-        )(w, z, *fixed, *exchange(sent))
-    z, partial = call(
+    z, *sent = call(
+        functools.partial(backward_kernel, swaps, tiles, 2),
+        [kept] + pieces,
+        [VMEM] * 2 + fixed_places + [VMEM] * n,
+        scratch,
+    )(w, z, *fixed, *exchange(sent))
+    z, *sent, partial = call(
+        functools.partial(backward_kernel, swaps, tiles, 1),
+        [kept] + pieces + [vec(tiles, 16, 128)],
+        [VMEM] * 2 + fixed_places + [VMEM] * (n + 3),
+        scratch,
+    )(w, z, *fixed, *exchange(sent), r_new, total, terms)
+    sums = lax.all_to_all(partial, "gx", 0, 0, tiled=True)
+    z = call(
         functools.partial(backward_kernel, swaps, tiles, 0),
-        [kept, vec(tiles, 16, 128)],
-        [VMEM] * 2 + fixed_places + [VMEM] * (n + 2),
+        [kept],
+        [VMEM] * 2 + fixed_places + [VMEM] * n,
         scratch,
-    )(w, z, *fixed, *exchange(sent), r_new, norm)
-    sums = lax.all_to_all(partial, "gx", 0, 0, tiled=True)
+        cost=10**9,
+    )(w, z, *fixed, *exchange(sent))[0]
     block_vec = vec(32, 8, 128)
     x_new, q_new, d_new, scalars = call(
         functools.partial(last_kernel, count),

time: 82.5 us -> 80.4 us (0.975)
  waiting for transfers between devices: 20.3 us -> 12.1 us
  local copies, waits for them, and re-layouts: 0.71 us -> 4.41 us
  Pallas kernels: 21.1 us -> 22.2 us
    all_to_all x1, waiting for transfers between devices: 7.24 us -> 0.01 us  [per_device(): sums = lax.all_to_all(partial, 'gx', 0, 0, tiled=True)]
    unnamed x23 -> x27, local copies, waits for them, and re-layouts: 0.71 us -> 4.41 us
    pallas_call x3 -> x5, Pallas kernels: 6.36 us -> 7.52 us  [the longest x1 2.74 us: per_device(): call(functools.partial(backward_kernel, swaps, tiles, 1), [kept] + pieces...]
    ppermute x28, waiting for transfers between devices: 13.1 us -> 12.1 us  [exchange(): lax.ppermute(piece, 'gx', swap[-1])]
  transfers between devices with their start and end apart: 29 -> 29, of which waited for: 11 -> 9; matrix products, arithmetic and copies ran while one was open for 1% -> 1% of each run, Pallas kernels for 3% -> 7%
where the time goes in v3:
time: 80.4 us; the launch traced here: 79.5 us
  starting transfers between devices  27.7 us (34%)
  Pallas kernels  22.2 us (28%)
  waiting for transfers between devices  12.1 us (15%)
  blocking collectives  12.1 us (15%)
  local copies, waits for them, and re-layouts  4.41 us (5%)
  between operations  0.97 us (1%)
    ppermute x28, starting transfers between devices, exchange(): lax.ppermute(piece, 'gx', swap[-1])  23.4 us
    all_to_all x1, blocking collectives, per_device(): sums = lax.all_to_all(partial, 'gx', 0, 0, tiled=True)  12.1 us
    ppermute x28, waiting for transfers between devices, exchange(): lax.ppermute(piece, 'gx', swap[-1])  12.1 us
    pallas_call x3, Pallas kernels, per_device(): call(functools.partial(forward_kernel, swaps, colour), [kept] * (2 if col...  4.86 us
    unnamed x27, local copies, waits for them, and re-layouts  4.41 us
    all_to_all x1, starting transfers between devices, per_device(): sums = lax.all_to_all(partial, 'gx', 0, 0, tiled=True)  4.31 us
    pallas_call x1, Pallas kernels, per_device(): call(functools.partial(image_kernel, swaps, tiles), [off_kept, kept, vec(...  3.75 us
    pallas_call x1, Pallas kernels, per_device(): call(functools.partial(backward_kernel, swaps, tiles, 1), [kept] + pieces...  2.74 us
  transfers between devices with their start and end apart: 29, of which 9 were waited for; matrix products, arithmetic and copies ran while one was open for 1% of the time, Pallas kernels for 7%

profile of v3, /device:TPU:0, one launch (start us, length us, event | category | flops | bytes accessed | tf_op | source)
XLA Modules:
  0.0 79.5 jit_solution(413444207847636767)
XLA Ops:
  0.7 1.0 %shard_map.191 = (f32[32,8,128]{2,1,0:T(8,128)S(1)}, s32[6,1,16]{2,1,0:T(1,128)S(4)}, bf16[128,128]{1,0:T(8,128)(2,1)S(1)}, bf16[128,128]{1,0:T(8,128)(2,1)S(1)}...) custom-call(f32[32,8,128]{2,1,0:T(8,128)} %q_hbm.1, s32[6,1,16]{2,1,0:T(1,128)} %bitcast.3), custom_call_target="tpu_custom_call" | custom-call | flops 10000000000 | tf_op jit(solution)/shard_map/pallas_call | solution.py:390
  1.7 0.0 copy-start.3
  1.7 0.5 collective-permute-start
  2.2 2.6 %collective-permute-start.1 = (bf16[128,128]{1,0:T(8,128)(2,1)S(1)}, bf16[128,128]{1,0:T(8,128)(2,1)S(1)}, u32[]{:S(2)}, u32[]{:S(2)}) collective-permute-start(bf16[128,128]{1,0:T(8,128)(2,1)S(1)} %get-tuple-element.63), channel_id=1, source_target_pairs={{0,3},{1,2},{2,1},{3,0},{4,7},{5,6},{6,5},{7,4},{8,11},{9,10},{10,... | collective-permute-start | bytes 98312 | tf_op jit(solution)/shard_map/ppermute | solution.py:388
  4.8 1.6 %collective-permute-start.2 = (bf16[128,128]{1,0:T(8,128)(2,1)S(1)}, bf16[128,128]{1,0:T(8,128)(2,1)S(1)}, u32[]{:S(2)}, u32[]{:S(2)}) collective-permute-start(bf16[128,128]{1,0:T(8,128)(2,1)S(1)} %get-tuple-element.64), channel_id=1, source_target_pairs={{0,4},{1,5},{2,6},{3,7},{4,0},{5,1},{6,2},{7,3},{8,12},{9,13},{10,... | collective-permute-start | bytes 98312 | tf_op jit(solution)/shard_map/ppermute | solution.py:388
  6.4 0.0 collective-permute-start.3
  6.4 2.4 %shard_map.192 = (bf16[32,9,128,128]{3,2,1,0:T(8,128)(2,1)S(1)}, s32[9,32]{1,0:T(8,128)S(4)}, s32[8,128]{1,0:T(8,128)S(4)}, f32[32,128]{1,0:T(8,128)S(1)}, f32[32,128]{1,0:T(8,128)S(1)}) custom-call(bf16[32,9,128,128]{3,2,1,0:T(8,128)(2,1)} %off_hbm.3, s32[9,32]{1,0:T(8,128)} %bitcast.2, s32[32]{0:T(128)} %colours_hbm.1, f32[32,128]{1,0:T(8,128)S(1)} %copy-done.7, ...), custom_call_target="tpu_custom_call" | custom-call | tf_op jit(solution)/shard_map/pallas_call | solution.py:398
  8.8 0.0 collective-permute-done.refs_0_
  8.8 0.0 collective-permute-done.3.refs_3_
  8.9 0.0 copy-start.2
  8.9 0.0 copy-start.4
  8.9 0.0 copy-start.10
  8.9 3.8 %shard_map.193 = (bf16[32,9,128,128]{3,2,1,0:T(8,128)(2,1)S(1)}, f32[32,8,128]{2,1,0:T(8,128)S(1)}, f32[16,8,128]{2,1,0:T(8,128)S(1)}) custom-call(f32[32,8,128]{2,1,0:T(8,128)S(1)} %get-tuple-element.59.q.q_ref, bf16[32,128,128]{2,1,0:T(8,128)(2,1)S(1)} %copy-done.3, bf16[32,9,128,128]{3,2,1,0:T(8,128)(2,1)} %off_hbm.3, ...), custom_call_target="tpu_custom_call", output_to_operand_aliasing={{0}: (3, {})} | custom-call | tf_op jit(solution)/shard_map/pallas_call | solution.py:404
  12.7 12.1 %all_to_all.10.sums = f32[16,8,128]{2,1,0:T(8,128)S(1)} all-to-all(f32[16,8,128]{2,1,0:T(8,128)S(1)} %get-tuple-element.66), channel_id=1, replica_groups=mesh['groups'=2,'gx'=16] {'gx'}, dimensions={0} | all-to-all | bytes 131072 | tf_op jit(solution)/shard_map/all_to_all | solution.py:411
  24.8 1.3 %shard_map.194 = (f32[32,8,128]{2,1,0:T(8,128)S(1)}, f32[32,8,128]{2,1,0:T(8,128)S(1)}, f32[8,128]{1,0:T(8,128)S(1)}, bf16[128,128]{1,0:T(8,128)(2,1)S(1)}, bf16...) custom-call(f32[16,8,128]{2,1,0:T(8,128)S(1)} %all_to_all.10.sums, ...), custom_call_target="tpu_custom_call" | custom-call | tf_op jit(solution)/shard_map/pallas_call | solution.py:412
  26.1 0.1 collective-permute-start.4
  26.2 0.3 collective-permute-start.5
  26.4 0.7 collective-permute-start.6
  27.1 0.0 collective-permute-start.7
  27.1 1.0 %shard_map.195 = (f32[128,8,128]{2,1,0:T(8,128)S(1)}, f32[16,128]{1,0:T(8,128)S(1)}) custom-call(f32[32,8,128]{2,1,0:T(8,128)S(1)} %get-tuple-element.114.r_new.refs_4_, f32[32,8,128]{2,1,0:T(8,128)S(1)} %get-tuple-element.73.w.w_in, bf16[32,9,128,128]{3,2,1,0:T(8,128)(2,1)S(1)} %get-tuple-element.74.off, s32[9,32]{1,0:T(8,128)S(4)} %get-tuple-element.61.columns, ...), custom_call_target="tpu_custom_call" | custom-call | flops 100000000 | tf_op jit(solution)/shard_map/pallas_call | solution.py:419
  28.1 0.0 collective-permute-done.4.refs_0_
  28.1 1.5 %collective-permute-done.5.refs_1_ = bf16[128,128]{1,0:T(8,128)(2,1)S(1)} collective-permute-done((bf16[128,128]{1,0:T(8,128)(2,1)S(1)}, bf16[128,128]{1,0:T(8,128)(2,1)S(1)}, u32[]{:S(2)}, u32[]{:S(2)}) %collective-permute-start.5) | collective-permute-done | bytes 32800 | tf_op jit(solution)/shard_map/ppermute | solution.py:388
  29.6 0.8 collective-permute-done.6.refs_2_
  30.4 0.0 collective-permute-done.7.refs_3_
  30.4 2.1 %shard_map.196 = (f32[32,8,128]{2,1,0:T(8,128)S(1)}, bf16[256,128]{1,0:T(8,128)(2,1)S(1)}, bf16[256,128]{1,0:T(8,128)(2,1)S(1)}, bf16[256,128]{1,0:T(8,128)(2,1)S(1)}, bf16[256,128]{1,0:T(8,128)(2,1)S(1)}) custom-call(f32[32,8,128]{2,1,0:T(8,128)S(1)} %get-tuple-element.114.r_new.refs_4_, f32[32,8,128]{2,1,0:T(8,128)S(1)} %get-tuple-element.73.w.w_in, ...), custom_call_target="tpu_custom_call" | custom-call | tf_op jit(solution)/shard_map/pallas_call | solution.py:431
  32.4 0.1 collective-permute-start.8
  32.5 1.5 %collective-permute-start.9 = (bf16[256,128]{1,0:T(8,128)(2,1)S(1)}, bf16[256,128]{1,0:T(8,128)(2,1)S(1)}, u32[]{:S(2)}, u32[]{:S(2)}) collective-permute-start(bf16[256,128]{1,0:T(8,128)(2,1)S(1)} %get-tuple-element.82), channel_id=1, source_target_pairs={{0,3},{1,2},{2,1},{3,0},{4,7},{5,6},{6,5},{7,4},{8,11},{9,10},{10,... | collective-permute-start | bytes 196616 | tf_op jit(solution)/shard_map/ppermute | solution.py:388
  34.1 2.0 %collective-permute-start.10 = (bf16[256,128]{1,0:T(8,128)(2,1)S(1)}, bf16[256,128]{1,0:T(8,128)(2,1)S(1)}, u32[]{:S(2)}, u32[]{:S(2)}) collective-permute-start(bf16[256,128]{1,0:T(8,128)(2,1)S(1)} %get-tuple-element.83), channel_id=1, source_target_pairs={{0,4},{1,5},{2,6},{3,7},{4,0},{5,1},{6,2},{7,3},{8,12},{9,13},{10,... | collective-permute-start | bytes 196616 | tf_op jit(solution)/shard_map/ppermute | solution.py:388
  36.1 0.0 collective-permute-start.11
  36.1 0.0 collective-permute-done.8.refs_0_
  36.1 0.3 collective-permute-done.9.refs_1_
  36.4 2.0 %collective-permute-done.10.refs_2_ = bf16[256,128]{1,0:T(8,128)(2,1)S(1)} collective-permute-done((bf16[256,128]{1,0:T(8,128)(2,1)S(1)}, bf16[256,128]{1,0:T(8,128)(2,1)S(1)}, u32[]{:S(2)}, u32[]{:S(2)}) %collective-permute-start.10) | collective-permute-done | bytes 65568 | tf_op jit(solution)/shard_map/ppermute | solution.py:388
  38.4 0.0 collective-permute-done.11.refs_3_
  38.4 1.6 %shard_map.197 = (f32[32,8,128]{2,1,0:T(8,128)S(1)}, bf16[128,128]{1,0:T(8,128)(2,1)S(1)}, bf16[128,128]{1,0:T(8,128)(2,1)S(1)}, bf16[128,128]{1,0:T(8,128)(2,1)S(1)}, bf16[128,128]{1,0:T(8,128)(2,1)S(1)}) custom-call(f32[32,8,128]{2,1,0:T(8,128)S(1)} %get-tuple-element.114.r_new.refs_4_, f32[32,8,128]{2,1,0:T(8,128)S(1)} %get-tuple-element.80.w_in, ...), custom_call_target="tpu_custom_call" | custom-call | tf_op jit(solution)/shard_map/pallas_call | solution.py:431
  40.0 0.5 collective-permute-start.12
  40.5 0.3 collective-permute-start.13
  40.8 2.4 %collective-permute-start.14 = (bf16[128,128]{1,0:T(8,128)(2,1)S(1)}, bf16[128,128]{1,0:T(8,128)(2,1)S(1)}, u32[]{:S(2)}, u32[]{:S(2)}) collective-permute-start(bf16[128,128]{1,0:T(8,128)(2,1)S(1)} %get-tuple-element.88), channel_id=1, source_target_pairs={{0,4},{1,5},{2,6},{3,7},{4,0},{5,1},{6,2},{7,3},{8,12},{9,13},{10,... | collective-permute-start | bytes 98312 | tf_op jit(solution)/shard_map/ppermute | solution.py:388
  43.2 0.7 collective-permute-done.13.refs_1_
  44.0 1.1 %collective-permute-done.14.refs_2_ = bf16[128,128]{1,0:T(8,128)(2,1)S(1)} collective-permute-done((bf16[128,128]{1,0:T(8,128)(2,1)S(1)}, bf16[128,128]{1,0:T(8,128)(2,1)S(1)}, u32[]{:S(2)}, u32[]{:S(2)}) %collective-permute-start.14) | collective-permute-done | bytes 32800 | tf_op jit(solution)/shard_map/ppermute | solution.py:388
  45.1 1.2 %shard_map.198 = (f32[32,8,128]{2,1,0:T(8,128)S(1)}, f32[32,8,128]{2,1,0:T(8,128)S(1)}, bf16[128,128]{1,0:T(8,128)(2,1)S(1)}, bf16[128,128]{1,0:T(8,128)(2,1)S(1...) custom-call(f32[32,8,128]{2,1,0:T(8,128)S(1)} %get-tuple-element.114.r_new.refs_4_, ...), custom_call_target="tpu_custom_call" | custom-call | tf_op jit(solution)/shard_map/pallas_call | solution.py:431
  46.3 0.1 collective-permute-start.16
  46.4 1.7 %collective-permute-start.17 = (bf16[128,128]{1,0:T(8,128)(2,1)S(1)}, bf16[128,128]{1,0:T(8,128)(2,1)S(1)}, u32[]{:S(2)}, u32[]{:S(2)}) collective-permute-start(bf16[128,128]{1,0:T(8,128)(2,1)S(1)} %get-tuple-element.93), channel_id=1, source_target_pairs={{0,3},{1,2},{2,1},{3,0},{4,7},{5,6},{6,5},{7,4},{8,11},{9,10},{10,... | collective-permute-start | bytes 98312 | tf_op jit(solution)/shard_map/ppermute | solution.py:388
  48.0 2.0 %collective-permute-start.18 = (bf16[128,128]{1,0:T(8,128)(2,1)S(1)}, bf16[128,128]{1,0:T(8,128)(2,1)S(1)}, u32[]{:S(2)}, u32[]{:S(2)}) collective-permute-start(bf16[128,128]{1,0:T(8,128)(2,1)S(1)} %get-tuple-element.94), channel_id=1, source_target_pairs={{0,4},{1,5},{2,6},{3,7},{4,0},{5,1},{6,2},{7,3},{8,12},{9,13},{10,... | collective-permute-start | bytes 98312 | tf_op jit(solution)/shard_map/ppermute | solution.py:388
  50.1 1.9 %collective-permute-done.18.refs_2_ = bf16[128,128]{1,0:T(8,128)(2,1)S(1)} collective-permute-done((bf16[128,128]{1,0:T(8,128)(2,1)S(1)}, bf16[128,128]{1,0:T(8,128)(2,1)S(1)}, u32[]{:S(2)}, u32[]{:S(2)}) %collective-permute-start.18) | collective-permute-done | bytes 32800 | tf_op jit(solution)/shard_map/ppermute | solution.py:388
  52.0 1.6 %shard_map.199 = (f32[32,8,128]{2,1,0:T(8,128)S(1)}, bf16[128,128]{1,0:T(8,128)(2,1)S(1)}, bf16[128,128]{1,0:T(8,128)(2,1)S(1)}, bf16[128,128]{1,0:T(8,128)(2,1)S(1)}, bf16[128,128]{1,0:T(8,128)(2,1)S(1)}) custom-call(f32[32,8,128]{2,1,0:T(8,128)S(1)} %get-tuple-element.90.w, f32[32,8,128]{2,1,0:T(8,128)S(1)} %get-tuple-element.91.z_in, ...), custom_call_target="tpu_custom_call" | custom-call | tf_op jit(solution)/shard_map/pallas_call | solution.py:438
  53.6 0.5 collective-permute-start.20
  54.0 0.7 collective-permute-start.21
  54.7 2.5 %collective-permute-start.22 = (bf16[128,128]{1,0:T(8,128)(2,1)S(1)}, bf16[128,128]{1,0:T(8,128)(2,1)S(1)}, u32[]{:S(2)}, u32[]{:S(2)}) collective-permute-start(bf16[128,128]{1,0:T(8,128)(2,1)S(1)} %get-tuple-element.99), channel_id=1, source_target_pairs={{0,4},{1,5},{2,6},{3,7},{4,0},{5,1},{6,2},{7,3},{8,12},{9,13},{10,... | collective-permute-start | bytes 98312 | tf_op jit(solution)/shard_map/ppermute | solution.py:388
  57.2 0.2 shard_map.200.refs_5_
  57.5 1.6 %collective-permute-done.22.refs_2_ = bf16[128,128]{1,0:T(8,128)(2,1)S(1)} collective-permute-done((bf16[128,128]{1,0:T(8,128)(2,1)S(1)}, bf16[128,128]{1,0:T(8,128)(2,1)S(1)}, u32[]{:S(2)}, u32[]{:S(2)}) %collective-permute-start.22) | collective-permute-done | bytes 32800 | tf_op jit(solution)/shard_map/ppermute | solution.py:388
  59.1 0.0 copy-start.6
  59.1 0.0 copy-start.11
  59.1 0.0 copy-start.12
  59.1 2.7 %shard_map.201 = (f32[32,8,128]{2,1,0:T(8,128)S(1)}, bf16[128,128]{1,0:T(8,128)(2,1)S(1)}, bf16[128,128]{1,0:T(8,128)(2,1)S(1)}, bf16[128,128]{1,0:T(8,128)(2,1)...) custom-call(f32[32,8,128]{2,1,0:T(8,128)S(1)} %get-tuple-element.90.w, ...), custom_call_target="tpu_custom_call" | custom-call | tf_op jit(solution)/shard_map/pallas_call | solution.py:444
  61.9 4.3 %all-to-all-start.1 = ((f32[16,16,128]{2,1,0:T(8,128)}), f32[16,16,128]{2,1,0:T(8,128)S(1)}, u32[]{:S(2)}, u32[]{:S(2)}) async-start(f32[16,16,128]{2,1,0:T(8,128)} %get-tuple-element.102), calls=%async_computation.1 | async-start | bytes 262144 | tf_op jit(solution)/shard_map/all_to_all | solution.py:450
  66.2 0.4 collective-permute-start.24
  66.6 1.6 %collective-permute-start.25 = (bf16[128,128]{1,0:T(8,128)(2,1)S(1)}, bf16[128,128]{1,0:T(8,128)(2,1)S(1)}, u32[]{:S(2)}, u32[]{:S(2)}) collective-permute-start(bf16[128,128]{1,0:T(8,128)(2,1)S(1)} %get-tuple-element.105), channel_id=1, source_target_pairs={{0,3},{1,2},{2,1},{3,0},{4,7},{5,6},{6,5},{7,4},{8,11},{9,10},{10,... | collective-permute-start | bytes 98312 | tf_op jit(solution)/shard_map/ppermute | solution.py:388
  68.2 1.5 %collective-permute-start.26 = (bf16[128,128]{1,0:T(8,128)(2,1)S(1)}, bf16[128,128]{1,0:T(8,128)(2,1)S(1)}, u32[]{:S(2)}, u32[]{:S(2)}) collective-permute-start(bf16[128,128]{1,0:T(8,128)(2,1)S(1)} %get-tuple-element.106), channel_id=1, source_target_pairs={{0,4},{1,5},{2,6},{3,7},{4,0},{5,1},{6,2},{7,3},{8,12},{9,13},{10,... | collective-permute-start | bytes 98312 | tf_op jit(solution)/shard_map/ppermute | solution.py:388
  69.7 0.7 copy.23
  70.4 2.0 %collective-permute-done.26.refs_2_ = bf16[128,128]{1,0:T(8,128)(2,1)S(1)} collective-permute-done((bf16[128,128]{1,0:T(8,128)(2,1)S(1)}, bf16[128,128]{1,0:T(8,128)(2,1)S(1)}, u32[]{:S(2)}, u32[]{:S(2)}) %collective-permute-start.26) | collective-permute-done | bytes 32800 | tf_op jit(solution)/shard_map/ppermute | solution.py:388
  72.4 3.7 %copy-done.1 = bf16[32,9,128,128]{3,2,1,0:T(8,128)(2,1)S(1)} copy-done((bf16[32,9,128,128]{3,2,1,0:T(8,128)(2,1)S(1)}, bf16[32,9,128,128]{3,2,1,0:T(8,128)(2,1)}, u32[]{:S(2)}) %copy-start.1) | copy-done | bytes 9437208
  76.1 2.0 %shard_map.202.z = f32[32,8,128]{2,1,0:T(8,128)S(1)} custom-call(f32[32,8,128]{2,1,0:T(8,128)S(1)} %get-tuple-element.90.w, f32[32,8,128]{2,1,0:T(8,128)S(1)} %get-tuple-element.103.z_in, bf16[32,9,128,128]{3,2,1,0:T(8,128)(2,1)S(1)} %copy-done.1, bf16[32,128,128]{2,1,0:T(8,128)(2,1)S(1)} %copy-done.2, f32[32,128]{1,0:T(8,128)S(1)} %get-tuple-element.68.straight, ...), custom_call_target="tpu_custom_call" | custom-call | flops 1000000000 | tf_op jit(solution)/shard_map/pallas_call | solution.py:451
  78.1 0.0 copy-done.5
  78.1 1.4 %shard_map.203 = (f32[32,8,128]{2,1,0:T(8,128)}, f32[32,8,128]{2,1,0:T(8,128)}, f32[32,8,128]{2,1,0:T(8,128)}, f32[3,8]{1,0:T(4,128)}) custom-call(f32[16,16,128]{2,1,0:T(8,128)S(1)} %all-to-all-done.1.sums, f32[32,8,128]{2,1,0:T(8,128)S(1)} %shard_map.202.z, f32[32,8,128]{2,1,0:T(8,128)S(1)} %get-tuple-element.59.q.q_ref, f32[32,8,128]{2,1,0:T(8,128)S(1)} %copy-done.5, ...), custom_call_target="tpu_custom_call" | custom-call | tf_op jit(solution)/shard_map/pallas_call | solution.py:459
  (35 shorter events, 0.1 us)
Async XLA Ops:
  0.6 5.8 %copy-start.7 = (f32[32,128]{1,0:T(8,128)S(1)}, f32[32,128]{1,0:T(8,128)}, u32[]{:S(2)}) copy-start(f32[32,128]{1,0:T(8,128)} %diag_ref.1) | copy-start | bytes 49156
  0.6 5.8 %copy-start.8 = (f32[32,64]{1,0:T(8,128)S(1)}, f32[32,64]{1,0:T(8,128)}, u32[]{:S(2)}) copy-start(f32[32,64]{1,0:T(8,128)} %off_ref.1) | copy-start | bytes 24580
  0.7 5.8 %copy-start.9 = (s32[32,64]{1,0:T(8,128)S(1)}, s32[32,64]{1,0:T(8,128)}, u32[]{:S(2)}) copy-start(s32[32,64]{1,0:T(8,128)} %pairs_ref.1) | copy-start | bytes 24580
  1.7 7.2 %copy-start.3 = (bf16[32,128,128]{2,1,0:T(8,128)(2,1)S(1)}, bf16[32,128,128]{2,1,0:T(8,128)(2,1)}, u32[]{:S(2)}) copy-start(bf16[32,128,128]{2,1,0:T(8,128)(2,1)} %diag.1) | copy-start | bytes 3145732
  1.7 7.1 %collective-permute-start = (bf16[128,128]{1,0:T(8,128)(2,1)S(1)}, bf16[128,128]{1,0:T(8,128)(2,1)S(1)}, u32[]{:S(2)}, u32[]{:S(2)}) collective-permute-start(bf16[128,128]{1,0:T(8,128)(2,1)S(1)} %get-tuple-element.62), channel_id=1, source_target_pairs={{0,1},{1,0},{2,3},{3,2},{4,5},{5,4},{6,7},{7,6},{8,9},{9,8},{10,11... | collective-permute-start | bytes 98312 | tf_op jit(solution)/shard_map/ppermute | solution.py:388
  2.2 6.6 %collective-permute-start.1 = (bf16[128,128]{1,0:T(8,128)(2,1)S(1)}, bf16[128,128]{1,0:T(8,128)(2,1)S(1)}, u32[]{:S(2)}, u32[]{:S(2)}) collective-permute-start(bf16[128,128]{1,0:T(8,128)(2,1)S(1)} %get-tuple-element.63), channel_id=1, source_target_pairs={{0,3},{1,2},{2,1},{3,0},{4,7},{5,6},{6,5},{7,4},{8,11},{9,10},{10,... | collective-permute-start | bytes 98312 | tf_op jit(solution)/shard_map/ppermute | solution.py:388
  4.8 4.0 %collective-permute-start.2 = (bf16[128,128]{1,0:T(8,128)(2,1)S(1)}, bf16[128,128]{1,0:T(8,128)(2,1)S(1)}, u32[]{:S(2)}, u32[]{:S(2)}) collective-permute-start(bf16[128,128]{1,0:T(8,128)(2,1)S(1)} %get-tuple-element.64), channel_id=1, source_target_pairs={{0,4},{1,5},{2,6},{3,7},{4,0},{5,1},{6,2},{7,3},{8,12},{9,13},{10,... | collective-permute-start | bytes 98312 | tf_op jit(solution)/shard_map/ppermute | solution.py:388
  6.4 2.4 %collective-permute-start.3 = (bf16[128,128]{1,0:T(8,128)(2,1)S(1)}, bf16[128,128]{1,0:T(8,128)(2,1)S(1)}, u32[]{:S(2)}, u32[]{:S(2)}) collective-permute-start(bf16[128,128]{1,0:T(8,128)(2,1)S(1)} %get-tuple-element.65), channel_id=1, source_target_pairs={{0,1},{1,0},{2,3},{3,2},{4,8},{5,9},{6,10},{7,11},{8,4},{9,5},{10,... | collective-permute-start | bytes 98312 | tf_op jit(solution)/shard_map/ppermute | solution.py:388
  8.9 15.9 %copy-start.2 = (bf16[32,128,128]{2,1,0:T(8,128)(2,1)S(1)}, bf16[32,128,128]{2,1,0:T(8,128)(2,1)}, u32[]{:S(2)}) copy-start(bf16[32,128,128]{2,1,0:T(8,128)(2,1)} %factor.13) | copy-start | bytes 3145732
  8.9 15.9 %copy-start.4 = (f32[32,8,128]{2,1,0:T(8,128)S(1)}, f32[32,8,128]{2,1,0:T(8,128)}, u32[]{:S(2)}) copy-start(f32[32,8,128]{2,1,0:T(8,128)} %r_ref.1) | copy-start | bytes 393220
  8.9 15.9 %copy-start.10 = (f32[8]{0:T(128)S(1)}, f32[8]{0:T(128)}, u32[]{:S(2)}) copy-start(f32[8]{0:T(128)} %rho.3) | copy-start | bytes 100
  12.7 46.4 %copy-start = (bf16[32,9,128,128]{3,2,1,0:T(8,128)(2,1)}, bf16[32,9,128,128]{3,2,1,0:T(8,128)(2,1)S(1)}, u32[]{:S(2)}) copy-start(bf16[32,9,128,128]{3,2,1,0:T(8,128)(2,1)S(1)} %get-tuple-element.74.off) | copy-start | bytes 28311556
  26.1 2.0 %collective-permute-start.4 = (bf16[128,128]{1,0:T(8,128)(2,1)S(1)}, bf16[128,128]{1,0:T(8,128)(2,1)S(1)}, u32[]{:S(2)}, u32[]{:S(2)}) collective-permute-start(bf16[128,128]{1,0:T(8,128)(2,1)S(1)} %get-tuple-element.75), channel_id=1, source_target_pairs={{0,1},{1,0},{2,3},{3,2},{4,5},{5,4},{6,7},{7,6},{8,9},{9,8},{10,11... | collective-permute-start | bytes 98312 | tf_op jit(solution)/shard_map/ppermute | solution.py:388
  26.2 3.4 %collective-permute-start.5 = (bf16[128,128]{1,0:T(8,128)(2,1)S(1)}, bf16[128,128]{1,0:T(8,128)(2,1)S(1)}, u32[]{:S(2)}, u32[]{:S(2)}) collective-permute-start(bf16[128,128]{1,0:T(8,128)(2,1)S(1)} %get-tuple-element.76), channel_id=1, source_target_pairs={{0,3},{1,2},{2,1},{3,0},{4,7},{5,6},{6,5},{7,4},{8,11},{9,10},{10,... | collective-permute-start | bytes 98312 | tf_op jit(solution)/shard_map/ppermute | solution.py:388
  26.4 3.9 %collective-permute-start.6 = (bf16[128,128]{1,0:T(8,128)(2,1)S(1)}, bf16[128,128]{1,0:T(8,128)(2,1)S(1)}, u32[]{:S(2)}, u32[]{:S(2)}) collective-permute-start(bf16[128,128]{1,0:T(8,128)(2,1)S(1)} %get-tuple-element.77), channel_id=1, source_target_pairs={{0,4},{1,5},{2,6},{3,7},{4,0},{5,1},{6,2},{7,3},{8,12},{9,13},{10,... | collective-permute-start | bytes 98312 | tf_op jit(solution)/shard_map/ppermute | solution.py:388
  27.1 3.3 %collective-permute-start.7 = (bf16[128,128]{1,0:T(8,128)(2,1)S(1)}, bf16[128,128]{1,0:T(8,128)(2,1)S(1)}, u32[]{:S(2)}, u32[]{:S(2)}) collective-permute-start(bf16[128,128]{1,0:T(8,128)(2,1)S(1)} %get-tuple-element.78), channel_id=1, source_target_pairs={{0,1},{1,0},{2,3},{3,2},{4,8},{5,9},{6,10},{7,11},{8,4},{9,5},{10,... | collective-permute-start | bytes 98312 | tf_op jit(solution)/shard_map/ppermute | solution.py:388
  32.4 3.7 %collective-permute-start.8 = (bf16[256,128]{1,0:T(8,128)(2,1)S(1)}, bf16[256,128]{1,0:T(8,128)(2,1)S(1)}, u32[]{:S(2)}, u32[]{:S(2)}) collective-permute-start(bf16[256,128]{1,0:T(8,128)(2,1)S(1)} %get-tuple-element.81), channel_id=1, source_target_pairs={{0,1},{1,0},{2,3},{3,2},{4,5},{5,4},{6,7},{7,6},{8,9},{9,8},{10,11... | collective-permute-start | bytes 196616 | tf_op jit(solution)/shard_map/ppermute | solution.py:388
  32.5 3.9 %collective-permute-start.9 = (bf16[256,128]{1,0:T(8,128)(2,1)S(1)}, bf16[256,128]{1,0:T(8,128)(2,1)S(1)}, u32[]{:S(2)}, u32[]{:S(2)}) collective-permute-start(bf16[256,128]{1,0:T(8,128)(2,1)S(1)} %get-tuple-element.82), channel_id=1, source_target_pairs={{0,3},{1,2},{2,1},{3,0},{4,7},{5,6},{6,5},{7,4},{8,11},{9,10},{10,... | collective-permute-start | bytes 196616 | tf_op jit(solution)/shard_map/ppermute | solution.py:388
  34.1 4.3 %collective-permute-start.10 = (bf16[256,128]{1,0:T(8,128)(2,1)S(1)}, bf16[256,128]{1,0:T(8,128)(2,1)S(1)}, u32[]{:S(2)}, u32[]{:S(2)}) collective-permute-start(bf16[256,128]{1,0:T(8,128)(2,1)S(1)} %get-tuple-element.83), channel_id=1, source_target_pairs={{0,4},{1,5},{2,6},{3,7},{4,0},{5,1},{6,2},{7,3},{8,12},{9,13},{10,... | collective-permute-start | bytes 196616 | tf_op jit(solution)/shard_map/ppermute | solution.py:388
  36.1 2.3 %collective-permute-start.11 = (bf16[256,128]{1,0:T(8,128)(2,1)S(1)}, bf16[256,128]{1,0:T(8,128)(2,1)S(1)}, u32[]{:S(2)}, u32[]{:S(2)}) collective-permute-start(bf16[256,128]{1,0:T(8,128)(2,1)S(1)} %get-tuple-element.84), channel_id=1, source_target_pairs={{0,1},{1,0},{2,3},{3,2},{4,8},{5,9},{6,10},{7,11},{8,4},{9,5},{10,... | collective-permute-start | bytes 196616 | tf_op jit(solution)/shard_map/ppermute | solution.py:388
  40.0 3.2 %collective-permute-start.12 = (bf16[128,128]{1,0:T(8,128)(2,1)S(1)}, bf16[128,128]{1,0:T(8,128)(2,1)S(1)}, u32[]{:S(2)}, u32[]{:S(2)}) collective-permute-start(bf16[128,128]{1,0:T(8,128)(2,1)S(1)} %get-tuple-element.86), channel_id=1, source_target_pairs={{0,1},{1,0},{2,3},{3,2},{4,5},{5,4},{6,7},{7,6},{8,9},{9,8},{10,11... | collective-permute-start | bytes 98312 | tf_op jit(solution)/shard_map/ppermute | solution.py:388
  40.5 3.4 %collective-permute-start.13 = (bf16[128,128]{1,0:T(8,128)(2,1)S(1)}, bf16[128,128]{1,0:T(8,128)(2,1)S(1)}, u32[]{:S(2)}, u32[]{:S(2)}) collective-permute-start(bf16[128,128]{1,0:T(8,128)(2,1)S(1)} %get-tuple-element.87), channel_id=1, source_target_pairs={{0,3},{1,2},{2,1},{3,0},{4,7},{5,6},{6,5},{7,4},{8,11},{9,10},{10,... | collective-permute-start | bytes 98312 | tf_op jit(solution)/shard_map/ppermute | solution.py:388
  40.8 4.3 %collective-permute-start.14 = (bf16[128,128]{1,0:T(8,128)(2,1)S(1)}, bf16[128,128]{1,0:T(8,128)(2,1)S(1)}, u32[]{:S(2)}, u32[]{:S(2)}) collective-permute-start(bf16[128,128]{1,0:T(8,128)(2,1)S(1)} %get-tuple-element.88), channel_id=1, source_target_pairs={{0,4},{1,5},{2,6},{3,7},{4,0},{5,1},{6,2},{7,3},{8,12},{9,13},{10,... | collective-permute-start | bytes 98312 | tf_op jit(solution)/shard_map/ppermute | solution.py:388
  43.2 1.9 %collective-permute-start.15 = (bf16[128,128]{1,0:T(8,128)(2,1)S(1)}, bf16[128,128]{1,0:T(8,128)(2,1)S(1)}, u32[]{:S(2)}, u32[]{:S(2)}) collective-permute-start(bf16[128,128]{1,0:T(8,128)(2,1)S(1)} %get-tuple-element.89), channel_id=1, source_target_pairs={{0,1},{1,0},{2,3},{3,2},{4,8},{5,9},{6,10},{7,11},{8,4},{9,5},{10,... | collective-permute-start | bytes 98312 | tf_op jit(solution)/shard_map/ppermute | solution.py:388
  46.3 3.8 %collective-permute-start.16 = (bf16[128,128]{1,0:T(8,128)(2,1)S(1)}, bf16[128,128]{1,0:T(8,128)(2,1)S(1)}, u32[]{:S(2)}, u32[]{:S(2)}) collective-permute-start(bf16[128,128]{1,0:T(8,128)(2,1)S(1)} %get-tuple-element.92), channel_id=1, source_target_pairs={{0,1},{1,0},{2,3},{3,2},{4,5},{5,4},{6,7},{7,6},{8,9},{9,8},{10,11... | collective-permute-start | bytes 98312 | tf_op jit(solution)/shard_map/ppermute | solution.py:388
  46.4 3.7 %collective-permute-start.17 = (bf16[128,128]{1,0:T(8,128)(2,1)S(1)}, bf16[128,128]{1,0:T(8,128)(2,1)S(1)}, u32[]{:S(2)}, u32[]{:S(2)}) collective-permute-start(bf16[128,128]{1,0:T(8,128)(2,1)S(1)} %get-tuple-element.93), channel_id=1, source_target_pairs={{0,3},{1,2},{2,1},{3,0},{4,7},{5,6},{6,5},{7,4},{8,11},{9,10},{10,... | collective-permute-start | bytes 98312 | tf_op jit(solution)/shard_map/ppermute | solution.py:388
  48.0 3.9 %collective-permute-start.18 = (bf16[128,128]{1,0:T(8,128)(2,1)S(1)}, bf16[128,128]{1,0:T(8,128)(2,1)S(1)}, u32[]{:S(2)}, u32[]{:S(2)}) collective-permute-start(bf16[128,128]{1,0:T(8,128)(2,1)S(1)} %get-tuple-element.94), channel_id=1, source_target_pairs={{0,4},{1,5},{2,6},{3,7},{4,0},{5,1},{6,2},{7,3},{8,12},{9,13},{10,... | collective-permute-start | bytes 98312 | tf_op jit(solution)/shard_map/ppermute | solution.py:388
  50.1 1.9 %collective-permute-start.19 = (bf16[128,128]{1,0:T(8,128)(2,1)S(1)}, bf16[128,128]{1,0:T(8,128)(2,1)S(1)}, u32[]{:S(2)}, u32[]{:S(2)}) collective-permute-start(bf16[128,128]{1,0:T(8,128)(2,1)S(1)} %get-tuple-element.95), channel_id=1, source_target_pairs={{0,1},{1,0},{2,3},{3,2},{4,8},{5,9},{6,10},{7,11},{8,4},{9,5},{10,... | collective-permute-start | bytes 98312 | tf_op jit(solution)/shard_map/ppermute | solution.py:388
  53.6 3.9 %collective-permute-start.20 = (bf16[128,128]{1,0:T(8,128)(2,1)S(1)}, bf16[128,128]{1,0:T(8,128)(2,1)S(1)}, u32[]{:S(2)}, u32[]{:S(2)}) collective-permute-start(bf16[128,128]{1,0:T(8,128)(2,1)S(1)} %get-tuple-element.97), channel_id=1, source_target_pairs={{0,1},{1,0},{2,3},{3,2},{4,5},{5,4},{6,7},{7,6},{8,9},{9,8},{10,11... | collective-permute-start | bytes 98312 | tf_op jit(solution)/shard_map/ppermute | solution.py:388
  54.0 3.4 %collective-permute-start.21 = (bf16[128,128]{1,0:T(8,128)(2,1)S(1)}, bf16[128,128]{1,0:T(8,128)(2,1)S(1)}, u32[]{:S(2)}, u32[]{:S(2)}) collective-permute-start(bf16[128,128]{1,0:T(8,128)(2,1)S(1)} %get-tuple-element.98), channel_id=1, source_target_pairs={{0,3},{1,2},{2,1},{3,0},{4,7},{5,6},{6,5},{7,4},{8,11},{9,10},{10,... | collective-permute-start | bytes 98312 | tf_op jit(solution)/shard_map/ppermute | solution.py:388
  54.7 4.4 %collective-permute-start.22 = (bf16[128,128]{1,0:T(8,128)(2,1)S(1)}, bf16[128,128]{1,0:T(8,128)(2,1)S(1)}, u32[]{:S(2)}, u32[]{:S(2)}) collective-permute-start(bf16[128,128]{1,0:T(8,128)(2,1)S(1)} %get-tuple-element.99), channel_id=1, source_target_pairs={{0,4},{1,5},{2,6},{3,7},{4,0},{5,1},{6,2},{7,3},{8,12},{9,13},{10,... | collective-permute-start | bytes 98312 | tf_op jit(solution)/shard_map/ppermute | solution.py:388
  57.2 1.9 %collective-permute-start.23 = (bf16[128,128]{1,0:T(8,128)(2,1)S(1)}, bf16[128,128]{1,0:T(8,128)(2,1)S(1)}, u32[]{:S(2)}, u32[]{:S(2)}) collective-permute-start(bf16[128,128]{1,0:T(8,128)(2,1)S(1)} %get-tuple-element.100), channel_id=1, source_target_pairs={{0,1},{1,0},{2,3},{3,2},{4,8},{5,9},{6,10},{7,11},{8,4},{9,5},{10,... | collective-permute-start | bytes 98312 | tf_op jit(solution)/shard_map/ppermute | solution.py:388
  59.1 19.0 %copy-start.5 = (f32[32,8,128]{2,1,0:T(8,128)S(1)}, f32[32,8,128]{2,1,0:T(8,128)}, u32[]{:S(2)}) copy-start(f32[32,8,128]{2,1,0:T(8,128)} %x_ref.1) | copy-start | bytes 393220
  59.1 19.0 %copy-start.6 = (f32[32,8,128]{2,1,0:T(8,128)S(1)}, f32[32,8,128]{2,1,0:T(8,128)}, u32[]{:S(2)}) copy-start(f32[32,8,128]{2,1,0:T(8,128)} %d_ref.1) | copy-start | bytes 393220
  59.1 19.0 %copy-start.11 = (f32[8]{0:T(128)S(1)}, f32[8]{0:T(128)}, u32[]{:S(2)}) copy-start(f32[8]{0:T(128)} %tau.1) | copy-start | bytes 100
  59.1 19.0 %copy-start.12 = (f32[8]{0:T(128)S(1)}, f32[8]{0:T(128)}, u32[]{:S(2)}) copy-start(f32[8]{0:T(128)} %theta_in.1) | copy-start | bytes 100
  61.9 16.2 %all-to-all-start.1 = ((f32[16,16,128]{2,1,0:T(8,128)}), f32[16,16,128]{2,1,0:T(8,128)S(1)}, u32[]{:S(2)}, u32[]{:S(2)}) async-start(f32[16,16,128]{2,1,0:T(8,128)} %get-tuple-element.102), calls=%async_computation.1 | async-start | bytes 262144 | tf_op jit(solution)/shard_map/all_to_all | solution.py:450
  66.2 4.2 %collective-permute-start.24 = (bf16[128,128]{1,0:T(8,128)(2,1)S(1)}, bf16[128,128]{1,0:T(8,128)(2,1)S(1)}, u32[]{:S(2)}, u32[]{:S(2)}) collective-permute-start(bf16[128,128]{1,0:T(8,128)(2,1)S(1)} %get-tuple-element.104), channel_id=1, source_target_pairs={{0,1},{1,0},{2,3},{3,2},{4,5},{5,4},{6,7},{7,6},{8,9},{9,8},{10,11... | collective-permute-start | bytes 98312 | tf_op jit(solution)/shard_map/ppermute | solution.py:388
  66.6 3.8 %collective-permute-start.25 = (bf16[128,128]{1,0:T(8,128)(2,1)S(1)}, bf16[128,128]{1,0:T(8,128)(2,1)S(1)}, u32[]{:S(2)}, u32[]{:S(2)}) collective-permute-start(bf16[128,128]{1,0:T(8,128)(2,1)S(1)} %get-tuple-element.105), channel_id=1, source_target_pairs={{0,3},{1,2},{2,1},{3,0},{4,7},{5,6},{6,5},{7,4},{8,11},{9,10},{10,... | collective-permute-start | bytes 98312 | tf_op jit(solution)/shard_map/ppermute | solution.py:388
  68.2 4.2 %collective-permute-start.26 = (bf16[128,128]{1,0:T(8,128)(2,1)S(1)}, bf16[128,128]{1,0:T(8,128)(2,1)S(1)}, u32[]{:S(2)}, u32[]{:S(2)}) collective-permute-start(bf16[128,128]{1,0:T(8,128)(2,1)S(1)} %get-tuple-element.106), channel_id=1, source_target_pairs={{0,4},{1,5},{2,6},{3,7},{4,0},{5,1},{6,2},{7,3},{8,12},{9,13},{10,... | collective-permute-start | bytes 98312 | tf_op jit(solution)/shard_map/ppermute | solution.py:388
  69.7 2.7 %collective-permute-start.27 = (bf16[128,128]{1,0:T(8,128)(2,1)S(1)}, bf16[128,128]{1,0:T(8,128)(2,1)S(1)}, u32[]{:S(2)}, u32[]{:S(2)}) collective-permute-start(bf16[128,128]{1,0:T(8,128)(2,1)S(1)} %get-tuple-element.107), channel_id=1, source_target_pairs={{0,1},{1,0},{2,3},{3,2},{4,8},{5,9},{6,10},{7,11},{8,4},{9,5},{10,... | collective-permute-start | bytes 98312 | tf_op jit(solution)/shard_map/ppermute | solution.py:388
  72.4 3.7 %copy-start.1 = (bf16[32,9,128,128]{3,2,1,0:T(8,128)(2,1)S(1)}, bf16[32,9,128,128]{3,2,1,0:T(8,128)(2,1)}, u32[]{:S(2)}) copy-start(bf16[32,9,128,128]{3,2,1,0:T(8,128)(2,1)} %copy-done) | copy-start | bytes 28311556

commit v4 on v3

--- a/solution.py
+++ b/solution.py
@@ -13,6 +13,7 @@
 SMEM = pltpu.SMEM
 HBM = pltpu.HBM
 SIDE = 4
+ORDER = (1, 2, 3, 0, 4, 5)
 COUPLE = 4
 SOLVE = 16
 
@@ -37,7 +38,7 @@
     for axis, (stride, extent) in enumerate(((1, SIDE), (SIDE, SIDE), (16, tiles // 16))):
         for phase in range(2 if extent > 2 else extent - 1):
             swaps.append((axis, phase, extent, swap_pairs(axis, stride, extent, phase, tiles)))
-    return swaps
+    return [swaps[i] for i in ORDER if i < len(swaps)]
 
 
 def partner(axis, phase, extent):
@@ -93,6 +94,17 @@
         row = pl.ds(b, 1)
         middles.append((straight[row, :] * first + crossed[row, :] * other).astype(BF16))
     return [jnp.dot(v, m, preferred_element_type=F32) for v, m in zip(middles, matrices)]
+
+
+def load_kernel(off_hbm, tables, after, off, sems):
+    count = tables[4, 0]
+
+    def copy(place):
+        block = tables[0, place]
+        return pltpu.make_async_copy(off_hbm.at[block], off.at[block], sems.at[place])
+
+    lax.fori_loop(0, count, lambda place, carry: (copy(place).start(), carry)[1], 0)
+    lax.fori_loop(0, count, lambda place, carry: (copy(place).wait(), carry)[1], 0)
 
 
 def for_colour(colour, tables, size, body):
@@ -448,13 +460,16 @@
         scratch,
     )(w, z, *fixed, *exchange(sent), r_new, total, terms)
     sums = lax.all_to_all(partial, "gx", 0, 0, tiled=True)
+    arrived = exchange(sent)
+    off = call(load_kernel, [off_kept], [HBM, SMEM, VMEM], [pltpu.SemaphoreType.DMA((32,))], cost=10**8)(
+        in_hbm(off_blocks), tables, arrived[0]
+    )[0]
     z = call(
         functools.partial(backward_kernel, swaps, tiles, 0),
         [kept],
         [VMEM] * 2 + fixed_places + [VMEM] * n,
         scratch,
-        cost=10**9,
-    )(w, z, *fixed, *exchange(sent))[0]
+    )(w, z, off, *fixed[1:], *arrived)[0]
     block_vec = vec(32, 8, 128)
     x_new, q_new, d_new, scalars = call(
         functools.partial(last_kernel, count),

time: 80.4 us -> 73.9 us (0.919)
  local copies, waits for them, and re-layouts: 4.41 us -> 0.72 us
  waiting for transfers between devices: 12.1 us -> 9.82 us
  Pallas kernels: 22.2 us -> 24.3 us
  starting transfers between devices: 27.7 us -> 25.7 us
    unnamed x27 -> x23, local copies, waits for them, and re-layouts: 4.41 us -> 0.72 us
    ppermute x28, starting transfers between devices: 23.4 us -> 21 us  [exchange(): lax.ppermute(piece, 'gx', swap[-1])]
    ppermute x28, waiting for transfers between devices: 12.1 us -> 9.82 us  [exchange(): lax.ppermute(piece, 'gx', swap[-1])]
    pallas_call x0 -> x1, Pallas kernels: none -> 2.04 us  [per_device(): call(load_kernel, [off_kept], [HBM, SMEM, VMEM], [pltpu.SemaphoreType.DMA...]
    pallas_call x1, Pallas kernels: 2.74 us -> 1.81 us  [per_device(): call(functools.partial(backward_kernel, swaps, tiles, 1), [kept] + pieces...]
  transfers between devices with their start and end apart: 29 -> 29, of which waited for: 9 -> 10; matrix products, arithmetic and copies ran while one was open for 1% -> 1% of each run, Pallas kernels for 7% -> 10%
where the time goes in v4:
time: 73.9 us; the launch traced here: 73.2 us
  starting transfers between devices  25.7 us (35%)
  Pallas kernels  24.3 us (33%)
  blocking collectives  11.7 us (16%)
  waiting for transfers between devices  9.82 us (13%)
  between operations  0.96 us (1%)
    ppermute x28, starting transfers between devices, exchange(): lax.ppermute(piece, 'gx', swap[-1])  21 us
    all_to_all x1, blocking collectives, per_device(): sums = lax.all_to_all(partial, 'gx', 0, 0, tiled=True)  11.7 us
    ppermute x28, waiting for transfers between devices, exchange(): lax.ppermute(piece, 'gx', swap[-1])  9.82 us
    pallas_call x3, Pallas kernels, per_device(): call(functools.partial(forward_kernel, swaps, colour), [kept] * (2 if col...  5.36 us
    all_to_all x1, starting transfers between devices, per_device(): sums = lax.all_to_all(partial, 'gx', 0, 0, tiled=True)  4.72 us
    pallas_call x1, Pallas kernels, per_device(): call(functools.partial(image_kernel, swaps, tiles), [off_kept, kept, vec(...  3.75 us
    pallas_call x1, Pallas kernels, per_device(): call(setup_kernel, [off_kept, SMEM((9, 32), jnp.int32), SMEM((8, 128), jn...  2.38 us
    pallas_call x1, Pallas kernels, per_device(): call(functools.partial(backward_kernel, swaps, tiles, 2), [kept] + pieces...  2.06 us
  transfers between devices with their start and end apart: 29, of which 10 were waited for; matrix products, arithmetic and copies ran while one was open for 1% of the time, Pallas kernels for 10%

profile of v4, /device:TPU:0, one launch (start us, length us, event | category | flops | bytes accessed | tf_op | source)
XLA Modules:
  0.0 73.2 jit_solution(7262966887789045931)
XLA Ops:
  0.7 1.0 %shard_map.191 = (f32[32,8,128]{2,1,0:T(8,128)S(1)}, s32[6,1,16]{2,1,0:T(1,128)S(4)}, bf16[128,128]{1,0:T(8,128)(2,1)S(1)}, bf16[128,128]{1,0:T(8,128)(2,1)S(1)}...) custom-call(f32[32,8,128]{2,1,0:T(8,128)} %q_hbm.1, s32[6,1,16]{2,1,0:T(1,128)} %bitcast.3), custom_call_target="tpu_custom_call" | custom-call | flops 10000000000 | tf_op jit(solution)/shard_map/pallas_call | solution.py:402
  1.7 0.0 copy-start.1
  1.7 2.4 %collective-permute-start = (bf16[128,128]{1,0:T(8,128)(2,1)S(1)}, bf16[128,128]{1,0:T(8,128)(2,1)S(1)}, u32[]{:S(2)}, u32[]{:S(2)}) collective-permute-start(bf16[128,128]{1,0:T(8,128)(2,1)S(1)} %get-tuple-element.62), channel_id=1, source_target_pairs={{0,3},{1,2},{2,1},{3,0},{4,7},{5,6},{6,5},{7,4},{8,11},{9,10},{10,... | collective-permute-start | bytes 98312 | tf_op jit(solution)/shard_map/ppermute | solution.py:400
  4.1 1.6 %collective-permute-start.1 = (bf16[128,128]{1,0:T(8,128)(2,1)S(1)}, bf16[128,128]{1,0:T(8,128)(2,1)S(1)}, u32[]{:S(2)}, u32[]{:S(2)}) collective-permute-start(bf16[128,128]{1,0:T(8,128)(2,1)S(1)} %get-tuple-element.63), channel_id=1, source_target_pairs={{0,4},{1,5},{2,6},{3,7},{4,0},{5,1},{6,2},{7,3},{8,12},{9,13},{10,... | collective-permute-start | bytes 98312 | tf_op jit(solution)/shard_map/ppermute | solution.py:400
  5.7 0.4 collective-permute-start.2
  6.1 0.1 collective-permute-start.3
  6.2 2.4 %shard_map.192 = (bf16[32,9,128,128]{3,2,1,0:T(8,128)(2,1)S(1)}, s32[9,32]{1,0:T(8,128)S(4)}, s32[8,128]{1,0:T(8,128)S(4)}, f32[32,128]{1,0:T(8,128)S(1)}, f32[32,128]{1,0:T(8,128)S(1)}) custom-call(bf16[32,9,128,128]{3,2,1,0:T(8,128)(2,1)} %off_hbm.5, s32[9,32]{1,0:T(8,128)} %bitcast.2, s32[32]{0:T(128)} %colours_hbm.1, f32[32,128]{1,0:T(8,128)S(1)} %copy-done.5, ...), custom_call_target="tpu_custom_call" | custom-call | tf_op jit(solution)/shard_map/pallas_call | solution.py:410
  8.6 0.0 collective-permute-done.refs_0_
  8.6 0.0 collective-permute-done.2.refs_2_
  8.6 0.0 collective-permute-done.3.refs_3_
  8.7 0.0 copy-start
  8.7 0.0 copy-start.2
  8.7 0.0 copy-start.8
  8.7 3.8 %shard_map.193 = (bf16[32,9,128,128]{3,2,1,0:T(8,128)(2,1)S(1)}, f32[32,8,128]{2,1,0:T(8,128)S(1)}, f32[16,8,128]{2,1,0:T(8,128)S(1)}) custom-call(f32[32,8,128]{2,1,0:T(8,128)S(1)} %get-tuple-element.59.q.q_ref, bf16[32,128,128]{2,1,0:T(8,128)(2,1)S(1)} %copy-done.1, bf16[32,9,128,128]{3,2,1,0:T(8,128)(2,1)} %off_hbm.5, ...), custom_call_target="tpu_custom_call", output_to_operand_aliasing={{0}: (3, {})} | custom-call | tf_op jit(solution)/shard_map/pallas_call | solution.py:416
  12.5 11.7 %all_to_all.10.sums = f32[16,8,128]{2,1,0:T(8,128)S(1)} all-to-all(f32[16,8,128]{2,1,0:T(8,128)S(1)} %get-tuple-element.66), channel_id=1, replica_groups=mesh['groups'=2,'gx'=16] {'gx'}, dimensions={0} | all-to-all | bytes 131072 | tf_op jit(solution)/shard_map/all_to_all | solution.py:423
  24.2 1.3 %shard_map.194 = (f32[32,8,128]{2,1,0:T(8,128)S(1)}, f32[32,8,128]{2,1,0:T(8,128)S(1)}, f32[8,128]{1,0:T(8,128)S(1)}, bf16[128,128]{1,0:T(8,128)(2,1)S(1)}, bf16...) custom-call(f32[16,8,128]{2,1,0:T(8,128)S(1)} %all_to_all.10.sums, ...), custom_call_target="tpu_custom_call" | custom-call | tf_op jit(solution)/shard_map/pallas_call | solution.py:424
  25.5 0.1 collective-permute-start.4
  25.6 0.5 collective-permute-start.5
  26.1 0.1 collective-permute-start.6
  26.2 0.4 collective-permute-start.7
  26.6 1.0 %shard_map.195 = (f32[128,8,128]{2,1,0:T(8,128)S(1)}, f32[16,128]{1,0:T(8,128)S(1)}) custom-call(f32[32,8,128]{2,1,0:T(8,128)S(1)} %get-tuple-element.114.r_new.refs_4_, f32[32,8,128]{2,1,0:T(8,128)S(1)} %get-tuple-element.73.w.w_in, bf16[32,9,128,128]{3,2,1,0:T(8,128)(2,1)S(1)} %get-tuple-element.74.off, s32[9,32]{1,0:T(8,128)S(4)} %get-tuple-element.61.columns, ...), custom_call_target="tpu_custom_call" | custom-call | flops 100000000 | tf_op jit(solution)/shard_map/pallas_call | solution.py:431
  27.5 1.4 %collective-permute-done.4.refs_0_ = bf16[128,128]{1,0:T(8,128)(2,1)S(1)} collective-permute-done((bf16[128,128]{1,0:T(8,128)(2,1)S(1)}, bf16[128,128]{1,0:T(8,128)(2,1)S(1)}, u32[]{:S(2)}, u32[]{:S(2)}) %collective-permute-start.4) | collective-permute-done | bytes 32800 | tf_op jit(solution)/shard_map/ppermute | solution.py:400
  29.0 0.6 collective-permute-done.5.refs_1_
  29.6 1.2 %shard_map.196 = (f32[32,8,128]{2,1,0:T(8,128)S(1)}, bf16[256,128]{1,0:T(8,128)(2,1)S(1)}, bf16[256,128]{1,0:T(8,128)(2,1)S(1)}, bf16[256,128]{1,0:T(8,128)(2,1)S(1)}, bf16[256,128]{1,0:T(8,128)(2,1)S(1)}) custom-call(f32[32,8,128]{2,1,0:T(8,128)S(1)} %get-tuple-element.114.r_new.refs_4_, f32[32,8,128]{2,1,0:T(8,128)S(1)} %get-tuple-element.73.w.w_in, ...), custom_call_target="tpu_custom_call" | custom-call | tf_op jit(solution)/shard_map/pallas_call | solution.py:443
  30.7 1.7 %collective-permute-start.8 = (bf16[256,128]{1,0:T(8,128)(2,1)S(1)}, bf16[256,128]{1,0:T(8,128)(2,1)S(1)}, u32[]{:S(2)}, u32[]{:S(2)}) collective-permute-start(bf16[256,128]{1,0:T(8,128)(2,1)S(1)} %get-tuple-element.81), channel_id=1, source_target_pairs={{0,3},{1,2},{2,1},{3,0},{4,7},{5,6},{6,5},{7,4},{8,11},{9,10},{10,... | collective-permute-start | bytes 196616 | tf_op jit(solution)/shard_map/ppermute | solution.py:400
  32.4 1.5 %collective-permute-start.9 = (bf16[256,128]{1,0:T(8,128)(2,1)S(1)}, bf16[256,128]{1,0:T(8,128)(2,1)S(1)}, u32[]{:S(2)}, u32[]{:S(2)}) collective-permute-start(bf16[256,128]{1,0:T(8,128)(2,1)S(1)} %get-tuple-element.82), channel_id=1, source_target_pairs={{0,4},{1,5},{2,6},{3,7},{4,0},{5,1},{6,2},{7,3},{8,12},{9,13},{10,... | collective-permute-start | bytes 196616 | tf_op jit(solution)/shard_map/ppermute | solution.py:400
  33.9 0.4 collective-permute-start.10
  34.3 0.1 collective-permute-start.11
  34.4 0.3 collective-permute-done.8.refs_0_
  34.7 2.6 %collective-permute-done.9.refs_1_ = bf16[256,128]{1,0:T(8,128)(2,1)S(1)} collective-permute-done((bf16[256,128]{1,0:T(8,128)(2,1)S(1)}, bf16[256,128]{1,0:T(8,128)(2,1)S(1)}, u32[]{:S(2)}, u32[]{:S(2)}) %collective-permute-start.9) | collective-permute-done | bytes 65568 | tf_op jit(solution)/shard_map/ppermute | solution.py:400
  37.3 2.1 %shard_map.197 = (f32[32,8,128]{2,1,0:T(8,128)S(1)}, bf16[128,128]{1,0:T(8,128)(2,1)S(1)}, bf16[128,128]{1,0:T(8,128)(2,1)S(1)}, bf16[128,128]{1,0:T(8,128)(2,1)S(1)}, bf16[128,128]{1,0:T(8,128)(2,1)S(1)}) custom-call(f32[32,8,128]{2,1,0:T(8,128)S(1)} %get-tuple-element.114.r_new.refs_4_, f32[32,8,128]{2,1,0:T(8,128)S(1)} %get-tuple-element.80.w_in, ...), custom_call_target="tpu_custom_call" | custom-call | tf_op jit(solution)/shard_map/pallas_call | solution.py:443
  39.3 0.1 collective-permute-start.12
  39.4 1.8 %collective-permute-start.13 = (bf16[128,128]{1,0:T(8,128)(2,1)S(1)}, bf16[128,128]{1,0:T(8,128)(2,1)S(1)}, u32[]{:S(2)}, u32[]{:S(2)}) collective-permute-start(bf16[128,128]{1,0:T(8,128)(2,1)S(1)} %get-tuple-element.87), channel_id=1, source_target_pairs={{0,4},{1,5},{2,6},{3,7},{4,0},{5,1},{6,2},{7,3},{8,12},{9,13},{10,... | collective-permute-start | bytes 98312 | tf_op jit(solution)/shard_map/ppermute | solution.py:400
  41.2 0.5 collective-permute-start.15
  41.7 1.2 %collective-permute-done.12.refs_0_ = bf16[128,128]{1,0:T(8,128)(2,1)S(1)} collective-permute-done((bf16[128,128]{1,0:T(8,128)(2,1)S(1)}, bf16[128,128]{1,0:T(8,128)(2,1)S(1)}, u32[]{:S(2)}, u32[]{:S(2)}) %collective-permute-start.12) | collective-permute-done | bytes 32800 | tf_op jit(solution)/shard_map/ppermute | solution.py:400
  42.9 0.5 collective-permute-done.13.refs_1_
  43.4 2.1 %shard_map.198 = (f32[32,8,128]{2,1,0:T(8,128)S(1)}, f32[32,8,128]{2,1,0:T(8,128)S(1)}, bf16[128,128]{1,0:T(8,128)(2,1)S(1)}, bf16[128,128]{1,0:T(8,128)(2,1)S(1...) custom-call(f32[32,8,128]{2,1,0:T(8,128)S(1)} %get-tuple-element.114.r_new.refs_4_, ...), custom_call_target="tpu_custom_call" | custom-call | tf_op jit(solution)/shard_map/pallas_call | solution.py:443
  45.6 1.1 %collective-permute-start.16 = (bf16[128,128]{1,0:T(8,128)(2,1)S(1)}, bf16[128,128]{1,0:T(8,128)(2,1)S(1)}, u32[]{:S(2)}, u32[]{:S(2)}) collective-permute-start(bf16[128,128]{1,0:T(8,128)(2,1)S(1)} %get-tuple-element.92), channel_id=1, source_target_pairs={{0,3},{1,2},{2,1},{3,0},{4,7},{5,6},{6,5},{7,4},{8,11},{9,10},{10,... | collective-permute-start | bytes 98312 | tf_op jit(solution)/shard_map/ppermute | solution.py:400
  46.7 1.0 %collective-permute-start.17 = (bf16[128,128]{1,0:T(8,128)(2,1)S(1)}, bf16[128,128]{1,0:T(8,128)(2,1)S(1)}, u32[]{:S(2)}, u32[]{:S(2)}) collective-permute-start(bf16[128,128]{1,0:T(8,128)(2,1)S(1)} %get-tuple-element.93), channel_id=1, source_target_pairs={{0,4},{1,5},{2,6},{3,7},{4,0},{5,1},{6,2},{7,3},{8,12},{9,13},{10,... | collective-permute-start | bytes 98312 | tf_op jit(solution)/shard_map/ppermute | solution.py:400
  47.7 0.9 %collective-permute-start.18 = (bf16[128,128]{1,0:T(8,128)(2,1)S(1)}, bf16[128,128]{1,0:T(8,128)(2,1)S(1)}, u32[]{:S(2)}, u32[]{:S(2)}) collective-permute-start(bf16[128,128]{1,0:T(8,128)(2,1)S(1)} %get-tuple-element.94), channel_id=1, source_target_pairs={{0,1},{1,0},{2,3},{3,2},{4,8},{5,9},{6,10},{7,11},{8,4},{9,5},{10,... | collective-permute-start | bytes 98312 | tf_op jit(solution)/shard_map/ppermute | solution.py:400
  48.6 0.6 collective-permute-done.16.refs_0_
  49.2 1.4 %collective-permute-done.17.refs_1_ = bf16[128,128]{1,0:T(8,128)(2,1)S(1)} collective-permute-done((bf16[128,128]{1,0:T(8,128)(2,1)S(1)}, bf16[128,128]{1,0:T(8,128)(2,1)S(1)}, u32[]{:S(2)}, u32[]{:S(2)}) %collective-permute-start.17) | collective-permute-done | bytes 32800 | tf_op jit(solution)/shard_map/ppermute | solution.py:400
  50.6 2.1 %shard_map.199 = (f32[32,8,128]{2,1,0:T(8,128)S(1)}, bf16[128,128]{1,0:T(8,128)(2,1)S(1)}, bf16[128,128]{1,0:T(8,128)(2,1)S(1)}, bf16[128,128]{1,0:T(8,128)(2,1)S(1)}, bf16[128,128]{1,0:T(8,128)(2,1)S(1)}) custom-call(f32[32,8,128]{2,1,0:T(8,128)S(1)} %get-tuple-element.90.w, f32[32,8,128]{2,1,0:T(8,128)S(1)} %get-tuple-element.91.z_in, ...), custom_call_target="tpu_custom_call" | custom-call | tf_op jit(solution)/shard_map/pallas_call | solution.py:450
  52.7 0.1 collective-permute-start.20
  52.8 2.1 %collective-permute-start.21 = (bf16[128,128]{1,0:T(8,128)(2,1)S(1)}, bf16[128,128]{1,0:T(8,128)(2,1)S(1)}, u32[]{:S(2)}, u32[]{:S(2)}) collective-permute-start(bf16[128,128]{1,0:T(8,128)(2,1)S(1)} %get-tuple-element.98), channel_id=1, source_target_pairs={{0,4},{1,5},{2,6},{3,7},{4,0},{5,1},{6,2},{7,3},{8,12},{9,13},{10,... | collective-permute-start | bytes 98312 | tf_op jit(solution)/shard_map/ppermute | solution.py:400
  54.8 0.5 collective-permute-start.23
  55.3 0.2 shard_map.200.refs_5_
  55.6 0.8 %collective-permute-done.20.refs_0_ = bf16[128,128]{1,0:T(8,128)(2,1)S(1)} collective-permute-done((bf16[128,128]{1,0:T(8,128)(2,1)S(1)}, bf16[128,128]{1,0:T(8,128)(2,1)S(1)}, u32[]{:S(2)}, u32[]{:S(2)}) %collective-permute-start.20) | collective-permute-done | bytes 32800 | tf_op jit(solution)/shard_map/ppermute | solution.py:400
  56.4 0.3 collective-permute-done.21.refs_1_
  56.7 1.8 %shard_map.201 = (f32[32,8,128]{2,1,0:T(8,128)S(1)}, bf16[128,128]{1,0:T(8,128)(2,1)S(1)}, bf16[128,128]{1,0:T(8,128)(2,1)S(1)}, bf16[128,128]{1,0:T(8,128)(2,1)...) custom-call(f32[32,8,128]{2,1,0:T(8,128)S(1)} %get-tuple-element.90.w, ...), custom_call_target="tpu_custom_call" | custom-call | tf_op jit(solution)/shard_map/pallas_call | solution.py:456
  58.5 4.7 %all-to-all-start.1 = ((f32[16,16,128]{2,1,0:T(8,128)}), f32[16,16,128]{2,1,0:T(8,128)S(1)}, u32[]{:S(2)}, u32[]{:S(2)}) async-start(f32[16,16,128]{2,1,0:T(8,128)} %get-tuple-element.102), calls=%async_computation.1 | async-start | bytes 262144 | tf_op jit(solution)/shard_map/all_to_all | solution.py:462
  63.3 1.7 %collective-permute-start.24 = (bf16[128,128]{1,0:T(8,128)(2,1)S(1)}, bf16[128,128]{1,0:T(8,128)(2,1)S(1)}, u32[]{:S(2)}, u32[]{:S(2)}) collective-permute-start(bf16[128,128]{1,0:T(8,128)(2,1)S(1)} %get-tuple-element.104), channel_id=1, source_target_pairs={{0,3},{1,2},{2,1},{3,0},{4,7},{5,6},{6,5},{7,4},{8,11},{9,10},{10,... | collective-permute-start | bytes 98312 | tf_op jit(solution)/shard_map/ppermute | solution.py:400
  65.0 1.5 %collective-permute-start.25 = (bf16[128,128]{1,0:T(8,128)(2,1)S(1)}, bf16[128,128]{1,0:T(8,128)(2,1)S(1)}, u32[]{:S(2)}, u32[]{:S(2)}) collective-permute-start(bf16[128,128]{1,0:T(8,128)(2,1)S(1)} %get-tuple-element.105), channel_id=1, source_target_pairs={{0,4},{1,5},{2,6},{3,7},{4,0},{5,1},{6,2},{7,3},{8,12},{9,13},{10,... | collective-permute-start | bytes 98312 | tf_op jit(solution)/shard_map/ppermute | solution.py:400
  66.4 0.1 collective-permute-start.26
  66.5 0.4 collective-permute-start.27
  66.9 0.7 copy.23
  67.6 2.0 %shard_map.202.off = bf16[32,9,128,128]{3,2,1,0:T(8,128)(2,1)S(1)} custom-call(bf16[32,9,128,128]{3,2,1,0:T(8,128)(2,1)} %off_hbm.5, s32[8,128]{1,0:T(8,128)S(4)} %get-tuple-element.70.tables, bf16[128,128]{1,0:T(8,128)(2,1)S(1)} %collective-permute-done.24.after.refs_0_), custom_call_target="tpu_custom_call" | custom-call | flops 100000000 | tf_op jit(solution)/shard_map/pallas_call | solution.py:464
  69.7 0.0 copy-start.3
  69.7 0.0 copy-start.4
  69.7 0.0 copy-start.9
  69.7 0.0 copy-start.10
  69.7 2.0 %shard_map.203.z = f32[32,8,128]{2,1,0:T(8,128)S(1)} custom-call(f32[32,8,128]{2,1,0:T(8,128)S(1)} %get-tuple-element.90.w, f32[32,8,128]{2,1,0:T(8,128)S(1)} %get-tuple-element.103.z_in, bf16[32,9,128,128]{3,2,1,0:T(8,128)(2,1)S(1)} %shard_map.202.off, bf16[32,128,128]{2,1,0:T(8,128)(2,1)S(1)} %copy-done, f32[32,128]{1,0:T(8,128)S(1)} %get-tuple-element.68.straight, ...), custom_call_target="tpu_custom_call" | custom-call | tf_op jit(solution)/shard_map/pallas_call | solution.py:467
  71.7 0.0 copy-done.3
  71.8 1.4 %shard_map.204 = (f32[32,8,128]{2,1,0:T(8,128)}, f32[32,8,128]{2,1,0:T(8,128)}, f32[32,8,128]{2,1,0:T(8,128)}, f32[3,8]{1,0:T(4,128)}) custom-call(f32[16,16,128]{2,1,0:T(8,128)S(1)} %all-to-all-done.1.sums, f32[32,8,128]{2,1,0:T(8,128)S(1)} %shard_map.203.z, f32[32,8,128]{2,1,0:T(8,128)S(1)} %get-tuple-element.59.q.q_ref, f32[32,8,128]{2,1,0:T(8,128)S(1)} %copy-done.3, ...), custom_call_target="tpu_custom_call" | custom-call | tf_op jit(solution)/shard_map/pallas_call | solution.py:474
  (32 shorter events, 0.1 us)
Async XLA Ops:
  0.6 5.6 %copy-start.5 = (f32[32,128]{1,0:T(8,128)S(1)}, f32[32,128]{1,0:T(8,128)}, u32[]{:S(2)}) copy-start(f32[32,128]{1,0:T(8,128)} %diag_ref.1) | copy-start | bytes 49156
  0.6 5.6 %copy-start.6 = (f32[32,64]{1,0:T(8,128)S(1)}, f32[32,64]{1,0:T(8,128)}, u32[]{:S(2)}) copy-start(f32[32,64]{1,0:T(8,128)} %off_ref.1) | copy-start | bytes 24580
  0.7 5.6 %copy-start.7 = (s32[32,64]{1,0:T(8,128)S(1)}, s32[32,64]{1,0:T(8,128)}, u32[]{:S(2)}) copy-start(s32[32,64]{1,0:T(8,128)} %pairs_ref.1) | copy-start | bytes 24580
  1.7 7.0 %copy-start.1 = (bf16[32,128,128]{2,1,0:T(8,128)(2,1)S(1)}, bf16[32,128,128]{2,1,0:T(8,128)(2,1)}, u32[]{:S(2)}) copy-start(bf16[32,128,128]{2,1,0:T(8,128)(2,1)} %diag.1) | copy-start | bytes 3145732
  1.7 6.9 %collective-permute-start = (bf16[128,128]{1,0:T(8,128)(2,1)S(1)}, bf16[128,128]{1,0:T(8,128)(2,1)S(1)}, u32[]{:S(2)}, u32[]{:S(2)}) collective-permute-start(bf16[128,128]{1,0:T(8,128)(2,1)S(1)} %get-tuple-element.62), channel_id=1, source_target_pairs={{0,3},{1,2},{2,1},{3,0},{4,7},{5,6},{6,5},{7,4},{8,11},{9,10},{10,... | collective-permute-start | bytes 98312 | tf_op jit(solution)/shard_map/ppermute | solution.py:400
  4.1 4.5 %collective-permute-start.1 = (bf16[128,128]{1,0:T(8,128)(2,1)S(1)}, bf16[128,128]{1,0:T(8,128)(2,1)S(1)}, u32[]{:S(2)}, u32[]{:S(2)}) collective-permute-start(bf16[128,128]{1,0:T(8,128)(2,1)S(1)} %get-tuple-element.63), channel_id=1, source_target_pairs={{0,4},{1,5},{2,6},{3,7},{4,0},{5,1},{6,2},{7,3},{8,12},{9,13},{10,... | collective-permute-start | bytes 98312 | tf_op jit(solution)/shard_map/ppermute | solution.py:400
  5.7 2.9 %collective-permute-start.2 = (bf16[128,128]{1,0:T(8,128)(2,1)S(1)}, bf16[128,128]{1,0:T(8,128)(2,1)S(1)}, u32[]{:S(2)}, u32[]{:S(2)}) collective-permute-start(bf16[128,128]{1,0:T(8,128)(2,1)S(1)} %get-tuple-element.64), channel_id=1, source_target_pairs={{0,1},{1,0},{2,3},{3,2},{4,8},{5,9},{6,10},{7,11},{8,4},{9,5},{10,... | collective-permute-start | bytes 98312 | tf_op jit(solution)/shard_map/ppermute | solution.py:400
  6.1 2.5 %collective-permute-start.3 = (bf16[128,128]{1,0:T(8,128)(2,1)S(1)}, bf16[128,128]{1,0:T(8,128)(2,1)S(1)}, u32[]{:S(2)}, u32[]{:S(2)}) collective-permute-start(bf16[128,128]{1,0:T(8,128)(2,1)S(1)} %get-tuple-element.65), channel_id=1, source_target_pairs={{0,1},{1,0},{2,3},{3,2},{4,5},{5,4},{6,7},{7,6},{8,9},{9,8},{10,11... | collective-permute-start | bytes 98312 | tf_op jit(solution)/shard_map/ppermute | solution.py:400
  8.7 15.5 %copy-start = (bf16[32,128,128]{2,1,0:T(8,128)(2,1)S(1)}, bf16[32,128,128]{2,1,0:T(8,128)(2,1)}, u32[]{:S(2)}) copy-start(bf16[32,128,128]{2,1,0:T(8,128)(2,1)} %factor.13) | copy-start | bytes 3145732
  8.7 15.5 %copy-start.2 = (f32[32,8,128]{2,1,0:T(8,128)S(1)}, f32[32,8,128]{2,1,0:T(8,128)}, u32[]{:S(2)}) copy-start(f32[32,8,128]{2,1,0:T(8,128)} %r_ref.1) | copy-start | bytes 393220
  8.7 15.5 %copy-start.8 = (f32[8]{0:T(128)S(1)}, f32[8]{0:T(128)}, u32[]{:S(2)}) copy-start(f32[8]{0:T(128)} %rho.3) | copy-start | bytes 100
  25.5 3.5 %collective-permute-start.4 = (bf16[128,128]{1,0:T(8,128)(2,1)S(1)}, bf16[128,128]{1,0:T(8,128)(2,1)S(1)}, u32[]{:S(2)}, u32[]{:S(2)}) collective-permute-start(bf16[128,128]{1,0:T(8,128)(2,1)S(1)} %get-tuple-element.75), channel_id=1, source_target_pairs={{0,3},{1,2},{2,1},{3,0},{4,7},{5,6},{6,5},{7,4},{8,11},{9,10},{10,... | collective-permute-start | bytes 98312 | tf_op jit(solution)/shard_map/ppermute | solution.py:400
  25.6 4.0 %collective-permute-start.5 = (bf16[128,128]{1,0:T(8,128)(2,1)S(1)}, bf16[128,128]{1,0:T(8,128)(2,1)S(1)}, u32[]{:S(2)}, u32[]{:S(2)}) collective-permute-start(bf16[128,128]{1,0:T(8,128)(2,1)S(1)} %get-tuple-element.76), channel_id=1, source_target_pairs={{0,4},{1,5},{2,6},{3,7},{4,0},{5,1},{6,2},{7,3},{8,12},{9,13},{10,... | collective-permute-start | bytes 98312 | tf_op jit(solution)/shard_map/ppermute | solution.py:400
  26.1 3.5 %collective-permute-start.6 = (bf16[128,128]{1,0:T(8,128)(2,1)S(1)}, bf16[128,128]{1,0:T(8,128)(2,1)S(1)}, u32[]{:S(2)}, u32[]{:S(2)}) collective-permute-start(bf16[128,128]{1,0:T(8,128)(2,1)S(1)} %get-tuple-element.77), channel_id=1, source_target_pairs={{0,1},{1,0},{2,3},{3,2},{4,8},{5,9},{6,10},{7,11},{8,4},{9,5},{10,... | collective-permute-start | bytes 98312 | tf_op jit(solution)/shard_map/ppermute | solution.py:400
  26.2 3.4 %collective-permute-start.7 = (bf16[128,128]{1,0:T(8,128)(2,1)S(1)}, bf16[128,128]{1,0:T(8,128)(2,1)S(1)}, u32[]{:S(2)}, u32[]{:S(2)}) collective-permute-start(bf16[128,128]{1,0:T(8,128)(2,1)S(1)} %get-tuple-element.78), channel_id=1, source_target_pairs={{0,1},{1,0},{2,3},{3,2},{4,5},{5,4},{6,7},{7,6},{8,9},{9,8},{10,11... | collective-permute-start | bytes 98312 | tf_op jit(solution)/shard_map/ppermute | solution.py:400
  30.7 4.0 %collective-permute-start.8 = (bf16[256,128]{1,0:T(8,128)(2,1)S(1)}, bf16[256,128]{1,0:T(8,128)(2,1)S(1)}, u32[]{:S(2)}, u32[]{:S(2)}) collective-permute-start(bf16[256,128]{1,0:T(8,128)(2,1)S(1)} %get-tuple-element.81), channel_id=1, source_target_pairs={{0,3},{1,2},{2,1},{3,0},{4,7},{5,6},{6,5},{7,4},{8,11},{9,10},{10,... | collective-permute-start | bytes 196616 | tf_op jit(solution)/shard_map/ppermute | solution.py:400
  32.4 4.9 %collective-permute-start.9 = (bf16[256,128]{1,0:T(8,128)(2,1)S(1)}, bf16[256,128]{1,0:T(8,128)(2,1)S(1)}, u32[]{:S(2)}, u32[]{:S(2)}) collective-permute-start(bf16[256,128]{1,0:T(8,128)(2,1)S(1)} %get-tuple-element.82), channel_id=1, source_target_pairs={{0,4},{1,5},{2,6},{3,7},{4,0},{5,1},{6,2},{7,3},{8,12},{9,13},{10,... | collective-permute-start | bytes 196616 | tf_op jit(solution)/shard_map/ppermute | solution.py:400
  33.9 3.4 %collective-permute-start.10 = (bf16[256,128]{1,0:T(8,128)(2,1)S(1)}, bf16[256,128]{1,0:T(8,128)(2,1)S(1)}, u32[]{:S(2)}, u32[]{:S(2)}) collective-permute-start(bf16[256,128]{1,0:T(8,128)(2,1)S(1)} %get-tuple-element.83), channel_id=1, source_target_pairs={{0,1},{1,0},{2,3},{3,2},{4,8},{5,9},{6,10},{7,11},{8,4},{9,5},{10,... | collective-permute-start | bytes 196616 | tf_op jit(solution)/shard_map/ppermute | solution.py:400
  34.3 3.0 %collective-permute-start.11 = (bf16[256,128]{1,0:T(8,128)(2,1)S(1)}, bf16[256,128]{1,0:T(8,128)(2,1)S(1)}, u32[]{:S(2)}, u32[]{:S(2)}) collective-permute-start(bf16[256,128]{1,0:T(8,128)(2,1)S(1)} %get-tuple-element.84), channel_id=1, source_target_pairs={{0,1},{1,0},{2,3},{3,2},{4,5},{5,4},{6,7},{7,6},{8,9},{9,8},{10,11... | collective-permute-start | bytes 196616 | tf_op jit(solution)/shard_map/ppermute | solution.py:400
  39.3 3.6 %collective-permute-start.12 = (bf16[128,128]{1,0:T(8,128)(2,1)S(1)}, bf16[128,128]{1,0:T(8,128)(2,1)S(1)}, u32[]{:S(2)}, u32[]{:S(2)}) collective-permute-start(bf16[128,128]{1,0:T(8,128)(2,1)S(1)} %get-tuple-element.86), channel_id=1, source_target_pairs={{0,3},{1,2},{2,1},{3,0},{4,7},{5,6},{6,5},{7,4},{8,11},{9,10},{10,... | collective-permute-start | bytes 98312 | tf_op jit(solution)/shard_map/ppermute | solution.py:400
  39.4 4.0 %collective-permute-start.13 = (bf16[128,128]{1,0:T(8,128)(2,1)S(1)}, bf16[128,128]{1,0:T(8,128)(2,1)S(1)}, u32[]{:S(2)}, u32[]{:S(2)}) collective-permute-start(bf16[128,128]{1,0:T(8,128)(2,1)S(1)} %get-tuple-element.87), channel_id=1, source_target_pairs={{0,4},{1,5},{2,6},{3,7},{4,0},{5,1},{6,2},{7,3},{8,12},{9,13},{10,... | collective-permute-start | bytes 98312 | tf_op jit(solution)/shard_map/ppermute | solution.py:400
  41.2 2.2 %collective-permute-start.14 = (bf16[128,128]{1,0:T(8,128)(2,1)S(1)}, bf16[128,128]{1,0:T(8,128)(2,1)S(1)}, u32[]{:S(2)}, u32[]{:S(2)}) collective-permute-start(bf16[128,128]{1,0:T(8,128)(2,1)S(1)} %get-tuple-element.88), channel_id=1, source_target_pairs={{0,1},{1,0},{2,3},{3,2},{4,8},{5,9},{6,10},{7,11},{8,4},{9,5},{10,... | collective-permute-start | bytes 98312 | tf_op jit(solution)/shard_map/ppermute | solution.py:400
  41.2 2.2 %collective-permute-start.15 = (bf16[128,128]{1,0:T(8,128)(2,1)S(1)}, bf16[128,128]{1,0:T(8,128)(2,1)S(1)}, u32[]{:S(2)}, u32[]{:S(2)}) collective-permute-start(bf16[128,128]{1,0:T(8,128)(2,1)S(1)} %get-tuple-element.89), channel_id=1, source_target_pairs={{0,1},{1,0},{2,3},{3,2},{4,5},{5,4},{6,7},{7,6},{8,9},{9,8},{10,11... | collective-permute-start | bytes 98312 | tf_op jit(solution)/shard_map/ppermute | solution.py:400
  45.6 3.6 %collective-permute-start.16 = (bf16[128,128]{1,0:T(8,128)(2,1)S(1)}, bf16[128,128]{1,0:T(8,128)(2,1)S(1)}, u32[]{:S(2)}, u32[]{:S(2)}) collective-permute-start(bf16[128,128]{1,0:T(8,128)(2,1)S(1)} %get-tuple-element.92), channel_id=1, source_target_pairs={{0,3},{1,2},{2,1},{3,0},{4,7},{5,6},{6,5},{7,4},{8,11},{9,10},{10,... | collective-permute-start | bytes 98312 | tf_op jit(solution)/shard_map/ppermute | solution.py:400
  46.7 3.9 %collective-permute-start.17 = (bf16[128,128]{1,0:T(8,128)(2,1)S(1)}, bf16[128,128]{1,0:T(8,128)(2,1)S(1)}, u32[]{:S(2)}, u32[]{:S(2)}) collective-permute-start(bf16[128,128]{1,0:T(8,128)(2,1)S(1)} %get-tuple-element.93), channel_id=1, source_target_pairs={{0,4},{1,5},{2,6},{3,7},{4,0},{5,1},{6,2},{7,3},{8,12},{9,13},{10,... | collective-permute-start | bytes 98312 | tf_op jit(solution)/shard_map/ppermute | solution.py:400
  47.7 2.9 %collective-permute-start.18 = (bf16[128,128]{1,0:T(8,128)(2,1)S(1)}, bf16[128,128]{1,0:T(8,128)(2,1)S(1)}, u32[]{:S(2)}, u32[]{:S(2)}) collective-permute-start(bf16[128,128]{1,0:T(8,128)(2,1)S(1)} %get-tuple-element.94), channel_id=1, source_target_pairs={{0,1},{1,0},{2,3},{3,2},{4,8},{5,9},{6,10},{7,11},{8,4},{9,5},{10,... | collective-permute-start | bytes 98312 | tf_op jit(solution)/shard_map/ppermute | solution.py:400
  48.6 2.0 %collective-permute-start.19 = (bf16[128,128]{1,0:T(8,128)(2,1)S(1)}, bf16[128,128]{1,0:T(8,128)(2,1)S(1)}, u32[]{:S(2)}, u32[]{:S(2)}) collective-permute-start(bf16[128,128]{1,0:T(8,128)(2,1)S(1)} %get-tuple-element.95), channel_id=1, source_target_pairs={{0,1},{1,0},{2,3},{3,2},{4,5},{5,4},{6,7},{7,6},{8,9},{9,8},{10,11... | collective-permute-start | bytes 98312 | tf_op jit(solution)/shard_map/ppermute | solution.py:400
  52.7 3.7 %collective-permute-start.20 = (bf16[128,128]{1,0:T(8,128)(2,1)S(1)}, bf16[128,128]{1,0:T(8,128)(2,1)S(1)}, u32[]{:S(2)}, u32[]{:S(2)}) collective-permute-start(bf16[128,128]{1,0:T(8,128)(2,1)S(1)} %get-tuple-element.97), channel_id=1, source_target_pairs={{0,3},{1,2},{2,1},{3,0},{4,7},{5,6},{6,5},{7,4},{8,11},{9,10},{10,... | collective-permute-start | bytes 98312 | tf_op jit(solution)/shard_map/ppermute | solution.py:400
  52.8 4.0 %collective-permute-start.21 = (bf16[128,128]{1,0:T(8,128)(2,1)S(1)}, bf16[128,128]{1,0:T(8,128)(2,1)S(1)}, u32[]{:S(2)}, u32[]{:S(2)}) collective-permute-start(bf16[128,128]{1,0:T(8,128)(2,1)S(1)} %get-tuple-element.98), channel_id=1, source_target_pairs={{0,4},{1,5},{2,6},{3,7},{4,0},{5,1},{6,2},{7,3},{8,12},{9,13},{10,... | collective-permute-start | bytes 98312 | tf_op jit(solution)/shard_map/ppermute | solution.py:400
  54.8 1.9 %collective-permute-start.22 = (bf16[128,128]{1,0:T(8,128)(2,1)S(1)}, bf16[128,128]{1,0:T(8,128)(2,1)S(1)}, u32[]{:S(2)}, u32[]{:S(2)}) collective-permute-start(bf16[128,128]{1,0:T(8,128)(2,1)S(1)} %get-tuple-element.99), channel_id=1, source_target_pairs={{0,1},{1,0},{2,3},{3,2},{4,8},{5,9},{6,10},{7,11},{8,4},{9,5},{10,... | collective-permute-start | bytes 98312 | tf_op jit(solution)/shard_map/ppermute | solution.py:400
  54.8 1.9 %collective-permute-start.23 = (bf16[128,128]{1,0:T(8,128)(2,1)S(1)}, bf16[128,128]{1,0:T(8,128)(2,1)S(1)}, u32[]{:S(2)}, u32[]{:S(2)}) collective-permute-start(bf16[128,128]{1,0:T(8,128)(2,1)S(1)} %get-tuple-element.100), channel_id=1, source_target_pairs={{0,1},{1,0},{2,3},{3,2},{4,5},{5,4},{6,7},{7,6},{8,9},{9,8},{10,11... | collective-permute-start | bytes 98312 | tf_op jit(solution)/shard_map/ppermute | solution.py:400
  58.5 13.2 %all-to-all-start.1 = ((f32[16,16,128]{2,1,0:T(8,128)}), f32[16,16,128]{2,1,0:T(8,128)S(1)}, u32[]{:S(2)}, u32[]{:S(2)}) async-start(f32[16,16,128]{2,1,0:T(8,128)} %get-tuple-element.102), calls=%async_computation.1 | async-start | bytes 262144 | tf_op jit(solution)/shard_map/all_to_all | solution.py:462
  63.3 4.3 %collective-permute-start.24 = (bf16[128,128]{1,0:T(8,128)(2,1)S(1)}, bf16[128,128]{1,0:T(8,128)(2,1)S(1)}, u32[]{:S(2)}, u32[]{:S(2)}) collective-permute-start(bf16[128,128]{1,0:T(8,128)(2,1)S(1)} %get-tuple-element.104), channel_id=1, source_target_pairs={{0,3},{1,2},{2,1},{3,0},{4,7},{5,6},{6,5},{7,4},{8,11},{9,10},{10,... | collective-permute-start | bytes 98312 | tf_op jit(solution)/shard_map/ppermute | solution.py:400
  65.0 4.8 %collective-permute-start.25 = (bf16[128,128]{1,0:T(8,128)(2,1)S(1)}, bf16[128,128]{1,0:T(8,128)(2,1)S(1)}, u32[]{:S(2)}, u32[]{:S(2)}) collective-permute-start(bf16[128,128]{1,0:T(8,128)(2,1)S(1)} %get-tuple-element.105), channel_id=1, source_target_pairs={{0,4},{1,5},{2,6},{3,7},{4,0},{5,1},{6,2},{7,3},{8,12},{9,13},{10,... | collective-permute-start | bytes 98312 | tf_op jit(solution)/shard_map/ppermute | solution.py:400
  66.4 3.3 %collective-permute-start.26 = (bf16[128,128]{1,0:T(8,128)(2,1)S(1)}, bf16[128,128]{1,0:T(8,128)(2,1)S(1)}, u32[]{:S(2)}, u32[]{:S(2)}) collective-permute-start(bf16[128,128]{1,0:T(8,128)(2,1)S(1)} %get-tuple-element.106), channel_id=1, source_target_pairs={{0,1},{1,0},{2,3},{3,2},{4,8},{5,9},{6,10},{7,11},{8,4},{9,5},{10,... | collective-permute-start | bytes 98312 | tf_op jit(solution)/shard_map/ppermute | solution.py:400
  66.5 3.2 %collective-permute-start.27 = (bf16[128,128]{1,0:T(8,128)(2,1)S(1)}, bf16[128,128]{1,0:T(8,128)(2,1)S(1)}, u32[]{:S(2)}, u32[]{:S(2)}) collective-permute-start(bf16[128,128]{1,0:T(8,128)(2,1)S(1)} %get-tuple-element.107), channel_id=1, source_target_pairs={{0,1},{1,0},{2,3},{3,2},{4,5},{5,4},{6,7},{7,6},{8,9},{9,8},{10,11... | collective-permute-start | bytes 98312 | tf_op jit(solution)/shard_map/ppermute | solution.py:400
  69.7 2.1 %copy-start.3 = (f32[32,8,128]{2,1,0:T(8,128)S(1)}, f32[32,8,128]{2,1,0:T(8,128)}, u32[]{:S(2)}) copy-start(f32[32,8,128]{2,1,0:T(8,128)} %x_ref.1) | copy-start | bytes 393220
  69.7 2.1 %copy-start.4 = (f32[32,8,128]{2,1,0:T(8,128)S(1)}, f32[32,8,128]{2,1,0:T(8,128)}, u32[]{:S(2)}) copy-start(f32[32,8,128]{2,1,0:T(8,128)} %d_ref.1) | copy-start | bytes 393220
  69.7 2.1 %copy-start.9 = (f32[8]{0:T(128)S(1)}, f32[8]{0:T(128)}, u32[]{:S(2)}) copy-start(f32[8]{0:T(128)} %tau.1) | copy-start | bytes 100
  69.7 2.1 %copy-start.10 = (f32[8]{0:T(128)S(1)}, f32[8]{0:T(128)}, u32[]{:S(2)}) copy-start(f32[8]{0:T(128)} %theta_in.1) | copy-start | bytes 100

commit v5 on v4

--- a/solution.py
+++ b/solution.py
@@ -14,8 +14,10 @@
 HBM = pltpu.HBM
 SIDE = 4
 ORDER = (1, 2, 3, 0, 4, 5)
-COUPLE = 4
-SOLVE = 16
+COUPLE = (8, 4)
+SOLVE = (16,)
+PART = 4
+PARTS = (0, 12, 16, 24, 32)
 
 
 def swap_pairs(axis, stride, extent, phase, tiles):
@@ -86,14 +88,23 @@
 
 def solved(blocks, vectors, factor, straight, crossed):
     matrices = [factor[b] for b in blocks]
-    firsts = [dot_t(v.astype(BF16), m) for v, m in zip(vectors, matrices)]
+    pairs = range(0, len(blocks), 2)
+    firsts = []
+    for j in pairs:
+        both = dot_t(jnp.concatenate(vectors[j : j + 2], axis=0).astype(BF16), jnp.concatenate(matrices[j : j + 2], axis=0))
+        firsts += [both[:8, :128], both[8:, 128:]]
     even = lax.broadcasted_iota(jnp.int32, (8, 128), 1) % 2 == 0
     middles = []
     for b, first in zip(blocks, firsts):
         other = jnp.where(even, pltpu.roll(first, 127, 1), pltpu.roll(first, 1, 1))
         row = pl.ds(b, 1)
-        middles.append((straight[row, :] * first + crossed[row, :] * other).astype(BF16))
-    return [jnp.dot(v, m, preferred_element_type=F32) for v, m in zip(middles, matrices)]
+        middles.append(straight[row, :] * first + crossed[row, :] * other)
+    values = []
+    for j in pairs:
+        left = jnp.concatenate(middles[j : j + 2], axis=0).astype(BF16)
+        both = jnp.dot(left, jnp.concatenate(matrices[j : j + 2], axis=1), preferred_element_type=F32)
+        values += [both[:8, :128], both[8:, 128:]]
+    return values
 
 
 def load_kernel(off_hbm, tables, after, off, sems):
@@ -107,12 +118,19 @@
     lax.fori_loop(0, count, lambda place, carry: (copy(place).wait(), carry)[1], 0)
 
 
-def for_colour(colour, tables, size, body):
-    def step(group, carry):
-        body([tables[colour, group * size + j] for j in range(size)])
-        return carry
-
-    lax.fori_loop(0, (tables[4, colour] + size - 1) // size, step, 0)
+def for_colour(colour, tables, sizes, body):
+    count = tables[4, colour]
+    done = 0
+    for size in sizes:
+        left = count - done
+        groups = (left + size - 1) // size if size == sizes[-1] else left // size
+
+        def step(group, carry, done=done, size=size):
+            body([tables[colour, done + group * size + j] for j in range(size)])
+            return carry
+
+        lax.fori_loop(0, groups, step, 0)
+        done = done + groups * size
 
 
 def first_kernel(swaps, q_hbm, faces_hbm, q, faces, *refs):
@@ -131,11 +149,10 @@
 def setup_kernel(
     off_hbm, columns_hbm, colours_hbm, diag_ref, off_ref, pairs_ref, off, columns, tables, straight, crossed, colours, sems
 ):
-    half = off_hbm.shape[0] // 2
     loads = [
         pltpu.make_async_copy(colours_hbm, colours, sems.at[0]),
         pltpu.make_async_copy(columns_hbm, columns, sems.at[1]),
-        pltpu.make_async_copy(off_hbm.at[pl.ds(0, half)], off.at[pl.ds(0, half)], sems.at[2]),
+        pltpu.make_async_copy(off_hbm.at[pl.ds(0, PARTS[1])], off.at[pl.ds(0, PARTS[1])], sems.at[2]),
     ]
     for load in loads:
         load.start()
@@ -167,26 +184,22 @@
 def image_kernel(swaps, tiles, q, diag, off_hbm, off_in, columns, *refs):
     n = len(swaps)
     arrived, (off, image, partial, extended, sems) = refs[:n], refs[n:]
-    half, part = off_hbm.shape[0] // 2, 4
-    loads = []
-    for index in range(half // part):
-        rows = pl.ds(half + index * part, part)
-        loads.append(pltpu.make_async_copy(off_hbm.at[rows], off.at[rows], sems.at[index]))
+    loads = [None]
+    for start, end in zip(PARTS[1:], PARTS[2:]):
+        rows = pl.ds(start, end - start)
+        loads.append(pltpu.make_async_copy(off_hbm.at[rows], off.at[rows], sems.at[len(loads) - 1]))
         loads[-1].start()
     extend(swaps, q, arrived, extended)
 
-    def step(group, total):
-        blocks = [group * part + j for j in range(part)]
+    total = jnp.zeros((8, 128), F32)
+    for load, start, end in zip(loads, PARTS, PARTS[1:]):
+        if load is not None:
+            load.wait()
+        blocks = range(start, end)
         values = [coupled(b, extended, off, columns, [(extended[b], diag[b])]) for b in blocks]
         for b, value in zip(blocks, values):
             image[b] = value
             total = total + q[b] * value
-        return total
-
-    total = lax.fori_loop(0, half // part, step, jnp.zeros((8, 128), F32))
-    for index, load in enumerate(loads):
-        load.wait()
-        total = step(half // part + index, total)
     for tile in range(tiles):
         partial[tile] = total
 
@@ -218,8 +231,9 @@
     send_faces(swaps, w, faces, sent)
 
 
-def adjoint_kernel(r_new, w, off, columns, tables, adjoint, terms):
+def adjoint_kernel(r_new, w, off, columns, tables, adjoint, terms, r_out):
     new = r_new[...]
+    r_out[...] = new
     terms[pl.ds(0, 8), :] = jnp.sum(new * w[...], axis=0)
     terms[pl.ds(8, 8), :] = jnp.sum(new * new, axis=0)
     adjoint[...] = jnp.zeros_like(adjoint)
@@ -227,8 +241,8 @@
 
     def step(group, carry):
         products = []
-        for j in range(COUPLE):
-            place = group * COUPLE + j
+        for j in range(PART):
+            place = group * PART + j
             block = tables[0, place]
             vector = jnp.where(place < count, w[block], 0.0)
             high = vector.astype(BF16)
@@ -242,7 +256,7 @@
                 adjoint[column] = adjoint[column] + product[:, k * 128 : k * 128 + 128]
         return carry
 
-    lax.fori_loop(0, (count + COUPLE - 1) // COUPLE, step, 0)
+    lax.fori_loop(0, (count + PART - 1) // PART, step, 0)
 
 
 def gather_kernel(swaps, adjoint, faces, *refs):
@@ -428,9 +442,9 @@
     )(sums, r_vec, image, rho_prev, factor_inv, straight, crossed, tables, faces)
     fixed = (off, factor_inv, straight, crossed, columns, tables, faces)
     fixed_places = [VMEM] * 4 + [SMEM] * 3
-    adjoint, terms = call(
+    adjoint, terms, r_out = call(
         adjoint_kernel,
-        [VMEM((128, 8, 128), F32), VMEM((16, 128), F32)],
+        [VMEM((128, 8, 128), F32), VMEM((16, 128), F32), vec(32, 8, 128)],
         [VMEM] * 3 + [SMEM] * 2,
         cost=10**8,
     )(r_new, w, off, columns, tables)
@@ -476,7 +490,7 @@
         [block_vec] * 3 + [vec(3, 8)],
         [VMEM] * 6 + [SMEM] * 3,
     )(sums, z, q, x_vec, d_vec, alpha, rho_prev, tau_prev, theta_prev)
-    return (x_new, r_new, q_new, d_new, scalars)
+    return (x_new, r_out, q_new, d_new, scalars)
 
 
 def solution(mesh):

time: 73.9 us -> 72.2 us (0.977)
  Pallas kernels: 24.3 us -> 23.2 us
  transfers between devices with their start and end apart: 29 -> 29, of which waited for: 10 -> 12; matrix products, arithmetic and copies ran while one was open for 1% -> 0% of each run, Pallas kernels for 10% -> 11%
where the time goes in v5:
time: 72.2 us; the launch traced here: 71.6 us
  starting transfers between devices  25.5 us (35%)
  Pallas kernels  23.2 us (32%)
  blocking collectives  12 us (17%)
  waiting for transfers between devices  9.89 us (14%)
  between operations  0.9 us (1%)
    ppermute x28, starting transfers between devices, exchange(): lax.ppermute(piece, 'gx', swap[-1])  20.8 us
    all_to_all x1, blocking collectives, per_device(): sums = lax.all_to_all(partial, 'gx', 0, 0, tiled=True)  12 us
    ppermute x28, waiting for transfers between devices, exchange(): lax.ppermute(piece, 'gx', swap[-1])  9.34 us
    pallas_call x3, Pallas kernels, per_device(): call(functools.partial(forward_kernel, swaps, colour), [kept] * (2 if col...  4.75 us
    all_to_all x1, starting transfers between devices, per_device(): sums = lax.all_to_all(partial, 'gx', 0, 0, tiled=True)  4.63 us
    pallas_call x1, Pallas kernels, per_device(): call(functools.partial(image_kernel, swaps, tiles), [off_kept, kept, vec(...  3.75 us
    pallas_call x1, Pallas kernels, per_device(): call(setup_kernel, [off_kept, SMEM((9, 32), jnp.int32), SMEM((8, 128), jn...  2.04 us
    pallas_call x1, Pallas kernels, per_device(): call(load_kernel, [off_kept], [HBM, SMEM, VMEM], [pltpu.SemaphoreType.DMA...  1.96 us
  transfers between devices with their start and end apart: 29, of which 12 were waited for; matrix products, arithmetic and copies ran while one was open for 0% of the time, Pallas kernels for 11%

profile of v5, /device:TPU:0, one launch (start us, length us, event | category | flops | bytes accessed | tf_op | source)
XLA Modules:
  0.0 71.6 jit_solution(2274685141627412346)
XLA Ops:
  0.7 1.0 %shard_map.191 = (f32[32,8,128]{2,1,0:T(8,128)S(1)}, s32[6,1,16]{2,1,0:T(1,128)S(4)}, bf16[128,128]{1,0:T(8,128)(2,1)S(1)}, bf16[128,128]{1,0:T(8,128)(2,1)S(1)}...) custom-call(f32[32,8,128]{2,1,0:T(8,128)} %q_hbm.1, s32[6,1,16]{2,1,0:T(1,128)} %bitcast.3), custom_call_target="tpu_custom_call" | custom-call | flops 10000000000 | tf_op jit(solution)/shard_map/pallas_call | solution.py:416
  1.7 0.0 copy-start.1
  1.7 2.4 %collective-permute-start = (bf16[128,128]{1,0:T(8,128)(2,1)S(1)}, bf16[128,128]{1,0:T(8,128)(2,1)S(1)}, u32[]{:S(2)}, u32[]{:S(2)}) collective-permute-start(bf16[128,128]{1,0:T(8,128)(2,1)S(1)} %get-tuple-element.63), channel_id=1, source_target_pairs={{0,3},{1,2},{2,1},{3,0},{4,7},{5,6},{6,5},{7,4},{8,11},{9,10},{10,... | collective-permute-start | bytes 98312 | tf_op jit(solution)/shard_map/ppermute | solution.py:414
  4.1 1.6 %collective-permute-start.1 = (bf16[128,128]{1,0:T(8,128)(2,1)S(1)}, bf16[128,128]{1,0:T(8,128)(2,1)S(1)}, u32[]{:S(2)}, u32[]{:S(2)}) collective-permute-start(bf16[128,128]{1,0:T(8,128)(2,1)S(1)} %get-tuple-element.64), channel_id=1, source_target_pairs={{0,4},{1,5},{2,6},{3,7},{4,0},{5,1},{6,2},{7,3},{8,12},{9,13},{10,... | collective-permute-start | bytes 98312 | tf_op jit(solution)/shard_map/ppermute | solution.py:414
  5.7 0.4 collective-permute-start.2
  6.1 0.1 collective-permute-start.3
  6.2 2.0 %shard_map.192 = (bf16[32,9,128,128]{3,2,1,0:T(8,128)(2,1)S(1)}, s32[9,32]{1,0:T(8,128)S(4)}, s32[8,128]{1,0:T(8,128)S(4)}, f32[32,128]{1,0:T(8,128)S(1)}, f32[32,128]{1,0:T(8,128)S(1)}) custom-call(bf16[32,9,128,128]{3,2,1,0:T(8,128)(2,1)} %off_hbm.5, s32[9,32]{1,0:T(8,128)} %bitcast.2, s32[32]{0:T(128)} %colours_hbm.1, f32[32,128]{1,0:T(8,128)S(1)} %copy-done.5, ...), custom_call_target="tpu_custom_call" | custom-call | tf_op jit(solution)/shard_map/pallas_call | solution.py:424
  8.3 0.0 collective-permute-done.1.refs_1_
  8.3 0.0 collective-permute-done.2.refs_2_
  8.3 0.0 copy-start
  8.3 0.0 copy-start.2
  8.3 0.0 copy-start.8
  8.4 3.8 %shard_map.193 = (bf16[32,9,128,128]{3,2,1,0:T(8,128)(2,1)S(1)}, f32[32,8,128]{2,1,0:T(8,128)S(1)}, f32[16,8,128]{2,1,0:T(8,128)S(1)}) custom-call(f32[32,8,128]{2,1,0:T(8,128)S(1)} %get-tuple-element.60.q.q_ref, bf16[32,128,128]{2,1,0:T(8,128)(2,1)S(1)} %copy-done.1, bf16[32,9,128,128]{3,2,1,0:T(8,128)(2,1)} %off_hbm.5, ...), custom_call_target="tpu_custom_call", output_to_operand_aliasing={{0}: (3, {})} | custom-call | tf_op jit(solution)/shard_map/pallas_call | solution.py:430
  12.1 12.0 %all_to_all.10.sums = f32[16,8,128]{2,1,0:T(8,128)S(1)} all-to-all(f32[16,8,128]{2,1,0:T(8,128)S(1)} %get-tuple-element.67), channel_id=1, replica_groups=mesh['groups'=2,'gx'=16] {'gx'}, dimensions={0} | all-to-all | bytes 131072 | tf_op jit(solution)/shard_map/all_to_all | solution.py:437
  24.2 1.2 %shard_map.194 = (f32[32,8,128]{2,1,0:T(8,128)S(1)}, f32[32,8,128]{2,1,0:T(8,128)S(1)}, f32[8,128]{1,0:T(8,128)S(1)}, bf16[128,128]{1,0:T(8,128)(2,1)S(1)}, bf16...) custom-call(f32[16,8,128]{2,1,0:T(8,128)S(1)} %all_to_all.10.sums, ...), custom_call_target="tpu_custom_call" | custom-call | tf_op jit(solution)/shard_map/pallas_call | solution.py:438
  25.4 0.1 collective-permute-start.4
  25.4 0.5 collective-permute-start.5
  25.9 0.1 collective-permute-start.6
  26.1 0.4 collective-permute-start.7
  26.4 1.6 %shard_map.195 = (f32[128,8,128]{2,1,0:T(8,128)S(1)}, f32[16,128]{1,0:T(8,128)S(1)}, f32[32,8,128]{2,1,0:T(8,128)}) custom-call(f32[32,8,128]{2,1,0:T(8,128)S(1)} %get-tuple-element.73.r_new.refs_4_, f32[32,8,128]{2,1,0:T(8,128)S(1)} %get-tuple-element.74.w.w_in, bf16[32,9,128,128]{3,2,1,0:T(8,128)(2,1)S(1)} %get-tuple-element.75.off, ...), custom_call_target="tpu_custom_call" | custom-call | flops 100000000 | tf_op jit(solution)/shard_map/pallas_call | solution.py:445
  28.1 0.8 %collective-permute-done.4.refs_0_ = bf16[128,128]{1,0:T(8,128)(2,1)S(1)} collective-permute-done((bf16[128,128]{1,0:T(8,128)(2,1)S(1)}, bf16[128,128]{1,0:T(8,128)(2,1)S(1)}, u32[]{:S(2)}, u32[]{:S(2)}) %collective-permute-start.4) | collective-permute-done | bytes 32800 | tf_op jit(solution)/shard_map/ppermute | solution.py:414
  28.9 0.6 collective-permute-done.5.refs_1_
  29.4 0.0 collective-permute-done.7.refs_3_
  29.4 1.0 %shard_map.196 = (f32[32,8,128]{2,1,0:T(8,128)S(1)}, bf16[256,128]{1,0:T(8,128)(2,1)S(1)}, bf16[256,128]{1,0:T(8,128)(2,1)S(1)}, bf16[256,128]{1,0:T(8,128)(2,1)S(1)}, bf16[256,128]{1,0:T(8,128)(2,1)S(1)}) custom-call(f32[32,8,128]{2,1,0:T(8,128)S(1)} %get-tuple-element.73.r_new.refs_4_, f32[32,8,128]{2,1,0:T(8,128)S(1)} %get-tuple-element.74.w.w_in, ...), custom_call_target="tpu_custom_call" | custom-call | tf_op jit(solution)/shard_map/pallas_call | solution.py:457
  30.5 1.7 %collective-permute-start.8 = (bf16[256,128]{1,0:T(8,128)(2,1)S(1)}, bf16[256,128]{1,0:T(8,128)(2,1)S(1)}, u32[]{:S(2)}, u32[]{:S(2)}) collective-permute-start(bf16[256,128]{1,0:T(8,128)(2,1)S(1)} %get-tuple-element.82), channel_id=1, source_target_pairs={{0,3},{1,2},{2,1},{3,0},{4,7},{5,6},{6,5},{7,4},{8,11},{9,10},{10,... | collective-permute-start | bytes 196616 | tf_op jit(solution)/shard_map/ppermute | solution.py:414
  32.1 1.5 %collective-permute-start.9 = (bf16[256,128]{1,0:T(8,128)(2,1)S(1)}, bf16[256,128]{1,0:T(8,128)(2,1)S(1)}, u32[]{:S(2)}, u32[]{:S(2)}) collective-permute-start(bf16[256,128]{1,0:T(8,128)(2,1)S(1)} %get-tuple-element.83), channel_id=1, source_target_pairs={{0,4},{1,5},{2,6},{3,7},{4,0},{5,1},{6,2},{7,3},{8,12},{9,13},{10,... | collective-permute-start | bytes 196616 | tf_op jit(solution)/shard_map/ppermute | solution.py:414
  33.6 0.7 %collective-permute-start.10 = (bf16[256,128]{1,0:T(8,128)(2,1)S(1)}, bf16[256,128]{1,0:T(8,128)(2,1)S(1)}, u32[]{:S(2)}, u32[]{:S(2)}) collective-permute-start(bf16[256,128]{1,0:T(8,128)(2,1)S(1)} %get-tuple-element.84), channel_id=1, source_target_pairs={{0,1},{1,0},{2,3},{3,2},{4,8},{5,9},{6,10},{7,11},{8,4},{9,5},{10,... | collective-permute-start | bytes 196616 | tf_op jit(solution)/shard_map/ppermute | solution.py:414
  34.4 0.2 collective-permute-done.8.refs_0_
  34.6 2.3 %collective-permute-done.9.refs_1_ = bf16[256,128]{1,0:T(8,128)(2,1)S(1)} collective-permute-done((bf16[256,128]{1,0:T(8,128)(2,1)S(1)}, bf16[256,128]{1,0:T(8,128)(2,1)S(1)}, u32[]{:S(2)}, u32[]{:S(2)}) %collective-permute-start.9) | collective-permute-done | bytes 65568 | tf_op jit(solution)/shard_map/ppermute | solution.py:414
  36.9 1.8 %shard_map.197 = (f32[32,8,128]{2,1,0:T(8,128)S(1)}, bf16[128,128]{1,0:T(8,128)(2,1)S(1)}, bf16[128,128]{1,0:T(8,128)(2,1)S(1)}, bf16[128,128]{1,0:T(8,128)(2,1)S(1)}, bf16[128,128]{1,0:T(8,128)(2,1)S(1)}) custom-call(f32[32,8,128]{2,1,0:T(8,128)S(1)} %get-tuple-element.73.r_new.refs_4_, f32[32,8,128]{2,1,0:T(8,128)S(1)} %get-tuple-element.81.w_in, ...), custom_call_target="tpu_custom_call" | custom-call | tf_op jit(solution)/shard_map/pallas_call | solution.py:457
  38.7 0.1 collective-permute-start.12
  38.8 1.8 %collective-permute-start.13 = (bf16[128,128]{1,0:T(8,128)(2,1)S(1)}, bf16[128,128]{1,0:T(8,128)(2,1)S(1)}, u32[]{:S(2)}, u32[]{:S(2)}) collective-permute-start(bf16[128,128]{1,0:T(8,128)(2,1)S(1)} %get-tuple-element.88), channel_id=1, source_target_pairs={{0,4},{1,5},{2,6},{3,7},{4,0},{5,1},{6,2},{7,3},{8,12},{9,13},{10,... | collective-permute-start | bytes 98312 | tf_op jit(solution)/shard_map/ppermute | solution.py:414
  40.6 0.5 collective-permute-start.15
  41.1 1.0 %collective-permute-done.12.refs_0_ = bf16[128,128]{1,0:T(8,128)(2,1)S(1)} collective-permute-done((bf16[128,128]{1,0:T(8,128)(2,1)S(1)}, bf16[128,128]{1,0:T(8,128)(2,1)S(1)}, u32[]{:S(2)}, u32[]{:S(2)}) %collective-permute-start.12) | collective-permute-done | bytes 32800 | tf_op jit(solution)/shard_map/ppermute | solution.py:414
  42.1 0.7 collective-permute-done.13.refs_1_
  42.8 1.9 %shard_map.198 = (f32[32,8,128]{2,1,0:T(8,128)S(1)}, f32[32,8,128]{2,1,0:T(8,128)S(1)}, bf16[128,128]{1,0:T(8,128)(2,1)S(1)}, bf16[128,128]{1,0:T(8,128)(2,1)S(1...) custom-call(f32[32,8,128]{2,1,0:T(8,128)S(1)} %get-tuple-element.73.r_new.refs_4_, ...), custom_call_target="tpu_custom_call" | custom-call | tf_op jit(solution)/shard_map/pallas_call | solution.py:457
  44.7 0.5 collective-permute-start.16
  45.2 1.3 %collective-permute-start.17 = (bf16[128,128]{1,0:T(8,128)(2,1)S(1)}, bf16[128,128]{1,0:T(8,128)(2,1)S(1)}, u32[]{:S(2)}, u32[]{:S(2)}) collective-permute-start(bf16[128,128]{1,0:T(8,128)(2,1)S(1)} %get-tuple-element.94), channel_id=1, source_target_pairs={{0,4},{1,5},{2,6},{3,7},{4,0},{5,1},{6,2},{7,3},{8,12},{9,13},{10,... | collective-permute-start | bytes 98312 | tf_op jit(solution)/shard_map/ppermute | solution.py:414
  46.5 1.1 %collective-permute-start.18 = (bf16[128,128]{1,0:T(8,128)(2,1)S(1)}, bf16[128,128]{1,0:T(8,128)(2,1)S(1)}, u32[]{:S(2)}, u32[]{:S(2)}) collective-permute-start(bf16[128,128]{1,0:T(8,128)(2,1)S(1)} %get-tuple-element.95), channel_id=1, source_target_pairs={{0,1},{1,0},{2,3},{3,2},{4,8},{5,9},{6,10},{7,11},{8,4},{9,5},{10,... | collective-permute-start | bytes 98312 | tf_op jit(solution)/shard_map/ppermute | solution.py:414
  47.6 0.5 collective-permute-done.16.refs_0_
  48.2 1.3 %collective-permute-done.17.refs_1_ = bf16[128,128]{1,0:T(8,128)(2,1)S(1)} collective-permute-done((bf16[128,128]{1,0:T(8,128)(2,1)S(1)}, bf16[128,128]{1,0:T(8,128)(2,1)S(1)}, u32[]{:S(2)}, u32[]{:S(2)}) %collective-permute-start.17) | collective-permute-done | bytes 32800 | tf_op jit(solution)/shard_map/ppermute | solution.py:414
  49.4 1.8 %shard_map.199 = (f32[32,8,128]{2,1,0:T(8,128)S(1)}, bf16[128,128]{1,0:T(8,128)(2,1)S(1)}, bf16[128,128]{1,0:T(8,128)(2,1)S(1)}, bf16[128,128]{1,0:T(8,128)(2,1)S(1)}, bf16[128,128]{1,0:T(8,128)(2,1)S(1)}) custom-call(f32[32,8,128]{2,1,0:T(8,128)S(1)} %get-tuple-element.91.w, f32[32,8,128]{2,1,0:T(8,128)S(1)} %get-tuple-element.92.z_in, ...), custom_call_target="tpu_custom_call" | custom-call | tf_op jit(solution)/shard_map/pallas_call | solution.py:464
  51.3 0.2 collective-permute-start.20
  51.4 1.7 %collective-permute-start.21 = (bf16[128,128]{1,0:T(8,128)(2,1)S(1)}, bf16[128,128]{1,0:T(8,128)(2,1)S(1)}, u32[]{:S(2)}, u32[]{:S(2)}) collective-permute-start(bf16[128,128]{1,0:T(8,128)(2,1)S(1)} %get-tuple-element.99), channel_id=1, source_target_pairs={{0,4},{1,5},{2,6},{3,7},{4,0},{5,1},{6,2},{7,3},{8,12},{9,13},{10,... | collective-permute-start | bytes 98312 | tf_op jit(solution)/shard_map/ppermute | solution.py:414
  53.2 0.2 collective-permute-start.22
  53.3 0.3 collective-permute-start.23
  53.7 0.2 shard_map.200.refs_5_
  53.9 0.9 %collective-permute-done.20.refs_0_ = bf16[128,128]{1,0:T(8,128)(2,1)S(1)} collective-permute-done((bf16[128,128]{1,0:T(8,128)(2,1)S(1)}, bf16[128,128]{1,0:T(8,128)(2,1)S(1)}, u32[]{:S(2)}, u32[]{:S(2)}) %collective-permute-start.20) | collective-permute-done | bytes 32800 | tf_op jit(solution)/shard_map/ppermute | solution.py:414
  54.8 0.7 collective-permute-done.21.refs_1_
  55.5 1.7 %shard_map.201 = (f32[32,8,128]{2,1,0:T(8,128)S(1)}, bf16[128,128]{1,0:T(8,128)(2,1)S(1)}, bf16[128,128]{1,0:T(8,128)(2,1)S(1)}, bf16[128,128]{1,0:T(8,128)(2,1)...) custom-call(f32[32,8,128]{2,1,0:T(8,128)S(1)} %get-tuple-element.91.w, ...), custom_call_target="tpu_custom_call" | custom-call | tf_op jit(solution)/shard_map/pallas_call | solution.py:470
  57.2 4.6 %all-to-all-start.1 = ((f32[16,16,128]{2,1,0:T(8,128)}), f32[16,16,128]{2,1,0:T(8,128)S(1)}, u32[]{:S(2)}, u32[]{:S(2)}) async-start(f32[16,16,128]{2,1,0:T(8,128)} %get-tuple-element.103), calls=%async_computation.1 | async-start | bytes 262144 | tf_op jit(solution)/shard_map/all_to_all | solution.py:476
  61.8 1.7 %collective-permute-start.24 = (bf16[128,128]{1,0:T(8,128)(2,1)S(1)}, bf16[128,128]{1,0:T(8,128)(2,1)S(1)}, u32[]{:S(2)}, u32[]{:S(2)}) collective-permute-start(bf16[128,128]{1,0:T(8,128)(2,1)S(1)} %get-tuple-element.105), channel_id=1, source_target_pairs={{0,3},{1,2},{2,1},{3,0},{4,7},{5,6},{6,5},{7,4},{8,11},{9,10},{10,... | collective-permute-start | bytes 98312 | tf_op jit(solution)/shard_map/ppermute | solution.py:414
  63.5 1.5 %collective-permute-start.25 = (bf16[128,128]{1,0:T(8,128)(2,1)S(1)}, bf16[128,128]{1,0:T(8,128)(2,1)S(1)}, u32[]{:S(2)}, u32[]{:S(2)}) collective-permute-start(bf16[128,128]{1,0:T(8,128)(2,1)S(1)} %get-tuple-element.106), channel_id=1, source_target_pairs={{0,4},{1,5},{2,6},{3,7},{4,0},{5,1},{6,2},{7,3},{8,12},{9,13},{10,... | collective-permute-start | bytes 98312 | tf_op jit(solution)/shard_map/ppermute | solution.py:414
  65.0 0.1 collective-permute-start.26
  65.1 0.4 collective-permute-start.27
  65.5 2.0 %shard_map.202.off = bf16[32,9,128,128]{3,2,1,0:T(8,128)(2,1)S(1)} custom-call(bf16[32,9,128,128]{3,2,1,0:T(8,128)(2,1)} %off_hbm.5, s32[8,128]{1,0:T(8,128)S(4)} %get-tuple-element.71.tables, bf16[128,128]{1,0:T(8,128)(2,1)S(1)} %collective-permute-done.24.after.refs_0_), custom_call_target="tpu_custom_call" | custom-call | flops 100000000 | tf_op jit(solution)/shard_map/pallas_call | solution.py:478
  67.5 0.0 copy-start.3
  67.5 0.0 copy-start.4
  67.5 0.0 copy-start.9
  67.5 0.0 copy-start.10
  67.5 0.3 collective-permute-done.25.refs_1_
  67.8 1.7 %shard_map.203.z = f32[32,8,128]{2,1,0:T(8,128)S(1)} custom-call(f32[32,8,128]{2,1,0:T(8,128)S(1)} %get-tuple-element.91.w, f32[32,8,128]{2,1,0:T(8,128)S(1)} %get-tuple-element.104.z_in, bf16[32,9,128,128]{3,2,1,0:T(8,128)(2,1)S(1)} %shard_map.202.off, bf16[32,128,128]{2,1,0:T(8,128)(2,1)S(1)} %copy-done, f32[32,128]{1,0:T(8,128)S(1)} %get-tuple-element.69.straight, ...), custom_call_target="tpu_custom_call" | custom-call | tf_op jit(solution)/shard_map/pallas_call | solution.py:481
  69.6 0.5 all-to-all-done.1.sums
  70.1 1.4 %shard_map.204 = (f32[32,8,128]{2,1,0:T(8,128)}, f32[32,8,128]{2,1,0:T(8,128)}, f32[32,8,128]{2,1,0:T(8,128)}, f32[3,8]{1,0:T(4,128)}) custom-call(f32[16,16,128]{2,1,0:T(8,128)S(1)} %all-to-all-done.1.sums, f32[32,8,128]{2,1,0:T(8,128)S(1)} %shard_map.203.z, f32[32,8,128]{2,1,0:T(8,128)S(1)} %get-tuple-element.60.q.q_ref, f32[32,8,128]{2,1,0:T(8,128)S(1)} %copy-done.3, ...), custom_call_target="tpu_custom_call" | custom-call | tf_op jit(solution)/shard_map/pallas_call | solution.py:488
  (31 shorter events, 0.1 us)
Async XLA Ops:
  0.6 5.6 %copy-start.5 = (f32[32,128]{1,0:T(8,128)S(1)}, f32[32,128]{1,0:T(8,128)}, u32[]{:S(2)}) copy-start(f32[32,128]{1,0:T(8,128)} %diag_ref.1) | copy-start | bytes 49156
  0.6 5.6 %copy-start.6 = (f32[32,64]{1,0:T(8,128)S(1)}, f32[32,64]{1,0:T(8,128)}, u32[]{:S(2)}) copy-start(f32[32,64]{1,0:T(8,128)} %off_ref.1) | copy-start | bytes 24580
  0.7 5.6 %copy-start.7 = (s32[32,64]{1,0:T(8,128)S(1)}, s32[32,64]{1,0:T(8,128)}, u32[]{:S(2)}) copy-start(s32[32,64]{1,0:T(8,128)} %pairs_ref.1) | copy-start | bytes 24580
  1.7 6.6 %copy-start.1 = (bf16[32,128,128]{2,1,0:T(8,128)(2,1)S(1)}, bf16[32,128,128]{2,1,0:T(8,128)(2,1)}, u32[]{:S(2)}) copy-start(bf16[32,128,128]{2,1,0:T(8,128)(2,1)} %diag.1) | copy-start | bytes 3145732
  1.7 6.6 %collective-permute-start = (bf16[128,128]{1,0:T(8,128)(2,1)S(1)}, bf16[128,128]{1,0:T(8,128)(2,1)S(1)}, u32[]{:S(2)}, u32[]{:S(2)}) collective-permute-start(bf16[128,128]{1,0:T(8,128)(2,1)S(1)} %get-tuple-element.63), channel_id=1, source_target_pairs={{0,3},{1,2},{2,1},{3,0},{4,7},{5,6},{6,5},{7,4},{8,11},{9,10},{10,... | collective-permute-start | bytes 98312 | tf_op jit(solution)/shard_map/ppermute | solution.py:414
  4.1 4.2 %collective-permute-start.1 = (bf16[128,128]{1,0:T(8,128)(2,1)S(1)}, bf16[128,128]{1,0:T(8,128)(2,1)S(1)}, u32[]{:S(2)}, u32[]{:S(2)}) collective-permute-start(bf16[128,128]{1,0:T(8,128)(2,1)S(1)} %get-tuple-element.64), channel_id=1, source_target_pairs={{0,4},{1,5},{2,6},{3,7},{4,0},{5,1},{6,2},{7,3},{8,12},{9,13},{10,... | collective-permute-start | bytes 98312 | tf_op jit(solution)/shard_map/ppermute | solution.py:414
  5.7 2.6 %collective-permute-start.2 = (bf16[128,128]{1,0:T(8,128)(2,1)S(1)}, bf16[128,128]{1,0:T(8,128)(2,1)S(1)}, u32[]{:S(2)}, u32[]{:S(2)}) collective-permute-start(bf16[128,128]{1,0:T(8,128)(2,1)S(1)} %get-tuple-element.65), channel_id=1, source_target_pairs={{0,1},{1,0},{2,3},{3,2},{4,8},{5,9},{6,10},{7,11},{8,4},{9,5},{10,... | collective-permute-start | bytes 98312 | tf_op jit(solution)/shard_map/ppermute | solution.py:414
  6.1 2.2 %collective-permute-start.3 = (bf16[128,128]{1,0:T(8,128)(2,1)S(1)}, bf16[128,128]{1,0:T(8,128)(2,1)S(1)}, u32[]{:S(2)}, u32[]{:S(2)}) collective-permute-start(bf16[128,128]{1,0:T(8,128)(2,1)S(1)} %get-tuple-element.66), channel_id=1, source_target_pairs={{0,1},{1,0},{2,3},{3,2},{4,5},{5,4},{6,7},{7,6},{8,9},{9,8},{10,11... | collective-permute-start | bytes 98312 | tf_op jit(solution)/shard_map/ppermute | solution.py:414
  8.3 15.8 %copy-start = (bf16[32,128,128]{2,1,0:T(8,128)(2,1)S(1)}, bf16[32,128,128]{2,1,0:T(8,128)(2,1)}, u32[]{:S(2)}) copy-start(bf16[32,128,128]{2,1,0:T(8,128)(2,1)} %factor.13) | copy-start | bytes 3145732
  8.3 15.8 %copy-start.2 = (f32[32,8,128]{2,1,0:T(8,128)S(1)}, f32[32,8,128]{2,1,0:T(8,128)}, u32[]{:S(2)}) copy-start(f32[32,8,128]{2,1,0:T(8,128)} %r_ref.1) | copy-start | bytes 393220
  8.3 15.8 %copy-start.8 = (f32[8]{0:T(128)S(1)}, f32[8]{0:T(128)}, u32[]{:S(2)}) copy-start(f32[8]{0:T(128)} %rho.3) | copy-start | bytes 100
  25.4 3.5 %collective-permute-start.4 = (bf16[128,128]{1,0:T(8,128)(2,1)S(1)}, bf16[128,128]{1,0:T(8,128)(2,1)S(1)}, u32[]{:S(2)}, u32[]{:S(2)}) collective-permute-start(bf16[128,128]{1,0:T(8,128)(2,1)S(1)} %get-tuple-element.76), channel_id=1, source_target_pairs={{0,3},{1,2},{2,1},{3,0},{4,7},{5,6},{6,5},{7,4},{8,11},{9,10},{10,... | collective-permute-start | bytes 98312 | tf_op jit(solution)/shard_map/ppermute | solution.py:414
  25.4 4.0 %collective-permute-start.5 = (bf16[128,128]{1,0:T(8,128)(2,1)S(1)}, bf16[128,128]{1,0:T(8,128)(2,1)S(1)}, u32[]{:S(2)}, u32[]{:S(2)}) collective-permute-start(bf16[128,128]{1,0:T(8,128)(2,1)S(1)} %get-tuple-element.77), channel_id=1, source_target_pairs={{0,4},{1,5},{2,6},{3,7},{4,0},{5,1},{6,2},{7,3},{8,12},{9,13},{10,... | collective-permute-start | bytes 98312 | tf_op jit(solution)/shard_map/ppermute | solution.py:414
  25.9 3.5 %collective-permute-start.6 = (bf16[128,128]{1,0:T(8,128)(2,1)S(1)}, bf16[128,128]{1,0:T(8,128)(2,1)S(1)}, u32[]{:S(2)}, u32[]{:S(2)}) collective-permute-start(bf16[128,128]{1,0:T(8,128)(2,1)S(1)} %get-tuple-element.78), channel_id=1, source_target_pairs={{0,1},{1,0},{2,3},{3,2},{4,8},{5,9},{6,10},{7,11},{8,4},{9,5},{10,... | collective-permute-start | bytes 98312 | tf_op jit(solution)/shard_map/ppermute | solution.py:414
  26.1 3.4 %collective-permute-start.7 = (bf16[128,128]{1,0:T(8,128)(2,1)S(1)}, bf16[128,128]{1,0:T(8,128)(2,1)S(1)}, u32[]{:S(2)}, u32[]{:S(2)}) collective-permute-start(bf16[128,128]{1,0:T(8,128)(2,1)S(1)} %get-tuple-element.79), channel_id=1, source_target_pairs={{0,1},{1,0},{2,3},{3,2},{4,5},{5,4},{6,7},{7,6},{8,9},{9,8},{10,11... | collective-permute-start | bytes 98312 | tf_op jit(solution)/shard_map/ppermute | solution.py:414
  30.5 4.1 %collective-permute-start.8 = (bf16[256,128]{1,0:T(8,128)(2,1)S(1)}, bf16[256,128]{1,0:T(8,128)(2,1)S(1)}, u32[]{:S(2)}, u32[]{:S(2)}) collective-permute-start(bf16[256,128]{1,0:T(8,128)(2,1)S(1)} %get-tuple-element.82), channel_id=1, source_target_pairs={{0,3},{1,2},{2,1},{3,0},{4,7},{5,6},{6,5},{7,4},{8,11},{9,10},{10,... | collective-permute-start | bytes 196616 | tf_op jit(solution)/shard_map/ppermute | solution.py:414
  32.1 4.7 %collective-permute-start.9 = (bf16[256,128]{1,0:T(8,128)(2,1)S(1)}, bf16[256,128]{1,0:T(8,128)(2,1)S(1)}, u32[]{:S(2)}, u32[]{:S(2)}) collective-permute-start(bf16[256,128]{1,0:T(8,128)(2,1)S(1)} %get-tuple-element.83), channel_id=1, source_target_pairs={{0,4},{1,5},{2,6},{3,7},{4,0},{5,1},{6,2},{7,3},{8,12},{9,13},{10,... | collective-permute-start | bytes 196616 | tf_op jit(solution)/shard_map/ppermute | solution.py:414
  33.6 3.3 %collective-permute-start.10 = (bf16[256,128]{1,0:T(8,128)(2,1)S(1)}, bf16[256,128]{1,0:T(8,128)(2,1)S(1)}, u32[]{:S(2)}, u32[]{:S(2)}) collective-permute-start(bf16[256,128]{1,0:T(8,128)(2,1)S(1)} %get-tuple-element.84), channel_id=1, source_target_pairs={{0,1},{1,0},{2,3},{3,2},{4,8},{5,9},{6,10},{7,11},{8,4},{9,5},{10,... | collective-permute-start | bytes 196616 | tf_op jit(solution)/shard_map/ppermute | solution.py:414
  34.4 2.5 %collective-permute-start.11 = (bf16[256,128]{1,0:T(8,128)(2,1)S(1)}, bf16[256,128]{1,0:T(8,128)(2,1)S(1)}, u32[]{:S(2)}, u32[]{:S(2)}) collective-permute-start(bf16[256,128]{1,0:T(8,128)(2,1)S(1)} %get-tuple-element.85), channel_id=1, source_target_pairs={{0,1},{1,0},{2,3},{3,2},{4,5},{5,4},{6,7},{7,6},{8,9},{9,8},{10,11... | collective-permute-start | bytes 196616 | tf_op jit(solution)/shard_map/ppermute | solution.py:414
  38.7 3.4 %collective-permute-start.12 = (bf16[128,128]{1,0:T(8,128)(2,1)S(1)}, bf16[128,128]{1,0:T(8,128)(2,1)S(1)}, u32[]{:S(2)}, u32[]{:S(2)}) collective-permute-start(bf16[128,128]{1,0:T(8,128)(2,1)S(1)} %get-tuple-element.87), channel_id=1, source_target_pairs={{0,3},{1,2},{2,1},{3,0},{4,7},{5,6},{6,5},{7,4},{8,11},{9,10},{10,... | collective-permute-start | bytes 98312 | tf_op jit(solution)/shard_map/ppermute | solution.py:414
  38.8 4.0 %collective-permute-start.13 = (bf16[128,128]{1,0:T(8,128)(2,1)S(1)}, bf16[128,128]{1,0:T(8,128)(2,1)S(1)}, u32[]{:S(2)}, u32[]{:S(2)}) collective-permute-start(bf16[128,128]{1,0:T(8,128)(2,1)S(1)} %get-tuple-element.88), channel_id=1, source_target_pairs={{0,4},{1,5},{2,6},{3,7},{4,0},{5,1},{6,2},{7,3},{8,12},{9,13},{10,... | collective-permute-start | bytes 98312 | tf_op jit(solution)/shard_map/ppermute | solution.py:414
  40.6 2.2 %collective-permute-start.14 = (bf16[128,128]{1,0:T(8,128)(2,1)S(1)}, bf16[128,128]{1,0:T(8,128)(2,1)S(1)}, u32[]{:S(2)}, u32[]{:S(2)}) collective-permute-start(bf16[128,128]{1,0:T(8,128)(2,1)S(1)} %get-tuple-element.89), channel_id=1, source_target_pairs={{0,1},{1,0},{2,3},{3,2},{4,8},{5,9},{6,10},{7,11},{8,4},{9,5},{10,... | collective-permute-start | bytes 98312 | tf_op jit(solution)/shard_map/ppermute | solution.py:414
  40.6 2.2 %collective-permute-start.15 = (bf16[128,128]{1,0:T(8,128)(2,1)S(1)}, bf16[128,128]{1,0:T(8,128)(2,1)S(1)}, u32[]{:S(2)}, u32[]{:S(2)}) collective-permute-start(bf16[128,128]{1,0:T(8,128)(2,1)S(1)} %get-tuple-element.90), channel_id=1, source_target_pairs={{0,1},{1,0},{2,3},{3,2},{4,5},{5,4},{6,7},{7,6},{8,9},{9,8},{10,11... | collective-permute-start | bytes 98312 | tf_op jit(solution)/shard_map/ppermute | solution.py:414
  44.7 3.5 %collective-permute-start.16 = (bf16[128,128]{1,0:T(8,128)(2,1)S(1)}, bf16[128,128]{1,0:T(8,128)(2,1)S(1)}, u32[]{:S(2)}, u32[]{:S(2)}) collective-permute-start(bf16[128,128]{1,0:T(8,128)(2,1)S(1)} %get-tuple-element.93), channel_id=1, source_target_pairs={{0,3},{1,2},{2,1},{3,0},{4,7},{5,6},{6,5},{7,4},{8,11},{9,10},{10,... | collective-permute-start | bytes 98312 | tf_op jit(solution)/shard_map/ppermute | solution.py:414
  45.2 4.2 %collective-permute-start.17 = (bf16[128,128]{1,0:T(8,128)(2,1)S(1)}, bf16[128,128]{1,0:T(8,128)(2,1)S(1)}, u32[]{:S(2)}, u32[]{:S(2)}) collective-permute-start(bf16[128,128]{1,0:T(8,128)(2,1)S(1)} %get-tuple-element.94), channel_id=1, source_target_pairs={{0,4},{1,5},{2,6},{3,7},{4,0},{5,1},{6,2},{7,3},{8,12},{9,13},{10,... | collective-permute-start | bytes 98312 | tf_op jit(solution)/shard_map/ppermute | solution.py:414
  46.5 2.9 %collective-permute-start.18 = (bf16[128,128]{1,0:T(8,128)(2,1)S(1)}, bf16[128,128]{1,0:T(8,128)(2,1)S(1)}, u32[]{:S(2)}, u32[]{:S(2)}) collective-permute-start(bf16[128,128]{1,0:T(8,128)(2,1)S(1)} %get-tuple-element.95), channel_id=1, source_target_pairs={{0,1},{1,0},{2,3},{3,2},{4,8},{5,9},{6,10},{7,11},{8,4},{9,5},{10,... | collective-permute-start | bytes 98312 | tf_op jit(solution)/shard_map/ppermute | solution.py:414
  47.6 1.8 %collective-permute-start.19 = (bf16[128,128]{1,0:T(8,128)(2,1)S(1)}, bf16[128,128]{1,0:T(8,128)(2,1)S(1)}, u32[]{:S(2)}, u32[]{:S(2)}) collective-permute-start(bf16[128,128]{1,0:T(8,128)(2,1)S(1)} %get-tuple-element.96), channel_id=1, source_target_pairs={{0,1},{1,0},{2,3},{3,2},{4,5},{5,4},{6,7},{7,6},{8,9},{9,8},{10,11... | collective-permute-start | bytes 98312 | tf_op jit(solution)/shard_map/ppermute | solution.py:414
  51.3 3.6 %collective-permute-start.20 = (bf16[128,128]{1,0:T(8,128)(2,1)S(1)}, bf16[128,128]{1,0:T(8,128)(2,1)S(1)}, u32[]{:S(2)}, u32[]{:S(2)}) collective-permute-start(bf16[128,128]{1,0:T(8,128)(2,1)S(1)} %get-tuple-element.98), channel_id=1, source_target_pairs={{0,3},{1,2},{2,1},{3,0},{4,7},{5,6},{6,5},{7,4},{8,11},{9,10},{10,... | collective-permute-start | bytes 98312 | tf_op jit(solution)/shard_map/ppermute | solution.py:414
  51.4 4.0 %collective-permute-start.21 = (bf16[128,128]{1,0:T(8,128)(2,1)S(1)}, bf16[128,128]{1,0:T(8,128)(2,1)S(1)}, u32[]{:S(2)}, u32[]{:S(2)}) collective-permute-start(bf16[128,128]{1,0:T(8,128)(2,1)S(1)} %get-tuple-element.99), channel_id=1, source_target_pairs={{0,4},{1,5},{2,6},{3,7},{4,0},{5,1},{6,2},{7,3},{8,12},{9,13},{10,... | collective-permute-start | bytes 98312 | tf_op jit(solution)/shard_map/ppermute | solution.py:414
  53.2 2.3 %collective-permute-start.22 = (bf16[128,128]{1,0:T(8,128)(2,1)S(1)}, bf16[128,128]{1,0:T(8,128)(2,1)S(1)}, u32[]{:S(2)}, u32[]{:S(2)}) collective-permute-start(bf16[128,128]{1,0:T(8,128)(2,1)S(1)} %get-tuple-element.100), channel_id=1, source_target_pairs={{0,1},{1,0},{2,3},{3,2},{4,8},{5,9},{6,10},{7,11},{8,4},{9,5},{10,... | collective-permute-start | bytes 98312 | tf_op jit(solution)/shard_map/ppermute | solution.py:414
  53.3 2.2 %collective-permute-start.23 = (bf16[128,128]{1,0:T(8,128)(2,1)S(1)}, bf16[128,128]{1,0:T(8,128)(2,1)S(1)}, u32[]{:S(2)}, u32[]{:S(2)}) collective-permute-start(bf16[128,128]{1,0:T(8,128)(2,1)S(1)} %get-tuple-element.101), channel_id=1, source_target_pairs={{0,1},{1,0},{2,3},{3,2},{4,5},{5,4},{6,7},{7,6},{8,9},{9,8},{10,11... | collective-permute-start | bytes 98312 | tf_op jit(solution)/shard_map/ppermute | solution.py:414
  57.2 12.9 %all-to-all-start.1 = ((f32[16,16,128]{2,1,0:T(8,128)}), f32[16,16,128]{2,1,0:T(8,128)S(1)}, u32[]{:S(2)}, u32[]{:S(2)}) async-start(f32[16,16,128]{2,1,0:T(8,128)} %get-tuple-element.103), calls=%async_computation.1 | async-start | bytes 262144 | tf_op jit(solution)/shard_map/all_to_all | solution.py:476
  61.8 3.7 %collective-permute-start.24 = (bf16[128,128]{1,0:T(8,128)(2,1)S(1)}, bf16[128,128]{1,0:T(8,128)(2,1)S(1)}, u32[]{:S(2)}, u32[]{:S(2)}) collective-permute-start(bf16[128,128]{1,0:T(8,128)(2,1)S(1)} %get-tuple-element.105), channel_id=1, source_target_pairs={{0,3},{1,2},{2,1},{3,0},{4,7},{5,6},{6,5},{7,4},{8,11},{9,10},{10,... | collective-permute-start | bytes 98312 | tf_op jit(solution)/shard_map/ppermute | solution.py:414
  63.5 4.3 %collective-permute-start.25 = (bf16[128,128]{1,0:T(8,128)(2,1)S(1)}, bf16[128,128]{1,0:T(8,128)(2,1)S(1)}, u32[]{:S(2)}, u32[]{:S(2)}) collective-permute-start(bf16[128,128]{1,0:T(8,128)(2,1)S(1)} %get-tuple-element.106), channel_id=1, source_target_pairs={{0,4},{1,5},{2,6},{3,7},{4,0},{5,1},{6,2},{7,3},{8,12},{9,13},{10,... | collective-permute-start | bytes 98312 | tf_op jit(solution)/shard_map/ppermute | solution.py:414
  65.0 2.8 %collective-permute-start.26 = (bf16[128,128]{1,0:T(8,128)(2,1)S(1)}, bf16[128,128]{1,0:T(8,128)(2,1)S(1)}, u32[]{:S(2)}, u32[]{:S(2)}) collective-permute-start(bf16[128,128]{1,0:T(8,128)(2,1)S(1)} %get-tuple-element.107), channel_id=1, source_target_pairs={{0,1},{1,0},{2,3},{3,2},{4,8},{5,9},{6,10},{7,11},{8,4},{9,5},{10,... | collective-permute-start | bytes 98312 | tf_op jit(solution)/shard_map/ppermute | solution.py:414
  65.1 2.8 %collective-permute-start.27 = (bf16[128,128]{1,0:T(8,128)(2,1)S(1)}, bf16[128,128]{1,0:T(8,128)(2,1)S(1)}, u32[]{:S(2)}, u32[]{:S(2)}) collective-permute-start(bf16[128,128]{1,0:T(8,128)(2,1)S(1)} %get-tuple-element.108), channel_id=1, source_target_pairs={{0,1},{1,0},{2,3},{3,2},{4,5},{5,4},{6,7},{7,6},{8,9},{9,8},{10,11... | collective-permute-start | bytes 98312 | tf_op jit(solution)/shard_map/ppermute | solution.py:414
  67.5 2.7 %copy-start.3 = (f32[32,8,128]{2,1,0:T(8,128)S(1)}, f32[32,8,128]{2,1,0:T(8,128)}, u32[]{:S(2)}) copy-start(f32[32,8,128]{2,1,0:T(8,128)} %x_ref.1) | copy-start | bytes 393220
  67.5 2.7 %copy-start.4 = (f32[32,8,128]{2,1,0:T(8,128)S(1)}, f32[32,8,128]{2,1,0:T(8,128)}, u32[]{:S(2)}) copy-start(f32[32,8,128]{2,1,0:T(8,128)} %d_ref.1) | copy-start | bytes 393220
  67.5 2.6 %copy-start.9 = (f32[8]{0:T(128)S(1)}, f32[8]{0:T(128)}, u32[]{:S(2)}) copy-start(f32[8]{0:T(128)} %tau.1) | copy-start | bytes 100
  67.5 2.6 %copy-start.10 = (f32[8]{0:T(128)S(1)}, f32[8]{0:T(128)}, u32[]{:S(2)}) copy-start(f32[8]{0:T(128)} %theta_in.1) | copy-start | bytes 100

commit v6 on v5

--- a/solution.py
+++ b/solution.py
@@ -14,10 +14,11 @@
 HBM = pltpu.HBM
 SIDE = 4
 ORDER = (1, 2, 3, 0, 4, 5)
-COUPLE = (8, 4)
+COUPLE = (8, 4, 2)
 SOLVE = (16,)
+LATE = 4
 PART = 4
-PARTS = (0, 12, 16, 24, 32)
+PARTS = (0, 16, 24, 32)
 
 
 def swap_pairs(axis, stride, extent, phase, tiles):
@@ -59,21 +60,21 @@
             out[pl.ds(slot * 8, 16), :] = jnp.concatenate(two, axis=0).astype(BF16)
 
 
-def extend(swaps, state, arrived, extended):
-    extended[pl.ds(0, 32)] = state[...].astype(BF16).astype(F32)
-    zeros = jnp.zeros((16, 8, 128), F32)
-    reached = set()
+def own_blocks(state, extended):
+    extended[pl.ds(0, 32)] = state[...].reshape(256, 128).astype(BF16).astype(F32).reshape(32, 8, 128)
+
+
+def face_blocks(swaps, arrived, extended):
     for (axis, phase, extent, _), piece in zip(swaps, arrived):
         up, real = partner(axis, phase, extent)
         value = piece[pl.ds(0, 128), :].astype(F32).reshape(16, 8, 128)
-        extended[pl.ds(32 + (2 * axis + up) * 16, 16)] = jnp.where(real, value, zeros)
-        reached.add((axis, phase))
-    for axis in range(3):
-        if (axis, 0) not in reached:
-            extended[pl.ds(32 + axis * 32, 32)] = jnp.zeros((32, 8, 128), F32)
-        elif (axis, 1) not in reached:
-            up, _ = partner(axis, 1, 2)
-            extended[pl.ds(32 + (2 * axis + up) * 16, 16)] = zeros
+        extended[pl.ds(32 + (2 * axis + up) * 16, 16)] = jnp.where(real, value, 0.0)
+
+
+def extend(swaps, state, arrived, extended):
+    own_blocks(state, extended)
+    extended[pl.ds(32, 96)] = jnp.zeros((96, 8, 128), F32)
+    face_blocks(swaps, arrived, extended)
 
 
 def dot_t(left, right):
@@ -133,17 +134,26 @@
         done = done + groups * size
 
 
-def first_kernel(swaps, q_hbm, faces_hbm, q, faces, *refs):
-    sent, sems = refs[:-1], refs[-1]
+def first_kernel(swaps, q_hbm, faces_hbm, colours_hbm, q, faces, *refs):
+    sent, (colours, sems) = refs[:-2], refs[-2:]
     copies = [
         pltpu.make_async_copy(faces_hbm, faces, sems.at[0]),
         pltpu.make_async_copy(q_hbm, q, sems.at[1]),
+        pltpu.make_async_copy(colours_hbm, colours, sems.at[2]),
     ]
     for copy in copies:
         copy.start()
     for copy in copies:
         copy.wait()
     send_faces(swaps, q, faces, sent)
+    lane = lax.broadcasted_iota(jnp.int32, (16, 128), 1)
+    for (axis, phase, extent, _), out in zip(swaps, sent):
+        up, _ = partner(axis, phase, extent)
+        face = 2 * axis + 1 - up
+        listed = jnp.zeros((16, 128), jnp.int32)
+        for slot in range(16):
+            listed = jnp.where(lane == slot, colours[faces[face, 0, slot]], listed)
+        out[pl.ds(128, 16), :] = listed.astype(F32).astype(BF16)
 
 
 def setup_kernel(
@@ -183,12 +193,19 @@
 
 def image_kernel(swaps, tiles, q, diag, off_hbm, off_in, columns, *refs):
     n = len(swaps)
-    arrived, (off, image, partial, extended, sems) = refs[:n], refs[n:]
+    arrived, (off, image, partial, remote, extended, listed, sems) = refs[:n], refs[n:]
     loads = [None]
     for start, end in zip(PARTS[1:], PARTS[2:]):
         rows = pl.ds(start, end - start)
         loads.append(pltpu.make_async_copy(off_hbm.at[rows], off.at[rows], sems.at[len(loads) - 1]))
         loads[-1].start()
+    listed[...] = jnp.full((8, 128), -1, jnp.int32)
+    for (axis, phase, extent, _), piece in zip(swaps, arrived):
+        up, real = partner(axis, phase, extent)
+        found = piece[pl.ds(128, 16), :].astype(F32)[:1].astype(jnp.int32)
+        listed[pl.ds(2 * axis + up, 1), :] = jnp.where(real, found, -1)
+    colours = pltpu.make_async_copy(listed, remote, sems.at[len(loads) - 1])
+    colours.start()
     extend(swaps, q, arrived, extended)
 
     total = jnp.zeros((8, 128), F32)
@@ -202,6 +219,7 @@
             total = total + q[b] * value
     for tile in range(tiles):
         partial[tile] = total
+    colours.wait()
 
 
 def column_of(values):
@@ -272,24 +290,66 @@
             total[block] = total[block] + value[slot]
 
 
-def forward_kernel(swaps, colour, r_new, w_in, off, factor, straight, crossed, columns, tables, faces, *refs):
+def early_kernel(colour, wanted, *refs):
+    state, off, columns, tables, remote, extended, rest, late = refs[-8:]
+    if len(refs) == 8:
+        extended[pl.ds(32, 96)] = jnp.zeros((96, 8, 128), F32)
+    own_blocks(state, extended)
+
+    def couple(blocks):
+        for b, value in zip(blocks, [coupled(b, extended, off, columns) for b in blocks]):
+            rest[b] = value
+
+    for_colour(colour, tables, COUPLE, couple)
+
+    def note(place, found):
+        block = tables[colour, place]
+        for k in range(9):
+            column = columns[k, block]
+            slot = jnp.maximum(column - 32, 0)
+            hit = (column >= 32) & (remote[slot >> 4, slot & 15] == wanted)
+            late[found >> 7, found & 127] = block * 16 + k
+            found = found + jnp.where(hit, 1, 0)
+        return found
+
+    found = lax.fori_loop(0, tables[4, colour], note, jnp.int32(0))
+    for j in range(LATE):
+        late[(found + j) >> 7, (found + j) & 127] = 0
+    late[3, 0] = found
+
+
+def couple_late(swaps, arrived, extended, rest, off, columns, late):
+    face_blocks(swaps, arrived, extended)
+    found = late[3, 0]
+
+    def step(group, carry):
+        products = []
+        for j in range(LATE):
+            place = group * LATE + j
+            code = late[place >> 7, place & 127]
+            block, k = code >> 4, code & 15
+            vector = jnp.where(place < found, extended[columns[k, block]], 0.0)
+            products.append((block, dot_t(vector.astype(BF16), off[block, k])))
+        for block, product in products:
+            rest[block] = rest[block] + product
+        return carry
+
+    lax.fori_loop(0, (found + LATE - 1) // LATE, step, 0)
+
+
+def forward_kernel(swaps, colour, _, __, r_new, w_in, off, factor, straight, crossed, columns, tables, faces, late, *refs):
     n = len(swaps)
-    arrived, others, (extended, rest) = refs[:n], refs[n:-2], refs[-2:]
+    arrived, others = refs[:n], refs[n:]
     if colour == 1:
         adjoint, others = others[0], others[1:]
-    w, sent = others[0], others[1:]
+    extended, rest, w, sent = others[0], others[1], others[2], others[3:]
     w[...] = w_in[...]
-    extend(swaps, w_in, arrived, extended)
-
-    def couple(blocks):
-        for b, value in zip(blocks, [coupled(b, extended, off, columns) for b in blocks]):
-            rest[b] = r_new[b] - value
+    couple_late(swaps, arrived, extended, rest, off, columns, late)
 
     def solve(blocks):
-        for b, value in zip(blocks, solved(blocks, [rest[b] for b in blocks], factor, straight, crossed)):
+        for b, value in zip(blocks, solved(blocks, [r_new[b] - rest[b] for b in blocks], factor, straight, crossed)):
             w[b] = value
 
-    for_colour(colour, tables, COUPLE, couple)
     for_colour(colour, tables, SOLVE, solve)
     if colour == 3:
         z = sent[0]
@@ -310,13 +370,38 @@
             out[pl.ds(128, 128), :] = value.reshape(128, 128).astype(BF16)
 
 
-def backward_kernel(swaps, tiles, colour, w, z_in, off, factor, straight, crossed, columns, tables, faces, *refs):
+def backward_kernel(swaps, tiles, colour, _, __, w, z_in, off, factor, straight, crossed, columns, tables, faces, late, *refs):
     n = len(swaps)
-    arrived, others, (extended, rest) = refs[:n], refs[n:-2], refs[-2:]
+    arrived, others = refs[:n], refs[n:]
     if colour == 1:
         r_new, total, terms, partial = others[0], others[1], others[2], others[-1]
         others = others[3:-1]
-    z, sent = others[0], others[1:]
+    extended, rest, z, sent = others[0], others[1], others[2], others[3:]
+    z[...] = z_in[...]
+    couple_late(swaps, arrived, extended, rest, off, columns, late)
+
+    def solve(blocks):
+        for b, value in zip(blocks, solved(blocks, [rest[b] for b in blocks], factor, straight, crossed)):
+            z[b] = w[b] - value
+
+    for_colour(colour, tables, SOLVE, solve)
+    if colour == 1:
+        rho = terms[pl.ds(0, 8), :]
+        for b in range(0, 32, 2):
+            both = jnp.concatenate([z[b], z[b + 1]], axis=0)
+            rounded = both.astype(BF16).astype(F32)
+            part = jnp.concatenate([r_new[b], r_new[b + 1]], axis=0) * both
+            part = part - jnp.concatenate([total[b], total[b + 1]], axis=0) * rounded
+            rho = rho + part[:8] + part[8:]
+        both = jnp.concatenate([rho, terms[pl.ds(8, 8), :]], axis=0)
+        for tile in range(tiles):
+            partial[tile] = both
+    send_faces(swaps, z, faces, sent)
+
+
+def final_kernel(swaps, w, z_in, off, factor, straight, crossed, columns, tables, faces, *refs):
+    n = len(swaps)
+    arrived, (z, extended, rest) = refs[:n], refs[n:]
     z[...] = z_in[...]
     extend(swaps, z_in, arrived, extended)
 
@@ -328,16 +413,8 @@
         for b, value in zip(blocks, solved(blocks, [rest[b] for b in blocks], factor, straight, crossed)):
             z[b] = w[b] - value
 
-    for_colour(colour, tables, COUPLE, couple)
-    for_colour(colour, tables, SOLVE, solve)
-    if colour == 1:
-        new = z[...]
-        rho = terms[pl.ds(0, 8), :] + jnp.sum(r_new[...] * new - total[...] * new.astype(BF16).astype(F32), axis=0)
-        both = jnp.concatenate([rho, terms[pl.ds(8, 8), :]], axis=0)
-        for tile in range(tiles):
-            partial[tile] = both
-    if colour > 0:
-        send_faces(swaps, z, faces, sent)
+    for_colour(0, tables, COUPLE, couple)
+    for_colour(0, tables, SOLVE, solve)
 
 
 def last_kernel(count, sums, z, q_ref, x_ref, d_ref, alpha, rho, tau, theta_in, x_new, q_new, d_new, scalars):
@@ -415,25 +492,25 @@
 
     q, faces, *sent = call(
         functools.partial(first_kernel, swaps),
-        [kept, SMEM((6, 1, 16), jnp.int32)] + pieces,
-        [HBM, HBM],
-        [pltpu.SemaphoreType.DMA((2,))],
+        [kept, SMEM((6, 1, 16), jnp.int32)] + [vec(144, 128, dtype=BF16)] * n,
+        [HBM, HBM, HBM],
+        [SMEM((32,), jnp.int32), pltpu.SemaphoreType.DMA((3,))],
         cost=10**10,
-    )(in_hbm(q_vec), in_hbm(face_lists.transpose(1, 0, 2)))
+    )(in_hbm(q_vec), in_hbm(face_lists.transpose(1, 0, 2)), in_hbm(colours))
     arrived = exchange(sent)
     off, columns, tables, straight, crossed = call(
         setup_kernel,
         [off_kept, SMEM((9, 32), jnp.int32), SMEM((8, 128), jnp.int32), vec(32, 128), vec(32, 128)],
         [HBM, HBM, HBM, VMEM, VMEM, VMEM],
         [SMEM((32,), jnp.int32), pltpu.SemaphoreType.DMA((3,))],
-    )(in_hbm(off_blocks), in_hbm(columns.T), in_hbm(colours), pivot_diag, pivot_off, pivot_pairs)
-    off, image, partial = call(
+    )(off_blocks, in_hbm(columns.T), in_hbm(colours), pivot_diag, pivot_off, pivot_pairs)
+    off, image, partial, remote = call(
         functools.partial(image_kernel, swaps, tiles),
-        [off_kept, kept, vec(tiles, 8, 128)],
+        [off_kept, kept, vec(tiles, 8, 128), SMEM((8, 128), jnp.int32)],
         [VMEM, VMEM, HBM, VMEM, SMEM] + [VMEM] * n,
-        [scratch[0], pltpu.SemaphoreType.DMA((4,))],
+        [scratch[0], VMEM((8, 128), jnp.int32), pltpu.SemaphoreType.DMA((4,))],
         aliases={3: 0},
-    )(q, diag_blocks, in_hbm(off_blocks), off, columns, *arrived)
+    )(q, diag_blocks, off_blocks, off, columns, *arrived)
     sums = lax.all_to_all(partial, "gx", 0, 0, tiled=True)
     r_new, w, alpha, *sent = call(
         functools.partial(start_kernel, swaps, count),
@@ -448,38 +525,56 @@
         [VMEM] * 3 + [SMEM] * 2,
         cost=10**8,
     )(r_new, w, off, columns, tables)
+    long = [VMEM((128, 8, 128), F32), kept]
+
+    def early(colour, wanted, state, extended):
+        given = [] if extended is None else [extended]
+        return call(
+            functools.partial(early_kernel, colour, wanted),
+            long + [SMEM((4, 128), jnp.int32)],
+            [VMEM] * (len(given) + 2) + [SMEM] * 3,
+            cost=10**8,
+            aliases={0: 0} if given else None,
+        )(*given, state, off, columns, tables, remote)
+
+    extended = None
     for colour in (1, 2, 3):
         arrived = exchange(sent)
+        extended, rest, late = early(colour, colour - 1, w, extended)
         if colour == 2:
             total = call(functools.partial(gather_kernel, swaps), [kept], [VMEM, SMEM] + [VMEM] * n, cost=10**8)(
                 adjoint, faces, *arrived
             )[0]
-        w, *sent = call(
+        extended, _, w, *sent = call(
             functools.partial(forward_kernel, swaps, colour),
-            [kept] * (2 if colour == 3 else 1) + ([vec(256, 128, dtype=BF16)] * n if colour == 1 else pieces),
-            [VMEM] * 2 + fixed_places + [VMEM] * (n + 1 if colour == 1 else n),
-            scratch,
-        )(r_new, w, *fixed, *arrived, *([adjoint] if colour == 1 else []))
+            long + [kept] * (2 if colour == 3 else 1) + ([vec(256, 128, dtype=BF16)] * n if colour == 1 else pieces),
+            [VMEM] * 4 + fixed_places + [SMEM] + [VMEM] * (n + 1 if colour == 1 else n),
+            aliases={0: 0, 1: 1},
+        )(extended, rest, r_new, w, *fixed, late, *arrived, *([adjoint] if colour == 1 else []))
     z, *sent = sent
-    z, *sent = call(
+    arrived = exchange(sent)
+    extended, rest, late = early(2, 3, z, None)
+    extended, _, z, *sent = call(
         functools.partial(backward_kernel, swaps, tiles, 2),
-        [kept] + pieces,
-        [VMEM] * 2 + fixed_places + [VMEM] * n,
-        scratch,
-    )(w, z, *fixed, *exchange(sent))
-    z, *sent, partial = call(
+        long + [kept] + pieces,
+        [VMEM] * 4 + fixed_places + [SMEM] + [VMEM] * n,
+        aliases={0: 0, 1: 1},
+    )(extended, rest, w, z, *fixed, late, *arrived)
+    arrived = exchange(sent)
+    extended, rest, late = early(1, 2, z, extended)
+    _, _, z, *sent, partial = call(
         functools.partial(backward_kernel, swaps, tiles, 1),
-        [kept] + pieces + [vec(tiles, 16, 128)],
-        [VMEM] * 2 + fixed_places + [VMEM] * (n + 3),
-        scratch,
-    )(w, z, *fixed, *exchange(sent), r_new, total, terms)
+        long + [kept] + pieces + [vec(tiles, 16, 128)],
+        [VMEM] * 4 + fixed_places + [SMEM] + [VMEM] * (n + 3),
+        aliases={0: 0, 1: 1},
+    )(extended, rest, w, z, *fixed, late, *arrived, r_new, total, terms)
     sums = lax.all_to_all(partial, "gx", 0, 0, tiled=True)
     arrived = exchange(sent)
     off = call(load_kernel, [off_kept], [HBM, SMEM, VMEM], [pltpu.SemaphoreType.DMA((32,))], cost=10**8)(
         in_hbm(off_blocks), tables, arrived[0]
     )[0]
     z = call(
-        functools.partial(backward_kernel, swaps, tiles, 0),
+        functools.partial(final_kernel, swaps),
         [kept],
         [VMEM] * 2 + fixed_places + [VMEM] * n,
         scratch,

time: 72.2 us -> 71.4 us (0.989)
  the two profiles are of different devices: /device:TPU:0 before, /device:TPU:20 now
where the time goes in v6:
time: 71.4 us; the launch traced here: 70.9 us
  Pallas kernels  27.4 us (38%)
  starting transfers between devices  22 us (31%)
  waiting for transfers between devices  12.1 us (17%)
  blocking collectives  8.37 us (12%)
  between operations  0.96 us (1%)
    ppermute x28, starting transfers between devices, exchange(): lax.ppermute(piece, 'gx', swap[-1])  15.7 us
    ppermute x28, waiting for transfers between devices, exchange(): lax.ppermute(piece, 'gx', swap[-1])  12.1 us
    all_to_all x1, blocking collectives, per_device(): sums = lax.all_to_all(partial, 'gx', 0, 0, tiled=True)  8.37 us
    pallas_call x5, Pallas kernels, early(): call(functools.partial(early_kernel, colour, wanted), long + [SMEM((4, 12...  7.75 us
    all_to_all x1, starting transfers between devices, per_device(): sums = lax.all_to_all(partial, 'gx', 0, 0, tiled=True)  6.28 us
    pallas_call x1, Pallas kernels, per_device(): call(functools.partial(image_kernel, swaps, tiles), [off_kept, kept, vec(...  3.46 us
    pallas_call x3, Pallas kernels, per_device(): call(functools.partial(forward_kernel, swaps, colour), long + [kept] * (2...  2.73 us
    pallas_call x1, Pallas kernels, per_device(): call(load_kernel, [off_kept], [HBM, SMEM, VMEM], [pltpu.SemaphoreType.DMA...  2.13 us
  transfers between devices with their start and end apart: 29, of which 13 were waited for; matrix products, arithmetic and copies ran while one was open for 0% of the time, Pallas kernels for 21%

profile of v6, /device:TPU:20, one launch (start us, length us, event | category | flops | bytes accessed | tf_op | source)
XLA Modules:
  0.0 70.9 jit_solution(16139381820507432549)
XLA Ops:
  0.6 0.0 copy-start
  0.7 1.2 %shard_map.191 = (f32[32,8,128]{2,1,0:T(8,128)S(1)}, s32[6,1,16]{2,1,0:T(1,128)S(4)}, bf16[144,128]{1,0:T(8,128)(2,1)S(1)}, bf16[144,128]{1,0:T(8,128)(2,1)S(1)}...) custom-call(f32[32,8,128]{2,1,0:T(8,128)} %q_hbm.1, s32[6,1,16]{2,1,0:T(1,128)} %bitcast.3, s32[32]{0:T(128)} %colours_hbm.3), custom_call_target="tpu_custom_call" | custom-call | flops 10000000000 | tf_op jit(solution)/shard_map/pallas_call | solution.py:493
  1.9 0.0 copy-start.2
  1.9 1.0 %collective-permute-start = (bf16[144,128]{1,0:T(8,128)(2,1)S(1)}, bf16[144,128]{1,0:T(8,128)(2,1)S(1)}, u32[]{:S(2)}, u32[]{:S(2)}) collective-permute-start(bf16[144,128]{1,0:T(8,128)(2,1)S(1)} %get-tuple-element.82), channel_id=1, source_target_pairs={{0,3},{1,2},{2,1},{3,0},{4,7},{5,6},{6,5},{7,4},{8,11},{9,10},{10,... | collective-permute-start | bytes 110600 | tf_op jit(solution)/shard_map/ppermute | solution.py:491
  2.9 1.6 %collective-permute-start.1 = (bf16[144,128]{1,0:T(8,128)(2,1)S(1)}, bf16[144,128]{1,0:T(8,128)(2,1)S(1)}, u32[]{:S(2)}, u32[]{:S(2)}) collective-permute-start(bf16[144,128]{1,0:T(8,128)(2,1)S(1)} %get-tuple-element.83), channel_id=1, source_target_pairs={{0,4},{1,5},{2,6},{3,7},{4,0},{5,1},{6,2},{7,3},{8,12},{9,13},{10,... | collective-permute-start | bytes 110600 | tf_op jit(solution)/shard_map/ppermute | solution.py:491
  4.5 0.4 collective-permute-start.3
  4.9 1.2 %shard_map.192 = (bf16[32,9,128,128]{3,2,1,0:T(8,128)(2,1)S(1)}, s32[9,32]{1,0:T(8,128)S(4)}, s32[8,128]{1,0:T(8,128)S(4)}, f32[32,128]{1,0:T(8,128)S(1)}, f32[32,128]{1,0:T(8,128)S(1)}) custom-call(bf16[32,9,128,128]{3,2,1,0:T(8,128)(2,1)S(1)} %copy-done, s32[9,32]{1,0:T(8,128)} %bitcast.2, s32[32]{0:T(128)} %colours_hbm.3, f32[32,128]{1,0:T(8,128)S(1)} %copy-done.6, ...), custom_call_target="tpu_custom_call" | custom-call | tf_op jit(solution)/shard_map/pallas_call | solution.py:501
  6.2 0.8 %collective-permute-done.1.refs_1_ = bf16[144,128]{1,0:T(8,128)(2,1)S(1)} collective-permute-done((bf16[144,128]{1,0:T(8,128)(2,1)S(1)}, bf16[144,128]{1,0:T(8,128)(2,1)S(1)}, u32[]{:S(2)}, u32[]{:S(2)}) %collective-permute-start.1) | collective-permute-done | bytes 36896 | tf_op jit(solution)/shard_map/ppermute | solution.py:491
  7.0 1.5 %collective-permute-done.2.refs_2_ = bf16[144,128]{1,0:T(8,128)(2,1)S(1)} collective-permute-done((bf16[144,128]{1,0:T(8,128)(2,1)S(1)}, bf16[144,128]{1,0:T(8,128)(2,1)S(1)}, u32[]{:S(2)}, u32[]{:S(2)}) %collective-permute-start.2) | collective-permute-done | bytes 36896 | tf_op jit(solution)/shard_map/ppermute | solution.py:491
  8.5 0.0 copy-start.3
  8.5 0.0 copy-start.9
  8.5 3.5 %shard_map.193 = (bf16[32,9,128,128]{3,2,1,0:T(8,128)(2,1)S(1)}, f32[32,8,128]{2,1,0:T(8,128)S(1)}, f32[16,8,128]{2,1,0:T(8,128)S(1)}, s32[8,128]{1,0:T(8,128)S(4)}) custom-call(f32[32,8,128]{2,1,0:T(8,128)S(1)} %get-tuple-element.79.q.q_ref, bf16[32,128,128]{2,1,0:T(8,128)(2,1)S(1)} %copy-done.2, ...), custom_call_target="tpu_custom_call", output_to_operand_aliasing={{0}: (3, {})} | custom-call | tf_op jit(solution)/shard_map/pallas_call | solution.py:507
  12.0 8.4 %all_to_all.10.sums = f32[16,8,128]{2,1,0:T(8,128)S(1)} all-to-all(f32[16,8,128]{2,1,0:T(8,128)S(1)} %get-tuple-element.86), channel_id=1, replica_groups=mesh['groups'=2,'gx'=16] {'gx'}, dimensions={0} | all-to-all | bytes 131072 | tf_op jit(solution)/shard_map/all_to_all | solution.py:514
  20.4 1.2 %shard_map.194 = (f32[32,8,128]{2,1,0:T(8,128)S(1)}, f32[32,8,128]{2,1,0:T(8,128)S(1)}, f32[8,128]{1,0:T(8,128)S(1)}, bf16[128,128]{1,0:T(8,128)(2,1)S(1)}, bf16...) custom-call(f32[16,8,128]{2,1,0:T(8,128)S(1)} %all_to_all.10.sums, ...), custom_call_target="tpu_custom_call" | custom-call | tf_op jit(solution)/shard_map/pallas_call | solution.py:515
  21.5 0.4 collective-permute-start.4
  22.0 0.9 %collective-permute-start.5 = (bf16[128,128]{1,0:T(8,128)(2,1)S(1)}, bf16[128,128]{1,0:T(8,128)(2,1)S(1)}, u32[]{:S(2)}, u32[]{:S(2)}) collective-permute-start(bf16[128,128]{1,0:T(8,128)(2,1)S(1)} %get-tuple-element.100), channel_id=1, source_target_pairs={{0,4},{1,5},{2,6},{3,7},{4,0},{5,1},{6,2},{7,3},{8,12},{9,13},{10,... | collective-permute-start | bytes 98312 | tf_op jit(solution)/shard_map/ppermute | solution.py:491
  22.9 2.1 %collective-permute-start.6 = (bf16[128,128]{1,0:T(8,128)(2,1)S(1)}, bf16[128,128]{1,0:T(8,128)(2,1)S(1)}, u32[]{:S(2)}, u32[]{:S(2)}) collective-permute-start(bf16[128,128]{1,0:T(8,128)(2,1)S(1)} %get-tuple-element.101), channel_id=1, source_target_pairs={{0,1},{1,0},{2,3},{3,2},{4,8},{5,9},{6,10},{7,11},{8,4},{9,5},{10,... | collective-permute-start | bytes 98312 | tf_op jit(solution)/shard_map/ppermute | solution.py:491
  25.0 2.2 %shard_map.195 = (f32[128,8,128]{2,1,0:T(8,128)S(1)}, f32[32,8,128]{2,1,0:T(8,128)S(1)}, s32[4,128]{1,0:T(4,128)S(4)}) custom-call(f32[32,8,128]{2,1,0:T(8,128)S(1)} %get-tuple-element.92.refs_0_.w.w_in, bf16[32,9,128,128]{3,2,1,0:T(8,128)(2,1)S(1)} %get-tuple-element.93.refs_1_.off.refs_2_, s32[9,32]{1,0:T(8,128)S(4)} %get-tuple-element.81.columns.refs_2_.refs_3_, ...), custom_call_target="tpu_custom_call" | custom-call | flops 100000000 | tf_op jit(solution)/shard_map/pallas_call | solution.py:532
  27.2 1.6 %shard_map.196 = (f32[128,8,128]{2,1,0:T(8,128)S(1)}, f32[16,128]{1,0:T(8,128)S(1)}, f32[32,8,128]{2,1,0:T(8,128)}) custom-call(f32[32,8,128]{2,1,0:T(8,128)S(1)} %get-tuple-element.97.r_new.refs_4_, f32[32,8,128]{2,1,0:T(8,128)S(1)} %get-tuple-element.92.refs_0_.w.w_in, bf16[32,9,128,128]{3,2,1,0:T(8,128)(2,1)S(1)} %get-tuple-element.93.refs_1_.off.refs_2_, ...), custom_call_target="tpu_custom_call" | custom-call | flops 100000000 | tf_op jit(solution)/shard_map/pallas_call | solution.py:522
  28.8 0.8 %shard_map.197 = (f32[128,8,128]{2,1,0:T(8,128)S(1)}, f32[32,8,128]{2,1,0:T(8,128)S(1)}, f32[32,8,128]{2,1,0:T(8,128)S(1)}, bf16[256,128]{1,0:T(8,128)(2,1)S(1)}...) custom-call(f32[128,8,128]{2,1,0:T(8,128)S(1)} %get-tuple-element.95, ...), custom_call_target="tpu_custom_call", output_to_operand_aliasing={{0}: (0, {}), {1}: (1, {})} | custom-call | tf_op jit(solution)/shard_map/pallas_call | solution.py:548
  29.6 1.5 %collective-permute-start.8 = (bf16[256,128]{1,0:T(8,128)(2,1)S(1)}, bf16[256,128]{1,0:T(8,128)(2,1)S(1)}, u32[]{:S(2)}, u32[]{:S(2)}) collective-permute-start(bf16[256,128]{1,0:T(8,128)(2,1)S(1)} %get-tuple-element.109), channel_id=1, source_target_pairs={{0,3},{1,2},{2,1},{3,0},{4,7},{5,6},{6,5},{7,4},{8,11},{9,10},{10,... | collective-permute-start | bytes 196616 | tf_op jit(solution)/shard_map/ppermute | solution.py:491
  31.1 0.6 collective-permute-start.10
  31.7 1.1 %shard_map.198 = (f32[128,8,128]{2,1,0:T(8,128)S(1)}, f32[32,8,128]{2,1,0:T(8,128)S(1)}, s32[4,128]{1,0:T(4,128)S(4)}) custom-call(f32[128,8,128]{2,1,0:T(8,128)S(1)} %get-tuple-element.104.refs_0_, f32[32,8,128]{2,1,0:T(8,128)S(1)} %get-tuple-element.105.refs_1_.w_in, ...), custom_call_target="tpu_custom_call", output_to_operand_aliasing={{0}: (0, {})} | custom-call | flops 100000000 | tf_op jit(solution)/shard_map/pallas_call | solution.py:532
  32.8 1.2 %collective-permute-done.8.refs_0_ = bf16[256,128]{1,0:T(8,128)(2,1)S(1)} collective-permute-done((bf16[256,128]{1,0:T(8,128)(2,1)S(1)}, bf16[256,128]{1,0:T(8,128)(2,1)S(1)}, u32[]{:S(2)}, u32[]{:S(2)}) %collective-permute-start.8) | collective-permute-done | bytes 65568 | tf_op jit(solution)/shard_map/ppermute | solution.py:491
  34.0 1.4 %collective-permute-done.9.refs_1_ = bf16[256,128]{1,0:T(8,128)(2,1)S(1)} collective-permute-done((bf16[256,128]{1,0:T(8,128)(2,1)S(1)}, bf16[256,128]{1,0:T(8,128)(2,1)S(1)}, u32[]{:S(2)}, u32[]{:S(2)}) %collective-permute-start.9) | collective-permute-done | bytes 65568 | tf_op jit(solution)/shard_map/ppermute | solution.py:491
  35.4 0.9 %shard_map.199 = (f32[128,8,128]{2,1,0:T(8,128)S(1)}, f32[32,8,128]{2,1,0:T(8,128)S(1)}, f32[32,8,128]{2,1,0:T(8,128)S(1)}, bf16[128,128]{1,0:T(8,128)(2,1)S(1)}...) custom-call(f32[128,8,128]{2,1,0:T(8,128)S(1)} %get-tuple-element.10, ...), custom_call_target="tpu_custom_call", output_to_operand_aliasing={{0}: (0, {}), {1}: (1, {})} | custom-call | tf_op jit(solution)/shard_map/pallas_call | solution.py:548
  36.3 0.1 collective-permute-start.12
  36.4 0.7 %collective-permute-start.13 = (bf16[128,128]{1,0:T(8,128)(2,1)S(1)}, bf16[128,128]{1,0:T(8,128)(2,1)S(1)}, u32[]{:S(2)}, u32[]{:S(2)}) collective-permute-start(bf16[128,128]{1,0:T(8,128)(2,1)S(1)} %get-tuple-element.119), channel_id=1, source_target_pairs={{0,4},{1,5},{2,6},{3,7},{4,0},{5,1},{6,2},{7,3},{8,12},{9,13},{10,... | collective-permute-start | bytes 98312 | tf_op jit(solution)/shard_map/ppermute | solution.py:491
  37.2 0.2 collective-permute-start.14
  37.4 1.1 %shard_map.200 = (f32[128,8,128]{2,1,0:T(8,128)S(1)}, f32[32,8,128]{2,1,0:T(8,128)S(1)}, s32[4,128]{1,0:T(4,128)S(4)}) custom-call(f32[128,8,128]{2,1,0:T(8,128)S(1)} %get-tuple-element.113.refs_0_, f32[32,8,128]{2,1,0:T(8,128)S(1)} %get-tuple-element.114.refs_1_.w_in, ...), custom_call_target="tpu_custom_call", output_to_operand_aliasing={{0}: (0, {})} | custom-call | flops 100000000 | tf_op jit(solution)/shard_map/pallas_call | solution.py:532
  38.4 1.3 %collective-permute-done.12.refs_0_ = bf16[128,128]{1,0:T(8,128)(2,1)S(1)} collective-permute-done((bf16[128,128]{1,0:T(8,128)(2,1)S(1)}, bf16[128,128]{1,0:T(8,128)(2,1)S(1)}, u32[]{:S(2)}, u32[]{:S(2)}) %collective-permute-start.12) | collective-permute-done | bytes 32800 | tf_op jit(solution)/shard_map/ppermute | solution.py:491
  39.7 0.9 %collective-permute-done.13.refs_1_ = bf16[128,128]{1,0:T(8,128)(2,1)S(1)} collective-permute-done((bf16[128,128]{1,0:T(8,128)(2,1)S(1)}, bf16[128,128]{1,0:T(8,128)(2,1)S(1)}, u32[]{:S(2)}, u32[]{:S(2)}) %collective-permute-start.13) | collective-permute-done | bytes 32800 | tf_op jit(solution)/shard_map/ppermute | solution.py:491
  40.6 0.4 collective-permute-done.14.refs_2_
  41.1 1.0 %shard_map.201 = (f32[128,8,128]{2,1,0:T(8,128)S(1)}, f32[32,8,128]{2,1,0:T(8,128)S(1)}, f32[32,8,128]{2,1,0:T(8,128)S(1)}, f32[32,8,128]{2,1,0:T(8,128)S(1)}, b...) custom-call(f32[128,8,128]{2,1,0:T(8,128)S(1)} %get-tuple-element.11, ...), custom_call_target="tpu_custom_call", output_to_operand_aliasing={{0}: (0, {}), {1}: (1, {})} | custom-call | tf_op jit(solution)/shard_map/pallas_call | solution.py:548
  42.1 0.5 collective-permute-start.16
  42.6 1.3 %collective-permute-start.17 = (bf16[128,128]{1,0:T(8,128)(2,1)S(1)}, bf16[128,128]{1,0:T(8,128)(2,1)S(1)}, u32[]{:S(2)}, u32[]{:S(2)}) collective-permute-start(bf16[128,128]{1,0:T(8,128)(2,1)S(1)} %get-tuple-element.128), channel_id=1, source_target_pairs={{0,4},{1,5},{2,6},{3,7},{4,0},{5,1},{6,2},{7,3},{8,12},{9,13},{10,... | collective-permute-start | bytes 98312 | tf_op jit(solution)/shard_map/ppermute | solution.py:491
  43.9 0.0 collective-permute-start.19
  44.0 1.1 %shard_map.202 = (f32[128,8,128]{2,1,0:T(8,128)S(1)}, f32[32,8,128]{2,1,0:T(8,128)S(1)}, s32[4,128]{1,0:T(4,128)S(4)}) custom-call(f32[32,8,128]{2,1,0:T(8,128)S(1)} %get-tuple-element.122.refs_0_.z_in, bf16[32,9,128,128]{3,2,1,0:T(8,128)(2,1)S(1)} %get-tuple-element.93.refs_1_.off.refs_2_, s32[9,32]{1,0:T(8,128)S(4)} %get-tuple-element.81.columns.refs_2_.refs_3_, ...), custom_call_target="tpu_custom_call" | custom-call | flops 100000000 | tf_op jit(solution)/shard_map/pallas_call | solution.py:532
  45.1 0.7 collective-permute-done.16.refs_0_
  45.7 0.8 %collective-permute-done.17.refs_1_ = bf16[128,128]{1,0:T(8,128)(2,1)S(1)} collective-permute-done((bf16[128,128]{1,0:T(8,128)(2,1)S(1)}, bf16[128,128]{1,0:T(8,128)(2,1)S(1)}, u32[]{:S(2)}, u32[]{:S(2)}) %collective-permute-start.17) | collective-permute-done | bytes 32800 | tf_op jit(solution)/shard_map/ppermute | solution.py:491
  46.5 1.3 %collective-permute-done.18.refs_2_ = bf16[128,128]{1,0:T(8,128)(2,1)S(1)} collective-permute-done((bf16[128,128]{1,0:T(8,128)(2,1)S(1)}, bf16[128,128]{1,0:T(8,128)(2,1)S(1)}, u32[]{:S(2)}, u32[]{:S(2)}) %collective-permute-start.18) | collective-permute-done | bytes 32800 | tf_op jit(solution)/shard_map/ppermute | solution.py:491
  47.8 0.7 %shard_map.203 = (f32[128,8,128]{2,1,0:T(8,128)S(1)}, f32[32,8,128]{2,1,0:T(8,128)S(1)}, f32[32,8,128]{2,1,0:T(8,128)S(1)}, bf16[128,128]{1,0:T(8,128)(2,1)S(1)}...) custom-call(f32[128,8,128]{2,1,0:T(8,128)S(1)} %get-tuple-element.12, ...), custom_call_target="tpu_custom_call", output_to_operand_aliasing={{0}: (0, {}), {1}: (1, {})} | custom-call | tf_op jit(solution)/shard_map/pallas_call | solution.py:557
  48.6 0.1 collective-permute-start.20
  48.7 0.1 collective-permute-start.21
  48.8 1.4 %collective-permute-start.22 = (bf16[128,128]{1,0:T(8,128)(2,1)S(1)}, bf16[128,128]{1,0:T(8,128)(2,1)S(1)}, u32[]{:S(2)}, u32[]{:S(2)}) collective-permute-start(bf16[128,128]{1,0:T(8,128)(2,1)S(1)} %get-tuple-element.138), channel_id=1, source_target_pairs={{0,1},{1,0},{2,3},{3,2},{4,8},{5,9},{6,10},{7,11},{8,4},{9,5},{10,... | collective-permute-start | bytes 98312 | tf_op jit(solution)/shard_map/ppermute | solution.py:491
  50.2 0.2 shard_map.205.refs_5_
  50.4 2.3 %shard_map.204 = (f32[128,8,128]{2,1,0:T(8,128)S(1)}, f32[32,8,128]{2,1,0:T(8,128)S(1)}, s32[4,128]{1,0:T(4,128)S(4)}) custom-call(f32[128,8,128]{2,1,0:T(8,128)S(1)} %get-tuple-element.131.refs_0_, f32[32,8,128]{2,1,0:T(8,128)S(1)} %get-tuple-element.132.refs_1_.z_in, ...), custom_call_target="tpu_custom_call", output_to_operand_aliasing={{0}: (0, {})} | custom-call | flops 100000000 | tf_op jit(solution)/shard_map/pallas_call | solution.py:532
  52.7 0.0 collective-permute-done.21.refs_1_
  52.7 0.2 collective-permute-done.22.refs_2_
  52.9 1.8 %shard_map.206 = (f32[128,8,128]{2,1,0:T(8,128)S(1)}, f32[32,8,128]{2,1,0:T(8,128)S(1)}, f32[32,8,128]{2,1,0:T(8,128)S(1)}, bf16[128,128]{1,0:T(8,128)(2,1)S(1)}...) custom-call(f32[128,8,128]{2,1,0:T(8,128)S(1)} %get-tuple-element.13, ...), custom_call_target="tpu_custom_call", output_to_operand_aliasing={{0}: (0, {}), {1}: (1, {})} | custom-call | tf_op jit(solution)/shard_map/pallas_call | solution.py:565
  54.7 6.3 %all-to-all-start.1 = ((f32[16,16,128]{2,1,0:T(8,128)}), f32[16,16,128]{2,1,0:T(8,128)S(1)}, u32[]{:S(2)}, u32[]{:S(2)}) async-start(f32[16,16,128]{2,1,0:T(8,128)} %get-tuple-element.141), calls=%async_computation.1 | async-start | bytes 262144 | tf_op jit(solution)/shard_map/all_to_all | solution.py:571
  61.0 1.2 %collective-permute-start.24 = (bf16[128,128]{1,0:T(8,128)(2,1)S(1)}, bf16[128,128]{1,0:T(8,128)(2,1)S(1)}, u32[]{:S(2)}, u32[]{:S(2)}) collective-permute-start(bf16[128,128]{1,0:T(8,128)(2,1)S(1)} %get-tuple-element.143), channel_id=1, source_target_pairs={{0,3},{1,2},{2,1},{3,0},{4,7},{5,6},{6,5},{7,4},{8,11},{9,10},{10,... | collective-permute-start | bytes 98312 | tf_op jit(solution)/shard_map/ppermute | solution.py:491
  62.2 1.5 %collective-permute-start.25 = (bf16[128,128]{1,0:T(8,128)(2,1)S(1)}, bf16[128,128]{1,0:T(8,128)(2,1)S(1)}, u32[]{:S(2)}, u32[]{:S(2)}) collective-permute-start(bf16[128,128]{1,0:T(8,128)(2,1)S(1)} %get-tuple-element.144), channel_id=1, source_target_pairs={{0,4},{1,5},{2,6},{3,7},{4,0},{5,1},{6,2},{7,3},{8,12},{9,13},{10,... | collective-permute-start | bytes 98312 | tf_op jit(solution)/shard_map/ppermute | solution.py:491
  63.7 0.1 collective-permute-start.27
  63.7 0.9 %collective-permute-done.24.after.refs_0_ = bf16[128,128]{1,0:T(8,128)(2,1)S(1)} collective-permute-done((bf16[128,128]{1,0:T(8,128)(2,1)S(1)}, bf16[128,128]{1,0:T(8,128)(2,1)S(1)}, u32[]{:S(2)}, u32[]{:S(2)}) %collective-permute-start.24) | collective-permute-done | bytes 32800 | tf_op jit(solution)/shard_map/ppermute | solution.py:491
  64.6 2.1 %shard_map.207.off = bf16[32,9,128,128]{3,2,1,0:T(8,128)(2,1)S(1)} custom-call(bf16[32,9,128,128]{3,2,1,0:T(8,128)(2,1)} %off_hbm.5, s32[8,128]{1,0:T(8,128)S(4)} %get-tuple-element.90.tables.refs_3_.refs_4_, bf16[128,128]{1,0:T(8,128)(2,1)S(1)} %collective-permute-done.24.after.refs_0_), custom_call_target="tpu_custom_call" | custom-call | flops 100000000 | tf_op jit(solution)/shard_map/pallas_call | solution.py:573
  66.8 0.0 copy-start.4
  66.8 0.0 copy-start.5
  66.8 0.0 copy-start.10
  66.8 0.0 copy-start.11
  66.8 0.8 %collective-permute-done.26.refs_2_ = bf16[128,128]{1,0:T(8,128)(2,1)S(1)} collective-permute-done((bf16[128,128]{1,0:T(8,128)(2,1)S(1)}, bf16[128,128]{1,0:T(8,128)(2,1)S(1)}, u32[]{:S(2)}, u32[]{:S(2)}) %collective-permute-start.26) | collective-permute-done | bytes 32800 | tf_op jit(solution)/shard_map/ppermute | solution.py:491
  67.6 1.9 %shard_map.208.z = f32[32,8,128]{2,1,0:T(8,128)S(1)} custom-call(f32[32,8,128]{2,1,0:T(8,128)S(1)} %get-tuple-element.125.w, f32[32,8,128]{2,1,0:T(8,128)S(1)} %get-tuple-element.142.z_in, bf16[32,9,128,128]{3,2,1,0:T(8,128)(2,1)S(1)} %shard_map.207.off, bf16[32,128,128]{2,1,0:T(8,128)(2,1)S(1)} %copy-done.1, f32[32,128]{1,0:T(8,128)S(1)} %get-tuple-element.88.straight, ...), custom_call_target="tpu_custom_call" | custom-call | tf_op jit(solution)/shard_map/pallas_call | solution.py:576
  69.4 0.0 copy-done.4
  69.5 1.4 %shard_map.209 = (f32[32,8,128]{2,1,0:T(8,128)}, f32[32,8,128]{2,1,0:T(8,128)}, f32[32,8,128]{2,1,0:T(8,128)}, f32[3,8]{1,0:T(4,128)}) custom-call(f32[16,16,128]{2,1,0:T(8,128)S(1)} %all-to-all-done.1.sums, f32[32,8,128]{2,1,0:T(8,128)S(1)} %shard_map.208.z, f32[32,8,128]{2,1,0:T(8,128)S(1)} %get-tuple-element.79.q.q_ref, f32[32,8,128]{2,1,0:T(8,128)S(1)} %copy-done.4, ...), custom_call_target="tpu_custom_call" | custom-call | tf_op jit(solution)/shard_map/pallas_call | solution.py:583
  (38 shorter events, 0.1 us)
Async XLA Ops:
  0.6 4.3 %copy-start = (bf16[32,9,128,128]{3,2,1,0:T(8,128)(2,1)S(1)}, bf16[32,9,128,128]{3,2,1,0:T(8,128)(2,1)}, u32[]{:S(2)}) copy-start(bf16[32,9,128,128]{3,2,1,0:T(8,128)(2,1)} %off_hbm.5) | copy-start | bytes 28311556
  0.6 4.3 %copy-start.6 = (f32[32,128]{1,0:T(8,128)S(1)}, f32[32,128]{1,0:T(8,128)}, u32[]{:S(2)}) copy-start(f32[32,128]{1,0:T(8,128)} %diag_ref.1) | copy-start | bytes 49156
  0.7 4.3 %copy-start.7 = (f32[32,64]{1,0:T(8,128)S(1)}, f32[32,64]{1,0:T(8,128)}, u32[]{:S(2)}) copy-start(f32[32,64]{1,0:T(8,128)} %off_ref.1) | copy-start | bytes 24580
  0.7 4.3 %copy-start.8 = (s32[32,64]{1,0:T(8,128)S(1)}, s32[32,64]{1,0:T(8,128)}, u32[]{:S(2)}) copy-start(s32[32,64]{1,0:T(8,128)} %pairs_ref.1) | copy-start | bytes 24580
  1.9 6.5 %copy-start.2 = (bf16[32,128,128]{2,1,0:T(8,128)(2,1)S(1)}, bf16[32,128,128]{2,1,0:T(8,128)(2,1)}, u32[]{:S(2)}) copy-start(bf16[32,128,128]{2,1,0:T(8,128)(2,1)} %diag.1) | copy-start | bytes 3145732
  1.9 4.2 %collective-permute-start = (bf16[144,128]{1,0:T(8,128)(2,1)S(1)}, bf16[144,128]{1,0:T(8,128)(2,1)S(1)}, u32[]{:S(2)}, u32[]{:S(2)}) collective-permute-start(bf16[144,128]{1,0:T(8,128)(2,1)S(1)} %get-tuple-element.82), channel_id=1, source_target_pairs={{0,3},{1,2},{2,1},{3,0},{4,7},{5,6},{6,5},{7,4},{8,11},{9,10},{10,... | collective-permute-start | bytes 110600 | tf_op jit(solution)/shard_map/ppermute | solution.py:491
  2.9 4.1 %collective-permute-start.1 = (bf16[144,128]{1,0:T(8,128)(2,1)S(1)}, bf16[144,128]{1,0:T(8,128)(2,1)S(1)}, u32[]{:S(2)}, u32[]{:S(2)}) collective-permute-start(bf16[144,128]{1,0:T(8,128)(2,1)S(1)} %get-tuple-element.83), channel_id=1, source_target_pairs={{0,4},{1,5},{2,6},{3,7},{4,0},{5,1},{6,2},{7,3},{8,12},{9,13},{10,... | collective-permute-start | bytes 110600 | tf_op jit(solution)/shard_map/ppermute | solution.py:491
  4.5 4.0 %collective-permute-start.2 = (bf16[144,128]{1,0:T(8,128)(2,1)S(1)}, bf16[144,128]{1,0:T(8,128)(2,1)S(1)}, u32[]{:S(2)}, u32[]{:S(2)}) collective-permute-start(bf16[144,128]{1,0:T(8,128)(2,1)S(1)} %get-tuple-element.84), channel_id=1, source_target_pairs={{0,1},{1,0},{2,3},{3,2},{4,8},{5,9},{6,10},{7,11},{8,4},{9,5},{10,... | collective-permute-start | bytes 110600 | tf_op jit(solution)/shard_map/ppermute | solution.py:491
  4.5 4.0 %collective-permute-start.3 = (bf16[144,128]{1,0:T(8,128)(2,1)S(1)}, bf16[144,128]{1,0:T(8,128)(2,1)S(1)}, u32[]{:S(2)}, u32[]{:S(2)}) collective-permute-start(bf16[144,128]{1,0:T(8,128)(2,1)S(1)} %get-tuple-element.85), channel_id=1, source_target_pairs={{0,1},{1,0},{2,3},{3,2},{4,5},{5,4},{6,7},{7,6},{8,9},{9,8},{10,11... | collective-permute-start | bytes 110600 | tf_op jit(solution)/shard_map/ppermute | solution.py:491
  8.5 11.9 %copy-start.1 = (bf16[32,128,128]{2,1,0:T(8,128)(2,1)S(1)}, bf16[32,128,128]{2,1,0:T(8,128)(2,1)}, u32[]{:S(2)}) copy-start(bf16[32,128,128]{2,1,0:T(8,128)(2,1)} %factor.13) | copy-start | bytes 3145732
  8.5 11.9 %copy-start.3 = (f32[32,8,128]{2,1,0:T(8,128)S(1)}, f32[32,8,128]{2,1,0:T(8,128)}, u32[]{:S(2)}) copy-start(f32[32,8,128]{2,1,0:T(8,128)} %r_ref.1) | copy-start | bytes 393220
  8.5 11.9 %copy-start.9 = (f32[8]{0:T(128)S(1)}, f32[8]{0:T(128)}, u32[]{:S(2)}) copy-start(f32[8]{0:T(128)} %rho.3) | copy-start | bytes 100
  21.5 7.3 %collective-permute-start.4 = (bf16[128,128]{1,0:T(8,128)(2,1)S(1)}, bf16[128,128]{1,0:T(8,128)(2,1)S(1)}, u32[]{:S(2)}, u32[]{:S(2)}) collective-permute-start(bf16[128,128]{1,0:T(8,128)(2,1)S(1)} %get-tuple-element.99), channel_id=1, source_target_pairs={{0,3},{1,2},{2,1},{3,0},{4,7},{5,6},{6,5},{7,4},{8,11},{9,10},{10,... | collective-permute-start | bytes 98312 | tf_op jit(solution)/shard_map/ppermute | solution.py:491
  22.0 6.8 %collective-permute-start.5 = (bf16[128,128]{1,0:T(8,128)(2,1)S(1)}, bf16[128,128]{1,0:T(8,128)(2,1)S(1)}, u32[]{:S(2)}, u32[]{:S(2)}) collective-permute-start(bf16[128,128]{1,0:T(8,128)(2,1)S(1)} %get-tuple-element.100), channel_id=1, source_target_pairs={{0,4},{1,5},{2,6},{3,7},{4,0},{5,1},{6,2},{7,3},{8,12},{9,13},{10,... | collective-permute-start | bytes 98312 | tf_op jit(solution)/shard_map/ppermute | solution.py:491
  22.9 5.9 %collective-permute-start.6 = (bf16[128,128]{1,0:T(8,128)(2,1)S(1)}, bf16[128,128]{1,0:T(8,128)(2,1)S(1)}, u32[]{:S(2)}, u32[]{:S(2)}) collective-permute-start(bf16[128,128]{1,0:T(8,128)(2,1)S(1)} %get-tuple-element.101), channel_id=1, source_target_pairs={{0,1},{1,0},{2,3},{3,2},{4,8},{5,9},{6,10},{7,11},{8,4},{9,5},{10,... | collective-permute-start | bytes 98312 | tf_op jit(solution)/shard_map/ppermute | solution.py:491
  25.0 3.9 %collective-permute-start.7 = (bf16[128,128]{1,0:T(8,128)(2,1)S(1)}, bf16[128,128]{1,0:T(8,128)(2,1)S(1)}, u32[]{:S(2)}, u32[]{:S(2)}) collective-permute-start(bf16[128,128]{1,0:T(8,128)(2,1)S(1)} %get-tuple-element.102), channel_id=1, source_target_pairs={{0,1},{1,0},{2,3},{3,2},{4,5},{5,4},{6,7},{7,6},{8,9},{9,8},{10,11... | collective-permute-start | bytes 98312 | tf_op jit(solution)/shard_map/ppermute | solution.py:491
  29.6 4.4 %collective-permute-start.8 = (bf16[256,128]{1,0:T(8,128)(2,1)S(1)}, bf16[256,128]{1,0:T(8,128)(2,1)S(1)}, u32[]{:S(2)}, u32[]{:S(2)}) collective-permute-start(bf16[256,128]{1,0:T(8,128)(2,1)S(1)} %get-tuple-element.109), channel_id=1, source_target_pairs={{0,3},{1,2},{2,1},{3,0},{4,7},{5,6},{6,5},{7,4},{8,11},{9,10},{10,... | collective-permute-start | bytes 196616 | tf_op jit(solution)/shard_map/ppermute | solution.py:491
  31.1 4.3 %collective-permute-start.9 = (bf16[256,128]{1,0:T(8,128)(2,1)S(1)}, bf16[256,128]{1,0:T(8,128)(2,1)S(1)}, u32[]{:S(2)}, u32[]{:S(2)}) collective-permute-start(bf16[256,128]{1,0:T(8,128)(2,1)S(1)} %get-tuple-element.110), channel_id=1, source_target_pairs={{0,4},{1,5},{2,6},{3,7},{4,0},{5,1},{6,2},{7,3},{8,12},{9,13},{10,... | collective-permute-start | bytes 196616 | tf_op jit(solution)/shard_map/ppermute | solution.py:491
  31.1 4.3 %collective-permute-start.10 = (bf16[256,128]{1,0:T(8,128)(2,1)S(1)}, bf16[256,128]{1,0:T(8,128)(2,1)S(1)}, u32[]{:S(2)}, u32[]{:S(2)}) collective-permute-start(bf16[256,128]{1,0:T(8,128)(2,1)S(1)} %get-tuple-element.111), channel_id=1, source_target_pairs={{0,1},{1,0},{2,3},{3,2},{4,8},{5,9},{6,10},{7,11},{8,4},{9,5},{10,... | collective-permute-start | bytes 196616 | tf_op jit(solution)/shard_map/ppermute | solution.py:491
  31.7 3.7 %collective-permute-start.11 = (bf16[256,128]{1,0:T(8,128)(2,1)S(1)}, bf16[256,128]{1,0:T(8,128)(2,1)S(1)}, u32[]{:S(2)}, u32[]{:S(2)}) collective-permute-start(bf16[256,128]{1,0:T(8,128)(2,1)S(1)} %get-tuple-element.112), channel_id=1, source_target_pairs={{0,1},{1,0},{2,3},{3,2},{4,5},{5,4},{6,7},{7,6},{8,9},{9,8},{10,11... | collective-permute-start | bytes 196616 | tf_op jit(solution)/shard_map/ppermute | solution.py:491
  36.3 3.4 %collective-permute-start.12 = (bf16[128,128]{1,0:T(8,128)(2,1)S(1)}, bf16[128,128]{1,0:T(8,128)(2,1)S(1)}, u32[]{:S(2)}, u32[]{:S(2)}) collective-permute-start(bf16[128,128]{1,0:T(8,128)(2,1)S(1)} %get-tuple-element.118), channel_id=1, source_target_pairs={{0,3},{1,2},{2,1},{3,0},{4,7},{5,6},{6,5},{7,4},{8,11},{9,10},{10,... | collective-permute-start | bytes 98312 | tf_op jit(solution)/shard_map/ppermute | solution.py:491
  36.4 4.2 %collective-permute-start.13 = (bf16[128,128]{1,0:T(8,128)(2,1)S(1)}, bf16[128,128]{1,0:T(8,128)(2,1)S(1)}, u32[]{:S(2)}, u32[]{:S(2)}) collective-permute-start(bf16[128,128]{1,0:T(8,128)(2,1)S(1)} %get-tuple-element.119), channel_id=1, source_target_pairs={{0,4},{1,5},{2,6},{3,7},{4,0},{5,1},{6,2},{7,3},{8,12},{9,13},{10,... | collective-permute-start | bytes 98312 | tf_op jit(solution)/shard_map/ppermute | solution.py:491
  37.2 3.9 %collective-permute-start.14 = (bf16[128,128]{1,0:T(8,128)(2,1)S(1)}, bf16[128,128]{1,0:T(8,128)(2,1)S(1)}, u32[]{:S(2)}, u32[]{:S(2)}) collective-permute-start(bf16[128,128]{1,0:T(8,128)(2,1)S(1)} %get-tuple-element.120), channel_id=1, source_target_pairs={{0,1},{1,0},{2,3},{3,2},{4,8},{5,9},{6,10},{7,11},{8,4},{9,5},{10,... | collective-permute-start | bytes 98312 | tf_op jit(solution)/shard_map/ppermute | solution.py:491
  37.4 3.7 %collective-permute-start.15 = (bf16[128,128]{1,0:T(8,128)(2,1)S(1)}, bf16[128,128]{1,0:T(8,128)(2,1)S(1)}, u32[]{:S(2)}, u32[]{:S(2)}) collective-permute-start(bf16[128,128]{1,0:T(8,128)(2,1)S(1)} %get-tuple-element.121), channel_id=1, source_target_pairs={{0,1},{1,0},{2,3},{3,2},{4,5},{5,4},{6,7},{7,6},{8,9},{9,8},{10,11... | collective-permute-start | bytes 98312 | tf_op jit(solution)/shard_map/ppermute | solution.py:491
  42.1 3.6 %collective-permute-start.16 = (bf16[128,128]{1,0:T(8,128)(2,1)S(1)}, bf16[128,128]{1,0:T(8,128)(2,1)S(1)}, u32[]{:S(2)}, u32[]{:S(2)}) collective-permute-start(bf16[128,128]{1,0:T(8,128)(2,1)S(1)} %get-tuple-element.127), channel_id=1, source_target_pairs={{0,3},{1,2},{2,1},{3,0},{4,7},{5,6},{6,5},{7,4},{8,11},{9,10},{10,... | collective-permute-start | bytes 98312 | tf_op jit(solution)/shard_map/ppermute | solution.py:491
  42.6 3.9 %collective-permute-start.17 = (bf16[128,128]{1,0:T(8,128)(2,1)S(1)}, bf16[128,128]{1,0:T(8,128)(2,1)S(1)}, u32[]{:S(2)}, u32[]{:S(2)}) collective-permute-start(bf16[128,128]{1,0:T(8,128)(2,1)S(1)} %get-tuple-element.128), channel_id=1, source_target_pairs={{0,4},{1,5},{2,6},{3,7},{4,0},{5,1},{6,2},{7,3},{8,12},{9,13},{10,... | collective-permute-start | bytes 98312 | tf_op jit(solution)/shard_map/ppermute | solution.py:491
  43.9 3.9 %collective-permute-start.18 = (bf16[128,128]{1,0:T(8,128)(2,1)S(1)}, bf16[128,128]{1,0:T(8,128)(2,1)S(1)}, u32[]{:S(2)}, u32[]{:S(2)}) collective-permute-start(bf16[128,128]{1,0:T(8,128)(2,1)S(1)} %get-tuple-element.129), channel_id=1, source_target_pairs={{0,1},{1,0},{2,3},{3,2},{4,8},{5,9},{6,10},{7,11},{8,4},{9,5},{10,... | collective-permute-start | bytes 98312 | tf_op jit(solution)/shard_map/ppermute | solution.py:491
  43.9 3.9 %collective-permute-start.19 = (bf16[128,128]{1,0:T(8,128)(2,1)S(1)}, bf16[128,128]{1,0:T(8,128)(2,1)S(1)}, u32[]{:S(2)}, u32[]{:S(2)}) collective-permute-start(bf16[128,128]{1,0:T(8,128)(2,1)S(1)} %get-tuple-element.130), channel_id=1, source_target_pairs={{0,1},{1,0},{2,3},{3,2},{4,5},{5,4},{6,7},{7,6},{8,9},{9,8},{10,11... | collective-permute-start | bytes 98312 | tf_op jit(solution)/shard_map/ppermute | solution.py:491
  48.6 4.1 %collective-permute-start.20 = (bf16[128,128]{1,0:T(8,128)(2,1)S(1)}, bf16[128,128]{1,0:T(8,128)(2,1)S(1)}, u32[]{:S(2)}, u32[]{:S(2)}) collective-permute-start(bf16[128,128]{1,0:T(8,128)(2,1)S(1)} %get-tuple-element.136), channel_id=1, source_target_pairs={{0,3},{1,2},{2,1},{3,0},{4,7},{5,6},{6,5},{7,4},{8,11},{9,10},{10,... | collective-permute-start | bytes 98312 | tf_op jit(solution)/shard_map/ppermute | solution.py:491
  48.7 4.0 %collective-permute-start.21 = (bf16[128,128]{1,0:T(8,128)(2,1)S(1)}, bf16[128,128]{1,0:T(8,128)(2,1)S(1)}, u32[]{:S(2)}, u32[]{:S(2)}) collective-permute-start(bf16[128,128]{1,0:T(8,128)(2,1)S(1)} %get-tuple-element.137), channel_id=1, source_target_pairs={{0,4},{1,5},{2,6},{3,7},{4,0},{5,1},{6,2},{7,3},{8,12},{9,13},{10,... | collective-permute-start | bytes 98312 | tf_op jit(solution)/shard_map/ppermute | solution.py:491
  48.8 4.1 %collective-permute-start.22 = (bf16[128,128]{1,0:T(8,128)(2,1)S(1)}, bf16[128,128]{1,0:T(8,128)(2,1)S(1)}, u32[]{:S(2)}, u32[]{:S(2)}) collective-permute-start(bf16[128,128]{1,0:T(8,128)(2,1)S(1)} %get-tuple-element.138), channel_id=1, source_target_pairs={{0,1},{1,0},{2,3},{3,2},{4,8},{5,9},{6,10},{7,11},{8,4},{9,5},{10,... | collective-permute-start | bytes 98312 | tf_op jit(solution)/shard_map/ppermute | solution.py:491
  50.2 2.7 %collective-permute-start.23 = (bf16[128,128]{1,0:T(8,128)(2,1)S(1)}, bf16[128,128]{1,0:T(8,128)(2,1)S(1)}, u32[]{:S(2)}, u32[]{:S(2)}) collective-permute-start(bf16[128,128]{1,0:T(8,128)(2,1)S(1)} %get-tuple-element.139), channel_id=1, source_target_pairs={{0,1},{1,0},{2,3},{3,2},{4,5},{5,4},{6,7},{7,6},{8,9},{9,8},{10,11... | collective-permute-start | bytes 98312 | tf_op jit(solution)/shard_map/ppermute | solution.py:491
  54.7 14.8 %all-to-all-start.1 = ((f32[16,16,128]{2,1,0:T(8,128)}), f32[16,16,128]{2,1,0:T(8,128)S(1)}, u32[]{:S(2)}, u32[]{:S(2)}) async-start(f32[16,16,128]{2,1,0:T(8,128)} %get-tuple-element.141), calls=%async_computation.1 | async-start | bytes 262144 | tf_op jit(solution)/shard_map/all_to_all | solution.py:571
  61.0 3.7 %collective-permute-start.24 = (bf16[128,128]{1,0:T(8,128)(2,1)S(1)}, bf16[128,128]{1,0:T(8,128)(2,1)S(1)}, u32[]{:S(2)}, u32[]{:S(2)}) collective-permute-start(bf16[128,128]{1,0:T(8,128)(2,1)S(1)} %get-tuple-element.143), channel_id=1, source_target_pairs={{0,3},{1,2},{2,1},{3,0},{4,7},{5,6},{6,5},{7,4},{8,11},{9,10},{10,... | collective-permute-start | bytes 98312 | tf_op jit(solution)/shard_map/ppermute | solution.py:491
  62.2 4.6 %collective-permute-start.25 = (bf16[128,128]{1,0:T(8,128)(2,1)S(1)}, bf16[128,128]{1,0:T(8,128)(2,1)S(1)}, u32[]{:S(2)}, u32[]{:S(2)}) collective-permute-start(bf16[128,128]{1,0:T(8,128)(2,1)S(1)} %get-tuple-element.144), channel_id=1, source_target_pairs={{0,4},{1,5},{2,6},{3,7},{4,0},{5,1},{6,2},{7,3},{8,12},{9,13},{10,... | collective-permute-start | bytes 98312 | tf_op jit(solution)/shard_map/ppermute | solution.py:491
  63.7 3.9 %collective-permute-start.26 = (bf16[128,128]{1,0:T(8,128)(2,1)S(1)}, bf16[128,128]{1,0:T(8,128)(2,1)S(1)}, u32[]{:S(2)}, u32[]{:S(2)}) collective-permute-start(bf16[128,128]{1,0:T(8,128)(2,1)S(1)} %get-tuple-element.145), channel_id=1, source_target_pairs={{0,1},{1,0},{2,3},{3,2},{4,8},{5,9},{6,10},{7,11},{8,4},{9,5},{10,... | collective-permute-start | bytes 98312 | tf_op jit(solution)/shard_map/ppermute | solution.py:491
  63.7 3.9 %collective-permute-start.27 = (bf16[128,128]{1,0:T(8,128)(2,1)S(1)}, bf16[128,128]{1,0:T(8,128)(2,1)S(1)}, u32[]{:S(2)}, u32[]{:S(2)}) collective-permute-start(bf16[128,128]{1,0:T(8,128)(2,1)S(1)} %get-tuple-element.146), channel_id=1, source_target_pairs={{0,1},{1,0},{2,3},{3,2},{4,5},{5,4},{6,7},{7,6},{8,9},{9,8},{10,11... | collective-permute-start | bytes 98312 | tf_op jit(solution)/shard_map/ppermute | solution.py:491
  66.8 2.7 %copy-start.4 = (f32[32,8,128]{2,1,0:T(8,128)S(1)}, f32[32,8,128]{2,1,0:T(8,128)}, u32[]{:S(2)}) copy-start(f32[32,8,128]{2,1,0:T(8,128)} %x_ref.1) | copy-start | bytes 393220
  66.8 2.7 %copy-start.5 = (f32[32,8,128]{2,1,0:T(8,128)S(1)}, f32[32,8,128]{2,1,0:T(8,128)}, u32[]{:S(2)}) copy-start(f32[32,8,128]{2,1,0:T(8,128)} %d_ref.1) | copy-start | bytes 393220
  66.8 2.7 %copy-start.10 = (f32[8]{0:T(128)S(1)}, f32[8]{0:T(128)}, u32[]{:S(2)}) copy-start(f32[8]{0:T(128)} %tau.1) | copy-start | bytes 100
  66.8 2.7 %copy-start.11 = (f32[8]{0:T(128)S(1)}, f32[8]{0:T(128)}, u32[]{:S(2)}) copy-start(f32[8]{0:T(128)} %theta_in.1) | copy-start | bytes 100

commit v7 on v6

--- a/solution.py
+++ b/solution.py
@@ -16,7 +16,7 @@
 ORDER = (1, 2, 3, 0, 4, 5)
 COUPLE = (8, 4, 2)
 SOLVE = (16,)
-LATE = 4
+LATE = 8
 PART = 4
 PARTS = (0, 16, 24, 32)
 
@@ -108,15 +108,18 @@
     return values
 
 
-def load_kernel(off_hbm, tables, after, off, sems):
+def load_kernel(off_hbm, tables, r_new, after, off, r_out, sems):
     count = tables[4, 0]
+    out = pltpu.make_async_copy(r_new, r_out, sems.at[32])
 
     def copy(place):
         block = tables[0, place]
         return pltpu.make_async_copy(off_hbm.at[block], off.at[block], sems.at[place])
 
     lax.fori_loop(0, count, lambda place, carry: (copy(place).start(), carry)[1], 0)
+    out.start()
     lax.fori_loop(0, count, lambda place, carry: (copy(place).wait(), carry)[1], 0)
+    out.wait()
 
 
 def for_colour(colour, tables, sizes, body):
@@ -127,7 +130,8 @@
         groups = (left + size - 1) // size if size == sizes[-1] else left // size
 
         def step(group, carry, done=done, size=size):
-            body([tables[colour, done + group * size + j] for j in range(size)])
+            places = [done + group * size + j for j in range(size)]
+            body([tables[colour, place] for place in places], places)
             return carry
 
         lax.fori_loop(0, groups, step, 0)
@@ -241,7 +245,7 @@
     r_new[...] = new
     w[...] = jnp.zeros_like(w)
 
-    def body(blocks):
+    def body(blocks, places):
         for b, value in zip(blocks, solved(blocks, [r_new[b] for b in blocks], factor, straight, crossed)):
             w[b] = value
 
@@ -249,9 +253,8 @@
     send_faces(swaps, w, faces, sent)
 
 
-def adjoint_kernel(r_new, w, off, columns, tables, adjoint, terms, r_out):
+def adjoint_kernel(r_new, w, off, columns, tables, adjoint, terms):
     new = r_new[...]
-    r_out[...] = new
     terms[pl.ds(0, 8), :] = jnp.sum(new * w[...], axis=0)
     terms[pl.ds(8, 8), :] = jnp.sum(new * new, axis=0)
     adjoint[...] = jnp.zeros_like(adjoint)
@@ -296,26 +299,26 @@
         extended[pl.ds(32, 96)] = jnp.zeros((96, 8, 128), F32)
     own_blocks(state, extended)
 
-    def couple(blocks):
+    count = tables[4, colour]
+    late[3, 0] = 0
+
+    def couple(blocks, places):
         for b, value in zip(blocks, [coupled(b, extended, off, columns) for b in blocks]):
             rest[b] = value
+        found = late[3, 0]
+        for block, place in zip(blocks, places):
+            for k in range(9):
+                column = columns[k, block]
+                slot = jnp.maximum(column - 32, 0)
+                hit = (column >= 32) & (remote[slot >> 4, slot & 15] == wanted) & (place < count)
+                late[found >> 7, found & 127] = block * 16 + k
+                found = found + jnp.where(hit, 1, 0)
+        late[3, 0] = found
 
     for_colour(colour, tables, COUPLE, couple)
-
-    def note(place, found):
-        block = tables[colour, place]
-        for k in range(9):
-            column = columns[k, block]
-            slot = jnp.maximum(column - 32, 0)
-            hit = (column >= 32) & (remote[slot >> 4, slot & 15] == wanted)
-            late[found >> 7, found & 127] = block * 16 + k
-            found = found + jnp.where(hit, 1, 0)
-        return found
-
-    found = lax.fori_loop(0, tables[4, colour], note, jnp.int32(0))
+    found = late[3, 0]
     for j in range(LATE):
         late[(found + j) >> 7, (found + j) & 127] = 0
-    late[3, 0] = found
 
 
 def couple_late(swaps, arrived, extended, rest, off, columns, late):
@@ -346,7 +349,7 @@
     w[...] = w_in[...]
     couple_late(swaps, arrived, extended, rest, off, columns, late)
 
-    def solve(blocks):
+    def solve(blocks, places):
         for b, value in zip(blocks, solved(blocks, [r_new[b] - rest[b] for b in blocks], factor, straight, crossed)):
             w[b] = value
 
@@ -355,7 +358,7 @@
         z = sent[0]
         z[...] = jnp.zeros_like(z)
 
-        def copy(blocks):
+        def copy(blocks, places):
             for b in blocks:
                 z[b] = w[b]
 
@@ -380,7 +383,7 @@
     z[...] = z_in[...]
     couple_late(swaps, arrived, extended, rest, off, columns, late)
 
-    def solve(blocks):
+    def solve(blocks, places):
         for b, value in zip(blocks, solved(blocks, [rest[b] for b in blocks], factor, straight, crossed)):
             z[b] = w[b] - value
 
@@ -405,11 +408,11 @@
     z[...] = z_in[...]
     extend(swaps, z_in, arrived, extended)
 
-    def couple(blocks):
+    def couple(blocks, places):
         for b, value in zip(blocks, [coupled(b, extended, off, columns) for b in blocks]):
             rest[b] = value
 
-    def solve(blocks):
+    def solve(blocks, places):
         for b, value in zip(blocks, solved(blocks, [rest[b] for b in blocks], factor, straight, crossed)):
             z[b] = w[b] - value
 
@@ -519,9 +522,9 @@
     )(sums, r_vec, image, rho_prev, factor_inv, straight, crossed, tables, faces)
     fixed = (off, factor_inv, straight, crossed, columns, tables, faces)
     fixed_places = [VMEM] * 4 + [SMEM] * 3
-    adjoint, terms, r_out = call(
+    adjoint, terms = call(
         adjoint_kernel,
-        [VMEM((128, 8, 128), F32), VMEM((16, 128), F32), vec(32, 8, 128)],
+        [VMEM((128, 8, 128), F32), VMEM((16, 128), F32)],
         [VMEM] * 3 + [SMEM] * 2,
         cost=10**8,
     )(r_new, w, off, columns, tables)
@@ -570,9 +573,13 @@
     )(extended, rest, w, z, *fixed, late, *arrived, r_new, total, terms)
     sums = lax.all_to_all(partial, "gx", 0, 0, tiled=True)
     arrived = exchange(sent)
-    off = call(load_kernel, [off_kept], [HBM, SMEM, VMEM], [pltpu.SemaphoreType.DMA((32,))], cost=10**8)(
-        in_hbm(off_blocks), tables, arrived[0]
-    )[0]
+    off, r_out = call(
+        load_kernel,
+        [off_kept, HBM((32, 8, 128), F32)],
+        [HBM, SMEM, VMEM, VMEM],
+        [pltpu.SemaphoreType.DMA((33,))],
+        cost=10**8,
+    )(in_hbm(off_blocks), tables, r_new, arrived[0])
     z = call(
         functools.partial(final_kernel, swaps),
         [kept],

time: 71.4 us -> 68.6 us (0.961)
  the two profiles are of different devices: /device:TPU:20 before, /device:TPU:0 now
where the time goes in v7:
time: 68.6 us; the launch traced here: 68.4 us
  starting transfers between devices  25.9 us (38%)
  Pallas kernels  22.8 us (33%)
  blocking collectives  12.2 us (18%)
  waiting for transfers between devices  6.56 us (10%)
  between operations  0.88 us (1%)
    ppermute x28, starting transfers between devices, exchange(): lax.ppermute(piece, 'gx', swap[-1])  21.3 us
    all_to_all x1, blocking collectives, per_device(): sums = lax.all_to_all(partial, 'gx', 0, 0, tiled=True)  12.2 us
    ppermute x28, waiting for transfers between devices, exchange(): lax.ppermute(piece, 'gx', swap[-1])  5.53 us
    pallas_call x5, Pallas kernels, early(): call(functools.partial(early_kernel, colour, wanted), long + [SMEM((4, 12...  5.29 us
    all_to_all x1, starting transfers between devices, per_device(): sums = lax.all_to_all(partial, 'gx', 0, 0, tiled=True)  4.56 us
    pallas_call x1, Pallas kernels, per_device(): call(functools.partial(image_kernel, swaps, tiles), [off_kept, kept, vec(...  3.47 us
    pallas_call x3, Pallas kernels, per_device(): call(functools.partial(forward_kernel, swaps, colour), long + [kept] * (2...  2.81 us
    pallas_call x1, Pallas kernels, per_device(): call(load_kernel, [off_kept, HBM((32, 8, 128), F32)], [HBM, SMEM, VMEM, V...  1.75 us
  transfers between devices with their start and end apart: 29, of which 12 were waited for; matrix products, arithmetic and copies ran while one was open for 0% of the time, Pallas kernels for 15%

profile of v7, /device:TPU:0, one launch (start us, length us, event | category | flops | bytes accessed | tf_op | source)
XLA Modules:
  0.0 68.4 jit_solution(8812396337854057768)
XLA Ops:
  0.6 0.0 copy-start
  0.7 1.2 %shard_map.191 = (f32[32,8,128]{2,1,0:T(8,128)S(1)}, s32[6,1,16]{2,1,0:T(1,128)S(4)}, bf16[144,128]{1,0:T(8,128)(2,1)S(1)}, bf16[144,128]{1,0:T(8,128)(2,1)S(1)}...) custom-call(f32[32,8,128]{2,1,0:T(8,128)} %q_hbm.1, s32[6,1,16]{2,1,0:T(1,128)} %bitcast.3, s32[32]{0:T(128)} %colours_hbm.3), custom_call_target="tpu_custom_call" | custom-call | flops 10000000000 | tf_op jit(solution)/shard_map/pallas_call | solution.py:496
  1.9 0.0 copy-start.2
  1.9 2.4 %collective-permute-start = (bf16[144,128]{1,0:T(8,128)(2,1)S(1)}, bf16[144,128]{1,0:T(8,128)(2,1)S(1)}, u32[]{:S(2)}, u32[]{:S(2)}) collective-permute-start(bf16[144,128]{1,0:T(8,128)(2,1)S(1)} %get-tuple-element.83), channel_id=1, source_target_pairs={{0,3},{1,2},{2,1},{3,0},{4,7},{5,6},{6,5},{7,4},{8,11},{9,10},{10,... | collective-permute-start | bytes 110600 | tf_op jit(solution)/shard_map/ppermute | solution.py:494
  4.4 1.6 %collective-permute-start.1 = (bf16[144,128]{1,0:T(8,128)(2,1)S(1)}, bf16[144,128]{1,0:T(8,128)(2,1)S(1)}, u32[]{:S(2)}, u32[]{:S(2)}) collective-permute-start(bf16[144,128]{1,0:T(8,128)(2,1)S(1)} %get-tuple-element.84), channel_id=1, source_target_pairs={{0,4},{1,5},{2,6},{3,7},{4,0},{5,1},{6,2},{7,3},{8,12},{9,13},{10,... | collective-permute-start | bytes 110600 | tf_op jit(solution)/shard_map/ppermute | solution.py:494
  6.0 0.4 collective-permute-start.2
  6.4 0.1 collective-permute-start.3
  6.5 1.2 %shard_map.192 = (bf16[32,9,128,128]{3,2,1,0:T(8,128)(2,1)S(1)}, s32[9,32]{1,0:T(8,128)S(4)}, s32[8,128]{1,0:T(8,128)S(4)}, f32[32,128]{1,0:T(8,128)S(1)}, f32[32,128]{1,0:T(8,128)S(1)}) custom-call(bf16[32,9,128,128]{3,2,1,0:T(8,128)(2,1)S(1)} %copy-done, s32[9,32]{1,0:T(8,128)} %bitcast.2, s32[32]{0:T(128)} %colours_hbm.3, f32[32,128]{1,0:T(8,128)S(1)} %copy-done.6, ...), custom_call_target="tpu_custom_call" | custom-call | tf_op jit(solution)/shard_map/pallas_call | solution.py:504
  7.7 0.7 %collective-permute-done.1.refs_1_ = bf16[144,128]{1,0:T(8,128)(2,1)S(1)} collective-permute-done((bf16[144,128]{1,0:T(8,128)(2,1)S(1)}, bf16[144,128]{1,0:T(8,128)(2,1)S(1)}, u32[]{:S(2)}, u32[]{:S(2)}) %collective-permute-start.1) | collective-permute-done | bytes 36896 | tf_op jit(solution)/shard_map/ppermute | solution.py:494
  8.4 0.0 copy-start.1
  8.5 0.0 copy-start.3
  8.5 0.0 copy-start.9
  8.5 3.5 %shard_map.193 = (bf16[32,9,128,128]{3,2,1,0:T(8,128)(2,1)S(1)}, f32[32,8,128]{2,1,0:T(8,128)S(1)}, f32[16,8,128]{2,1,0:T(8,128)S(1)}, s32[8,128]{1,0:T(8,128)S(4)}) custom-call(f32[32,8,128]{2,1,0:T(8,128)S(1)} %get-tuple-element.80.q.q_ref, bf16[32,128,128]{2,1,0:T(8,128)(2,1)S(1)} %copy-done.2, ...), custom_call_target="tpu_custom_call", output_to_operand_aliasing={{0}: (3, {})} | custom-call | tf_op jit(solution)/shard_map/pallas_call | solution.py:510
  12.0 12.2 %all_to_all.10.sums = f32[16,8,128]{2,1,0:T(8,128)S(1)} all-to-all(f32[16,8,128]{2,1,0:T(8,128)S(1)} %get-tuple-element.87), channel_id=1, replica_groups=mesh['groups'=2,'gx'=16] {'gx'}, dimensions={0} | all-to-all | bytes 131072 | tf_op jit(solution)/shard_map/all_to_all | solution.py:517
  24.2 1.2 %shard_map.194 = (f32[32,8,128]{2,1,0:T(8,128)S(1)}, f32[32,8,128]{2,1,0:T(8,128)S(1)}, f32[8,128]{1,0:T(8,128)S(1)}, bf16[128,128]{1,0:T(8,128)(2,1)S(1)}, bf16...) custom-call(f32[16,8,128]{2,1,0:T(8,128)S(1)} %all_to_all.10.sums, ...), custom_call_target="tpu_custom_call" | custom-call | tf_op jit(solution)/shard_map/pallas_call | solution.py:518
  25.4 0.1 collective-permute-start.4
  25.4 0.5 collective-permute-start.5
  25.9 0.1 collective-permute-start.6
  26.1 0.4 collective-permute-start.7
  26.4 0.7 shard_map.196
  27.1 1.3 %shard_map.195 = (f32[128,8,128]{2,1,0:T(8,128)S(1)}, f32[32,8,128]{2,1,0:T(8,128)S(1)}, s32[4,128]{1,0:T(4,128)S(4)}) custom-call(f32[32,8,128]{2,1,0:T(8,128)S(1)} %get-tuple-element.93.refs_0_.w.w_in, bf16[32,9,128,128]{3,2,1,0:T(8,128)(2,1)S(1)} %get-tuple-element.94.refs_1_.off.refs_2_, s32[9,32]{1,0:T(8,128)S(4)} %get-tuple-element.82.columns.refs_2_.refs_3_, ...), custom_call_target="tpu_custom_call" | custom-call | flops 100000000 | tf_op jit(solution)/shard_map/pallas_call | solution.py:535
  28.4 0.4 collective-permute-done.4.refs_0_
  28.9 0.6 collective-permute-done.5.refs_1_
  29.4 1.1 %shard_map.197 = (f32[128,8,128]{2,1,0:T(8,128)S(1)}, f32[32,8,128]{2,1,0:T(8,128)S(1)}, f32[32,8,128]{2,1,0:T(8,128)S(1)}, bf16[256,128]{1,0:T(8,128)(2,1)S(1)}...) custom-call(f32[128,8,128]{2,1,0:T(8,128)S(1)} %get-tuple-element.96, ...), custom_call_target="tpu_custom_call", output_to_operand_aliasing={{0}: (0, {}), {1}: (1, {})} | custom-call | tf_op jit(solution)/shard_map/pallas_call | solution.py:551
  30.5 0.9 %collective-permute-start.8 = (bf16[256,128]{1,0:T(8,128)(2,1)S(1)}, bf16[256,128]{1,0:T(8,128)(2,1)S(1)}, u32[]{:S(2)}, u32[]{:S(2)}) collective-permute-start(bf16[256,128]{1,0:T(8,128)(2,1)S(1)} %get-tuple-element.110), channel_id=1, source_target_pairs={{0,3},{1,2},{2,1},{3,0},{4,7},{5,6},{6,5},{7,4},{8,11},{9,10},{10,... | collective-permute-start | bytes 196616 | tf_op jit(solution)/shard_map/ppermute | solution.py:494
  31.5 1.5 %collective-permute-start.9 = (bf16[256,128]{1,0:T(8,128)(2,1)S(1)}, bf16[256,128]{1,0:T(8,128)(2,1)S(1)}, u32[]{:S(2)}, u32[]{:S(2)}) collective-permute-start(bf16[256,128]{1,0:T(8,128)(2,1)S(1)} %get-tuple-element.111), channel_id=1, source_target_pairs={{0,4},{1,5},{2,6},{3,7},{4,0},{5,1},{6,2},{7,3},{8,12},{9,13},{10,... | collective-permute-start | bytes 196616 | tf_op jit(solution)/shard_map/ppermute | solution.py:494
  32.9 0.4 collective-permute-start.10
  33.4 0.1 collective-permute-start.11
  33.5 0.8 %shard_map.198 = (f32[128,8,128]{2,1,0:T(8,128)S(1)}, f32[32,8,128]{2,1,0:T(8,128)S(1)}, s32[4,128]{1,0:T(4,128)S(4)}) custom-call(f32[128,8,128]{2,1,0:T(8,128)S(1)} %get-tuple-element.105.refs_0_, f32[32,8,128]{2,1,0:T(8,128)S(1)} %get-tuple-element.106.refs_1_.w_in, ...), custom_call_target="tpu_custom_call", output_to_operand_aliasing={{0}: (0, {})} | custom-call | flops 100000000 | tf_op jit(solution)/shard_map/pallas_call | solution.py:535
  34.3 0.7 %collective-permute-done.8.refs_0_ = bf16[256,128]{1,0:T(8,128)(2,1)S(1)} collective-permute-done((bf16[256,128]{1,0:T(8,128)(2,1)S(1)}, bf16[256,128]{1,0:T(8,128)(2,1)S(1)}, u32[]{:S(2)}, u32[]{:S(2)}) %collective-permute-start.8) | collective-permute-done | bytes 65568 | tf_op jit(solution)/shard_map/ppermute | solution.py:494
  35.0 1.2 %collective-permute-done.9.refs_1_ = bf16[256,128]{1,0:T(8,128)(2,1)S(1)} collective-permute-done((bf16[256,128]{1,0:T(8,128)(2,1)S(1)}, bf16[256,128]{1,0:T(8,128)(2,1)S(1)}, u32[]{:S(2)}, u32[]{:S(2)}) %collective-permute-start.9) | collective-permute-done | bytes 65568 | tf_op jit(solution)/shard_map/ppermute | solution.py:494
  36.2 0.8 %shard_map.199 = (f32[128,8,128]{2,1,0:T(8,128)S(1)}, f32[32,8,128]{2,1,0:T(8,128)S(1)}, f32[32,8,128]{2,1,0:T(8,128)S(1)}, bf16[128,128]{1,0:T(8,128)(2,1)S(1)}...) custom-call(f32[128,8,128]{2,1,0:T(8,128)S(1)} %get-tuple-element.10, ...), custom_call_target="tpu_custom_call", output_to_operand_aliasing={{0}: (0, {}), {1}: (1, {})} | custom-call | tf_op jit(solution)/shard_map/pallas_call | solution.py:551
  37.0 0.1 collective-permute-start.12
  37.1 2.0 %collective-permute-start.13 = (bf16[128,128]{1,0:T(8,128)(2,1)S(1)}, bf16[128,128]{1,0:T(8,128)(2,1)S(1)}, u32[]{:S(2)}, u32[]{:S(2)}) collective-permute-start(bf16[128,128]{1,0:T(8,128)(2,1)S(1)} %get-tuple-element.120), channel_id=1, source_target_pairs={{0,4},{1,5},{2,6},{3,7},{4,0},{5,1},{6,2},{7,3},{8,12},{9,13},{10,... | collective-permute-start | bytes 98312 | tf_op jit(solution)/shard_map/ppermute | solution.py:494
  39.0 0.5 collective-permute-start.14
  39.5 0.1 collective-permute-start.15
  39.6 0.8 %shard_map.200 = (f32[128,8,128]{2,1,0:T(8,128)S(1)}, f32[32,8,128]{2,1,0:T(8,128)S(1)}, s32[4,128]{1,0:T(4,128)S(4)}) custom-call(f32[128,8,128]{2,1,0:T(8,128)S(1)} %get-tuple-element.114.refs_0_, f32[32,8,128]{2,1,0:T(8,128)S(1)} %get-tuple-element.115.refs_1_.w_in, ...), custom_call_target="tpu_custom_call", output_to_operand_aliasing={{0}: (0, {})} | custom-call | flops 100000000 | tf_op jit(solution)/shard_map/pallas_call | solution.py:535
  40.3 0.1 collective-permute-done.12.refs_0_
  40.5 0.8 %collective-permute-done.13.refs_1_ = bf16[128,128]{1,0:T(8,128)(2,1)S(1)} collective-permute-done((bf16[128,128]{1,0:T(8,128)(2,1)S(1)}, bf16[128,128]{1,0:T(8,128)(2,1)S(1)}, u32[]{:S(2)}, u32[]{:S(2)}) %collective-permute-start.13) | collective-permute-done | bytes 32800 | tf_op jit(solution)/shard_map/ppermute | solution.py:494
  41.3 0.9 %shard_map.201 = (f32[128,8,128]{2,1,0:T(8,128)S(1)}, f32[32,8,128]{2,1,0:T(8,128)S(1)}, f32[32,8,128]{2,1,0:T(8,128)S(1)}, f32[32,8,128]{2,1,0:T(8,128)S(1)}, b...) custom-call(f32[128,8,128]{2,1,0:T(8,128)S(1)} %get-tuple-element.11, ...), custom_call_target="tpu_custom_call", output_to_operand_aliasing={{0}: (0, {}), {1}: (1, {})} | custom-call | tf_op jit(solution)/shard_map/pallas_call | solution.py:551
  42.2 0.7 %collective-permute-start.16 = (bf16[128,128]{1,0:T(8,128)(2,1)S(1)}, bf16[128,128]{1,0:T(8,128)(2,1)S(1)}, u32[]{:S(2)}, u32[]{:S(2)}) collective-permute-start(bf16[128,128]{1,0:T(8,128)(2,1)S(1)} %get-tuple-element.128), channel_id=1, source_target_pairs={{0,3},{1,2},{2,1},{3,0},{4,7},{5,6},{6,5},{7,4},{8,11},{9,10},{10,... | collective-permute-start | bytes 98312 | tf_op jit(solution)/shard_map/ppermute | solution.py:494
  43.0 1.9 %collective-permute-start.17 = (bf16[128,128]{1,0:T(8,128)(2,1)S(1)}, bf16[128,128]{1,0:T(8,128)(2,1)S(1)}, u32[]{:S(2)}, u32[]{:S(2)}) collective-permute-start(bf16[128,128]{1,0:T(8,128)(2,1)S(1)} %get-tuple-element.129), channel_id=1, source_target_pairs={{0,4},{1,5},{2,6},{3,7},{4,0},{5,1},{6,2},{7,3},{8,12},{9,13},{10,... | collective-permute-start | bytes 98312 | tf_op jit(solution)/shard_map/ppermute | solution.py:494
  44.9 0.9 %collective-permute-start.18 = (bf16[128,128]{1,0:T(8,128)(2,1)S(1)}, bf16[128,128]{1,0:T(8,128)(2,1)S(1)}, u32[]{:S(2)}, u32[]{:S(2)}) collective-permute-start(bf16[128,128]{1,0:T(8,128)(2,1)S(1)} %get-tuple-element.130), channel_id=1, source_target_pairs={{0,1},{1,0},{2,3},{3,2},{4,8},{5,9},{6,10},{7,11},{8,4},{9,5},{10,... | collective-permute-start | bytes 98312 | tf_op jit(solution)/shard_map/ppermute | solution.py:494
  45.8 1.0 %shard_map.202 = (f32[128,8,128]{2,1,0:T(8,128)S(1)}, f32[32,8,128]{2,1,0:T(8,128)S(1)}, s32[4,128]{1,0:T(4,128)S(4)}) custom-call(f32[32,8,128]{2,1,0:T(8,128)S(1)} %get-tuple-element.123.refs_0_.z_in, bf16[32,9,128,128]{3,2,1,0:T(8,128)(2,1)S(1)} %get-tuple-element.94.refs_1_.off.refs_2_, s32[9,32]{1,0:T(8,128)S(4)} %get-tuple-element.82.columns.refs_2_.refs_3_, ...), custom_call_target="tpu_custom_call" | custom-call | flops 100000000 | tf_op jit(solution)/shard_map/pallas_call | solution.py:535
  46.8 0.1 collective-permute-done.17.refs_1_
  46.9 0.1 collective-permute-done.19.refs_3_
  47.0 0.8 %shard_map.203 = (f32[128,8,128]{2,1,0:T(8,128)S(1)}, f32[32,8,128]{2,1,0:T(8,128)S(1)}, f32[32,8,128]{2,1,0:T(8,128)S(1)}, bf16[128,128]{1,0:T(8,128)(2,1)S(1)}...) custom-call(f32[128,8,128]{2,1,0:T(8,128)S(1)} %get-tuple-element.12, ...), custom_call_target="tpu_custom_call", output_to_operand_aliasing={{0}: (0, {}), {1}: (1, {})} | custom-call | tf_op jit(solution)/shard_map/pallas_call | solution.py:560
  47.8 0.7 %collective-permute-start.20 = (bf16[128,128]{1,0:T(8,128)(2,1)S(1)}, bf16[128,128]{1,0:T(8,128)(2,1)S(1)}, u32[]{:S(2)}, u32[]{:S(2)}) collective-permute-start(bf16[128,128]{1,0:T(8,128)(2,1)S(1)} %get-tuple-element.137), channel_id=1, source_target_pairs={{0,3},{1,2},{2,1},{3,0},{4,7},{5,6},{6,5},{7,4},{8,11},{9,10},{10,... | collective-permute-start | bytes 98312 | tf_op jit(solution)/shard_map/ppermute | solution.py:494
  48.5 1.6 %collective-permute-start.21 = (bf16[128,128]{1,0:T(8,128)(2,1)S(1)}, bf16[128,128]{1,0:T(8,128)(2,1)S(1)}, u32[]{:S(2)}, u32[]{:S(2)}) collective-permute-start(bf16[128,128]{1,0:T(8,128)(2,1)S(1)} %get-tuple-element.138), channel_id=1, source_target_pairs={{0,4},{1,5},{2,6},{3,7},{4,0},{5,1},{6,2},{7,3},{8,12},{9,13},{10,... | collective-permute-start | bytes 98312 | tf_op jit(solution)/shard_map/ppermute | solution.py:494
  50.1 0.6 collective-permute-start.22
  50.8 0.2 shard_map.205.refs_5_
  51.0 1.3 %shard_map.204 = (f32[128,8,128]{2,1,0:T(8,128)S(1)}, f32[32,8,128]{2,1,0:T(8,128)S(1)}, s32[4,128]{1,0:T(4,128)S(4)}) custom-call(f32[128,8,128]{2,1,0:T(8,128)S(1)} %get-tuple-element.132.refs_0_, f32[32,8,128]{2,1,0:T(8,128)S(1)} %get-tuple-element.133.refs_1_.z_in, ...), custom_call_target="tpu_custom_call", output_to_operand_aliasing={{0}: (0, {})} | custom-call | flops 100000000 | tf_op jit(solution)/shard_map/pallas_call | solution.py:535
  52.3 0.3 collective-permute-done.21.refs_1_
  52.6 1.5 %shard_map.206 = (f32[128,8,128]{2,1,0:T(8,128)S(1)}, f32[32,8,128]{2,1,0:T(8,128)S(1)}, f32[32,8,128]{2,1,0:T(8,128)S(1)}, bf16[128,128]{1,0:T(8,128)(2,1)S(1)}...) custom-call(f32[128,8,128]{2,1,0:T(8,128)S(1)} %get-tuple-element.13, ...), custom_call_target="tpu_custom_call", output_to_operand_aliasing={{0}: (0, {}), {1}: (1, {})} | custom-call | tf_op jit(solution)/shard_map/pallas_call | solution.py:568
  54.1 4.6 %all-to-all-start.1 = ((f32[16,16,128]{2,1,0:T(8,128)}), f32[16,16,128]{2,1,0:T(8,128)S(1)}, u32[]{:S(2)}, u32[]{:S(2)}) async-start(f32[16,16,128]{2,1,0:T(8,128)} %get-tuple-element.142), calls=%async_computation.1 | async-start | bytes 262144 | tf_op jit(solution)/shard_map/all_to_all | solution.py:574
  58.7 1.7 %collective-permute-start.24 = (bf16[128,128]{1,0:T(8,128)(2,1)S(1)}, bf16[128,128]{1,0:T(8,128)(2,1)S(1)}, u32[]{:S(2)}, u32[]{:S(2)}) collective-permute-start(bf16[128,128]{1,0:T(8,128)(2,1)S(1)} %get-tuple-element.144), channel_id=1, source_target_pairs={{0,3},{1,2},{2,1},{3,0},{4,7},{5,6},{6,5},{7,4},{8,11},{9,10},{10,... | collective-permute-start | bytes 98312 | tf_op jit(solution)/shard_map/ppermute | solution.py:494
  60.3 1.5 %collective-permute-start.25 = (bf16[128,128]{1,0:T(8,128)(2,1)S(1)}, bf16[128,128]{1,0:T(8,128)(2,1)S(1)}, u32[]{:S(2)}, u32[]{:S(2)}) collective-permute-start(bf16[128,128]{1,0:T(8,128)(2,1)S(1)} %get-tuple-element.146), channel_id=1, source_target_pairs={{0,4},{1,5},{2,6},{3,7},{4,0},{5,1},{6,2},{7,3},{8,12},{9,13},{10,... | collective-permute-start | bytes 98312 | tf_op jit(solution)/shard_map/ppermute | solution.py:494
  61.8 0.1 collective-permute-start.26
  61.9 0.5 collective-permute-start.27
  62.4 1.7 %shard_map.207 = (bf16[32,9,128,128]{3,2,1,0:T(8,128)(2,1)S(1)}, f32[32,8,128]{2,1,0:T(8,128)}) custom-call(bf16[32,9,128,128]{3,2,1,0:T(8,128)(2,1)} %off_hbm.5, s32[8,128]{1,0:T(8,128)S(4)} %get-tuple-element.91.tables.refs_3_.refs_4_, f32[32,8,128]{2,1,0:T(8,128)S(1)} %get-tuple-element.98.r_new.refs_4_, ...), custom_call_target="tpu_custom_call" | custom-call | flops 100000000 | tf_op jit(solution)/shard_map/pallas_call | solution.py:576
  64.2 0.5 collective-permute-done.25.refs_1_
  64.7 1.3 %shard_map.208.z = f32[32,8,128]{2,1,0:T(8,128)S(1)} custom-call(f32[32,8,128]{2,1,0:T(8,128)S(1)} %get-tuple-element.126.w, f32[32,8,128]{2,1,0:T(8,128)S(1)} %get-tuple-element.143.z_in, bf16[32,9,128,128]{3,2,1,0:T(8,128)(2,1)S(1)} %get-tuple-element.145.off, bf16[32,128,128]{2,1,0:T(8,128)(2,1)S(1)} %copy-done.1, ...), custom_call_target="tpu_custom_call" | custom-call | tf_op jit(solution)/shard_map/pallas_call | solution.py:583
  65.9 1.0 %all-to-all-done.1.sums = f32[16,16,128]{2,1,0:T(8,128)S(1)} async-done(((f32[16,16,128]{2,1,0:T(8,128)}), f32[16,16,128]{2,1,0:T(8,128)S(1)}, u32[]{:S(2)}, u32[]{:S(2)}) %all-to-all-start.1) | async-done | bytes 131104 | tf_op jit(solution)/shard_map/all_to_all | solution.py:574
  67.0 1.4 %shard_map.209 = (f32[32,8,128]{2,1,0:T(8,128)}, f32[32,8,128]{2,1,0:T(8,128)}, f32[32,8,128]{2,1,0:T(8,128)}, f32[3,8]{1,0:T(4,128)}) custom-call(f32[16,16,128]{2,1,0:T(8,128)S(1)} %all-to-all-done.1.sums, f32[32,8,128]{2,1,0:T(8,128)S(1)} %shard_map.208.z, f32[32,8,128]{2,1,0:T(8,128)S(1)} %get-tuple-element.80.q.q_ref, f32[32,8,128]{2,1,0:T(8,128)S(1)} %copy-done.4, ...), custom_call_target="tpu_custom_call" | custom-call | tf_op jit(solution)/shard_map/pallas_call | solution.py:590
  (38 shorter events, 0.1 us)
Async XLA Ops:
  0.6 5.8 %copy-start = (bf16[32,9,128,128]{3,2,1,0:T(8,128)(2,1)S(1)}, bf16[32,9,128,128]{3,2,1,0:T(8,128)(2,1)}, u32[]{:S(2)}) copy-start(bf16[32,9,128,128]{3,2,1,0:T(8,128)(2,1)} %off_hbm.5) | copy-start | bytes 28311556
  0.6 5.8 %copy-start.6 = (f32[32,128]{1,0:T(8,128)S(1)}, f32[32,128]{1,0:T(8,128)}, u32[]{:S(2)}) copy-start(f32[32,128]{1,0:T(8,128)} %diag_ref.1) | copy-start | bytes 49156
  0.7 5.8 %copy-start.7 = (f32[32,64]{1,0:T(8,128)S(1)}, f32[32,64]{1,0:T(8,128)}, u32[]{:S(2)}) copy-start(f32[32,64]{1,0:T(8,128)} %off_ref.1) | copy-start | bytes 24580
  0.7 5.8 %copy-start.8 = (s32[32,64]{1,0:T(8,128)S(1)}, s32[32,64]{1,0:T(8,128)}, u32[]{:S(2)}) copy-start(s32[32,64]{1,0:T(8,128)} %pairs_ref.1) | copy-start | bytes 24580
  1.9 6.5 %copy-start.2 = (bf16[32,128,128]{2,1,0:T(8,128)(2,1)S(1)}, bf16[32,128,128]{2,1,0:T(8,128)(2,1)}, u32[]{:S(2)}) copy-start(bf16[32,128,128]{2,1,0:T(8,128)(2,1)} %diag.1) | copy-start | bytes 3145732
  1.9 5.8 %collective-permute-start = (bf16[144,128]{1,0:T(8,128)(2,1)S(1)}, bf16[144,128]{1,0:T(8,128)(2,1)S(1)}, u32[]{:S(2)}, u32[]{:S(2)}) collective-permute-start(bf16[144,128]{1,0:T(8,128)(2,1)S(1)} %get-tuple-element.83), channel_id=1, source_target_pairs={{0,3},{1,2},{2,1},{3,0},{4,7},{5,6},{6,5},{7,4},{8,11},{9,10},{10,... | collective-permute-start | bytes 110600 | tf_op jit(solution)/shard_map/ppermute | solution.py:494
  4.4 4.1 %collective-permute-start.1 = (bf16[144,128]{1,0:T(8,128)(2,1)S(1)}, bf16[144,128]{1,0:T(8,128)(2,1)S(1)}, u32[]{:S(2)}, u32[]{:S(2)}) collective-permute-start(bf16[144,128]{1,0:T(8,128)(2,1)S(1)} %get-tuple-element.84), channel_id=1, source_target_pairs={{0,4},{1,5},{2,6},{3,7},{4,0},{5,1},{6,2},{7,3},{8,12},{9,13},{10,... | collective-permute-start | bytes 110600 | tf_op jit(solution)/shard_map/ppermute | solution.py:494
  6.0 2.5 %collective-permute-start.2 = (bf16[144,128]{1,0:T(8,128)(2,1)S(1)}, bf16[144,128]{1,0:T(8,128)(2,1)S(1)}, u32[]{:S(2)}, u32[]{:S(2)}) collective-permute-start(bf16[144,128]{1,0:T(8,128)(2,1)S(1)} %get-tuple-element.85), channel_id=1, source_target_pairs={{0,1},{1,0},{2,3},{3,2},{4,8},{5,9},{6,10},{7,11},{8,4},{9,5},{10,... | collective-permute-start | bytes 110600 | tf_op jit(solution)/shard_map/ppermute | solution.py:494
  6.4 2.1 %collective-permute-start.3 = (bf16[144,128]{1,0:T(8,128)(2,1)S(1)}, bf16[144,128]{1,0:T(8,128)(2,1)S(1)}, u32[]{:S(2)}, u32[]{:S(2)}) collective-permute-start(bf16[144,128]{1,0:T(8,128)(2,1)S(1)} %get-tuple-element.86), channel_id=1, source_target_pairs={{0,1},{1,0},{2,3},{3,2},{4,5},{5,4},{6,7},{7,6},{8,9},{9,8},{10,11... | collective-permute-start | bytes 110600 | tf_op jit(solution)/shard_map/ppermute | solution.py:494
  8.4 15.7 %copy-start.1 = (bf16[32,128,128]{2,1,0:T(8,128)(2,1)S(1)}, bf16[32,128,128]{2,1,0:T(8,128)(2,1)}, u32[]{:S(2)}) copy-start(bf16[32,128,128]{2,1,0:T(8,128)(2,1)} %factor.13) | copy-start | bytes 3145732
  8.5 15.7 %copy-start.3 = (f32[32,8,128]{2,1,0:T(8,128)S(1)}, f32[32,8,128]{2,1,0:T(8,128)}, u32[]{:S(2)}) copy-start(f32[32,8,128]{2,1,0:T(8,128)} %r_ref.1) | copy-start | bytes 393220
  8.5 15.7 %copy-start.9 = (f32[8]{0:T(128)S(1)}, f32[8]{0:T(128)}, u32[]{:S(2)}) copy-start(f32[8]{0:T(128)} %rho.3) | copy-start | bytes 100
  25.4 3.5 %collective-permute-start.4 = (bf16[128,128]{1,0:T(8,128)(2,1)S(1)}, bf16[128,128]{1,0:T(8,128)(2,1)S(1)}, u32[]{:S(2)}, u32[]{:S(2)}) collective-permute-start(bf16[128,128]{1,0:T(8,128)(2,1)S(1)} %get-tuple-element.100), channel_id=1, source_target_pairs={{0,3},{1,2},{2,1},{3,0},{4,7},{5,6},{6,5},{7,4},{8,11},{9,10},{10,... | collective-permute-start | bytes 98312 | tf_op jit(solution)/shard_map/ppermute | solution.py:494
  25.4 4.0 %collective-permute-start.5 = (bf16[128,128]{1,0:T(8,128)(2,1)S(1)}, bf16[128,128]{1,0:T(8,128)(2,1)S(1)}, u32[]{:S(2)}, u32[]{:S(2)}) collective-permute-start(bf16[128,128]{1,0:T(8,128)(2,1)S(1)} %get-tuple-element.101), channel_id=1, source_target_pairs={{0,4},{1,5},{2,6},{3,7},{4,0},{5,1},{6,2},{7,3},{8,12},{9,13},{10,... | collective-permute-start | bytes 98312 | tf_op jit(solution)/shard_map/ppermute | solution.py:494
  25.9 3.5 %collective-permute-start.6 = (bf16[128,128]{1,0:T(8,128)(2,1)S(1)}, bf16[128,128]{1,0:T(8,128)(2,1)S(1)}, u32[]{:S(2)}, u32[]{:S(2)}) collective-permute-start(bf16[128,128]{1,0:T(8,128)(2,1)S(1)} %get-tuple-element.102), channel_id=1, source_target_pairs={{0,1},{1,0},{2,3},{3,2},{4,8},{5,9},{6,10},{7,11},{8,4},{9,5},{10,... | collective-permute-start | bytes 98312 | tf_op jit(solution)/shard_map/ppermute | solution.py:494
  26.1 3.4 %collective-permute-start.7 = (bf16[128,128]{1,0:T(8,128)(2,1)S(1)}, bf16[128,128]{1,0:T(8,128)(2,1)S(1)}, u32[]{:S(2)}, u32[]{:S(2)}) collective-permute-start(bf16[128,128]{1,0:T(8,128)(2,1)S(1)} %get-tuple-element.103), channel_id=1, source_target_pairs={{0,1},{1,0},{2,3},{3,2},{4,5},{5,4},{6,7},{7,6},{8,9},{9,8},{10,11... | collective-permute-start | bytes 98312 | tf_op jit(solution)/shard_map/ppermute | solution.py:494
  30.5 4.5 %collective-permute-start.8 = (bf16[256,128]{1,0:T(8,128)(2,1)S(1)}, bf16[256,128]{1,0:T(8,128)(2,1)S(1)}, u32[]{:S(2)}, u32[]{:S(2)}) collective-permute-start(bf16[256,128]{1,0:T(8,128)(2,1)S(1)} %get-tuple-element.110), channel_id=1, source_target_pairs={{0,3},{1,2},{2,1},{3,0},{4,7},{5,6},{6,5},{7,4},{8,11},{9,10},{10,... | collective-permute-start | bytes 196616 | tf_op jit(solution)/shard_map/ppermute | solution.py:494
  31.5 4.7 %collective-permute-start.9 = (bf16[256,128]{1,0:T(8,128)(2,1)S(1)}, bf16[256,128]{1,0:T(8,128)(2,1)S(1)}, u32[]{:S(2)}, u32[]{:S(2)}) collective-permute-start(bf16[256,128]{1,0:T(8,128)(2,1)S(1)} %get-tuple-element.111), channel_id=1, source_target_pairs={{0,4},{1,5},{2,6},{3,7},{4,0},{5,1},{6,2},{7,3},{8,12},{9,13},{10,... | collective-permute-start | bytes 196616 | tf_op jit(solution)/shard_map/ppermute | solution.py:494
  32.9 3.2 %collective-permute-start.10 = (bf16[256,128]{1,0:T(8,128)(2,1)S(1)}, bf16[256,128]{1,0:T(8,128)(2,1)S(1)}, u32[]{:S(2)}, u32[]{:S(2)}) collective-permute-start(bf16[256,128]{1,0:T(8,128)(2,1)S(1)} %get-tuple-element.112), channel_id=1, source_target_pairs={{0,1},{1,0},{2,3},{3,2},{4,8},{5,9},{6,10},{7,11},{8,4},{9,5},{10,... | collective-permute-start | bytes 196616 | tf_op jit(solution)/shard_map/ppermute | solution.py:494
  33.4 2.8 %collective-permute-start.11 = (bf16[256,128]{1,0:T(8,128)(2,1)S(1)}, bf16[256,128]{1,0:T(8,128)(2,1)S(1)}, u32[]{:S(2)}, u32[]{:S(2)}) collective-permute-start(bf16[256,128]{1,0:T(8,128)(2,1)S(1)} %get-tuple-element.113), channel_id=1, source_target_pairs={{0,1},{1,0},{2,3},{3,2},{4,5},{5,4},{6,7},{7,6},{8,9},{9,8},{10,11... | collective-permute-start | bytes 196616 | tf_op jit(solution)/shard_map/ppermute | solution.py:494
  37.0 3.5 %collective-permute-start.12 = (bf16[128,128]{1,0:T(8,128)(2,1)S(1)}, bf16[128,128]{1,0:T(8,128)(2,1)S(1)}, u32[]{:S(2)}, u32[]{:S(2)}) collective-permute-start(bf16[128,128]{1,0:T(8,128)(2,1)S(1)} %get-tuple-element.119), channel_id=1, source_target_pairs={{0,3},{1,2},{2,1},{3,0},{4,7},{5,6},{6,5},{7,4},{8,11},{9,10},{10,... | collective-permute-start | bytes 98312 | tf_op jit(solution)/shard_map/ppermute | solution.py:494
  37.1 4.3 %collective-permute-start.13 = (bf16[128,128]{1,0:T(8,128)(2,1)S(1)}, bf16[128,128]{1,0:T(8,128)(2,1)S(1)}, u32[]{:S(2)}, u32[]{:S(2)}) collective-permute-start(bf16[128,128]{1,0:T(8,128)(2,1)S(1)} %get-tuple-element.120), channel_id=1, source_target_pairs={{0,4},{1,5},{2,6},{3,7},{4,0},{5,1},{6,2},{7,3},{8,12},{9,13},{10,... | collective-permute-start | bytes 98312 | tf_op jit(solution)/shard_map/ppermute | solution.py:494
  39.0 2.3 %collective-permute-start.14 = (bf16[128,128]{1,0:T(8,128)(2,1)S(1)}, bf16[128,128]{1,0:T(8,128)(2,1)S(1)}, u32[]{:S(2)}, u32[]{:S(2)}) collective-permute-start(bf16[128,128]{1,0:T(8,128)(2,1)S(1)} %get-tuple-element.121), channel_id=1, source_target_pairs={{0,1},{1,0},{2,3},{3,2},{4,8},{5,9},{6,10},{7,11},{8,4},{9,5},{10,... | collective-permute-start | bytes 98312 | tf_op jit(solution)/shard_map/ppermute | solution.py:494
  39.5 1.8 %collective-permute-start.15 = (bf16[128,128]{1,0:T(8,128)(2,1)S(1)}, bf16[128,128]{1,0:T(8,128)(2,1)S(1)}, u32[]{:S(2)}, u32[]{:S(2)}) collective-permute-start(bf16[128,128]{1,0:T(8,128)(2,1)S(1)} %get-tuple-element.122), channel_id=1, source_target_pairs={{0,1},{1,0},{2,3},{3,2},{4,5},{5,4},{6,7},{7,6},{8,9},{9,8},{10,11... | collective-permute-start | bytes 98312 | tf_op jit(solution)/shard_map/ppermute | solution.py:494
  42.2 4.6 %collective-permute-start.16 = (bf16[128,128]{1,0:T(8,128)(2,1)S(1)}, bf16[128,128]{1,0:T(8,128)(2,1)S(1)}, u32[]{:S(2)}, u32[]{:S(2)}) collective-permute-start(bf16[128,128]{1,0:T(8,128)(2,1)S(1)} %get-tuple-element.128), channel_id=1, source_target_pairs={{0,3},{1,2},{2,1},{3,0},{4,7},{5,6},{6,5},{7,4},{8,11},{9,10},{10,... | collective-permute-start | bytes 98312 | tf_op jit(solution)/shard_map/ppermute | solution.py:494
  43.0 3.9 %collective-permute-start.17 = (bf16[128,128]{1,0:T(8,128)(2,1)S(1)}, bf16[128,128]{1,0:T(8,128)(2,1)S(1)}, u32[]{:S(2)}, u32[]{:S(2)}) collective-permute-start(bf16[128,128]{1,0:T(8,128)(2,1)S(1)} %get-tuple-element.129), channel_id=1, source_target_pairs={{0,4},{1,5},{2,6},{3,7},{4,0},{5,1},{6,2},{7,3},{8,12},{9,13},{10,... | collective-permute-start | bytes 98312 | tf_op jit(solution)/shard_map/ppermute | solution.py:494
  44.9 2.0 %collective-permute-start.18 = (bf16[128,128]{1,0:T(8,128)(2,1)S(1)}, bf16[128,128]{1,0:T(8,128)(2,1)S(1)}, u32[]{:S(2)}, u32[]{:S(2)}) collective-permute-start(bf16[128,128]{1,0:T(8,128)(2,1)S(1)} %get-tuple-element.130), channel_id=1, source_target_pairs={{0,1},{1,0},{2,3},{3,2},{4,8},{5,9},{6,10},{7,11},{8,4},{9,5},{10,... | collective-permute-start | bytes 98312 | tf_op jit(solution)/shard_map/ppermute | solution.py:494
  45.8 1.2 %collective-permute-start.19 = (bf16[128,128]{1,0:T(8,128)(2,1)S(1)}, bf16[128,128]{1,0:T(8,128)(2,1)S(1)}, u32[]{:S(2)}, u32[]{:S(2)}) collective-permute-start(bf16[128,128]{1,0:T(8,128)(2,1)S(1)} %get-tuple-element.131), channel_id=1, source_target_pairs={{0,1},{1,0},{2,3},{3,2},{4,5},{5,4},{6,7},{7,6},{8,9},{9,8},{10,11... | collective-permute-start | bytes 98312 | tf_op jit(solution)/shard_map/ppermute | solution.py:494
  47.8 4.5 %collective-permute-start.20 = (bf16[128,128]{1,0:T(8,128)(2,1)S(1)}, bf16[128,128]{1,0:T(8,128)(2,1)S(1)}, u32[]{:S(2)}, u32[]{:S(2)}) collective-permute-start(bf16[128,128]{1,0:T(8,128)(2,1)S(1)} %get-tuple-element.137), channel_id=1, source_target_pairs={{0,3},{1,2},{2,1},{3,0},{4,7},{5,6},{6,5},{7,4},{8,11},{9,10},{10,... | collective-permute-start | bytes 98312 | tf_op jit(solution)/shard_map/ppermute | solution.py:494
  48.5 4.1 %collective-permute-start.21 = (bf16[128,128]{1,0:T(8,128)(2,1)S(1)}, bf16[128,128]{1,0:T(8,128)(2,1)S(1)}, u32[]{:S(2)}, u32[]{:S(2)}) collective-permute-start(bf16[128,128]{1,0:T(8,128)(2,1)S(1)} %get-tuple-element.138), channel_id=1, source_target_pairs={{0,4},{1,5},{2,6},{3,7},{4,0},{5,1},{6,2},{7,3},{8,12},{9,13},{10,... | collective-permute-start | bytes 98312 | tf_op jit(solution)/shard_map/ppermute | solution.py:494
  50.1 2.5 %collective-permute-start.22 = (bf16[128,128]{1,0:T(8,128)(2,1)S(1)}, bf16[128,128]{1,0:T(8,128)(2,1)S(1)}, u32[]{:S(2)}, u32[]{:S(2)}) collective-permute-start(bf16[128,128]{1,0:T(8,128)(2,1)S(1)} %get-tuple-element.139), channel_id=1, source_target_pairs={{0,1},{1,0},{2,3},{3,2},{4,8},{5,9},{6,10},{7,11},{8,4},{9,5},{10,... | collective-permute-start | bytes 98312 | tf_op jit(solution)/shard_map/ppermute | solution.py:494
  50.8 1.8 %collective-permute-start.23 = (bf16[128,128]{1,0:T(8,128)(2,1)S(1)}, bf16[128,128]{1,0:T(8,128)(2,1)S(1)}, u32[]{:S(2)}, u32[]{:S(2)}) collective-permute-start(bf16[128,128]{1,0:T(8,128)(2,1)S(1)} %get-tuple-element.140), channel_id=1, source_target_pairs={{0,1},{1,0},{2,3},{3,2},{4,5},{5,4},{6,7},{7,6},{8,9},{9,8},{10,11... | collective-permute-start | bytes 98312 | tf_op jit(solution)/shard_map/ppermute | solution.py:494
  54.1 12.9 %all-to-all-start.1 = ((f32[16,16,128]{2,1,0:T(8,128)}), f32[16,16,128]{2,1,0:T(8,128)S(1)}, u32[]{:S(2)}, u32[]{:S(2)}) async-start(f32[16,16,128]{2,1,0:T(8,128)} %get-tuple-element.142), calls=%async_computation.1 | async-start | bytes 262144 | tf_op jit(solution)/shard_map/all_to_all | solution.py:574
  58.7 3.8 %collective-permute-start.24 = (bf16[128,128]{1,0:T(8,128)(2,1)S(1)}, bf16[128,128]{1,0:T(8,128)(2,1)S(1)}, u32[]{:S(2)}, u32[]{:S(2)}) collective-permute-start(bf16[128,128]{1,0:T(8,128)(2,1)S(1)} %get-tuple-element.144), channel_id=1, source_target_pairs={{0,3},{1,2},{2,1},{3,0},{4,7},{5,6},{6,5},{7,4},{8,11},{9,10},{10,... | collective-permute-start | bytes 98312 | tf_op jit(solution)/shard_map/ppermute | solution.py:494
  60.3 4.3 %collective-permute-start.25 = (bf16[128,128]{1,0:T(8,128)(2,1)S(1)}, bf16[128,128]{1,0:T(8,128)(2,1)S(1)}, u32[]{:S(2)}, u32[]{:S(2)}) collective-permute-start(bf16[128,128]{1,0:T(8,128)(2,1)S(1)} %get-tuple-element.146), channel_id=1, source_target_pairs={{0,4},{1,5},{2,6},{3,7},{4,0},{5,1},{6,2},{7,3},{8,12},{9,13},{10,... | collective-permute-start | bytes 98312 | tf_op jit(solution)/shard_map/ppermute | solution.py:494
  61.8 2.8 %collective-permute-start.26 = (bf16[128,128]{1,0:T(8,128)(2,1)S(1)}, bf16[128,128]{1,0:T(8,128)(2,1)S(1)}, u32[]{:S(2)}, u32[]{:S(2)}) collective-permute-start(bf16[128,128]{1,0:T(8,128)(2,1)S(1)} %get-tuple-element.147), channel_id=1, source_target_pairs={{0,1},{1,0},{2,3},{3,2},{4,8},{5,9},{6,10},{7,11},{8,4},{9,5},{10,... | collective-permute-start | bytes 98312 | tf_op jit(solution)/shard_map/ppermute | solution.py:494
  61.9 5.1 %copy-start.4 = (f32[32,8,128]{2,1,0:T(8,128)S(1)}, f32[32,8,128]{2,1,0:T(8,128)}, u32[]{:S(2)}) copy-start(f32[32,8,128]{2,1,0:T(8,128)} %x_ref.1) | copy-start | bytes 393220
  61.9 5.1 %copy-start.5 = (f32[32,8,128]{2,1,0:T(8,128)S(1)}, f32[32,8,128]{2,1,0:T(8,128)}, u32[]{:S(2)}) copy-start(f32[32,8,128]{2,1,0:T(8,128)} %d_ref.1) | copy-start | bytes 393220
  61.9 5.1 %copy-start.10 = (f32[8]{0:T(128)S(1)}, f32[8]{0:T(128)}, u32[]{:S(2)}) copy-start(f32[8]{0:T(128)} %tau.1) | copy-start | bytes 100
  61.9 5.1 %copy-start.11 = (f32[8]{0:T(128)S(1)}, f32[8]{0:T(128)}, u32[]{:S(2)}) copy-start(f32[8]{0:T(128)} %theta_in.1) | copy-start | bytes 100
  61.9 2.8 %collective-permute-start.27 = (bf16[128,128]{1,0:T(8,128)(2,1)S(1)}, bf16[128,128]{1,0:T(8,128)(2,1)S(1)}, u32[]{:S(2)}, u32[]{:S(2)}) collective-permute-start(bf16[128,128]{1,0:T(8,128)(2,1)S(1)} %get-tuple-element.148), channel_id=1, source_target_pairs={{0,1},{1,0},{2,3},{3,2},{4,5},{5,4},{6,7},{7,6},{8,9},{9,8},{10,11... | collective-permute-start | bytes 98312 | tf_op jit(solution)/shard_map/ppermute | solution.py:494

commit v8 on v7

--- a/solution.py
+++ b/solution.py
@@ -18,7 +18,7 @@
 SOLVE = (16,)
 LATE = 8
 PART = 4
-PARTS = (0, 16, 24, 32)
+PARTS = (0, 16, 32)
 
 
 def swap_pairs(axis, stride, extent, phase, tiles):
@@ -346,7 +346,6 @@
     if colour == 1:
         adjoint, others = others[0], others[1:]
     extended, rest, w, sent = others[0], others[1], others[2], others[3:]
-    w[...] = w_in[...]
     couple_late(swaps, arrived, extended, rest, off, columns, late)
 
     def solve(blocks, places):
@@ -380,7 +379,6 @@
         r_new, total, terms, partial = others[0], others[1], others[2], others[-1]
         others = others[3:-1]
     extended, rest, z, sent = others[0], others[1], others[2], others[3:]
-    z[...] = z_in[...]
     couple_late(swaps, arrived, extended, rest, off, columns, late)
 
     def solve(blocks, places):
@@ -405,7 +403,6 @@
 def final_kernel(swaps, w, z_in, off, factor, straight, crossed, columns, tables, faces, *refs):
     n = len(swaps)
     arrived, (z, extended, rest) = refs[:n], refs[n:]
-    z[...] = z_in[...]
     extend(swaps, z_in, arrived, extended)
 
     def couple(blocks, places):
@@ -552,7 +549,7 @@
             functools.partial(forward_kernel, swaps, colour),
             long + [kept] * (2 if colour == 3 else 1) + ([vec(256, 128, dtype=BF16)] * n if colour == 1 else pieces),
             [VMEM] * 4 + fixed_places + [SMEM] + [VMEM] * (n + 1 if colour == 1 else n),
-            aliases={0: 0, 1: 1},
+            aliases={0: 0, 1: 1, 3: 2},
         )(extended, rest, r_new, w, *fixed, late, *arrived, *([adjoint] if colour == 1 else []))
     z, *sent = sent
     arrived = exchange(sent)
@@ -561,7 +558,7 @@
         functools.partial(backward_kernel, swaps, tiles, 2),
         long + [kept] + pieces,
         [VMEM] * 4 + fixed_places + [SMEM] + [VMEM] * n,
-        aliases={0: 0, 1: 1},
+        aliases={0: 0, 1: 1, 3: 2},
     )(extended, rest, w, z, *fixed, late, *arrived)
     arrived = exchange(sent)
     extended, rest, late = early(1, 2, z, extended)
@@ -569,7 +566,7 @@
         functools.partial(backward_kernel, swaps, tiles, 1),
         long + [kept] + pieces + [vec(tiles, 16, 128)],
         [VMEM] * 4 + fixed_places + [SMEM] + [VMEM] * (n + 3),
-        aliases={0: 0, 1: 1},
+        aliases={0: 0, 1: 1, 3: 2},
     )(extended, rest, w, z, *fixed, late, *arrived, r_new, total, terms)
     sums = lax.all_to_all(partial, "gx", 0, 0, tiled=True)
     arrived = exchange(sent)
@@ -585,6 +582,7 @@
         [kept],
         [VMEM] * 2 + fixed_places + [VMEM] * n,
         scratch,
+        aliases={1: 0},
     )(w, z, off, *fixed[1:], *arrived)[0]
     block_vec = vec(32, 8, 128)
     x_new, q_new, d_new, scalars = call(

time: 68.6 us -> 68.1 us (level)
  waiting for transfers between devices: 6.56 us -> 5.82 us
  Pallas kernels: 22.8 us -> 23.5 us
    pallas_call x5, Pallas kernels: 5.29 us -> 5.98 us  [early(): call(functools.partial(early_kernel, colour, wanted), long + [SMEM((4, 12...]
  transfers between devices with their start and end apart: 29 -> 29, of which waited for: 12 -> 9; matrix products, arithmetic and copies ran while one was open for 0% -> 0% of each run, Pallas kernels for 15% -> 17%
where the time goes in v8:
time: 68.1 us; the launch traced here: 67.8 us
  starting transfers between devices  25.4 us (37%)
  Pallas kernels  23.5 us (35%)
  blocking collectives  12.2 us (18%)
  waiting for transfers between devices  5.82 us (9%)
  between operations  0.88 us (1%)
    ppermute x28, starting transfers between devices, exchange(): lax.ppermute(piece, 'gx', swap[-1])  21.2 us
    all_to_all x1, blocking collectives, per_device(): sums = lax.all_to_all(partial, 'gx', 0, 0, tiled=True)  12.2 us
    pallas_call x5, Pallas kernels, early(): call(functools.partial(early_kernel, colour, wanted), long + [SMEM((4, 12...  5.98 us
    ppermute x28, waiting for transfers between devices, exchange(): lax.ppermute(piece, 'gx', swap[-1])  5.07 us
    all_to_all x1, starting transfers between devices, per_device(): sums = lax.all_to_all(partial, 'gx', 0, 0, tiled=True)  4.15 us
    pallas_call x1, Pallas kernels, per_device(): call(functools.partial(image_kernel, swaps, tiles), [off_kept, kept, vec(...  3.35 us
    pallas_call x3, Pallas kernels, per_device(): call(functools.partial(forward_kernel, swaps, colour), long + [kept] * (2...  2.55 us
    pallas_call x1, Pallas kernels, per_device(): call(load_kernel, [off_kept, HBM((32, 8, 128), F32)], [HBM, SMEM, VMEM, V...  1.84 us
  transfers between devices with their start and end apart: 29, of which 9 were waited for; matrix products, arithmetic and copies ran while one was open for 0% of the time, Pallas kernels for 17%

profile of v8, /device:TPU:0, one launch (start us, length us, event | category | flops | bytes accessed | tf_op | source)
XLA Modules:
  0.0 67.8 jit_solution(7464312528636805893)
XLA Ops:
  0.6 0.0 copy-start
  0.7 1.2 %shard_map.191 = (f32[32,8,128]{2,1,0:T(8,128)S(1)}, s32[6,1,16]{2,1,0:T(1,128)S(4)}, bf16[144,128]{1,0:T(8,128)(2,1)S(1)}, bf16[144,128]{1,0:T(8,128)(2,1)S(1)}...) custom-call(f32[32,8,128]{2,1,0:T(8,128)} %q_hbm.1, s32[6,1,16]{2,1,0:T(1,128)} %bitcast.3, s32[32]{0:T(128)} %colours_hbm.3), custom_call_target="tpu_custom_call" | custom-call | flops 10000000000 | tf_op jit(solution)/shard_map/pallas_call | solution.py:493
  1.9 0.0 copy-start.2
  1.9 2.4 %collective-permute-start = (bf16[144,128]{1,0:T(8,128)(2,1)S(1)}, bf16[144,128]{1,0:T(8,128)(2,1)S(1)}, u32[]{:S(2)}, u32[]{:S(2)}) collective-permute-start(bf16[144,128]{1,0:T(8,128)(2,1)S(1)} %get-tuple-element.83), channel_id=1, source_target_pairs={{0,3},{1,2},{2,1},{3,0},{4,7},{5,6},{6,5},{7,4},{8,11},{9,10},{10,... | collective-permute-start | bytes 110600 | tf_op jit(solution)/shard_map/ppermute | solution.py:491
  4.4 1.6 %collective-permute-start.1 = (bf16[144,128]{1,0:T(8,128)(2,1)S(1)}, bf16[144,128]{1,0:T(8,128)(2,1)S(1)}, u32[]{:S(2)}, u32[]{:S(2)}) collective-permute-start(bf16[144,128]{1,0:T(8,128)(2,1)S(1)} %get-tuple-element.84), channel_id=1, source_target_pairs={{0,4},{1,5},{2,6},{3,7},{4,0},{5,1},{6,2},{7,3},{8,12},{9,13},{10,... | collective-permute-start | bytes 110600 | tf_op jit(solution)/shard_map/ppermute | solution.py:491
  6.0 0.4 collective-permute-start.2
  6.4 0.1 collective-permute-start.3
  6.5 1.2 %shard_map.192 = (bf16[32,9,128,128]{3,2,1,0:T(8,128)(2,1)S(1)}, s32[9,32]{1,0:T(8,128)S(4)}, s32[8,128]{1,0:T(8,128)S(4)}, f32[32,128]{1,0:T(8,128)S(1)}, f32[32,128]{1,0:T(8,128)S(1)}) custom-call(bf16[32,9,128,128]{3,2,1,0:T(8,128)(2,1)S(1)} %copy-done, s32[9,32]{1,0:T(8,128)} %bitcast.2, s32[32]{0:T(128)} %colours_hbm.3, f32[32,128]{1,0:T(8,128)S(1)} %copy-done.6, ...), custom_call_target="tpu_custom_call" | custom-call | tf_op jit(solution)/shard_map/pallas_call | solution.py:501
  7.7 0.0 collective-permute-done.refs_0_
  7.7 0.7 %collective-permute-done.1.refs_1_ = bf16[144,128]{1,0:T(8,128)(2,1)S(1)} collective-permute-done((bf16[144,128]{1,0:T(8,128)(2,1)S(1)}, bf16[144,128]{1,0:T(8,128)(2,1)S(1)}, u32[]{:S(2)}, u32[]{:S(2)}) %collective-permute-start.1) | collective-permute-done | bytes 36896 | tf_op jit(solution)/shard_map/ppermute | solution.py:491
  8.4 0.0 collective-permute-done.2.refs_2_
  8.4 0.0 copy-start.1
  8.5 0.0 copy-start.3
  8.5 0.0 copy-start.9
  8.5 3.3 %shard_map.193 = (bf16[32,9,128,128]{3,2,1,0:T(8,128)(2,1)S(1)}, f32[32,8,128]{2,1,0:T(8,128)S(1)}, f32[16,8,128]{2,1,0:T(8,128)S(1)}, s32[8,128]{1,0:T(8,128)S(4)}) custom-call(f32[32,8,128]{2,1,0:T(8,128)S(1)} %get-tuple-element.80.q.q_ref, bf16[32,128,128]{2,1,0:T(8,128)(2,1)S(1)} %copy-done.2, ...), custom_call_target="tpu_custom_call", output_to_operand_aliasing={{0}: (3, {})} | custom-call | tf_op jit(solution)/shard_map/pallas_call | solution.py:507
  11.8 12.2 %all_to_all.10.sums = f32[16,8,128]{2,1,0:T(8,128)S(1)} all-to-all(f32[16,8,128]{2,1,0:T(8,128)S(1)} %get-tuple-element.87), channel_id=1, replica_groups=mesh['groups'=2,'gx'=16] {'gx'}, dimensions={0} | all-to-all | bytes 131072 | tf_op jit(solution)/shard_map/all_to_all | solution.py:514
  24.1 1.2 %shard_map.194 = (f32[32,8,128]{2,1,0:T(8,128)S(1)}, f32[32,8,128]{2,1,0:T(8,128)S(1)}, f32[8,128]{1,0:T(8,128)S(1)}, bf16[128,128]{1,0:T(8,128)(2,1)S(1)}, bf16...) custom-call(f32[16,8,128]{2,1,0:T(8,128)S(1)} %all_to_all.10.sums, ...), custom_call_target="tpu_custom_call" | custom-call | tf_op jit(solution)/shard_map/pallas_call | solution.py:515
  25.2 0.1 collective-permute-start.4
  25.3 0.5 collective-permute-start.5
  25.8 0.1 collective-permute-start.6
  26.0 0.4 collective-permute-start.7
  26.3 0.7 shard_map.196
  27.0 0.8 %shard_map.195 = (f32[128,8,128]{2,1,0:T(8,128)S(1)}, f32[32,8,128]{2,1,0:T(8,128)S(1)}, s32[4,128]{1,0:T(4,128)S(4)}) custom-call(f32[32,8,128]{2,1,0:T(8,128)S(1)} %get-tuple-element.93.refs_0_.w.w_in, bf16[32,9,128,128]{3,2,1,0:T(8,128)(2,1)S(1)} %get-tuple-element.94.refs_1_.off.refs_2_, s32[9,32]{1,0:T(8,128)S(4)} %get-tuple-element.82.columns.refs_2_.refs_3_, ...), custom_call_target="tpu_custom_call" | custom-call | flops 100000000 | tf_op jit(solution)/shard_map/pallas_call | solution.py:532
  27.8 0.9 %collective-permute-done.4.refs_0_ = bf16[128,128]{1,0:T(8,128)(2,1)S(1)} collective-permute-done((bf16[128,128]{1,0:T(8,128)(2,1)S(1)}, bf16[128,128]{1,0:T(8,128)(2,1)S(1)}, u32[]{:S(2)}, u32[]{:S(2)}) %collective-permute-start.4) | collective-permute-done | bytes 32800 | tf_op jit(solution)/shard_map/ppermute | solution.py:491
  28.7 0.6 collective-permute-done.5.refs_1_
  29.3 0.8 %shard_map.197 = (f32[128,8,128]{2,1,0:T(8,128)S(1)}, f32[32,8,128]{2,1,0:T(8,128)S(1)}, f32[32,8,128]{2,1,0:T(8,128)S(1)}, bf16[256,128]{1,0:T(8,128)(2,1)S(1)}...) custom-call(f32[128,8,128]{2,1,0:T(8,128)S(1)} %get-tuple-element.96, ...), custom_call_target="tpu_custom_call", output_to_operand_aliasing={{0}: (0, {}), {1}: (1, {}), {2}: (3, {})} | custom-call | tf_op jit(solution)/shard_map/pallas_call | solution.py:548
  30.2 1.2 %collective-permute-start.8 = (bf16[256,128]{1,0:T(8,128)(2,1)S(1)}, bf16[256,128]{1,0:T(8,128)(2,1)S(1)}, u32[]{:S(2)}, u32[]{:S(2)}) collective-permute-start(bf16[256,128]{1,0:T(8,128)(2,1)S(1)} %get-tuple-element.110), channel_id=1, source_target_pairs={{0,3},{1,2},{2,1},{3,0},{4,7},{5,6},{6,5},{7,4},{8,11},{9,10},{10,... | collective-permute-start | bytes 196616 | tf_op jit(solution)/shard_map/ppermute | solution.py:491
  31.4 1.5 %collective-permute-start.9 = (bf16[256,128]{1,0:T(8,128)(2,1)S(1)}, bf16[256,128]{1,0:T(8,128)(2,1)S(1)}, u32[]{:S(2)}, u32[]{:S(2)}) collective-permute-start(bf16[256,128]{1,0:T(8,128)(2,1)S(1)} %get-tuple-element.111), channel_id=1, source_target_pairs={{0,4},{1,5},{2,6},{3,7},{4,0},{5,1},{6,2},{7,3},{8,12},{9,13},{10,... | collective-permute-start | bytes 196616 | tf_op jit(solution)/shard_map/ppermute | solution.py:491
  32.8 0.4 collective-permute-start.10
  33.2 0.1 collective-permute-start.11
  33.3 1.6 %shard_map.198 = (f32[128,8,128]{2,1,0:T(8,128)S(1)}, f32[32,8,128]{2,1,0:T(8,128)S(1)}, s32[4,128]{1,0:T(4,128)S(4)}) custom-call(f32[128,8,128]{2,1,0:T(8,128)S(1)} %get-tuple-element.105.refs_0_, f32[32,8,128]{2,1,0:T(8,128)S(1)} %get-tuple-element.106.refs_1_.w_in, ...), custom_call_target="tpu_custom_call", output_to_operand_aliasing={{0}: (0, {})} | custom-call | flops 100000000 | tf_op jit(solution)/shard_map/pallas_call | solution.py:532
  34.9 0.9 %collective-permute-done.9.refs_1_ = bf16[256,128]{1,0:T(8,128)(2,1)S(1)} collective-permute-done((bf16[256,128]{1,0:T(8,128)(2,1)S(1)}, bf16[256,128]{1,0:T(8,128)(2,1)S(1)}, u32[]{:S(2)}, u32[]{:S(2)}) %collective-permute-start.9) | collective-permute-done | bytes 65568 | tf_op jit(solution)/shard_map/ppermute | solution.py:491
  35.8 0.8 %shard_map.199 = (f32[128,8,128]{2,1,0:T(8,128)S(1)}, f32[32,8,128]{2,1,0:T(8,128)S(1)}, f32[32,8,128]{2,1,0:T(8,128)S(1)}, bf16[128,128]{1,0:T(8,128)(2,1)S(1)}...) custom-call(f32[128,8,128]{2,1,0:T(8,128)S(1)} %get-tuple-element.10, ...), custom_call_target="tpu_custom_call", output_to_operand_aliasing={{0}: (0, {}), {1}: (1, {}), {2}: (3, {})} | custom-call | tf_op jit(solution)/shard_map/pallas_call | solution.py:548
  36.6 0.6 collective-permute-start.12
  37.2 1.7 %collective-permute-start.13 = (bf16[128,128]{1,0:T(8,128)(2,1)S(1)}, bf16[128,128]{1,0:T(8,128)(2,1)S(1)}, u32[]{:S(2)}, u32[]{:S(2)}) collective-permute-start(bf16[128,128]{1,0:T(8,128)(2,1)S(1)} %get-tuple-element.120), channel_id=1, source_target_pairs={{0,4},{1,5},{2,6},{3,7},{4,0},{5,1},{6,2},{7,3},{8,12},{9,13},{10,... | collective-permute-start | bytes 98312 | tf_op jit(solution)/shard_map/ppermute | solution.py:491
  38.9 0.4 collective-permute-start.14
  39.4 0.1 collective-permute-start.15
  39.4 1.1 %shard_map.200 = (f32[128,8,128]{2,1,0:T(8,128)S(1)}, f32[32,8,128]{2,1,0:T(8,128)S(1)}, s32[4,128]{1,0:T(4,128)S(4)}) custom-call(f32[128,8,128]{2,1,0:T(8,128)S(1)} %get-tuple-element.114.refs_0_, f32[32,8,128]{2,1,0:T(8,128)S(1)} %get-tuple-element.115.refs_1_.w_in, ...), custom_call_target="tpu_custom_call", output_to_operand_aliasing={{0}: (0, {})} | custom-call | flops 100000000 | tf_op jit(solution)/shard_map/pallas_call | solution.py:532
  40.5 0.7 %collective-permute-done.13.refs_1_ = bf16[128,128]{1,0:T(8,128)(2,1)S(1)} collective-permute-done((bf16[128,128]{1,0:T(8,128)(2,1)S(1)}, bf16[128,128]{1,0:T(8,128)(2,1)S(1)}, u32[]{:S(2)}, u32[]{:S(2)}) %collective-permute-start.13) | collective-permute-done | bytes 32800 | tf_op jit(solution)/shard_map/ppermute | solution.py:491
  41.2 0.9 %shard_map.201 = (f32[128,8,128]{2,1,0:T(8,128)S(1)}, f32[32,8,128]{2,1,0:T(8,128)S(1)}, f32[32,8,128]{2,1,0:T(8,128)S(1)}, f32[32,8,128]{2,1,0:T(8,128)S(1)}, b...) custom-call(f32[128,8,128]{2,1,0:T(8,128)S(1)} %get-tuple-element.11, ...), custom_call_target="tpu_custom_call", output_to_operand_aliasing={{0}: (0, {}), {1}: (1, {}), {2}: (3, {})} | custom-call | tf_op jit(solution)/shard_map/pallas_call | solution.py:548
  42.1 0.5 collective-permute-start.16
  42.6 2.6 %collective-permute-start.17 = (bf16[128,128]{1,0:T(8,128)(2,1)S(1)}, bf16[128,128]{1,0:T(8,128)(2,1)S(1)}, u32[]{:S(2)}, u32[]{:S(2)}) collective-permute-start(bf16[128,128]{1,0:T(8,128)(2,1)S(1)} %get-tuple-element.129), channel_id=1, source_target_pairs={{0,4},{1,5},{2,6},{3,7},{4,0},{5,1},{6,2},{7,3},{8,12},{9,13},{10,... | collective-permute-start | bytes 98312 | tf_op jit(solution)/shard_map/ppermute | solution.py:491
  45.2 0.5 collective-permute-start.19
  45.7 1.7 %shard_map.202 = (f32[128,8,128]{2,1,0:T(8,128)S(1)}, f32[32,8,128]{2,1,0:T(8,128)S(1)}, s32[4,128]{1,0:T(4,128)S(4)}) custom-call(f32[32,8,128]{2,1,0:T(8,128)S(1)} %get-tuple-element.123.refs_0_.z_in, bf16[32,9,128,128]{3,2,1,0:T(8,128)(2,1)S(1)} %get-tuple-element.94.refs_1_.off.refs_2_, s32[9,32]{1,0:T(8,128)S(4)} %get-tuple-element.82.columns.refs_2_.refs_3_, ...), custom_call_target="tpu_custom_call" | custom-call | flops 100000000 | tf_op jit(solution)/shard_map/pallas_call | solution.py:532
  47.5 0.8 %shard_map.203 = (f32[128,8,128]{2,1,0:T(8,128)S(1)}, f32[32,8,128]{2,1,0:T(8,128)S(1)}, f32[32,8,128]{2,1,0:T(8,128)S(1)}, bf16[128,128]{1,0:T(8,128)(2,1)S(1)}...) custom-call(f32[128,8,128]{2,1,0:T(8,128)S(1)} %get-tuple-element.12, ...), custom_call_target="tpu_custom_call", output_to_operand_aliasing={{0}: (0, {}), {1}: (1, {}), {2}: (3, {})} | custom-call | tf_op jit(solution)/shard_map/pallas_call | solution.py:557
  48.3 0.2 collective-permute-start.20
  48.5 1.6 %collective-permute-start.21 = (bf16[128,128]{1,0:T(8,128)(2,1)S(1)}, bf16[128,128]{1,0:T(8,128)(2,1)S(1)}, u32[]{:S(2)}, u32[]{:S(2)}) collective-permute-start(bf16[128,128]{1,0:T(8,128)(2,1)S(1)} %get-tuple-element.138), channel_id=1, source_target_pairs={{0,4},{1,5},{2,6},{3,7},{4,0},{5,1},{6,2},{7,3},{8,12},{9,13},{10,... | collective-permute-start | bytes 98312 | tf_op jit(solution)/shard_map/ppermute | solution.py:491
  50.1 0.2 collective-permute-start.22
  50.4 0.3 collective-permute-start.23
  50.6 0.2 shard_map.205.refs_5_
  50.8 0.8 %shard_map.204 = (f32[128,8,128]{2,1,0:T(8,128)S(1)}, f32[32,8,128]{2,1,0:T(8,128)S(1)}, s32[4,128]{1,0:T(4,128)S(4)}) custom-call(f32[128,8,128]{2,1,0:T(8,128)S(1)} %get-tuple-element.132.refs_0_, f32[32,8,128]{2,1,0:T(8,128)S(1)} %get-tuple-element.133.refs_1_.z_in, ...), custom_call_target="tpu_custom_call", output_to_operand_aliasing={{0}: (0, {})} | custom-call | flops 100000000 | tf_op jit(solution)/shard_map/pallas_call | solution.py:532
  51.6 0.3 collective-permute-done.20.refs_0_
  51.9 0.5 collective-permute-done.21.refs_1_
  52.5 1.5 %shard_map.206 = (f32[128,8,128]{2,1,0:T(8,128)S(1)}, f32[32,8,128]{2,1,0:T(8,128)S(1)}, f32[32,8,128]{2,1,0:T(8,128)S(1)}, bf16[128,128]{1,0:T(8,128)(2,1)S(1)}...) custom-call(f32[128,8,128]{2,1,0:T(8,128)S(1)} %get-tuple-element.13, ...), custom_call_target="tpu_custom_call", output_to_operand_aliasing={{0}: (0, {}), {1}: (1, {}), {2}: (3, {})} | custom-call | tf_op jit(solution)/shard_map/pallas_call | solution.py:565
  54.0 4.2 %all-to-all-start.1 = ((f32[16,16,128]{2,1,0:T(8,128)}), f32[16,16,128]{2,1,0:T(8,128)S(1)}, u32[]{:S(2)}, u32[]{:S(2)}) async-start(f32[16,16,128]{2,1,0:T(8,128)} %get-tuple-element.142), calls=%async_computation.1 | async-start | bytes 262144 | tf_op jit(solution)/shard_map/all_to_all | solution.py:571
  58.1 1.7 %collective-permute-start.24 = (bf16[128,128]{1,0:T(8,128)(2,1)S(1)}, bf16[128,128]{1,0:T(8,128)(2,1)S(1)}, u32[]{:S(2)}, u32[]{:S(2)}) collective-permute-start(bf16[128,128]{1,0:T(8,128)(2,1)S(1)} %get-tuple-element.144), channel_id=1, source_target_pairs={{0,3},{1,2},{2,1},{3,0},{4,7},{5,6},{6,5},{7,4},{8,11},{9,10},{10,... | collective-permute-start | bytes 98312 | tf_op jit(solution)/shard_map/ppermute | solution.py:491
  59.8 1.5 %collective-permute-start.25 = (bf16[128,128]{1,0:T(8,128)(2,1)S(1)}, bf16[128,128]{1,0:T(8,128)(2,1)S(1)}, u32[]{:S(2)}, u32[]{:S(2)}) collective-permute-start(bf16[128,128]{1,0:T(8,128)(2,1)S(1)} %get-tuple-element.146), channel_id=1, source_target_pairs={{0,4},{1,5},{2,6},{3,7},{4,0},{5,1},{6,2},{7,3},{8,12},{9,13},{10,... | collective-permute-start | bytes 98312 | tf_op jit(solution)/shard_map/ppermute | solution.py:491
  61.3 0.1 collective-permute-start.26
  61.4 0.5 collective-permute-start.27
  61.9 1.8 %shard_map.207 = (bf16[32,9,128,128]{3,2,1,0:T(8,128)(2,1)S(1)}, f32[32,8,128]{2,1,0:T(8,128)}) custom-call(bf16[32,9,128,128]{3,2,1,0:T(8,128)(2,1)} %off_hbm.5, s32[8,128]{1,0:T(8,128)S(4)} %get-tuple-element.91.tables.refs_3_.refs_4_, f32[32,8,128]{2,1,0:T(8,128)S(1)} %get-tuple-element.98.r_new.refs_4_, ...), custom_call_target="tpu_custom_call" | custom-call | flops 100000000 | tf_op jit(solution)/shard_map/pallas_call | solution.py:573
  63.7 0.4 collective-permute-done.25.refs_1_
  64.1 1.5 %shard_map.208.z = f32[32,8,128]{2,1,0:T(8,128)S(1)} custom-call(f32[32,8,128]{2,1,0:T(8,128)S(1)} %get-tuple-element.126.w, f32[32,8,128]{2,1,0:T(8,128)S(1)} %get-tuple-element.143.z_in, bf16[32,9,128,128]{3,2,1,0:T(8,128)(2,1)S(1)} %get-tuple-element.145.off, bf16[32,128,128]{2,1,0:T(8,128)(2,1)S(1)} %copy-done.1, ...), custom_call_target="tpu_custom_call", output_to_operand_aliasing={{}: (1, {})} | custom-call | tf_op jit(solution)/shard_map/pallas_call | solution.py:580
  65.7 0.8 %all-to-all-done.1.sums = f32[16,16,128]{2,1,0:T(8,128)S(1)} async-done(((f32[16,16,128]{2,1,0:T(8,128)}), f32[16,16,128]{2,1,0:T(8,128)S(1)}, u32[]{:S(2)}, u32[]{:S(2)}) %all-to-all-start.1) | async-done | bytes 131104 | tf_op jit(solution)/shard_map/all_to_all | solution.py:571
  66.4 1.4 %shard_map.209 = (f32[32,8,128]{2,1,0:T(8,128)}, f32[32,8,128]{2,1,0:T(8,128)}, f32[32,8,128]{2,1,0:T(8,128)}, f32[3,8]{1,0:T(4,128)}) custom-call(f32[16,16,128]{2,1,0:T(8,128)S(1)} %all-to-all-done.1.sums, f32[32,8,128]{2,1,0:T(8,128)S(1)} %shard_map.208.z, f32[32,8,128]{2,1,0:T(8,128)S(1)} %get-tuple-element.80.q.q_ref, f32[32,8,128]{2,1,0:T(8,128)S(1)} %copy-done.4, ...), custom_call_target="tpu_custom_call" | custom-call | tf_op jit(solution)/shard_map/pallas_call | solution.py:588
  (38 shorter events, 0.1 us)
Async XLA Ops:
  0.6 5.8 %copy-start = (bf16[32,9,128,128]{3,2,1,0:T(8,128)(2,1)S(1)}, bf16[32,9,128,128]{3,2,1,0:T(8,128)(2,1)}, u32[]{:S(2)}) copy-start(bf16[32,9,128,128]{3,2,1,0:T(8,128)(2,1)} %off_hbm.5) | copy-start | bytes 28311556
  0.6 5.8 %copy-start.6 = (f32[32,128]{1,0:T(8,128)S(1)}, f32[32,128]{1,0:T(8,128)}, u32[]{:S(2)}) copy-start(f32[32,128]{1,0:T(8,128)} %diag_ref.1) | copy-start | bytes 49156
  0.7 5.8 %copy-start.7 = (f32[32,64]{1,0:T(8,128)S(1)}, f32[32,64]{1,0:T(8,128)}, u32[]{:S(2)}) copy-start(f32[32,64]{1,0:T(8,128)} %off_ref.1) | copy-start | bytes 24580
  0.7 5.8 %copy-start.8 = (s32[32,64]{1,0:T(8,128)S(1)}, s32[32,64]{1,0:T(8,128)}, u32[]{:S(2)}) copy-start(s32[32,64]{1,0:T(8,128)} %pairs_ref.1) | copy-start | bytes 24580
  1.9 6.5 %copy-start.2 = (bf16[32,128,128]{2,1,0:T(8,128)(2,1)S(1)}, bf16[32,128,128]{2,1,0:T(8,128)(2,1)}, u32[]{:S(2)}) copy-start(bf16[32,128,128]{2,1,0:T(8,128)(2,1)} %diag.1) | copy-start | bytes 3145732
  1.9 5.8 %collective-permute-start = (bf16[144,128]{1,0:T(8,128)(2,1)S(1)}, bf16[144,128]{1,0:T(8,128)(2,1)S(1)}, u32[]{:S(2)}, u32[]{:S(2)}) collective-permute-start(bf16[144,128]{1,0:T(8,128)(2,1)S(1)} %get-tuple-element.83), channel_id=1, source_target_pairs={{0,3},{1,2},{2,1},{3,0},{4,7},{5,6},{6,5},{7,4},{8,11},{9,10},{10,... | collective-permute-start | bytes 110600 | tf_op jit(solution)/shard_map/ppermute | solution.py:491
  4.4 4.1 %collective-permute-start.1 = (bf16[144,128]{1,0:T(8,128)(2,1)S(1)}, bf16[144,128]{1,0:T(8,128)(2,1)S(1)}, u32[]{:S(2)}, u32[]{:S(2)}) collective-permute-start(bf16[144,128]{1,0:T(8,128)(2,1)S(1)} %get-tuple-element.84), channel_id=1, source_target_pairs={{0,4},{1,5},{2,6},{3,7},{4,0},{5,1},{6,2},{7,3},{8,12},{9,13},{10,... | collective-permute-start | bytes 110600 | tf_op jit(solution)/shard_map/ppermute | solution.py:491
  6.0 2.5 %collective-permute-start.2 = (bf16[144,128]{1,0:T(8,128)(2,1)S(1)}, bf16[144,128]{1,0:T(8,128)(2,1)S(1)}, u32[]{:S(2)}, u32[]{:S(2)}) collective-permute-start(bf16[144,128]{1,0:T(8,128)(2,1)S(1)} %get-tuple-element.85), channel_id=1, source_target_pairs={{0,1},{1,0},{2,3},{3,2},{4,8},{5,9},{6,10},{7,11},{8,4},{9,5},{10,... | collective-permute-start | bytes 110600 | tf_op jit(solution)/shard_map/ppermute | solution.py:491
  6.4 2.1 %collective-permute-start.3 = (bf16[144,128]{1,0:T(8,128)(2,1)S(1)}, bf16[144,128]{1,0:T(8,128)(2,1)S(1)}, u32[]{:S(2)}, u32[]{:S(2)}) collective-permute-start(bf16[144,128]{1,0:T(8,128)(2,1)S(1)} %get-tuple-element.86), channel_id=1, source_target_pairs={{0,1},{1,0},{2,3},{3,2},{4,5},{5,4},{6,7},{7,6},{8,9},{9,8},{10,11... | collective-permute-start | bytes 110600 | tf_op jit(solution)/shard_map/ppermute | solution.py:491
  8.4 15.6 %copy-start.1 = (bf16[32,128,128]{2,1,0:T(8,128)(2,1)S(1)}, bf16[32,128,128]{2,1,0:T(8,128)(2,1)}, u32[]{:S(2)}) copy-start(bf16[32,128,128]{2,1,0:T(8,128)(2,1)} %factor.13) | copy-start | bytes 3145732
  8.5 15.6 %copy-start.3 = (f32[32,8,128]{2,1,0:T(8,128)S(1)}, f32[32,8,128]{2,1,0:T(8,128)}, u32[]{:S(2)}) copy-start(f32[32,8,128]{2,1,0:T(8,128)} %r_ref.1) | copy-start | bytes 393220
  8.5 15.6 %copy-start.9 = (f32[8]{0:T(128)S(1)}, f32[8]{0:T(128)}, u32[]{:S(2)}) copy-start(f32[8]{0:T(128)} %rho.3) | copy-start | bytes 100
  25.2 3.5 %collective-permute-start.4 = (bf16[128,128]{1,0:T(8,128)(2,1)S(1)}, bf16[128,128]{1,0:T(8,128)(2,1)S(1)}, u32[]{:S(2)}, u32[]{:S(2)}) collective-permute-start(bf16[128,128]{1,0:T(8,128)(2,1)S(1)} %get-tuple-element.100), channel_id=1, source_target_pairs={{0,3},{1,2},{2,1},{3,0},{4,7},{5,6},{6,5},{7,4},{8,11},{9,10},{10,... | collective-permute-start | bytes 98312 | tf_op jit(solution)/shard_map/ppermute | solution.py:491
  25.3 4.0 %collective-permute-start.5 = (bf16[128,128]{1,0:T(8,128)(2,1)S(1)}, bf16[128,128]{1,0:T(8,128)(2,1)S(1)}, u32[]{:S(2)}, u32[]{:S(2)}) collective-permute-start(bf16[128,128]{1,0:T(8,128)(2,1)S(1)} %get-tuple-element.101), channel_id=1, source_target_pairs={{0,4},{1,5},{2,6},{3,7},{4,0},{5,1},{6,2},{7,3},{8,12},{9,13},{10,... | collective-permute-start | bytes 98312 | tf_op jit(solution)/shard_map/ppermute | solution.py:491
  25.8 3.5 %collective-permute-start.6 = (bf16[128,128]{1,0:T(8,128)(2,1)S(1)}, bf16[128,128]{1,0:T(8,128)(2,1)S(1)}, u32[]{:S(2)}, u32[]{:S(2)}) collective-permute-start(bf16[128,128]{1,0:T(8,128)(2,1)S(1)} %get-tuple-element.102), channel_id=1, source_target_pairs={{0,1},{1,0},{2,3},{3,2},{4,8},{5,9},{6,10},{7,11},{8,4},{9,5},{10,... | collective-permute-start | bytes 98312 | tf_op jit(solution)/shard_map/ppermute | solution.py:491
  26.0 3.4 %collective-permute-start.7 = (bf16[128,128]{1,0:T(8,128)(2,1)S(1)}, bf16[128,128]{1,0:T(8,128)(2,1)S(1)}, u32[]{:S(2)}, u32[]{:S(2)}) collective-permute-start(bf16[128,128]{1,0:T(8,128)(2,1)S(1)} %get-tuple-element.103), channel_id=1, source_target_pairs={{0,1},{1,0},{2,3},{3,2},{4,5},{5,4},{6,7},{7,6},{8,9},{9,8},{10,11... | collective-permute-start | bytes 98312 | tf_op jit(solution)/shard_map/ppermute | solution.py:491
  30.2 4.8 %collective-permute-start.8 = (bf16[256,128]{1,0:T(8,128)(2,1)S(1)}, bf16[256,128]{1,0:T(8,128)(2,1)S(1)}, u32[]{:S(2)}, u32[]{:S(2)}) collective-permute-start(bf16[256,128]{1,0:T(8,128)(2,1)S(1)} %get-tuple-element.110), channel_id=1, source_target_pairs={{0,3},{1,2},{2,1},{3,0},{4,7},{5,6},{6,5},{7,4},{8,11},{9,10},{10,... | collective-permute-start | bytes 196616 | tf_op jit(solution)/shard_map/ppermute | solution.py:491
  31.4 4.4 %collective-permute-start.9 = (bf16[256,128]{1,0:T(8,128)(2,1)S(1)}, bf16[256,128]{1,0:T(8,128)(2,1)S(1)}, u32[]{:S(2)}, u32[]{:S(2)}) collective-permute-start(bf16[256,128]{1,0:T(8,128)(2,1)S(1)} %get-tuple-element.111), channel_id=1, source_target_pairs={{0,4},{1,5},{2,6},{3,7},{4,0},{5,1},{6,2},{7,3},{8,12},{9,13},{10,... | collective-permute-start | bytes 196616 | tf_op jit(solution)/shard_map/ppermute | solution.py:491
  32.8 3.0 %collective-permute-start.10 = (bf16[256,128]{1,0:T(8,128)(2,1)S(1)}, bf16[256,128]{1,0:T(8,128)(2,1)S(1)}, u32[]{:S(2)}, u32[]{:S(2)}) collective-permute-start(bf16[256,128]{1,0:T(8,128)(2,1)S(1)} %get-tuple-element.112), channel_id=1, source_target_pairs={{0,1},{1,0},{2,3},{3,2},{4,8},{5,9},{6,10},{7,11},{8,4},{9,5},{10,... | collective-permute-start | bytes 196616 | tf_op jit(solution)/shard_map/ppermute | solution.py:491
  33.2 2.6 %collective-permute-start.11 = (bf16[256,128]{1,0:T(8,128)(2,1)S(1)}, bf16[256,128]{1,0:T(8,128)(2,1)S(1)}, u32[]{:S(2)}, u32[]{:S(2)}) collective-permute-start(bf16[256,128]{1,0:T(8,128)(2,1)S(1)} %get-tuple-element.113), channel_id=1, source_target_pairs={{0,1},{1,0},{2,3},{3,2},{4,5},{5,4},{6,7},{7,6},{8,9},{9,8},{10,11... | collective-permute-start | bytes 196616 | tf_op jit(solution)/shard_map/ppermute | solution.py:491
  36.6 3.9 %collective-permute-start.12 = (bf16[128,128]{1,0:T(8,128)(2,1)S(1)}, bf16[128,128]{1,0:T(8,128)(2,1)S(1)}, u32[]{:S(2)}, u32[]{:S(2)}) collective-permute-start(bf16[128,128]{1,0:T(8,128)(2,1)S(1)} %get-tuple-element.119), channel_id=1, source_target_pairs={{0,3},{1,2},{2,1},{3,0},{4,7},{5,6},{6,5},{7,4},{8,11},{9,10},{10,... | collective-permute-start | bytes 98312 | tf_op jit(solution)/shard_map/ppermute | solution.py:491
  37.2 4.0 %collective-permute-start.13 = (bf16[128,128]{1,0:T(8,128)(2,1)S(1)}, bf16[128,128]{1,0:T(8,128)(2,1)S(1)}, u32[]{:S(2)}, u32[]{:S(2)}) collective-permute-start(bf16[128,128]{1,0:T(8,128)(2,1)S(1)} %get-tuple-element.120), channel_id=1, source_target_pairs={{0,4},{1,5},{2,6},{3,7},{4,0},{5,1},{6,2},{7,3},{8,12},{9,13},{10,... | collective-permute-start | bytes 98312 | tf_op jit(solution)/shard_map/ppermute | solution.py:491
  38.9 2.3 %collective-permute-start.14 = (bf16[128,128]{1,0:T(8,128)(2,1)S(1)}, bf16[128,128]{1,0:T(8,128)(2,1)S(1)}, u32[]{:S(2)}, u32[]{:S(2)}) collective-permute-start(bf16[128,128]{1,0:T(8,128)(2,1)S(1)} %get-tuple-element.121), channel_id=1, source_target_pairs={{0,1},{1,0},{2,3},{3,2},{4,8},{5,9},{6,10},{7,11},{8,4},{9,5},{10,... | collective-permute-start | bytes 98312 | tf_op jit(solution)/shard_map/ppermute | solution.py:491
  39.4 1.8 %collective-permute-start.15 = (bf16[128,128]{1,0:T(8,128)(2,1)S(1)}, bf16[128,128]{1,0:T(8,128)(2,1)S(1)}, u32[]{:S(2)}, u32[]{:S(2)}) collective-permute-start(bf16[128,128]{1,0:T(8,128)(2,1)S(1)} %get-tuple-element.122), channel_id=1, source_target_pairs={{0,1},{1,0},{2,3},{3,2},{4,5},{5,4},{6,7},{7,6},{8,9},{9,8},{10,11... | collective-permute-start | bytes 98312 | tf_op jit(solution)/shard_map/ppermute | solution.py:491
  42.1 5.3 %collective-permute-start.16 = (bf16[128,128]{1,0:T(8,128)(2,1)S(1)}, bf16[128,128]{1,0:T(8,128)(2,1)S(1)}, u32[]{:S(2)}, u32[]{:S(2)}) collective-permute-start(bf16[128,128]{1,0:T(8,128)(2,1)S(1)} %get-tuple-element.128), channel_id=1, source_target_pairs={{0,3},{1,2},{2,1},{3,0},{4,7},{5,6},{6,5},{7,4},{8,11},{9,10},{10,... | collective-permute-start | bytes 98312 | tf_op jit(solution)/shard_map/ppermute | solution.py:491
  42.6 4.8 %collective-permute-start.17 = (bf16[128,128]{1,0:T(8,128)(2,1)S(1)}, bf16[128,128]{1,0:T(8,128)(2,1)S(1)}, u32[]{:S(2)}, u32[]{:S(2)}) collective-permute-start(bf16[128,128]{1,0:T(8,128)(2,1)S(1)} %get-tuple-element.129), channel_id=1, source_target_pairs={{0,4},{1,5},{2,6},{3,7},{4,0},{5,1},{6,2},{7,3},{8,12},{9,13},{10,... | collective-permute-start | bytes 98312 | tf_op jit(solution)/shard_map/ppermute | solution.py:491
  45.2 2.2 %collective-permute-start.18 = (bf16[128,128]{1,0:T(8,128)(2,1)S(1)}, bf16[128,128]{1,0:T(8,128)(2,1)S(1)}, u32[]{:S(2)}, u32[]{:S(2)}) collective-permute-start(bf16[128,128]{1,0:T(8,128)(2,1)S(1)} %get-tuple-element.130), channel_id=1, source_target_pairs={{0,1},{1,0},{2,3},{3,2},{4,8},{5,9},{6,10},{7,11},{8,4},{9,5},{10,... | collective-permute-start | bytes 98312 | tf_op jit(solution)/shard_map/ppermute | solution.py:491
  45.2 2.3 %collective-permute-start.19 = (bf16[128,128]{1,0:T(8,128)(2,1)S(1)}, bf16[128,128]{1,0:T(8,128)(2,1)S(1)}, u32[]{:S(2)}, u32[]{:S(2)}) collective-permute-start(bf16[128,128]{1,0:T(8,128)(2,1)S(1)} %get-tuple-element.131), channel_id=1, source_target_pairs={{0,1},{1,0},{2,3},{3,2},{4,5},{5,4},{6,7},{7,6},{8,9},{9,8},{10,11... | collective-permute-start | bytes 98312 | tf_op jit(solution)/shard_map/ppermute | solution.py:491
  48.3 3.6 %collective-permute-start.20 = (bf16[128,128]{1,0:T(8,128)(2,1)S(1)}, bf16[128,128]{1,0:T(8,128)(2,1)S(1)}, u32[]{:S(2)}, u32[]{:S(2)}) collective-permute-start(bf16[128,128]{1,0:T(8,128)(2,1)S(1)} %get-tuple-element.137), channel_id=1, source_target_pairs={{0,3},{1,2},{2,1},{3,0},{4,7},{5,6},{6,5},{7,4},{8,11},{9,10},{10,... | collective-permute-start | bytes 98312 | tf_op jit(solution)/shard_map/ppermute | solution.py:491
  48.5 3.9 %collective-permute-start.21 = (bf16[128,128]{1,0:T(8,128)(2,1)S(1)}, bf16[128,128]{1,0:T(8,128)(2,1)S(1)}, u32[]{:S(2)}, u32[]{:S(2)}) collective-permute-start(bf16[128,128]{1,0:T(8,128)(2,1)S(1)} %get-tuple-element.138), channel_id=1, source_target_pairs={{0,4},{1,5},{2,6},{3,7},{4,0},{5,1},{6,2},{7,3},{8,12},{9,13},{10,... | collective-permute-start | bytes 98312 | tf_op jit(solution)/shard_map/ppermute | solution.py:491
  50.1 2.4 %collective-permute-start.22 = (bf16[128,128]{1,0:T(8,128)(2,1)S(1)}, bf16[128,128]{1,0:T(8,128)(2,1)S(1)}, u32[]{:S(2)}, u32[]{:S(2)}) collective-permute-start(bf16[128,128]{1,0:T(8,128)(2,1)S(1)} %get-tuple-element.139), channel_id=1, source_target_pairs={{0,1},{1,0},{2,3},{3,2},{4,8},{5,9},{6,10},{7,11},{8,4},{9,5},{10,... | collective-permute-start | bytes 98312 | tf_op jit(solution)/shard_map/ppermute | solution.py:491
  50.4 2.1 %collective-permute-start.23 = (bf16[128,128]{1,0:T(8,128)(2,1)S(1)}, bf16[128,128]{1,0:T(8,128)(2,1)S(1)}, u32[]{:S(2)}, u32[]{:S(2)}) collective-permute-start(bf16[128,128]{1,0:T(8,128)(2,1)S(1)} %get-tuple-element.140), channel_id=1, source_target_pairs={{0,1},{1,0},{2,3},{3,2},{4,5},{5,4},{6,7},{7,6},{8,9},{9,8},{10,11... | collective-permute-start | bytes 98312 | tf_op jit(solution)/shard_map/ppermute | solution.py:491
  54.0 12.5 %all-to-all-start.1 = ((f32[16,16,128]{2,1,0:T(8,128)}), f32[16,16,128]{2,1,0:T(8,128)S(1)}, u32[]{:S(2)}, u32[]{:S(2)}) async-start(f32[16,16,128]{2,1,0:T(8,128)} %get-tuple-element.142), calls=%async_computation.1 | async-start | bytes 262144 | tf_op jit(solution)/shard_map/all_to_all | solution.py:571
  58.1 3.8 %collective-permute-start.24 = (bf16[128,128]{1,0:T(8,128)(2,1)S(1)}, bf16[128,128]{1,0:T(8,128)(2,1)S(1)}, u32[]{:S(2)}, u32[]{:S(2)}) collective-permute-start(bf16[128,128]{1,0:T(8,128)(2,1)S(1)} %get-tuple-element.144), channel_id=1, source_target_pairs={{0,3},{1,2},{2,1},{3,0},{4,7},{5,6},{6,5},{7,4},{8,11},{9,10},{10,... | collective-permute-start | bytes 98312 | tf_op jit(solution)/shard_map/ppermute | solution.py:491
  59.8 4.3 %collective-permute-start.25 = (bf16[128,128]{1,0:T(8,128)(2,1)S(1)}, bf16[128,128]{1,0:T(8,128)(2,1)S(1)}, u32[]{:S(2)}, u32[]{:S(2)}) collective-permute-start(bf16[128,128]{1,0:T(8,128)(2,1)S(1)} %get-tuple-element.146), channel_id=1, source_target_pairs={{0,4},{1,5},{2,6},{3,7},{4,0},{5,1},{6,2},{7,3},{8,12},{9,13},{10,... | collective-permute-start | bytes 98312 | tf_op jit(solution)/shard_map/ppermute | solution.py:491
  61.3 2.8 %collective-permute-start.26 = (bf16[128,128]{1,0:T(8,128)(2,1)S(1)}, bf16[128,128]{1,0:T(8,128)(2,1)S(1)}, u32[]{:S(2)}, u32[]{:S(2)}) collective-permute-start(bf16[128,128]{1,0:T(8,128)(2,1)S(1)} %get-tuple-element.147), channel_id=1, source_target_pairs={{0,1},{1,0},{2,3},{3,2},{4,8},{5,9},{6,10},{7,11},{8,4},{9,5},{10,... | collective-permute-start | bytes 98312 | tf_op jit(solution)/shard_map/ppermute | solution.py:491
  61.3 5.1 %copy-start.4 = (f32[32,8,128]{2,1,0:T(8,128)S(1)}, f32[32,8,128]{2,1,0:T(8,128)}, u32[]{:S(2)}) copy-start(f32[32,8,128]{2,1,0:T(8,128)} %x_ref.1) | copy-start | bytes 393220
  61.3 5.1 %copy-start.5 = (f32[32,8,128]{2,1,0:T(8,128)S(1)}, f32[32,8,128]{2,1,0:T(8,128)}, u32[]{:S(2)}) copy-start(f32[32,8,128]{2,1,0:T(8,128)} %d_ref.1) | copy-start | bytes 393220
  61.3 5.1 %copy-start.10 = (f32[8]{0:T(128)S(1)}, f32[8]{0:T(128)}, u32[]{:S(2)}) copy-start(f32[8]{0:T(128)} %tau.1) | copy-start | bytes 100
  61.4 5.1 %copy-start.11 = (f32[8]{0:T(128)S(1)}, f32[8]{0:T(128)}, u32[]{:S(2)}) copy-start(f32[8]{0:T(128)} %theta_in.1) | copy-start | bytes 100
  61.4 2.8 %collective-permute-start.27 = (bf16[128,128]{1,0:T(8,128)(2,1)S(1)}, bf16[128,128]{1,0:T(8,128)(2,1)S(1)}, u32[]{:S(2)}, u32[]{:S(2)}) collective-permute-start(bf16[128,128]{1,0:T(8,128)(2,1)S(1)} %get-tuple-element.148), channel_id=1, source_target_pairs={{0,1},{1,0},{2,3},{3,2},{4,5},{5,4},{6,7},{7,6},{8,9},{9,8},{10,11... | collective-permute-start | bytes 98312 | tf_op jit(solution)/shard_map/ppermute | solution.py:491
